TPU v7x, 128 devices: a whole 4x4x4 slice. The times are simulated.
128 devices in a mesh: queue: 8 (over y_lo, x), spatial: 16 (over y_hi, z, core).
Axes of the slice: x: 4, y: 4 (y_hi: 2, y_lo: 2; y = y_hi * 2 + y_lo), z: 4, core: 2. Of those that a mesh axis runs over, the one named last changes fastest.
Arguments:
- hidden: bfloat16 [16, 1024, 5120], P('queue', 'spatial'), may hold values from -6 to 6
- queries: bfloat16 [16, 1024, 4096], P('queue', 'spatial'), may hold values from -6 to 6, as said below
- keys: bfloat16 [16, 1024, 4096], P('queue', 'spatial'), may hold values from -6 to 6, as said below
- values: bfloat16 [16, 1024, 4096], P('queue', 'spatial'), may hold values from -6 to 6
- out_weight: bfloat16 [4096, 5120], P('spatial', 'queue'), may hold values from -5 to 5
- gate_table: float32 [50, 5120], P(None, 'queue'), may hold values from 0.5 to 2
- levels: int32 [16], replicated, may hold values from 0 to 49
- entering: bfloat16 [1024, 5120], P('spatial'), may hold values from -6 to 6
Outputs:
- next_queue: bfloat16 [16, 1024, 5120], P('queue', 'spatial')
Inputs may be any that keep to these rules, and one draw needn't show every extreme that they name: `queries`: queries are of order one, with absolute values up to 6. `keys`: keys are of order one, with absolute values up to 6.
All inputs are finite; a program needn't handle non-finite values.
Results may differ from a plain program's by a relative error of at most 0.0057.
Values may be sent and summed in bfloat16 or wider, within the bound.
No kernel may reach another device: no remote copies, remote signals or barrier semaphores. Data moves between devices by JAX's collectives and lax.ppermute only.
A program may use at most 64 MiB of HBM per device.

v0:
```python
import jax
import jax.numpy as jnp
from jax import lax
from jax.sharding import PartitionSpec as P

HEADS = 32
HD = 128
WMAX = 2


NEG_FILL = -1e30


def with_halo(array, sides, width):
    for axis, dim in sides:
        devices, length = (lax.axis_size(axis), array.shape[dim])
        up = [(i, (i + 1) % devices) for i in range(devices - 1)]
        down = [(j, i) for i, j in up]
        last = lax.slice_in_dim(array, length - width, length, axis=dim)
        initial = lax.slice_in_dim(array, 0, width, axis=dim)
        before = lax.ppermute(last, axis, up)
        after = lax.ppermute(initial, axis, down)
        array = jnp.concatenate([before, array, after], axis=dim)
    return array


def passed_along(block, axis, distance):
    devices = range(lax.axis_size(axis))
    route = [(i - distance, i) for i in devices if i - distance in devices]
    return lax.ppermute(block, axis, route)


def attend_head(query_head, key_head, value_head, allowed):
    frame_count, row_count, head_width = query_head.shape
    block_rows = min(512, row_count)
    scaling = head_width ** (-0.5)

    def one_frame(operands):
        frame_query, frame_allowed = operands
        blocks = frame_query.reshape(row_count // block_rows, block_rows, head_width)

        def one_block(query_block):
            scores = (
                jnp.einsum("qd,kd->qk", query_block, key_head, preferred_element_type=jnp.float32)
                * scaling
            )
            scores = jnp.where(frame_allowed[None, :], scores, NEG_FILL)
            row_max = jnp.max(scores, axis=1, keepdims=True)
            lifted = jnp.exp(scores - row_max)
            weights = (lifted / jnp.sum(lifted, axis=1, keepdims=True)).astype(jnp.bfloat16)
            return jnp.dot(weights, value_head, preferred_element_type=jnp.float32).astype(
                jnp.bfloat16
            )

        return lax.map(one_block, blocks).reshape(row_count, head_width)

    return lax.map(one_frame, (query_head, allowed))


def body(hidden, queries, keys, values, out_weight, gate_table, levels, entering):
    frames_dev, tok_dev, qkv_width = queries.shape
    groups = lax.axis_size("spatial")
    queue_len = lax.axis_size("queue")
    heads_dev = HEADS // groups
    position = lax.axis_index("queue")
    first_frame = position * frames_dev
    total_frames = frames_dev * queue_len
    tok_frame = tok_dev * groups
    own_frames = first_frame + jnp.arange(frames_dev, dtype=jnp.int32)
    nearby = first_frame - WMAX + jnp.arange(frames_dev + 2 * WMAX, dtype=jnp.int32)
    allowed = (
        (nearby[None, :] >= 0)
        & (nearby[None, :] < total_frames)
        & (jnp.abs(nearby[None, :] - own_frames[:, None]) <= WMAX)
    )
    allowed = jnp.repeat(allowed, tok_frame, axis=1)

    def split_heads(array):
        return array.reshape(array.shape[0], tok_dev, groups, heads_dev, HD)

    query = lax.all_to_all(split_heads(queries), "spatial", split_axis=2, concat_axis=1, tiled=True)
    keyset = lax.all_to_all(split_heads(keys), "spatial", split_axis=2, concat_axis=1, tiled=True)
    valueset = lax.all_to_all(
        split_heads(values), "spatial", split_axis=2, concat_axis=1, tiled=True
    )
    stacked = jnp.stack((keyset, valueset))
    widened = with_halo(stacked, (("queue", 1),), WMAX)
    query_heads = jnp.moveaxis(query[:, :, 0], 2, 0)
    key_heads = jnp.moveaxis(widened[0][:, :, 0], 2, 0)
    value_heads = jnp.moveaxis(widened[1][:, :, 0], 2, 0)
    item_count = key_heads.shape[0]
    key_heads = key_heads.reshape(item_count, -1, key_heads.shape[-1])
    value_heads = value_heads.reshape(item_count, -1, value_heads.shape[-1])

    def per_head(operands):
        return attend_head(operands[0], operands[1], operands[2], allowed)

    outputs = lax.map(per_head, (query_heads, key_heads, value_heads))
    head_outputs = jnp.moveaxis(outputs, 0, 2)[:, :, None]
    token_outputs = lax.all_to_all(
        head_outputs, "spatial", split_axis=1, concat_axis=2, tiled=True
    ).reshape(frames_dev, tok_dev, qkv_width)
    weight_block = lax.all_gather(out_weight, "spatial", axis=0, tiled=True)
    level_count = gate_table.shape[0]
    projected = jnp.einsum(
        "ftc,cd->ftd",
        lax.all_gather(token_outputs, "queue", axis=0, tiled=True),
        weight_block,
        preferred_element_type=jnp.float32,
    )
    selector = (levels[:, None] == jnp.arange(level_count, dtype=jnp.int32)[None, :]).astype(
        jnp.float32
    )
    gates = jnp.dot(
        selector, gate_table, precision=lax.Precision.HIGHEST, preferred_element_type=jnp.float32
    )
    branch_all = (gates[:, None, :] * projected).astype(jnp.bfloat16)
    returned = lax.all_to_all(branch_all, "queue", split_axis=0, concat_axis=2, tiled=True)
    updated = (hidden.astype(jnp.float32) + returned.astype(jnp.float32)).astype(jnp.bfloat16)
    advanced = passed_along(updated[frames_dev - 1 :], "queue", 1)
    first_slot = jnp.where(position == 0, entering[None], advanced)
    return jnp.concatenate((first_slot, updated[: frames_dev - 1]), 0)


def solution(mesh):
    return jax.shard_map(
        body,
        mesh=mesh,
        in_specs=(
            P("queue", "spatial", None),
            P("queue", "spatial", None),
            P("queue", "spatial", None),
            P("queue", "spatial", None),
            P("spatial", "queue"),
            P(None, "queue"),
            P(),
            P("spatial", None),
        ),
        out_specs=P("queue", "spatial", None),
        check_vma=False,
    )
```

profile of v0, /device:TPU:0, one launch (start us, length us, event | category | flops | bytes accessed | tf_op | source)
XLA Modules:
  0.0 395.1 jit_solution(12523391961830545642)
XLA Ops:
  6.5 1.9 reshape.57
  8.4 2.1 copy.29
  10.5 8.1 %all-to-all-start.1 = ((bf16[2,64,16,2,128]{4,3,1,0,2:T(2,128)(2,1)}), bf16[2,64,16,2,128]{4,3,1,0,2:T(2,128)(2,1)S(1)}, u32[]{:S(2)}, u32[]{:S(2)}) async-start(bf16[2,64,16,2,128]{4,3,1,0,2:T(2,128)(2,1)} %copy.29), calls=%async_computation.1 | async-start | bytes 2097152 | tf_op jit(solution)/shard_map/all_to_all | solution.py:82
  19.4 2.1 copy.31
  21.5 15.2 %all-to-all-done.1 = bf16[2,64,16,2,128]{4,3,1,0,2:T(2,128)(2,1)S(1)} async-done(((bf16[2,64,16,2,128]{4,3,1,0,2:T(2,128)(2,1)}), bf16[2,64,16,2,128]{4,3,1,0,2:T(2,128)(2,1)S(1)}, u32[]{:S(2)}, u32[]{:S(2)}) %all-to-all-start.1) | async-done | bytes 1048608 | tf_op jit(solution)/shard_map/all_to_all | solution.py:82
  36.7 3.7 all-to-all-start.2
  40.6 17.7 %all-to-all-done.2 = bf16[2,64,16,2,128]{4,3,1,0,2:T(2,128)(2,1)S(1)} async-done(((bf16[2,64,16,2,128]{4,3,1,0,2:T(2,128)(2,1)}), bf16[2,64,16,2,128]{4,3,1,0,2:T(2,128)(2,1)S(1)}, u32[]{:S(2)}, u32[]{:S(2)}) %all-to-all-start.2) | async-done | bytes 1048608 | tf_op jit(solution)/shard_map/all_to_all | solution.py:83
  58.6 1.6 pad_maximum_fusion.1
  60.2 4.7 %collective-permute-start = (bf16[2,2,1024,1,2,128]{5,2,4,1,3,0:T(8,128)(2,1)}, bf16[2,2,1024,1,2,128]{5,2,4,1,3,0:T(8,128)(2,1)}, u32[]{:S(2)}, u32[]{:S(2)}) collective-permute-start(bf16[2,2,1024,1,2,128]{5,2,4,1,3,0:T(8,128)(2,1)} %pad_maximum_fusion.1), channel_id=1, source_target_pairs={{0,16},{16,32},{32,48},{48,64},{64,80},{80,96},{96,112},{1,17},{17... | collective-permute-start | bytes 6291464 | tf_op jit(solution)/shard_map/ppermute | solution.py:21
  64.9 1.3 collective-permute-start.1
  66.2 1.8 reshape.56
  68.0 1.4 copy.27
  69.4 3.7 all-to-all-start
  74.6 53.0 %all-to-all-done = bf16[2,64,16,2,128]{4,1,0,3,2:T(8,128)(2,1)S(1)} async-done(((bf16[2,64,16,2,128]{4,1,0,3,2:T(8,128)(2,1)}), bf16[2,64,16,2,128]{4,1,0,3,2:T(8,128)(2,1)S(1)}, u32[]{:S(2)}, u32[]{:S(2)}) %all-to-all-start) | async-done | bytes 1048608 | tf_op jit(solution)/shard_map/all_to_all | solution.py:81
  127.6 1.1 copy.28
  128.7 3.3 pad_maximum_fusion
  132.6 1.9 copy.33
  134.6 1.9 copy.34
  136.5 84.3 %while.34 = (s32[]{:T(128)}, bf16[2,2,1024,128]{3,1,0,2:T(2,128)(2,1)}, bf16[2,2,1024,128]{3,2,0,1:T(8,128)(2,1)}, bf16[2,6144,128]{2,1,0:T(8,128)(2,1)}, bf16[2...) while((s32[]{:T(128)}, ...), condition=%wide.region_7.8_spmd.clone, body=%wide.region_0.7_spmd.clone.sunk | while | flops 1648425984 | bytes 56964072 | solution.py:98
  136.5 3.4 dynamic-slice_bitcast_fusion.6
  139.9 1.1 dynamic-slice_bitcast_fusion.5
  141.7 35.7 %while.35 = (s32[]{:T(128)}, bf16[2,1024,128]{2,1,0:T(8,128)(2,1)S(1)}, bf16[2,1024,128]{2,1,0:T(8,128)(2,1)S(1)}, pred[2,6144]{1,0:T(4,128)(4,1)S(1)}, bf16[614...) while((s32[]{:T(128)}, ...), condition=%wide.region_6.6_spmd, body=%wide.region_1.5_spmd.sunk | while | flops 1648425984 | bytes 48537880 | solution.py:57
  141.8 17.6 %while.36 = (s32[]{:T(128)}, bf16[2,512,128]{2,1,0:T(8,128)(2,1)S(1)}, pred[6144]{0:T(1024)(128)(4,1)S(1)}, bf16[2,512,128]{2,1,0:T(8,128)(2,1)S(1)}, bf16[6144,...) while((s32[]{:T(128)}, bf16[2,512,128]{2,1,0:T(8,128)(2,1)S(1)}, ...), condition=%wide.region_5.4_spmd, body=%wide.region_2.3_spmd.sunk | while | flops 1648425984 | bytes 47476848 | solution.py:55
  141.8 2.1 fusion.32
  144.0 2.9 fusion.33
  146.8 3.8 fusion.34
  150.6 2.2 fusion.32
  152.8 2.9 fusion.33
  155.7 3.8 fusion.34
  159.6 17.6 %while.36 = (s32[]{:T(128)}, bf16[2,512,128]{2,1,0:T(8,128)(2,1)S(1)}, pred[6144]{0:T(1024)(128)(4,1)S(1)}, bf16[2,512,128]{2,1,0:T(8,128)(2,1)S(1)}, bf16[6144,...) while((s32[]{:T(128)}, bf16[2,512,128]{2,1,0:T(8,128)(2,1)S(1)}, ...), condition=%wide.region_5.4_spmd, body=%wide.region_2.3_spmd.sunk | while | flops 1648425984 | bytes 47476848 | solution.py:55
  159.7 2.1 fusion.32
  161.8 2.9 fusion.33
  164.7 3.8 fusion.34
  168.5 2.2 fusion.32
  170.6 2.9 fusion.33
  173.5 3.8 fusion.34
  177.4 1.3 copy_dynamic-update-slice_fusion.2
  178.7 3.3 dynamic-slice_bitcast_fusion.6
  182.0 1.1 dynamic-slice_bitcast_fusion.5
  183.8 35.7 %while.35 = (s32[]{:T(128)}, bf16[2,1024,128]{2,1,0:T(8,128)(2,1)S(1)}, bf16[2,1024,128]{2,1,0:T(8,128)(2,1)S(1)}, pred[2,6144]{1,0:T(4,128)(4,1)S(1)}, bf16[614...) while((s32[]{:T(128)}, ...), condition=%wide.region_6.6_spmd, body=%wide.region_1.5_spmd.sunk | while | flops 1648425984 | bytes 48537880 | solution.py:57
  183.9 17.6 %while.36 = (s32[]{:T(128)}, bf16[2,512,128]{2,1,0:T(8,128)(2,1)S(1)}, pred[6144]{0:T(1024)(128)(4,1)S(1)}, bf16[2,512,128]{2,1,0:T(8,128)(2,1)S(1)}, bf16[6144,...) while((s32[]{:T(128)}, bf16[2,512,128]{2,1,0:T(8,128)(2,1)S(1)}, ...), condition=%wide.region_5.4_spmd, body=%wide.region_2.3_spmd.sunk | while | flops 1648425984 | bytes 47476848 | solution.py:55
  183.9 2.1 fusion.32
  186.1 2.9 fusion.33
  188.9 3.8 fusion.34
  192.7 2.2 fusion.32
  194.9 2.9 fusion.33
  197.8 3.8 fusion.34
  201.7 17.6 %while.36 = (s32[]{:T(128)}, bf16[2,512,128]{2,1,0:T(8,128)(2,1)S(1)}, pred[6144]{0:T(1024)(128)(4,1)S(1)}, bf16[2,512,128]{2,1,0:T(8,128)(2,1)S(1)}, bf16[6144,...) while((s32[]{:T(128)}, bf16[2,512,128]{2,1,0:T(8,128)(2,1)S(1)}, ...), condition=%wide.region_5.4_spmd, body=%wide.region_2.3_spmd.sunk | while | flops 1648425984 | bytes 47476848 | solution.py:55
  201.8 2.1 fusion.32
  203.9 2.9 fusion.33
  206.8 3.8 fusion.34
  210.6 2.2 fusion.32
  212.7 2.9 fusion.33
  215.6 3.8 fusion.34
  219.4 1.3 copy_dynamic-update-slice_fusion.2
  220.8 22.4 %all_to_all.69 = bf16[2,1024,1,2,128]{4,0,3,2,1:T(2,128)(2,1)S(1)} all-to-all(bf16[2,1024,1,2,128]{4,0,3,2,1:T(2,128)(2,1)} %bitcast.112), channel_id=1, replica_groups=mesh['queue'=8,'spatial'=16] {'spatial'}, dimensions={1} | all-to-all | bytes 2097152 | tf_op jit(solution)/shard_map/all_to_all | solution.py:100
  243.8 1.6 reshape.62
  245.7 91.8 %all-gather.3.cloned.1.call-done = bf16[16,64,4096]{2,1,0:T(8,128)(2,1)} async-done(((bf16[2,64,4096]{2,1,0:T(8,128)(2,1)}), bf16[16,64,4096]{2,1,0:T(8,128)(2,1)}) %all-gather.3.cloned.1.call-update) | async-done | bytes 8388624 | tf_op jit(solution)/shard_map/all_gather | solution.py:107
  337.5 10.6 %multiply_convert_fusion = bf16[16,64,640]{2,1,0:T(8,128)(2,1)S(1)} fusion(bf16[16,64,4096]{2,1,0:T(8,128)(2,1)} %all-gather.3.cloned.1.call-done, bf16[4096,640]{1,0:T(8,128)(2,1)} %all-gather.5.cloned.1.call-done, f32[16,640]{1,0:T(8,128)S(1)} %fusion.18), kind=kOutput, calls=%fused_computation.31 | convolution fusion | flops 5370019840 | bytes 14983168 | tf_op jit(solution)/shard_map/ftc,cd->ftd/dot_general | solution.py:105
  348.1 21.2 %all_to_all.70 = bf16[16,64,640]{2,1,0:T(8,128)(2,1)S(1)} all-to-all(bf16[16,64,640]{2,1,0:T(8,128)(2,1)S(1)} %multiply_convert_fusion), channel_id=1, replica_groups=mesh['queue'=8,'spatial'=16] {'queue'}, dimensions={0} | all-to-all | bytes 2621440 | tf_op jit(solution)/shard_map/all_to_all | solution.py:118
  369.9 1.0 copy-done.2
  371.3 2.9 collective-permute-start.2
  374.3 12.7 %collective-permute-done.2 = bf16[1,64,5120]{2,1,0:T(8,128)(2,1)S(1)} collective-permute-done((bf16[1,64,5120]{2,1,0:T(8,128)(2,1)S(1)}, bf16[1,64,5120]{2,1,0:T(8,128)(2,1)S(1)}, u32[]{:S(2)}, u32[]{:S(2)}) %collective-permute-start.2) | collective-permute-done | bytes 655392 | tf_op jit(solution)/shard_map/ppermute | solution.py:30
  387.1 1.2 pad_maximum_fusion.2
  (70 shorter events, 7.3 us)
Async XLA Ops:
  6.5 238.9 %copy-start = (f32[50,640]{1,0:T(8,128)S(1)}, f32[50,640]{1,0:T(8,128)}, u32[]{:S(2)}) copy-start(f32[50,640]{1,0:T(8,128)} %param.19) | copy-start | bytes 384004
  6.5 12.1 %copy-start.3 = (bf16[2,64,4096]{2,1,0:T(8,128)(2,1)S(1)}, bf16[2,64,4096]{2,1,0:T(8,128)(2,1)}, u32[]{:S(2)}) copy-start(bf16[2,64,4096]{2,1,0:T(8,128)(2,1)} %param.17) | copy-start | bytes 3145732
  10.5 26.2 %all-to-all-start.1 = ((bf16[2,64,16,2,128]{4,3,1,0,2:T(2,128)(2,1)}), bf16[2,64,16,2,128]{4,3,1,0,2:T(2,128)(2,1)S(1)}, u32[]{:S(2)}, u32[]{:S(2)}) async-start(bf16[2,64,16,2,128]{4,3,1,0,2:T(2,128)(2,1)} %copy.29), calls=%async_computation.1 | async-start | bytes 2097152 | tf_op jit(solution)/shard_map/all_to_all | solution.py:82
  36.7 21.7 %all-to-all-start.2 = ((bf16[2,64,16,2,128]{4,3,1,0,2:T(2,128)(2,1)}), bf16[2,64,16,2,128]{4,3,1,0,2:T(2,128)(2,1)S(1)}, u32[]{:S(2)}, u32[]{:S(2)}) async-start(bf16[2,64,16,2,128]{4,3,1,0,2:T(2,128)(2,1)} %copy.31), calls=%async_computation.2 | async-start | bytes 2097152 | tf_op jit(solution)/shard_map/all_to_all | solution.py:83
  60.2 68.6 %collective-permute-start = (bf16[2,2,1024,1,2,128]{5,2,4,1,3,0:T(8,128)(2,1)}, bf16[2,2,1024,1,2,128]{5,2,4,1,3,0:T(8,128)(2,1)}, u32[]{:S(2)}, u32[]{:S(2)}) collective-permute-start(bf16[2,2,1024,1,2,128]{5,2,4,1,3,0:T(8,128)(2,1)} %pad_maximum_fusion.1), channel_id=1, source_target_pairs={{0,16},{16,32},{32,48},{48,64},{64,80},{80,96},{96,112},{1,17},{17... | collective-permute-start | bytes 6291464 | tf_op jit(solution)/shard_map/ppermute | solution.py:21
  64.9 63.8 %collective-permute-start.1 = (bf16[2,2,1024,1,2,128]{5,2,4,1,3,0:T(8,128)(2,1)}, bf16[2,2,1024,1,2,128]{5,2,4,1,3,0:T(8,128)(2,1)}, u32[]{:S(2)}, u32[]{:S(2)}) collective-permute-start(bf16[2,2,1024,1,2,128]{5,2,4,1,3,0:T(8,128)(2,1)} %pad_maximum_fusion.1), channel_id=1, source_target_pairs={{16,0},{32,16},{48,32},{64,48},{80,64},{96,80},{112,96},{17,1},{33... | collective-permute-start | bytes 6291464 | tf_op jit(solution)/shard_map/ppermute | solution.py:22
  69.4 58.3 %all-to-all-start = ((bf16[2,64,16,2,128]{4,1,0,3,2:T(8,128)(2,1)}), bf16[2,64,16,2,128]{4,1,0,3,2:T(8,128)(2,1)S(1)}, u32[]{:S(2)}, u32[]{:S(2)}) async-start(bf16[2,64,16,2,128]{4,1,0,3,2:T(8,128)(2,1)} %copy.27), calls=%async_computation | async-start | bytes 2097152 | tf_op jit(solution)/shard_map/all_to_all | solution.py:81
  73.0 172.7 %all-gather.5.cloned.1.call-start = ((), (), s32[]{:S(2)}) async-start(), calls=%async_computation.6 | async-start | bytes 5570560 | tf_op jit(solution)/shard_map/all_gather | solution.py:103
  73.8 263.8 %all-gather.3.cloned.1.call-start = ((), (), s32[]{:S(2)}) async-start(), calls=%async_computation.5 | async-start | bytes 9437184 | tf_op jit(solution)/shard_map/all_gather | solution.py:107
  144.0 2.9 copy-start.1
  152.8 2.9 copy-start.1
  161.8 2.9 copy-start.1
  170.6 2.9 copy-start.1
  186.1 2.9 copy-start.1
  194.9 2.9 copy-start.1
  203.9 2.9 copy-start.1
  212.7 2.9 copy-start.1
  243.2 2.3 copy-start.5
  369.6 1.3 copy-start.2
  371.0 16.0 %copy-start.4 = (bf16[64,5120]{1,0:T(8,128)(2,1)S(1)}, bf16[64,5120]{1,0:T(8,128)(2,1)}, u32[]{:S(2)}) copy-start(bf16[64,5120]{1,0:T(8,128)(2,1)} %param.21) | copy-start | bytes 1966084
  371.3 15.7 %collective-permute-start.2 = (bf16[1,64,5120]{2,1,0:T(8,128)(2,1)S(1)}, bf16[1,64,5120]{2,1,0:T(8,128)(2,1)S(1)}, u32[]{:S(2)}, u32[]{:S(2)}) collective-permute-start(bf16[1,64,5120]{2,1,0:T(8,128)(2,1)S(1)} %get-tuple-element.172), channel_id=1, source_target_pairs={{0,16},{16,32},{32,48},{48,64},{64,80},{80,96},{96,112},{1,17},{17... | collective-permute-start | bytes 1966088 | tf_op jit(solution)/shard_map/ppermute | solution.py:30
Sparse Core Ops, SparseCore 0:
  76.3 88.5 all-gather.4
  245.6 91.9 all-gather.2
where the time goes:
time: 398 us; the launch traced here: 395 us
  waiting for transfers between devices  191 us (48%)
  matrix products  58.2 us (15%)
  blocking collectives  43.6 us (11%)
  local copies, waits for them, and re-layouts  33.2 us (8%)
  other arithmetic  30.2 us (8%)
  starting transfers between devices  24.6 us (6%)
  between operations  13.7 us (3%)
    all_gather x1, waiting for transfers between devices, body(): lax.all_gather(token_outputs, 'queue', axis=0, tiled=True)  91.8 us
    all_to_all x1, waiting for transfers between devices, body(): lax.all_to_all(split_heads(queries), 'spatial', split_axis=2, concat_axis...  53 us
    dot_general x8, matrix products, one_block(): jnp.dot(weights, value_head, preferred_element_type=jnp.float32)  30.2 us
    reduce_sum x8, other arithmetic, one_block(): jnp.sum(lifted, axis=1, keepdims=True)  23 us
    all_to_all x1, blocking collectives, body(): lax.all_to_all(head_outputs, 'spatial', split_axis=1, concat_axis=2, tile...  22.4 us
    all_to_all x1, blocking collectives, body(): lax.all_to_all(branch_all, 'queue', split_axis=0, concat_axis=2, tiled=True)  21.2 us
    all_to_all x1, waiting for transfers between devices, body(): lax.all_to_all(split_heads(values), 'spatial', split_axis=2, concat_axis=...  17.7 us
    dot_general x8, matrix products, one_block(): jnp.einsum('qd,kd->qk', query_block, key_head, preferred_element_type=jnp...  17.2 us
  transfers between devices with their start and end apart: 8, of which 5 were waited for; matrix products, arithmetic and copies ran while one was open for 26% of the time, Pallas kernels for 0%

commit v1 on v0

v1 whole, which is shorter than its diff:
```python
import functools

import jax
import jax.numpy as jnp
from jax import lax
from jax.experimental import pallas as pl
from jax.experimental.pallas import tpu as pltpu
from jax.sharding import PartitionSpec as P

HEADS = 32
HD = 128
WMAX = 2
NEG_FILL = -1e30
SCALE_LOG2 = (HD ** -0.5) * 1.4426950408889634
BLOCK_Q = 512
VMEM = 48 * 1024 * 1024
QUEUE = 8
RING = 4
SPATIAL = 16
CORES = 2
PACK = 4
SPAN = 2 * WMAX + 1
ANY = pl.BlockSpec(memory_space=pl.ANY)
TOKEN = (8, 128)


def corner(array):
    rows = 8 if array.dtype == jnp.float32 else 16
    block = (1,) * (array.ndim - 2) + (rows, 128)
    return pl.BlockSpec(block, lambda *at: (0,) * array.ndim)


def pack(queries, keys, values):
    frames, tok, width = keys.shape
    group = width // SPATIAL
    piece = width // PACK
    count = SPATIAL // PACK

    def kernel(q_ref, k_ref, v_ref, kv0_ref, kv1_ref, out_ref):
        for i in range(count):
            for head, kv_ref in enumerate((kv0_ref, kv1_ref)):
                cols = slice(i * group + head * HD, i * group + (head + 1) * HD)
                kv_ref[i, 0] = k_ref[:, :, cols]
                kv_ref[i, 1] = v_ref[:, :, cols]
            out_ref[i] = q_ref[:, :, i * group : (i + 1) * group]

    spec = pl.BlockSpec((frames, tok, piece), lambda s: (0, 0, s))
    kv_spec = pl.BlockSpec((count, 2, frames, tok, HD), lambda s: (s, 0, 0, 0, 0))
    kv_shape = jax.ShapeDtypeStruct((SPATIAL, 2, frames, tok, HD), keys.dtype)
    return pl.pallas_call(
        kernel,
        grid=(PACK,),
        in_specs=[spec] * 3,
        out_specs=[kv_spec, kv_spec, pl.BlockSpec((count, frames, tok, group), lambda s: (s, 0, 0, 0))],
        out_shape=[
            kv_shape,
            kv_shape,
            jax.ShapeDtypeStruct((SPATIAL, frames, tok, group), queries.dtype),
        ],
        name="pack",
    )(queries, keys, values)


def last_frame(hidden, *earlier):
    frames, tok, width = hidden.shape

    def kernel(hidden_ref, *rest):
        rest[-1][...] = hidden_ref[...]

    return pl.pallas_call(
        kernel,
        grid=(1,),
        in_specs=[pl.BlockSpec((1, tok, width), lambda i: (frames - 1, 0, 0))]
        + [corner(e) for e in earlier],
        out_specs=pl.BlockSpec((1, tok, width), lambda i: (0, 0, 0)),
        out_shape=jax.ShapeDtypeStruct((1, tok, width), hidden.dtype),
        name="last_frame",
    )(hidden, *earlier)


def hold(array, *earlier):
    def kernel(*refs):
        pass

    return pl.pallas_call(
        kernel,
        grid=(1,),
        in_specs=[ANY] + [corner(e) for e in earlier],
        out_specs=ANY,
        out_shape=jax.ShapeDtypeStruct(array.shape, array.dtype),
        input_output_aliases={0: 0},
        name="hold",
    )(array, *earlier)


def attend(frame, head, position, query, own, before, after, partial, *earlier):
    groups, frames, tok, both = query.shape
    width = own.shape[-1]
    row_count = groups * tok
    groups_block = BLOCK_Q // tok
    order = ((2, 1, 3, 0, 4) if frame == 0 else (1, 2, 0, 3, 4))
    before_from = frame
    before_count = frames - frame
    after_count = frame + 1

    def kernel(pos_ref, q_ref, own_ref, before_ref, after_ref, *rest):
        out_ref, token_ref, kt_ref, vx_ref = rest[-4:]

        sources = (
            [(before_ref, f) for f in range(before_count)]
            + [(own_ref, f) for f in range(frames)]
            + [(after_ref, f) for f in range(after_count)]
        )

        @pl.when(pl.program_id(0) == 0)
        def _():
            for at, (ref, f) in enumerate(sources):
                rows = slice(at * row_count, (at + 1) * row_count)
                turned = ref[:, 0, f].reshape(row_count, width).T
                kt_ref[:width, rows] = turned
                kt_ref[width:, rows] = turned
                vx_ref[rows, :width] = ref[:, 1, f].reshape(row_count, width)
                vx_ref[rows, width:] = jnp.ones((row_count, width), vx_ref.dtype)

        q = q_ref[:, 0].reshape(BLOCK_Q, width).astype(jnp.float32) * SCALE_LOG2
        high = q.astype(jnp.bfloat16)
        low = (q - high.astype(jnp.float32)).astype(jnp.bfloat16)
        q = jnp.concatenate((high, low), axis=1)
        position_now = pos_ref[0]

        def scores(at):
            cols = slice(at * row_count, (at + 1) * row_count)
            return jnp.dot(q, kt_ref[:, cols], preferred_element_type=jnp.float32)

        top = jnp.full((BLOCK_Q, 1), NEG_FILL, jnp.float32)
        total = jnp.zeros((BLOCK_Q, 2 * width), jnp.float32)
        ahead = scores(order[0])
        for turn, at in enumerate(order):
            s = ahead
            if turn + 1 < SPAN:
                ahead = scores(order[turn + 1])
            peak = jnp.max(s, axis=1, keepdims=True)
            absent = None
            if at < before_count:
                absent = position_now == 0
            elif at >= before_count + frames:
                absent = position_now == QUEUE - 1
            if absent is not None:
                peak = jnp.where(absent, NEG_FILL, peak)
            lifted_top = jnp.maximum(top, peak)
            less = lifted_top if absent is None else jnp.where(absent, -NEG_FILL, lifted_top)
            weights = jnp.exp2(s - less).astype(jnp.bfloat16)
            rows = slice(at * row_count, (at + 1) * row_count)
            part = jnp.dot(weights, vx_ref[rows], preferred_element_type=jnp.float32)
            total = total * jnp.exp2(top - lifted_top) + part
            top = lifted_top
        result = total[:, :width] / total[:, width:]
        out_ref[...] = result.astype(out_ref.dtype).reshape(groups_block, tok, width)
        token_ref[...] = jnp.zeros_like(token_ref)

    in_specs = [
        pl.BlockSpec((groups_block, 1, tok, width), lambda b, pos: (b, frame, 0, head)),
        pl.BlockSpec(own.shape, lambda b, pos: (0, 0, 0, 0, 0)),
        pl.BlockSpec(
            (groups, 2, before_count, tok, width),
            lambda b, pos: (0, 0, before_from // before_count, 0, 0),
        ),
        pl.BlockSpec((groups, 2, after_count, tok, width), lambda b, pos: (0, 0, 0, 0, 0)),
    ]
    operands = [query, own, before, after]
    aliases = {}
    if partial is not None:
        aliases = {1 + len(operands): 0}
        operands.append(partial)
        in_specs.append(ANY)
    operands += earlier
    in_specs += [corner(e) for e in earlier]
    return pl.pallas_call(
        kernel,
        grid_spec=pltpu.PrefetchScalarGridSpec(
            num_scalar_prefetch=1,
            grid=(row_count // BLOCK_Q,),
            in_specs=in_specs,
            out_specs=[
                pl.BlockSpec((groups_block, tok, width), lambda b, pos: (b, 0, head)),
                pl.BlockSpec(TOKEN, lambda b, pos: (0, 0)),
            ],
            scratch_shapes=[
                pltpu.VMEM((2 * width, SPAN * row_count), jnp.bfloat16),
                pltpu.VMEM((SPAN * row_count, 2 * width), jnp.bfloat16),
            ],
        ),
        out_shape=[
            jax.ShapeDtypeStruct((groups, tok, both), query.dtype),
            jax.ShapeDtypeStruct(TOKEN, jnp.float32),
        ],
        input_output_aliases=aliases,
        compiler_params=pltpu.CompilerParams(vmem_limit_bytes=VMEM),
        cost_estimate=pl.CostEstimate(
            flops=row_count * SPAN * row_count * width * 8,
            bytes_accessed=4 * 1024 * 1024,
            transcendentals=row_count * SPAN * row_count,
        ),
        name="attend",
    )(position, *operands)


def project(frame, slot_shift, place, sources, weight_own, weight_pair, gates, *earlier):
    mine, left, right, far_low, far_high = sources
    groups, tok, width = mine.shape
    steps, sides, halves, rows_dev, cols_dev = weight_own.shape
    half = steps * sides
    depth = sides * width

    def kernel(
        place_ref, mine_ref, left_ref, right_ref, low_ref, high_ref, wo_ref, wp_ref, gates_ref, *rest
    ):
        out_ref, a_ref, total_ref = rest[-3:]
        x, core = place_ref[0], place_ref[1]
        step = pl.program_id(1)

        @pl.when((pl.program_id(0) == 0) & (step == 0))
        def _():
            for i in range(half):
                z, side = i // sides, i % sides
                for part in range(CORES):
                    group = side * half + CORES * z + (core if part == 0 else 1 - core)
                    cols = slice((part * half + i) * width, (part * half + i + 1) * width)
                    a_ref[0:tok, cols] = mine_ref[group]
                    a_ref[tok : 2 * tok, cols] = right_ref[group]
                    far = high_ref[group - half] if side else low_ref[group]
                    a_ref[2 * tok : 3 * tok, cols] = far
                    a_ref[3 * tok :, cols] = left_ref[group]

        @pl.when(step == 0)
        def _():
            total_ref[...] = jnp.zeros_like(total_ref)

        total = total_ref[...]
        for part, ref in enumerate((wo_ref, wp_ref)):
            start = pl.multiple_of(part * half * width + step * depth, depth)
            total += jnp.dot(
                a_ref[:, pl.ds(start, depth)],
                ref[0, :, 0].reshape(depth, cols_dev),
                preferred_element_type=jnp.float32,
            )
        total_ref[...] = total

        @pl.when(step == steps - 1)
        def _():
            for source in range(RING):
                at = lax.rem(x + source, RING)
                gate = gates_ref[0, pl.ds(at * 2 + frame, 1), :]
                rows = slice(source * tok, (source + 1) * tok)
                out_ref[lax.rem(at + slot_shift, RING), 0] = (gate * total_ref[rows]).astype(
                    out_ref.dtype
                )

    whole = pl.BlockSpec(mine.shape, lambda n, k, place: (0, 0, 0))
    part = pl.BlockSpec(far_low.shape, lambda n, k, place: (0, 0, 0))
    weight = pl.BlockSpec(
        (1, sides, 1, rows_dev, cols_dev), lambda n, k, place: (k, 0, n, 0, 0)
    )
    return pl.pallas_call(
        kernel,
        grid_spec=pltpu.PrefetchScalarGridSpec(
            num_scalar_prefetch=1,
            grid=(halves, steps),
            in_specs=[
                whole, whole, whole, part, part, weight, weight,
                pl.BlockSpec((1,) + gates.shape[1:], lambda n, k, place: (n, 0, 0)),
                *[corner(e) for e in earlier],
            ],
            out_specs=pl.BlockSpec((RING, 1, tok, cols_dev), lambda n, k, place: (0, n, 0, 0)),
            scratch_shapes=[
                pltpu.VMEM((RING * tok, groups * width), jnp.bfloat16),
                pltpu.VMEM((RING * tok, cols_dev), jnp.float32),
            ],
        ),
        out_shape=jax.ShapeDtypeStruct((RING, halves, tok, cols_dev), jnp.bfloat16),
        compiler_params=pltpu.CompilerParams(vmem_limit_bytes=VMEM),
        cost_estimate=pl.CostEstimate(
            flops=2 * RING * tok * groups * width * halves * cols_dev,
            bytes_accessed=12 * 1024 * 1024,
            transcendentals=0,
        ),
        name="project",
    )(place, *sources, weight_own, weight_pair, gates, *earlier)


def add_branch(slot, position, branch, base, entering, partial):
    sources, halves, tok, cols = branch.shape
    frames = 2
    first = slot == 0

    def kernel(pos_ref, b_ref, base_ref, *rest):
        out_ref = rest[-1]
        for half in range(halves):
            for source in range(sources):
                at = slice((half * sources + source) * cols, (half * sources + source + 1) * cols)
                value = base_ref[0, :, at].astype(jnp.float32) + b_ref[source, half].astype(jnp.float32)
                if first:
                    value = jnp.where(pos_ref[0] == 0, rest[0][:, at].astype(jnp.float32), value)
                out_ref[0, :, at] = value.astype(out_ref.dtype)

    frame_spec = pl.BlockSpec((1, tok, base.shape[-1]), lambda i, pos: (0, 0, 0))
    in_specs = [pl.BlockSpec(branch.shape, lambda i, pos: (0, 0, 0, 0)), frame_spec]
    if first:
        in_specs.append(pl.BlockSpec(entering.shape, lambda i, pos: (0, 0)))
        operands, aliases = [branch, base, entering], {}
    else:
        in_specs.append(ANY)
        operands, aliases = [branch, base, partial], {3: 0}
    return pl.pallas_call(
        kernel,
        grid_spec=pltpu.PrefetchScalarGridSpec(
            num_scalar_prefetch=1,
            grid=(1,),
            in_specs=in_specs,
            out_specs=pl.BlockSpec((1, tok, base.shape[-1]), lambda i, pos: (slot, 0, 0)),
        ),
        out_shape=jax.ShapeDtypeStruct((frames, tok, base.shape[-1]), base.dtype),
        input_output_aliases=aliases,
        name="add_branch",
    )(position, *operands)


def body(hidden, queries, keys, values, out_weight, gate_table, levels, entering):
    frames = queries.shape[0]
    position = lax.axis_index("queue")
    spatial = lax.axis_index("spatial")
    y_low, x = position // RING, position % RING
    core = spatial % CORES
    position_now = position.astype(jnp.int32)[None]
    place = jnp.stack((x, core)).astype(jnp.int32)

    up = [(p, p + 1) for p in range(QUEUE - 1)]
    down = [(p + 1, p) for p in range(QUEUE - 1)]
    ring = [[r * RING + i for i in range(RING)] for r in range(QUEUE // RING)]
    ring_up = [(g[i], g[(i + 1) % RING]) for g in ring for i in range(RING)]
    ring_down = [(g[(i + 1) % RING], g[i]) for g in ring for i in range(RING)]
    swap_low = [(p, (p + RING) % QUEUE) for p in range(QUEUE)]
    swap_core = [(s, s ^ 1) for s in range(SPATIAL)]
    along_y = [
        [(low * RING + i) * SPATIAL + side * (SPATIAL // 2) + r for side in range(2) for low in range(2)]
        for i in range(RING)
        for r in range(SPATIAL // 2)
    ]
    along_z = [
        [side * (SPATIAL // 2) + z * CORES + c for z in range(SPATIAL // 2 // CORES)]
        for side in range(2)
        for c in range(CORES)
    ]

    to_heads = functools.partial(
        lax.all_to_all, axis_name="spatial", split_axis=0, concat_axis=0, tiled=True
    )

    kv0, kv1, query = pack(queries, keys, values)
    kv0 = to_heads(kv0)
    kv1 = to_heads(hold(kv1, kv0))
    kv0 = hold(kv0, kv1)
    kv0_before, kv0_after = lax.ppermute(kv0, "queue", up), lax.ppermute(kv0, "queue", down)
    query = to_heads(hold(query, kv1))
    kv1 = hold(kv1, query)
    kv1_before, kv1_after = lax.ppermute(kv1, "queue", up), lax.ppermute(kv1, "queue", down)

    weight = lax.all_gather(out_weight, ("queue", "spatial"), axis_index_groups=along_y, axis=0)
    weight = hold(weight, query)
    weight = lax.all_gather(weight, "spatial", axis_index_groups=along_z, axis=0)
    weight = weight.reshape(-1, 2, 2, *out_weight.shape)

    selector = (levels[:, None] == jnp.arange(gate_table.shape[0], dtype=jnp.int32)[None, :]).astype(
        jnp.float32
    )
    gates = jnp.dot(
        selector, gate_table, precision=lax.Precision.HIGHEST, preferred_element_type=jnp.float32
    )
    other_gates = lax.ppermute(gates, "queue", swap_low)
    gates = jnp.where(y_low == 0, jnp.stack((gates, other_gates)), jnp.stack((other_gates, gates)))
    gates = lax.dynamic_slice_in_dim(gates, y_low * RING * frames, RING * frames, axis=1)

    def spread(attended):
        mine = to_heads(attended)
        left = lax.ppermute(mine, "queue", ring_up)
        right = lax.ppermute(mine, "queue", ring_down)
        far_low = lax.ppermute(left[: SPATIAL // 2], "queue", ring_up)
        far_high = lax.ppermute(right[SPATIAL // 2 :], "queue", ring_down)
        return mine, left, right, far_low, far_high

    head0 = (position_now, query, kv0, kv0_before, kv0_after)
    head1 = (position_now, query, kv1, kv1_before, kv1_after)
    odd, token = attend(1, 0, *head0, None)
    even, token = attend(0, 0, *head0, None, token, gates)
    shifted = lax.ppermute(last_frame(hidden, token), "queue", up)
    odd, token = attend(1, 1, *head1, odd, token)
    odd_sources = spread(odd)
    even, token = attend(0, 1, *head1, even, token)
    even_sources = spread(even)
    weight_own = hold(weight, token)
    weight_pair = lax.ppermute(weight_own, "spatial", swap_core)

    branch = project(1, 1, place, odd_sources, weight_own, weight_pair, gates, shifted)
    crossing = lax.ppermute(branch[:1], "queue", [(p, p + RING) for p in range(QUEUE - RING)])
    branch = jnp.concatenate((crossing, branch[1:]))
    to_positions = functools.partial(
        lax.all_to_all, axis_name="queue", split_axis=0, concat_axis=0, axis_index_groups=ring, tiled=True
    )
    result = add_branch(0, position_now, to_positions(branch), shifted, entering, None)
    branch = project(0, 0, place, even_sources, weight_own, weight_pair, gates)
    return add_branch(1, position_now, to_positions(branch), hidden, None, result)


def solution(mesh):
    return jax.shard_map(
        body,
        mesh=mesh,
        in_specs=(
            P("queue", "spatial", None),
            P("queue", "spatial", None),
            P("queue", "spatial", None),
            P("queue", "spatial", None),
            P("spatial", "queue"),
            P(None, "queue"),
            P(),
            P("spatial", None),
        ),
        out_specs=P("queue", "spatial", None),
        check_vma=False,
    )
```

time: 398 us -> 291 us (0.73)
  waiting for transfers between devices: 191 us -> 103 us
  Pallas kernels: 0 us -> 70.2 us
  matrix products: 58.2 us -> 0.22 us
  other arithmetic: 30.2 us -> 0.99 us
  starting transfers between devices: 24.6 us -> 50.8 us
  local copies, waits for them, and re-layouts: 33.2 us -> 7.16 us
    all_gather x2, waiting for transfers between devices: 91.8 us -> 16.7 us  [the longest x1 16.7 us: body(): lax.all_gather(out_weight, ('queue', 'spatial'), axis_index_groups=along_...]
    pallas_call x0 -> x16, Pallas kernels: none -> 70.2 us  [the longest x4 34.7 us: attend(): pl.pallas_call(kernel, grid_spec=pltpu.PrefetchScalarGridSpec(num_scalar_...]
    dot_general x17 -> x0, matrix products: 58 us -> none  [the longest x8 30.2 us: one_block(): jnp.dot(weights, value_head, preferred_element_type=jnp.float32)]
    all_to_all x3 -> x5, waiting for transfers between devices: 85.9 us -> 40.9 us  [the longest x1 17.2 us: body(): kv1 = to_heads(hold(kv1, kv0))]
    ppermute x3 -> x16, waiting for transfers between devices: 12.8 us -> 44.9 us  [the longest x1 38.3 us: body(): other_gates = lax.ppermute(gates, 'queue', swap_low)]
    reduce_sum x8 -> x0, other arithmetic: 23 us -> none  [one_block(): jnp.sum(lifted, axis=1, keepdims=True)]
    ppermute x3 -> x16, starting transfers between devices: 8.93 us -> 31 us  [the longest x2 9.57 us: spread(): right = lax.ppermute(mine, 'queue', ring_down)]
    reshape x7 -> x0, local copies, waits for them, and re-layouts: 11.6 us -> none  [the longest x6 10 us: split_heads(): return array.reshape(array.shape[0], tok_dev, groups, heads_dev, HD)]
  transfers between devices with their start and end apart: 8 -> 23, of which waited for: 5 -> 9; matrix products, arithmetic and copies ran while one was open for 26% -> 1% of each run, Pallas kernels for 0% -> 21%
where the time goes in v1:
time: 291 us; the launch traced here: 289 us
  waiting for transfers between devices  103 us (35%)
  Pallas kernels  70.2 us (24%)
  starting transfers between devices  50.8 us (17%)
  blocking collectives  42.8 us (15%)
  between operations  13.7 us (5%)
  local copies, waits for them, and re-layouts  7.16 us (2%)
    ppermute x1, waiting for transfers between devices, body(): other_gates = lax.ppermute(gates, 'queue', swap_low)  38.3 us
    pallas_call x4, Pallas kernels, attend(): pl.pallas_call(kernel, grid_spec=pltpu.PrefetchScalarGridSpec(num_scalar_...  34.7 us
    all_to_all x1, blocking collectives, body(): kv0 = to_heads(kv0)  26.2 us
    pallas_call x2, Pallas kernels, project(): pl.pallas_call(kernel, grid_spec=pltpu.PrefetchScalarGridSpec(num_scalar_...  20.3 us
    all_to_all x1, waiting for transfers between devices, body(): kv1 = to_heads(hold(kv1, kv0))  17.2 us
    all_gather x1, waiting for transfers between devices, body(): lax.all_gather(out_weight, ('queue', 'spatial'), axis_index_groups=along_...  16.7 us
    all_to_all x1, blocking collectives, spread(): mine = to_heads(attended)  16.6 us
    all_to_all x1, waiting for transfers between devices, spread(): mine = to_heads(attended)  14.9 us
  transfers between devices with their start and end apart: 23, of which 9 were waited for; matrix products, arithmetic and copies ran while one was open for 1% of the time, Pallas kernels for 21%

profile of v1, /device:TPU:0, one launch (start us, length us, event | category | flops | bytes accessed | tf_op | source)
XLA Modules:
  0.0 289.2 jit_solution(13255843983413356957)
XLA Ops:
  6.5 4.3 %pack.1 = (bf16[16,2,2,64,128]{4,3,2,1,0:T(8,128)(2,1)}, bf16[16,2,2,64,128]{4,3,2,1,0:T(8,128)(2,1)}, bf16[16,2,64,256]{3,2,1,0:T(8,128)(2,1)}) custom-call(bf16[2,64,4096]{2,1,0:T(8,128)(2,1)} %q_ref.1, bf16[2,64,4096]{2,1,0:T(8,128)(2,1)} %k_ref.1, bf16[2,64,4096]{2,1,0:T(8,128)(2,1)} %v_ref.1), custom_call_target="tpu_custom_call" | custom-call | tf_op jit(solution)/shard_map/pack/pallas_call | solution.py:50
  10.8 26.2 %all_to_all.35.refs_1_.refs_0_ = bf16[16,2,2,64,128]{4,3,2,1,0:T(8,128)(2,1)} all-to-all(bf16[16,2,2,64,128]{4,3,2,1,0:T(8,128)(2,1)} %get-tuple-element.18), channel_id=1, replica_groups=mesh['queue'=8,'spatial'=16] {'spatial'}, dimensions={0} | all-to-all | bytes 2097152 | tf_op jit(solution)/shard_map/all_to_all | solution.py:360
  37.0 0.7 hold.6
  37.7 3.7 %all-to-all-start.1 = ((bf16[16,2,2,64,128]{4,3,2,1,0:T(8,128)(2,1)}), bf16[16,2,2,64,128]{4,3,2,1,0:T(8,128)(2,1)S(1)}, u32[]{:S(2)}, u32[]{:S(2)}) async-start(bf16[16,2,2,64,128]{4,3,2,1,0:T(8,128)(2,1)} %hold.6), calls=%async_computation.1 | async-start | bytes 2097152 | tf_op jit(solution)/shard_map/all_to_all | solution.py:361
  41.4 0.0 all-gather.5.cloned.1.call-start
  41.4 0.7 all-gather.5.cloned.1.call-update
  42.1 17.2 %all-to-all-done.1.refs_1_.refs_0_ = bf16[16,2,2,64,128]{4,3,2,1,0:T(8,128)(2,1)S(1)} async-done(((bf16[16,2,2,64,128]{4,3,2,1,0:T(8,128)(2,1)}), bf16[16,2,2,64,128]{4,3,2,1,0:T(8,128)(2,1)S(1)}, u32[]{:S(2)}, u32[]{:S(2)}) %all-to-all-start.1) | async-done | bytes 1048608 | tf_op jit(solution)/shard_map/all_to_all | solution.py:361
  59.4 1.0 copy-done.1
  60.3 0.7 hold.7
  61.0 3.7 %all-to-all-start.2 = ((bf16[16,2,64,256]{3,2,1,0:T(8,128)(2,1)}), bf16[16,2,64,256]{3,2,1,0:T(8,128)(2,1)S(1)}, u32[]{:S(2)}, u32[]{:S(2)}) async-start(bf16[16,2,64,256]{3,2,1,0:T(8,128)(2,1)} %hold.7), calls=%async_computation.2 | async-start | bytes 2097152 | tf_op jit(solution)/shard_map/all_to_all | solution.py:364
  64.7 0.0 all-gather.7.cloned.1.call-start
  64.7 16.7 %all-gather.5.cloned.1.call-done = bf16[1024,640]{1,0:T(8,128)(2,1)} async-done(((bf16[256,640]{1,0:T(8,128)(2,1)}), bf16[1024,640]{1,0:T(8,128)(2,1)}) %all-gather.5.cloned.1.call-update) | async-done | bytes 1310736 | tf_op jit(solution)/shard_map/all_gather | solution.py:368
  81.5 1.9 all-to-all-done.2.refs_1_.q_ref
  83.3 1.0 copy-done.3
  84.3 0.7 hold.10
  85.0 0.0 all-gather.7.cloned.1.call-update
  85.0 0.0 copy-start.15
  85.0 0.7 hold.9.own_ref
  85.7 3.4 %collective-permute-start.2 = (bf16[16,2,2,64,128]{4,3,2,1,0:T(8,128)(2,1)}, bf16[16,2,2,64,128]{4,3,2,1,0:T(8,128)(2,1)S(1)}, u32[]{:S(2)}, u32[]{:S(2)}) collective-permute-start(bf16[16,2,2,64,128]{4,3,2,1,0:T(8,128)(2,1)} %hold.9.own_ref), channel_id=1, source_target_pairs={{0,16},{16,32},{32,48},{48,64},{64,80},{80,96},{96,112},{1,17},{17... | collective-permute-start | bytes 3145736 | tf_op jit(solution)/shard_map/ppermute | solution.py:363
  89.1 1.3 collective-permute-start.3
  90.5 0.2 fusion.3
  90.7 4.8 %collective-permute-start.4 = (f32[16,640]{1,0:T(8,128)S(1)}, f32[16,640]{1,0:T(8,128)S(1)}, u32[]{:S(2)}, u32[]{:S(2)}) collective-permute-start(f32[16,640]{1,0:T(8,128)S(1)} %fusion.3), channel_id=1, source_target_pairs={{0,64},{16,80},{32,96},{48,112},{64,0},{80,16},{96,32},{112,48},{1... | collective-permute-start | bytes 122888 | tf_op jit(solution)/shard_map/ppermute | solution.py:379
  95.5 0.8 hold.8.own_ref
  96.3 1.5 collective-permute-start
  97.7 1.3 collective-permute-start.1
  99.0 38.3 %collective-permute-done.4 = f32[16,640]{1,0:T(8,128)S(1)} collective-permute-done((f32[16,640]{1,0:T(8,128)S(1)}, f32[16,640]{1,0:T(8,128)S(1)}, u32[]{:S(2)}, u32[]{:S(2)}) %collective-permute-start.4) | collective-permute-done | bytes 40992 | tf_op jit(solution)/shard_map/ppermute | solution.py:379
  137.4 0.0 collective-permute-done.2.before_ref
  137.4 0.9 copy-done.11
  138.3 1.2 copy-done.12
  139.6 8.9 %attend.4 = (bf16[16,64,256]{2,1,0:T(8,128)(2,1)S(1)}, f32[8,128]{1,0:T(8,128)S(1)}) custom-call(s32[1]{0:T(128)} %bitcast.pos_ref, bf16[16,2,64,256]{3,2,1,0:T(8,128)(2,1)S(1)} %copy-done.4, bf16[16,2,2,64,128]{4,3,2,1,0:T(8,128)(2,1)S(1)} %copy-done.5, bf16[16,2,2,64,128]{4,3,2,1,0:T(8,128)(2,1)S(1)} %copy-done.12, ...), custom_call_target="tpu_custom_call" | custom-call | flops 5368709120 | bytes 4194304 | tf_op jit(solution)/shard_map/attend/pallas_call | solution.py:178
  148.5 0.0 copy-start.2
  148.5 9.5 %attend.5 = (bf16[16,64,256]{2,1,0:T(8,128)(2,1)}, f32[8,128]{1,0:T(8,128)S(1)}) custom-call(s32[1]{0:T(128)} %bitcast.pos_ref, bf16[16,2,64,256]{3,2,1,0:T(8,128)(2,1)S(1)} %copy-done.4, bf16[16,2,2,64,128]{4,3,2,1,0:T(8,128)(2,1)S(1)} %copy-done.5, bf16[16,2,2,64,128]{4,3,2,1,0:T(8,128)(2,1)S(1)} %copy-done.13, ...), custom_call_target="tpu_custom_call" | custom-call | flops 5368709120 | bytes 4194304 | tf_op jit(solution)/shard_map/attend/pallas_call | solution.py:178
  158.0 0.0 collective-permute-done.1.after_ref
  158.0 7.8 %attend.6 = (bf16[16,64,256]{2,1,0:T(8,128)(2,1)S(1)}, f32[8,128]{1,0:T(8,128)S(1)}) custom-call(s32[1]{0:T(128)} %bitcast.pos_ref, bf16[16,2,64,256]{3,2,1,0:T(8,128)(2,1)S(1)} %copy-done.4, bf16[16,2,2,64,128]{4,3,2,1,0:T(8,128)(2,1)S(1)} %copy-done.2, ...), custom_call_target="tpu_custom_call", output_to_operand_aliasing={{0}: (5, {})} | custom-call | flops 5368709120 | bytes 4194304 | tf_op jit(solution)/shard_map/attend/pallas_call | solution.py:178
  165.9 8.4 %attend.7 = (bf16[16,64,256]{2,1,0:T(8,128)(2,1)}, f32[8,128]{1,0:T(8,128)S(1)}) custom-call(s32[1]{0:T(128)} %bitcast.pos_ref, bf16[16,2,64,256]{3,2,1,0:T(8,128)(2,1)S(1)} %copy-done.4, bf16[16,2,2,64,128]{4,3,2,1,0:T(8,128)(2,1)S(1)} %copy-done.2, ...), custom_call_target="tpu_custom_call", output_to_operand_aliasing={{0}: (5, {})} | custom-call | flops 5368709120 | bytes 4194304 | tf_op jit(solution)/shard_map/attend/pallas_call | solution.py:178
  174.3 0.6 copy-done.10
  174.9 0.7 hold.11.wo_ref
  175.6 0.0 collective-permute-start.9
  175.6 16.6 %all_to_all.36.mine_ref = bf16[16,64,256]{2,1,0:T(8,128)(2,1)S(1)} all-to-all(bf16[16,64,256]{2,1,0:T(8,128)(2,1)S(1)} %get-tuple-element.26), channel_id=1, replica_groups=mesh['queue'=8,'spatial'=16] {'spatial'}, dimensions={0} | all-to-all | bytes 1048576 | tf_op jit(solution)/shard_map/all_to_all | solution.py:384
  192.2 6.3 %collective-permute-start.11 = (bf16[16,64,256]{2,1,0:T(8,128)(2,1)S(1)}, bf16[16,64,256]{2,1,0:T(8,128)(2,1)S(1)}, u32[]{:S(2)}, u32[]{:S(2)}) collective-permute-start(bf16[16,64,256]{2,1,0:T(8,128)(2,1)S(1)} %all_to_all.36.mine_ref), channel_id=1, source_target_pairs={{16,0},{32,16},{48,32},{0,48},{80,64},{96,80},{112,96},{64,112},{1... | collective-permute-start | bytes 1572872 | tf_op jit(solution)/shard_map/ppermute | solution.py:386
  198.5 2.0 last_frame.1
  200.5 1.3 collective-permute-start.14
  201.8 3.6 %all-to-all-start.3 = ((bf16[16,64,256]{2,1,0:T(8,128)(2,1)}), bf16[16,64,256]{2,1,0:T(8,128)(2,1)S(1)}, u32[]{:S(2)}, u32[]{:S(2)}) async-start(bf16[16,64,256]{2,1,0:T(8,128)(2,1)} %get-tuple-element.24), calls=%async_computation.3 | async-start | bytes 1048576 | tf_op jit(solution)/shard_map/all_to_all | solution.py:384
  205.4 5.9 %collective-permute-done.10.left_ref = bf16[16,64,256]{2,1,0:T(8,128)(2,1)S(1)} collective-permute-done((bf16[16,64,256]{2,1,0:T(8,128)(2,1)S(1)}, bf16[16,64,256]{2,1,0:T(8,128)(2,1)S(1)}, u32[]{:S(2)}, u32[]{:S(2)}) %collective-permute-start.10) | collective-permute-done | bytes 524320 | tf_op jit(solution)/shard_map/ppermute | solution.py:385
  211.3 0.7 slice.26
  212.1 0.7 slice.27
  212.8 3.2 %collective-permute-start.13 = (bf16[8,64,256]{2,1,0:T(8,128)(2,1)}, bf16[8,64,256]{2,1,0:T(8,128)(2,1)}, u32[]{:S(2)}, u32[]{:S(2)}) collective-permute-start(bf16[8,64,256]{2,1,0:T(8,128)(2,1)} %slice.27), channel_id=1, source_target_pairs={{16,0},{32,16},{48,32},{0,48},{80,64},{96,80},{112,96},{64,112},{1... | collective-permute-start | bytes 786440 | tf_op jit(solution)/shard_map/ppermute | solution.py:388
  216.0 14.9 %all-to-all-done.3.mine_ref = bf16[16,64,256]{2,1,0:T(8,128)(2,1)S(1)} async-done(((bf16[16,64,256]{2,1,0:T(8,128)(2,1)}), bf16[16,64,256]{2,1,0:T(8,128)(2,1)S(1)}, u32[]{:S(2)}, u32[]{:S(2)}) %all-to-all-start.3) | async-done | bytes 524320 | tf_op jit(solution)/shard_map/all_to_all | solution.py:384
  231.0 3.2 %collective-permute-start.6 = (bf16[16,64,256]{2,1,0:T(8,128)(2,1)S(1)}, bf16[16,64,256]{2,1,0:T(8,128)(2,1)S(1)}, u32[]{:S(2)}, u32[]{:S(2)}) collective-permute-start(bf16[16,64,256]{2,1,0:T(8,128)(2,1)S(1)} %all-to-all-done.3.mine_ref), channel_id=1, source_target_pairs={{16,0},{32,16},{48,32},{0,48},{80,64},{96,80},{112,96},{64,112},{1... | collective-permute-start | bytes 1572872 | tf_op jit(solution)/shard_map/ppermute | solution.py:386
  234.2 0.1 pad_add_fusion.place_ref
  234.3 9.9 %project.3 = bf16[4,2,64,640]{3,2,1,0:T(8,128)(2,1)S(1)} custom-call(s32[2]{0:T(128)S(1)} %pad_add_fusion.place_ref, bf16[16,64,256]{2,1,0:T(8,128)(2,1)S(1)} %all_to_all.36.mine_ref, bf16[16,64,256]{2,1,0:T(8,128)(2,1)S(1)} %collective-permute-done.10.left_ref, bf16[16,64,256]{2,1,0:T(8,128)(2,1)S(1)} %collective-permute-done.11.right_ref, ...), custom_call_target="tpu_custom_call" | custom-call | flops 2684354560 | bytes 12582912 | tf_op jit(solution)/shard_map/project/pallas_call | solution.py:264
  244.3 1.3 collective-permute-start.15
  245.6 0.5 collective-permute-done.5.left_ref
  246.1 0.1 collective-permute-start.7
  246.2 3.3 %collective-permute-start.8 = (bf16[8,64,256]{2,1,0:T(8,128)(2,1)S(1)}, bf16[8,64,256]{2,1,0:T(8,128)(2,1)S(1)}, u32[]{:S(2)}, u32[]{:S(2)}) collective-permute-start(bf16[8,64,256]{2,1,0:T(8,128)(2,1)S(1)} %slice.25), channel_id=1, source_target_pairs={{16,0},{32,16},{48,32},{0,48},{80,64},{96,80},{112,96},{64,112},{1... | collective-permute-start | bytes 786440 | tf_op jit(solution)/shard_map/ppermute | solution.py:388
  249.6 0.9 pad_maximum_fusion
  250.5 4.2 %all-to-all-start.6 = ((bf16[4,2,64,640]{3,2,1,0:T(8,128)(2,1)}), bf16[4,2,64,640]{3,2,1,0:T(8,128)(2,1)}, u32[]{:S(2)}, u32[]{:S(2)}) async-start(bf16[4,2,64,640]{3,2,1,0:T(8,128)(2,1)} %pad_maximum_fusion), calls=%async_computation.6 | async-start | bytes 1310720 | tf_op jit(solution)/shard_map/all_to_all | solution.py:409
  254.7 0.2 collective-permute-done.7.low_ref
  254.8 10.3 %project.2 = bf16[4,2,64,640]{3,2,1,0:T(8,128)(2,1)} custom-call(s32[2]{0:T(128)S(1)} %pad_add_fusion.place_ref, bf16[16,64,256]{2,1,0:T(8,128)(2,1)S(1)} %all-to-all-done.3.mine_ref, bf16[16,64,256]{2,1,0:T(8,128)(2,1)S(1)} %collective-permute-done.5.left_ref, bf16[16,64,256]{2,1,0:T(8,128)(2,1)S(1)} %copy-done.8, ...), custom_call_target="tpu_custom_call" | custom-call | flops 2684354560 | bytes 12582912 | tf_op jit(solution)/shard_map/project/pallas_call | solution.py:264
  265.2 4.6 %all-to-all-start.4 = ((bf16[4,2,64,640]{3,2,1,0:T(8,128)(2,1)}), bf16[4,2,64,640]{3,2,1,0:T(8,128)(2,1)S(1)}, u32[]{:S(2)}, u32[]{:S(2)}) async-start(bf16[4,2,64,640]{3,2,1,0:T(8,128)(2,1)} %project.2), calls=%async_computation.4 | async-start | bytes 1310720 | tf_op jit(solution)/shard_map/all_to_all | solution.py:411
  269.8 2.6 add_branch.2.rest_0_
  272.3 6.9 %all-to-all-done.4.b_ref = bf16[4,2,64,640]{3,2,1,0:T(8,128)(2,1)S(1)} async-done(((bf16[4,2,64,640]{3,2,1,0:T(8,128)(2,1)}), bf16[4,2,64,640]{3,2,1,0:T(8,128)(2,1)S(1)}, u32[]{:S(2)}, u32[]{:S(2)}) %all-to-all-start.4) | async-done | bytes 655392 | tf_op jit(solution)/shard_map/all_to_all | solution.py:411
  279.2 0.9 copy-done.14
  280.1 2.3 add_branch.3
  (44 shorter events, 0.2 us)
Async XLA Ops:
  6.5 83.9 %copy-start = (f32[50,640]{1,0:T(8,128)S(1)}, f32[50,640]{1,0:T(8,128)}, u32[]{:S(2)}) copy-start(f32[50,640]{1,0:T(8,128)} %param.13) | copy-start | bytes 384004
  37.7 21.6 %all-to-all-start.1 = ((bf16[16,2,2,64,128]{4,3,2,1,0:T(8,128)(2,1)}), bf16[16,2,2,64,128]{4,3,2,1,0:T(8,128)(2,1)S(1)}, u32[]{:S(2)}, u32[]{:S(2)}) async-start(bf16[16,2,2,64,128]{4,3,2,1,0:T(8,128)(2,1)} %hold.6), calls=%async_computation.1 | async-start | bytes 2097152 | tf_op jit(solution)/shard_map/all_to_all | solution.py:361
  41.4 40.1 %all-gather.5.cloned.1.call-start = ((), (), s32[]{:S(2)}) async-start(), calls=%async_computation.7 | async-start | bytes 1638400 | tf_op jit(solution)/shard_map/all_gather | solution.py:368
  59.4 1.0 copy-start.1
  61.0 22.3 %all-to-all-start.2 = ((bf16[16,2,64,256]{3,2,1,0:T(8,128)(2,1)}), bf16[16,2,64,256]{3,2,1,0:T(8,128)(2,1)S(1)}, u32[]{:S(2)}, u32[]{:S(2)}) async-start(bf16[16,2,64,256]{3,2,1,0:T(8,128)(2,1)} %hold.7), calls=%async_computation.2 | async-start | bytes 2097152 | tf_op jit(solution)/shard_map/all_to_all | solution.py:364
  64.7 110.2 %all-gather.7.cloned.1.call-start = ((), (), s32[]{:S(2)}) async-start(), calls=%async_computation.8 | async-start | bytes 6553600 | tf_op jit(solution)/shard_map/all_gather | solution.py:370
  83.3 1.0 copy-start.3
  85.0 5.5 %copy-start.15 = (s32[16]{0:T(128)S(1)}, s32[16]{0:T(128)}, u32[]{:S(2)}) copy-start(s32[16]{0:T(128)} %param.14) | copy-start | bytes 196
  85.7 51.7 %collective-permute-start.2 = (bf16[16,2,2,64,128]{4,3,2,1,0:T(8,128)(2,1)}, bf16[16,2,2,64,128]{4,3,2,1,0:T(8,128)(2,1)S(1)}, u32[]{:S(2)}, u32[]{:S(2)}) collective-permute-start(bf16[16,2,2,64,128]{4,3,2,1,0:T(8,128)(2,1)} %hold.9.own_ref), channel_id=1, source_target_pairs={{0,16},{16,32},{32,48},{48,64},{64,80},{80,96},{96,112},{1,17},{17... | collective-permute-start | bytes 3145736 | tf_op jit(solution)/shard_map/ppermute | solution.py:363
  89.1 49.2 %collective-permute-start.3 = (bf16[16,2,2,64,128]{4,3,2,1,0:T(8,128)(2,1)}, bf16[16,2,2,64,128]{4,3,2,1,0:T(8,128)(2,1)}, u32[]{:S(2)}, u32[]{:S(2)}) collective-permute-start(bf16[16,2,2,64,128]{4,3,2,1,0:T(8,128)(2,1)} %hold.9.own_ref), channel_id=1, source_target_pairs={{16,0},{32,16},{48,32},{64,48},{80,64},{96,80},{112,96},{17,1},{33... | collective-permute-start | bytes 3145736 | tf_op jit(solution)/shard_map/ppermute | solution.py:363
  90.7 46.7 %collective-permute-start.4 = (f32[16,640]{1,0:T(8,128)S(1)}, f32[16,640]{1,0:T(8,128)S(1)}, u32[]{:S(2)}, u32[]{:S(2)}) collective-permute-start(f32[16,640]{1,0:T(8,128)S(1)} %fusion.3), channel_id=1, source_target_pairs={{0,64},{16,80},{32,96},{48,112},{64,0},{80,16},{96,32},{112,48},{1... | collective-permute-start | bytes 122888 | tf_op jit(solution)/shard_map/ppermute | solution.py:379
  95.5 42.9 %copy-start.4 = (bf16[16,2,64,256]{3,2,1,0:T(8,128)(2,1)S(1)}, bf16[16,2,64,256]{3,2,1,0:T(8,128)(2,1)}, u32[]{:S(2)}) copy-start(bf16[16,2,64,256]{3,2,1,0:T(8,128)(2,1)} %copy-done.3) | copy-start | bytes 3145732
  95.5 42.9 %copy-start.5 = (bf16[16,2,2,64,128]{4,3,2,1,0:T(8,128)(2,1)S(1)}, bf16[16,2,2,64,128]{4,3,2,1,0:T(8,128)(2,1)}, u32[]{:S(2)}) copy-start(bf16[16,2,2,64,128]{4,3,2,1,0:T(8,128)(2,1)} %hold.9.own_ref) | copy-start | bytes 3145732
  96.3 61.7 %collective-permute-start = (bf16[16,2,2,64,128]{4,3,2,1,0:T(8,128)(2,1)}, bf16[16,2,2,64,128]{4,3,2,1,0:T(8,128)(2,1)S(1)}, u32[]{:S(2)}, u32[]{:S(2)}) collective-permute-start(bf16[16,2,2,64,128]{4,3,2,1,0:T(8,128)(2,1)} %hold.8.own_ref), channel_id=1, source_target_pairs={{0,16},{16,32},{32,48},{48,64},{64,80},{80,96},{96,112},{1,17},{17... | collective-permute-start | bytes 3145736 | tf_op jit(solution)/shard_map/ppermute | solution.py:366
  97.7 60.3 %collective-permute-start.1 = (bf16[16,2,2,64,128]{4,3,2,1,0:T(8,128)(2,1)}, bf16[16,2,2,64,128]{4,3,2,1,0:T(8,128)(2,1)S(1)}, u32[]{:S(2)}, u32[]{:S(2)}) collective-permute-start(bf16[16,2,2,64,128]{4,3,2,1,0:T(8,128)(2,1)} %hold.8.own_ref), channel_id=1, source_target_pairs={{16,0},{32,16},{48,32},{64,48},{80,64},{96,80},{112,96},{17,1},{33... | collective-permute-start | bytes 3145736 | tf_op jit(solution)/shard_map/ppermute | solution.py:366
  137.4 1.0 copy-start.11
  138.3 1.2 copy-start.12
  139.6 8.9 %copy-start.13 = (bf16[16,2,2,64,128]{4,3,2,1,0:T(8,128)(2,1)S(1)}, bf16[16,2,2,64,128]{4,3,2,1,0:T(8,128)(2,1)}, u32[]{:S(2)}) copy-start(bf16[16,2,2,64,128]{4,3,2,1,0:T(8,128)(2,1)} %copy-done.11) | copy-start | bytes 3145732
  148.5 9.5 %copy-start.2 = (bf16[16,2,2,64,128]{4,3,2,1,0:T(8,128)(2,1)S(1)}, bf16[16,2,2,64,128]{4,3,2,1,0:T(8,128)(2,1)}, u32[]{:S(2)}) copy-start(bf16[16,2,2,64,128]{4,3,2,1,0:T(8,128)(2,1)} %hold.8.own_ref) | copy-start | bytes 3145732
  158.0 7.9 %copy-start.9 = (f32[8,128]{1,0:T(8,128)}, f32[8,128]{1,0:T(8,128)S(1)}, u32[]{:S(2)}) copy-start(f32[8,128]{1,0:T(8,128)S(1)} %get-tuple-element.22.rest_1_.rest_0_) | copy-start | bytes 12292
  174.3 0.6 copy-start.10
  175.6 58.7 %collective-permute-start.9 = (bf16[4,2,2,256,640]{4,3,2,1,0:T(8,128)(2,1)}, bf16[4,2,2,256,640]{4,3,2,1,0:T(8,128)(2,1)}, u32[]{:S(2)}, u32[]{:S(2)}) collective-permute-start(bf16[4,2,2,256,640]{4,3,2,1,0:T(8,128)(2,1)} %hold.11.wo_ref), channel_id=1, source_target_pairs={{0,1},{1,0},{2,3},{3,2},{4,5},{5,4},{6,7},{7,6},{8,9},{9,8},{10,11... | collective-permute-start | bytes 15728648 | tf_op jit(solution)/shard_map/ppermute | solution.py:401
  192.2 19.2 %collective-permute-start.10 = (bf16[16,64,256]{2,1,0:T(8,128)(2,1)S(1)}, bf16[16,64,256]{2,1,0:T(8,128)(2,1)S(1)}, u32[]{:S(2)}, u32[]{:S(2)}) collective-permute-start(bf16[16,64,256]{2,1,0:T(8,128)(2,1)S(1)} %all_to_all.36.mine_ref), channel_id=1, source_target_pairs={{0,16},{16,32},{32,48},{48,0},{64,80},{80,96},{96,112},{112,64},{1... | collective-permute-start | bytes 1572872 | tf_op jit(solution)/shard_map/ppermute | solution.py:385
  192.2 19.9 %collective-permute-start.11 = (bf16[16,64,256]{2,1,0:T(8,128)(2,1)S(1)}, bf16[16,64,256]{2,1,0:T(8,128)(2,1)S(1)}, u32[]{:S(2)}, u32[]{:S(2)}) collective-permute-start(bf16[16,64,256]{2,1,0:T(8,128)(2,1)S(1)} %all_to_all.36.mine_ref), channel_id=1, source_target_pairs={{16,0},{32,16},{48,32},{0,48},{80,64},{96,80},{112,96},{64,112},{1... | collective-permute-start | bytes 1572872 | tf_op jit(solution)/shard_map/ppermute | solution.py:386
  200.5 30.5 %collective-permute-start.14 = (bf16[1,64,5120]{2,1,0:T(8,128)(2,1)}, bf16[1,64,5120]{2,1,0:T(8,128)(2,1)S(1)}, u32[]{:S(2)}, u32[]{:S(2)}) collective-permute-start(bf16[1,64,5120]{2,1,0:T(8,128)(2,1)} %last_frame.1), channel_id=1, source_target_pairs={{0,16},{16,32},{32,48},{48,64},{64,80},{80,96},{96,112},{1,17},{17... | collective-permute-start | bytes 1966088 | tf_op jit(solution)/shard_map/ppermute | solution.py:395
  201.8 29.2 %all-to-all-start.3 = ((bf16[16,64,256]{2,1,0:T(8,128)(2,1)}), bf16[16,64,256]{2,1,0:T(8,128)(2,1)S(1)}, u32[]{:S(2)}, u32[]{:S(2)}) async-start(bf16[16,64,256]{2,1,0:T(8,128)(2,1)} %get-tuple-element.24), calls=%async_computation.3 | async-start | bytes 1048576 | tf_op jit(solution)/shard_map/all_to_all | solution.py:384
  212.1 22.2 %collective-permute-start.12 = (bf16[8,64,256]{2,1,0:T(8,128)(2,1)}, bf16[8,64,256]{2,1,0:T(8,128)(2,1)}, u32[]{:S(2)}, u32[]{:S(2)}) collective-permute-start(bf16[8,64,256]{2,1,0:T(8,128)(2,1)} %slice.26), channel_id=1, source_target_pairs={{0,16},{16,32},{32,48},{48,0},{64,80},{80,96},{96,112},{112,64},{1... | collective-permute-start | bytes 786440 | tf_op jit(solution)/shard_map/ppermute | solution.py:387
  212.8 21.5 %collective-permute-start.13 = (bf16[8,64,256]{2,1,0:T(8,128)(2,1)}, bf16[8,64,256]{2,1,0:T(8,128)(2,1)}, u32[]{:S(2)}, u32[]{:S(2)}) collective-permute-start(bf16[8,64,256]{2,1,0:T(8,128)(2,1)} %slice.27), channel_id=1, source_target_pairs={{16,0},{32,16},{48,32},{0,48},{80,64},{96,80},{112,96},{64,112},{1... | collective-permute-start | bytes 786440 | tf_op jit(solution)/shard_map/ppermute | solution.py:388
  231.0 15.1 %collective-permute-start.5 = (bf16[16,64,256]{2,1,0:T(8,128)(2,1)S(1)}, bf16[16,64,256]{2,1,0:T(8,128)(2,1)S(1)}, u32[]{:S(2)}, u32[]{:S(2)}) collective-permute-start(bf16[16,64,256]{2,1,0:T(8,128)(2,1)S(1)} %all-to-all-done.3.mine_ref), channel_id=1, source_target_pairs={{0,16},{16,32},{32,48},{48,0},{64,80},{80,96},{96,112},{112,64},{1... | collective-permute-start | bytes 1572872 | tf_op jit(solution)/shard_map/ppermute | solution.py:385
  231.0 13.3 %copy-start.6 = (bf16[1,64,5120]{2,1,0:T(8,128)(2,1)}, bf16[1,64,5120]{2,1,0:T(8,128)(2,1)S(1)}, u32[]{:S(2)}) copy-start(bf16[1,64,5120]{2,1,0:T(8,128)(2,1)S(1)} %collective-permute-done.14.rest_0_.base_ref) | copy-start | bytes 1966084
  231.0 15.2 %collective-permute-start.6 = (bf16[16,64,256]{2,1,0:T(8,128)(2,1)S(1)}, bf16[16,64,256]{2,1,0:T(8,128)(2,1)S(1)}, u32[]{:S(2)}, u32[]{:S(2)}) collective-permute-start(bf16[16,64,256]{2,1,0:T(8,128)(2,1)S(1)} %all-to-all-done.3.mine_ref), channel_id=1, source_target_pairs={{16,0},{32,16},{48,32},{0,48},{80,64},{96,80},{112,96},{64,112},{1... | collective-permute-start | bytes 1572872 | tf_op jit(solution)/shard_map/ppermute | solution.py:386
  244.3 5.3 %collective-permute-start.15 = (bf16[1,2,64,640]{3,2,1,0:T(8,128)(2,1)S(1)}, bf16[1,2,64,640]{3,2,1,0:T(8,128)(2,1)S(1)}, u32[]{:S(2)}, u32[]{:S(2)}) collective-permute-start(bf16[1,2,64,640]{3,2,1,0:T(8,128)(2,1)S(1)} %slice.28), channel_id=1, source_target_pairs={{0,64},{16,80},{32,96},{48,112},{1,65},{17,81},{33,97},{49,113},{2... | collective-permute-start | bytes 491528 | tf_op jit(solution)/shard_map/ppermute | solution.py:404
  246.1 8.7 %collective-permute-start.7 = (bf16[8,64,256]{2,1,0:T(8,128)(2,1)S(1)}, bf16[8,64,256]{2,1,0:T(8,128)(2,1)S(1)}, u32[]{:S(2)}, u32[]{:S(2)}) collective-permute-start(bf16[8,64,256]{2,1,0:T(8,128)(2,1)S(1)} %slice.24), channel_id=1, source_target_pairs={{0,16},{16,32},{32,48},{48,0},{64,80},{80,96},{96,112},{112,64},{1... | collective-permute-start | bytes 786440 | tf_op jit(solution)/shard_map/ppermute | solution.py:387
  246.2 3.4 %copy-start.7 = (bf16[16,64,256]{2,1,0:T(8,128)(2,1)}, bf16[16,64,256]{2,1,0:T(8,128)(2,1)S(1)}, u32[]{:S(2)}) copy-start(bf16[16,64,256]{2,1,0:T(8,128)(2,1)S(1)} %collective-permute-done.6.right_ref) | copy-start | bytes 1572868
  246.2 8.6 %collective-permute-start.8 = (bf16[8,64,256]{2,1,0:T(8,128)(2,1)S(1)}, bf16[8,64,256]{2,1,0:T(8,128)(2,1)S(1)}, u32[]{:S(2)}, u32[]{:S(2)}) collective-permute-start(bf16[8,64,256]{2,1,0:T(8,128)(2,1)S(1)} %slice.25), channel_id=1, source_target_pairs={{16,0},{32,16},{48,32},{0,48},{80,64},{96,80},{112,96},{64,112},{1... | collective-permute-start | bytes 786440 | tf_op jit(solution)/shard_map/ppermute | solution.py:388
  249.6 5.3 %copy-start.8 = (bf16[16,64,256]{2,1,0:T(8,128)(2,1)S(1)}, bf16[16,64,256]{2,1,0:T(8,128)(2,1)}, u32[]{:S(2)}) copy-start(bf16[16,64,256]{2,1,0:T(8,128)(2,1)} %copy-done.7) | copy-start | bytes 1572868
  250.5 14.7 %all-to-all-start.6 = ((bf16[4,2,64,640]{3,2,1,0:T(8,128)(2,1)}), bf16[4,2,64,640]{3,2,1,0:T(8,128)(2,1)}, u32[]{:S(2)}, u32[]{:S(2)}) async-start(bf16[4,2,64,640]{3,2,1,0:T(8,128)(2,1)} %pad_maximum_fusion), calls=%async_computation.6 | async-start | bytes 1310720 | tf_op jit(solution)/shard_map/all_to_all | solution.py:409
  265.2 14.0 %all-to-all-start.4 = ((bf16[4,2,64,640]{3,2,1,0:T(8,128)(2,1)}), bf16[4,2,64,640]{3,2,1,0:T(8,128)(2,1)S(1)}, u32[]{:S(2)}, u32[]{:S(2)}) async-start(bf16[4,2,64,640]{3,2,1,0:T(8,128)(2,1)} %project.2), calls=%async_computation.4 | async-start | bytes 1310720 | tf_op jit(solution)/shard_map/all_to_all | solution.py:411
  279.2 0.9 copy-start.14
Sparse Core Ops, SparseCore 0:
  43.9 37.5 all-gather.4
  85.1 56.4 all-gather.6

commit v2 on v1

--- a/solution.py
+++ b/solution.py
@@ -93,26 +93,28 @@
     )(array, *earlier)
 
 
-def attend(frame, head, position, query, own, before, after, partial, *earlier):
+def attend(frame, position, query, head, own, before, after, *earlier):
     groups, frames, tok, both = query.shape
     width = own.shape[-1]
     row_count = groups * tok
     groups_block = BLOCK_Q // tok
-    order = ((2, 1, 3, 0, 4) if frame == 0 else (1, 2, 0, 3, 4))
-    before_from = frame
-    before_count = frames - frame
-    after_count = frame + 1
+    blocks = row_count // BLOCK_Q
+    asked = range(frames) if frame is None else (frame,)
+    before_from = min(asked)
+    before_count = frames - before_from
+    after_count = max(asked) + 1
+    loaded = before_count + frames + after_count
 
     def kernel(pos_ref, q_ref, own_ref, before_ref, after_ref, *rest):
         out_ref, token_ref, kt_ref, vx_ref = rest[-4:]
-
         sources = (
             [(before_ref, f) for f in range(before_count)]
             + [(own_ref, f) for f in range(frames)]
             + [(after_ref, f) for f in range(after_count)]
         )
-
-        @pl.when(pl.program_id(0) == 0)
+        turn_frame = pl.program_id(0)
+
+        @pl.when((turn_frame == 0) & (pl.program_id(1) == 0))
         def _():
             for at, (ref, f) in enumerate(sources):
                 rows = slice(at * row_count, (at + 1) * row_count)
@@ -128,94 +130,87 @@
         q = jnp.concatenate((high, low), axis=1)
         position_now = pos_ref[0]
 
-        def scores(at):
-            cols = slice(at * row_count, (at + 1) * row_count)
-            return jnp.dot(q, kt_ref[:, cols], preferred_element_type=jnp.float32)
+        def rows_of(step):
+            start = (turn_frame + step) * row_count
+            return pl.ds(pl.multiple_of(start, row_count), row_count)
+
+        def scores(step):
+            return jnp.dot(q, kt_ref[:, rows_of(step)], preferred_element_type=jnp.float32)
 
         top = jnp.full((BLOCK_Q, 1), NEG_FILL, jnp.float32)
         total = jnp.zeros((BLOCK_Q, 2 * width), jnp.float32)
+        order = (2, 1, 3, 0, 4)
         ahead = scores(order[0])
-        for turn, at in enumerate(order):
+        for turn, step in enumerate(order):
             s = ahead
             if turn + 1 < SPAN:
                 ahead = scores(order[turn + 1])
+            at = turn_frame + step
+            absent = ((position_now == 0) & (at < before_count)) | (
+                (position_now == QUEUE - 1) & (at >= before_count + frames)
+            )
             peak = jnp.max(s, axis=1, keepdims=True)
-            absent = None
-            if at < before_count:
-                absent = position_now == 0
-            elif at >= before_count + frames:
-                absent = position_now == QUEUE - 1
-            if absent is not None:
-                peak = jnp.where(absent, NEG_FILL, peak)
+            peak = jnp.where(absent, NEG_FILL, peak)
             lifted_top = jnp.maximum(top, peak)
-            less = lifted_top if absent is None else jnp.where(absent, -NEG_FILL, lifted_top)
+            less = jnp.where(absent, -NEG_FILL, lifted_top)
             weights = jnp.exp2(s - less).astype(jnp.bfloat16)
-            rows = slice(at * row_count, (at + 1) * row_count)
-            part = jnp.dot(weights, vx_ref[rows], preferred_element_type=jnp.float32)
+            part = jnp.dot(weights, vx_ref[rows_of(step)], preferred_element_type=jnp.float32)
             total = total * jnp.exp2(top - lifted_top) + part
             top = lifted_top
         result = total[:, :width] / total[:, width:]
-        out_ref[...] = result.astype(out_ref.dtype).reshape(groups_block, tok, width)
+        out_ref[:, 0] = result.astype(out_ref.dtype).reshape(groups_block, tok, width)
         token_ref[...] = jnp.zeros_like(token_ref)
 
+    first = asked[0]
     in_specs = [
-        pl.BlockSpec((groups_block, 1, tok, width), lambda b, pos: (b, frame, 0, head)),
-        pl.BlockSpec(own.shape, lambda b, pos: (0, 0, 0, 0, 0)),
+        pl.BlockSpec((groups_block, 1, tok, width), lambda f, b, pos: (b, first + f, 0, head)),
+        pl.BlockSpec(own.shape, lambda f, b, pos: (0, 0, 0, 0, 0)),
         pl.BlockSpec(
             (groups, 2, before_count, tok, width),
-            lambda b, pos: (0, 0, before_from // before_count, 0, 0),
-        ),
-        pl.BlockSpec((groups, 2, after_count, tok, width), lambda b, pos: (0, 0, 0, 0, 0)),
+            lambda f, b, pos: (0, 0, before_from // before_count, 0, 0),
+        ),
+        pl.BlockSpec((groups, 2, after_count, tok, width), lambda f, b, pos: (0, 0, 0, 0, 0)),
     ]
-    operands = [query, own, before, after]
-    aliases = {}
-    if partial is not None:
-        aliases = {1 + len(operands): 0}
-        operands.append(partial)
-        in_specs.append(ANY)
-    operands += earlier
-    in_specs += [corner(e) for e in earlier]
     return pl.pallas_call(
         kernel,
         grid_spec=pltpu.PrefetchScalarGridSpec(
             num_scalar_prefetch=1,
-            grid=(row_count // BLOCK_Q,),
-            in_specs=in_specs,
+            grid=(len(asked), blocks),
+            in_specs=in_specs + [corner(e) for e in earlier],
             out_specs=[
-                pl.BlockSpec((groups_block, tok, width), lambda b, pos: (b, 0, head)),
-                pl.BlockSpec(TOKEN, lambda b, pos: (0, 0)),
+                pl.BlockSpec((groups_block, 1, tok, width), lambda f, b, pos: (b, f, 0, 0)),
+                pl.BlockSpec(TOKEN, lambda f, b, pos: (0, 0)),
             ],
             scratch_shapes=[
-                pltpu.VMEM((2 * width, SPAN * row_count), jnp.bfloat16),
-                pltpu.VMEM((SPAN * row_count, 2 * width), jnp.bfloat16),
+                pltpu.VMEM((2 * width, loaded * row_count), jnp.bfloat16),
+                pltpu.VMEM((loaded * row_count, 2 * width), jnp.bfloat16),
             ],
         ),
         out_shape=[
-            jax.ShapeDtypeStruct((groups, tok, both), query.dtype),
+            jax.ShapeDtypeStruct((groups, len(asked), tok, width), query.dtype),
             jax.ShapeDtypeStruct(TOKEN, jnp.float32),
         ],
-        input_output_aliases=aliases,
         compiler_params=pltpu.CompilerParams(vmem_limit_bytes=VMEM),
         cost_estimate=pl.CostEstimate(
-            flops=row_count * SPAN * row_count * width * 8,
+            flops=len(asked) * row_count * SPAN * row_count * width * 8,
             bytes_accessed=4 * 1024 * 1024,
-            transcendentals=row_count * SPAN * row_count,
+            transcendentals=len(asked) * row_count * SPAN * row_count,
         ),
         name="attend",
-    )(position, *operands)
-
-
-def project(frame, slot_shift, place, sources, weight_own, weight_pair, gates, *earlier):
-    mine, left, right, far_low, far_high = sources
-    groups, tok, width = mine.shape
+    )(position, query, own, before, after, *earlier)
+
+
+def project(frame, slot_shift, place, whole_sources, frame_sources, weight_own, weight_pair, gates, *earlier):
+    groups, _, tok, width = frame_sources[0].shape
     steps, sides, halves, rows_dev, cols_dev = weight_own.shape
     half = steps * sides
-    depth = sides * width
-
-    def kernel(
-        place_ref, mine_ref, left_ref, right_ref, low_ref, high_ref, wo_ref, wp_ref, gates_ref, *rest
-    ):
-        out_ref, a_ref, total_ref = rest[-3:]
+    depth = sides * rows_dev
+    count = len(frame_sources)
+
+    def kernel(place_ref, *refs):
+        heads = refs[:count], refs[count : 2 * count]
+        wo_ref, wp_ref, gates_ref = refs[2 * count : 2 * count + 3]
+        out_ref, a_ref, total_ref = refs[-3:]
         x, core = place_ref[0], place_ref[1]
         step = pl.program_id(1)
 
@@ -225,12 +220,14 @@
                 z, side = i // sides, i % sides
                 for part in range(CORES):
                     group = side * half + CORES * z + (core if part == 0 else 1 - core)
-                    cols = slice((part * half + i) * width, (part * half + i + 1) * width)
-                    a_ref[0:tok, cols] = mine_ref[group]
-                    a_ref[tok : 2 * tok, cols] = right_ref[group]
-                    far = high_ref[group - half] if side else low_ref[group]
-                    a_ref[2 * tok : 3 * tok, cols] = far
-                    a_ref[3 * tok :, cols] = left_ref[group]
+                    for head, (mine_ref, left_ref, right_ref, low_ref, high_ref) in enumerate(heads):
+                        start = (part * half + i) * rows_dev + head * width
+                        cols = slice(start, start + width)
+                        a_ref[0:tok, cols] = mine_ref[group, 0]
+                        a_ref[tok : 2 * tok, cols] = right_ref[group, 0]
+                        far = high_ref[group - half, 0] if side else low_ref[group, 0]
+                        a_ref[2 * tok : 3 * tok, cols] = far
+                        a_ref[3 * tok :, cols] = left_ref[group, 0]
 
         @pl.when(step == 0)
         def _():
@@ -238,7 +235,7 @@
 
         total = total_ref[...]
         for part, ref in enumerate((wo_ref, wp_ref)):
-            start = pl.multiple_of(part * half * width + step * depth, depth)
+            start = pl.multiple_of(part * half * rows_dev + step * depth, depth)
             total += jnp.dot(
                 a_ref[:, pl.ds(start, depth)],
                 ref[0, :, 0].reshape(depth, cols_dev),
@@ -256,36 +253,38 @@
                     out_ref.dtype
                 )
 
-    whole = pl.BlockSpec(mine.shape, lambda n, k, place: (0, 0, 0))
-    part = pl.BlockSpec(far_low.shape, lambda n, k, place: (0, 0, 0))
-    weight = pl.BlockSpec(
-        (1, sides, 1, rows_dev, cols_dev), lambda n, k, place: (k, 0, n, 0, 0)
-    )
+    def source_spec(array, at):
+        return pl.BlockSpec((array.shape[0], 1, tok, width), lambda n, k, place: (0, at, 0, 0))
+
+    weight = pl.BlockSpec((1, sides, 1, rows_dev, cols_dev), lambda n, k, place: (k, 0, n, 0, 0))
     return pl.pallas_call(
         kernel,
         grid_spec=pltpu.PrefetchScalarGridSpec(
             num_scalar_prefetch=1,
             grid=(halves, steps),
             in_specs=[
-                whole, whole, whole, part, part, weight, weight,
+                *[source_spec(a, frame) for a in whole_sources],
+                *[source_spec(a, 0) for a in frame_sources],
+                weight,
+                weight,
                 pl.BlockSpec((1,) + gates.shape[1:], lambda n, k, place: (n, 0, 0)),
                 *[corner(e) for e in earlier],
             ],
             out_specs=pl.BlockSpec((RING, 1, tok, cols_dev), lambda n, k, place: (0, n, 0, 0)),
             scratch_shapes=[
-                pltpu.VMEM((RING * tok, groups * width), jnp.bfloat16),
+                pltpu.VMEM((RING * tok, groups * rows_dev), jnp.bfloat16),
                 pltpu.VMEM((RING * tok, cols_dev), jnp.float32),
             ],
         ),
         out_shape=jax.ShapeDtypeStruct((RING, halves, tok, cols_dev), jnp.bfloat16),
         compiler_params=pltpu.CompilerParams(vmem_limit_bytes=VMEM),
         cost_estimate=pl.CostEstimate(
-            flops=2 * RING * tok * groups * width * halves * cols_dev,
+            flops=2 * RING * tok * groups * rows_dev * halves * cols_dev,
             bytes_accessed=12 * 1024 * 1024,
             transcendentals=0,
         ),
         name="project",
-    )(place, *sources, weight_own, weight_pair, gates, *earlier)
+    )(place, *whole_sources, *frame_sources, weight_own, weight_pair, gates, *earlier)
 
 
 def add_branch(slot, position, branch, base, entering, partial):
@@ -356,20 +355,6 @@
         lax.all_to_all, axis_name="spatial", split_axis=0, concat_axis=0, tiled=True
     )
 
-    kv0, kv1, query = pack(queries, keys, values)
-    kv0 = to_heads(kv0)
-    kv1 = to_heads(hold(kv1, kv0))
-    kv0 = hold(kv0, kv1)
-    kv0_before, kv0_after = lax.ppermute(kv0, "queue", up), lax.ppermute(kv0, "queue", down)
-    query = to_heads(hold(query, kv1))
-    kv1 = hold(kv1, query)
-    kv1_before, kv1_after = lax.ppermute(kv1, "queue", up), lax.ppermute(kv1, "queue", down)
-
-    weight = lax.all_gather(out_weight, ("queue", "spatial"), axis_index_groups=along_y, axis=0)
-    weight = hold(weight, query)
-    weight = lax.all_gather(weight, "spatial", axis_index_groups=along_z, axis=0)
-    weight = weight.reshape(-1, 2, 2, *out_weight.shape)
-
     selector = (levels[:, None] == jnp.arange(gate_table.shape[0], dtype=jnp.int32)[None, :]).astype(
         jnp.float32
     )
@@ -380,6 +365,20 @@
     gates = jnp.where(y_low == 0, jnp.stack((gates, other_gates)), jnp.stack((other_gates, gates)))
     gates = lax.dynamic_slice_in_dim(gates, y_low * RING * frames, RING * frames, axis=1)
 
+    kv0, kv1, query = pack(queries, keys, values)
+    kv0 = to_heads(kv0)
+    kv0_before, kv0_after = lax.ppermute(kv0, "queue", up), lax.ppermute(kv0, "queue", down)
+    kv1 = to_heads(hold(kv1, kv0, gates))
+    query = to_heads(hold(query, kv1, kv0_before, kv0_after))
+    shifted = lax.ppermute(last_frame(hidden, kv0_before), "queue", up)
+    kv1 = hold(kv1, query, shifted)
+    kv1_before, kv1_after = lax.ppermute(kv1, "queue", up), lax.ppermute(kv1, "queue", down)
+
+    weight = lax.all_gather(out_weight, ("queue", "spatial"), axis_index_groups=along_y, axis=0)
+    weight = hold(weight, query)
+    weight = lax.all_gather(weight, "spatial", axis_index_groups=along_z, axis=0)
+    weight = weight.reshape(-1, 2, 2, *out_weight.shape)
+
     def spread(attended):
         mine = to_heads(attended)
         left = lax.ppermute(mine, "queue", ring_up)
@@ -388,26 +387,25 @@
         far_high = lax.ppermute(right[SPATIAL // 2 :], "queue", ring_down)
         return mine, left, right, far_low, far_high
 
-    head0 = (position_now, query, kv0, kv0_before, kv0_after)
-    head1 = (position_now, query, kv1, kv1_before, kv1_after)
-    odd, token = attend(1, 0, *head0, None)
-    even, token = attend(0, 0, *head0, None, token, gates)
-    shifted = lax.ppermute(last_frame(hidden, token), "queue", up)
-    odd, token = attend(1, 1, *head1, odd, token)
+    first, token = attend(None, position_now, query, 0, kv0, kv0_before, kv0_after)
+    whole_sources = spread(first)
+    head1 = (position_now, query, 1, kv1, kv1_before, kv1_after)
+    odd, token = attend(1, *head1, token, whole_sources[0])
     odd_sources = spread(odd)
-    even, token = attend(0, 1, *head1, even, token)
+    even, token = attend(0, *head1, token, *whole_sources[1:3])
     even_sources = spread(even)
     weight_own = hold(weight, token)
     weight_pair = lax.ppermute(weight_own, "spatial", swap_core)
-
-    branch = project(1, 1, place, odd_sources, weight_own, weight_pair, gates, shifted)
+    weights = (weight_own, weight_pair, gates)
+
+    branch = project(1, 1, place, whole_sources, odd_sources, *weights)
     crossing = lax.ppermute(branch[:1], "queue", [(p, p + RING) for p in range(QUEUE - RING)])
     branch = jnp.concatenate((crossing, branch[1:]))
     to_positions = functools.partial(
         lax.all_to_all, axis_name="queue", split_axis=0, concat_axis=0, axis_index_groups=ring, tiled=True
     )
     result = add_branch(0, position_now, to_positions(branch), shifted, entering, None)
-    branch = project(0, 0, place, even_sources, weight_own, weight_pair, gates)
+    branch = project(0, 0, place, whole_sources, even_sources, *weights)
     return add_branch(1, position_now, to_positions(branch), hidden, None, result)
 
 

time: 291 us -> 341 us (1.17)
  waiting for transfers between devices: 103 us -> 127 us
  starting transfers between devices: 50.8 us -> 63.1 us
  local copies, waits for them, and re-layouts: 7.16 us -> 13.4 us
  blocking collectives: 42.8 us -> 48.7 us
    all_to_all x2 -> x3, waiting for transfers between devices: 19.1 us -> 88.9 us  [the longest x1 39.5 us: body(): kv1 = to_heads(hold(kv1, kv0, gates))]
    ppermute x1, waiting for transfers between devices: 38.3 us -> 0.01 us  [body(): other_gates = lax.ppermute(gates, 'queue', swap_low)]
    all_to_all x1 -> x2, blocking collectives: 16.6 us -> 48.7 us  [spread(): mine = to_heads(attended)]
    all_to_all x1 -> x0, blocking collectives: 26.2 us -> none  [body(): kv0 = to_heads(kv0)]
    all_gather x1, waiting for transfers between devices: 16.7 us -> 0.02 us  [body(): lax.all_gather(out_weight, ('queue', 'spatial'), axis_index_groups=along_...]
    all_to_all x1, waiting for transfers between devices: 14.9 us -> 0.01 us  [spread(): mine = to_heads(attended)]
    ppermute x1, waiting for transfers between devices: 0.01 us -> 13.5 us  [body(): shifted = lax.ppermute(last_frame(hidden, kv0_before), 'queue', up)]
    all_to_all x2 -> x3, starting transfers between devices: 7.31 us -> 17.6 us  [the longest x1 8.26 us: body(): kv0 = to_heads(kv0)]
  transfers between devices with their start and end apart: 23 -> 28, of which waited for: 9 -> 11; matrix products, arithmetic and copies ran while one was open for 1% -> 2% of each run, Pallas kernels for 21% -> 18%
where the time goes in v2:
time: 341 us; the launch traced here: 338 us
  waiting for transfers between devices  127 us (37%)
  Pallas kernels  68.9 us (20%)
  starting transfers between devices  63.1 us (19%)
  blocking collectives  48.7 us (14%)
  between operations  13.7 us (4%)
  local copies, waits for them, and re-layouts  13.4 us (4%)
    all_to_all x2, blocking collectives, spread(): mine = to_heads(attended)  48.7 us
    all_to_all x1, waiting for transfers between devices, body(): kv1 = to_heads(hold(kv1, kv0, gates))  39.5 us
    pallas_call x3, Pallas kernels, attend(): pl.pallas_call(kernel, grid_spec=pltpu.PrefetchScalarGridSpec(num_scalar_...  33.6 us
    all_to_all x1, waiting for transfers between devices, body(): query = to_heads(hold(query, kv1, kv0_before, kv0_after))  32 us
    pallas_call x2, Pallas kernels, project(): pl.pallas_call(kernel, grid_spec=pltpu.PrefetchScalarGridSpec(num_scalar_...  20.7 us
    all_to_all x1, waiting for transfers between devices, body(): kv0 = to_heads(kv0)  17.4 us
    ppermute x1, waiting for transfers between devices, body(): shifted = lax.ppermute(last_frame(hidden, kv0_before), 'queue', up)  13.5 us
    unnamed x44, local copies, waits for them, and re-layouts  10.3 us
  transfers between devices with their start and end apart: 28, of which 11 were waited for; matrix products, arithmetic and copies ran while one was open for 2% of the time, Pallas kernels for 18%

profile of v2, /device:TPU:0, one launch (start us, length us, event | category | flops | bytes accessed | tf_op | source)
XLA Modules:
  0.0 337.8 jit_solution(16704746205205691286)
XLA Ops:
  6.5 4.3 %pack.1 = (bf16[16,2,2,64,128]{4,3,2,1,0:T(8,128)(2,1)}, bf16[16,2,2,64,128]{4,3,2,1,0:T(8,128)(2,1)}, bf16[16,2,64,256]{3,2,1,0:T(8,128)(2,1)}) custom-call(bf16[2,64,4096]{2,1,0:T(8,128)(2,1)} %q_ref.1, bf16[2,64,4096]{2,1,0:T(8,128)(2,1)} %k_ref.1, bf16[2,64,4096]{2,1,0:T(8,128)(2,1)} %v_ref.1), custom_call_target="tpu_custom_call" | custom-call | tf_op jit(solution)/shard_map/pack/pallas_call | solution.py:50
  10.8 8.3 %all-to-all-start = ((bf16[16,2,2,64,128]{4,3,2,1,0:T(8,128)(2,1)}), bf16[16,2,2,64,128]{4,3,2,1,0:T(8,128)(2,1)S(1)}, u32[]{:S(2)}, u32[]{:S(2)}) async-start(bf16[16,2,2,64,128]{4,3,2,1,0:T(8,128)(2,1)} %get-tuple-element.16), calls=%async_computation | async-start | bytes 2097152 | tf_op jit(solution)/shard_map/all_to_all | solution.py:369
  19.3 0.8 collective-permute-start
  20.1 17.4 %all-to-all-done.refs_1_.own_ref = bf16[16,2,2,64,128]{4,3,2,1,0:T(8,128)(2,1)S(1)} async-done(((bf16[16,2,2,64,128]{4,3,2,1,0:T(8,128)(2,1)}), bf16[16,2,2,64,128]{4,3,2,1,0:T(8,128)(2,1)S(1)}, u32[]{:S(2)}, u32[]{:S(2)}) %all-to-all-start) | async-done | bytes 1048608 | tf_op jit(solution)/shard_map/all_to_all | solution.py:369
  37.5 3.5 %collective-permute-start.1 = (bf16[16,2,2,64,128]{4,3,2,1,0:T(8,128)(2,1)S(1)}, bf16[16,2,2,64,128]{4,3,2,1,0:T(8,128)(2,1)S(1)}, u32[]{:S(2)}, u32[]{:S(2)}) collective-permute-start(bf16[16,2,2,64,128]{4,3,2,1,0:T(8,128)(2,1)S(1)} %all-to-all-done.refs_1_.own_ref), channel_id=1, source_target_pairs={{0,16},{16,32},{32,48},{48,64},{64,80},{80,96},{96,112},{1,17},{17... | collective-permute-start | bytes 3145736 | tf_op jit(solution)/shard_map/ppermute | solution.py:370
  41.0 1.3 collective-permute-start.2
  42.3 0.6 fusion.1.refs_2_.refs_12_
  42.9 0.7 hold.5
  43.6 3.7 %all-to-all-start.1 = ((bf16[16,2,2,64,128]{4,3,2,1,0:T(8,128)(2,1)}), bf16[16,2,2,64,128]{4,3,2,1,0:T(8,128)(2,1)S(1)}, u32[]{:S(2)}, u32[]{:S(2)}) async-start(bf16[16,2,2,64,128]{4,3,2,1,0:T(8,128)(2,1)} %hold.5), calls=%async_computation.1 | async-start | bytes 2097152 | tf_op jit(solution)/shard_map/all_to_all | solution.py:371
  47.3 0.7 all-gather.5.cloned.1.call-update
  48.0 39.5 %all-to-all-done.1.refs_1_.refs_0_ = bf16[16,2,2,64,128]{4,3,2,1,0:T(8,128)(2,1)S(1)} async-done(((bf16[16,2,2,64,128]{4,3,2,1,0:T(8,128)(2,1)}), bf16[16,2,2,64,128]{4,3,2,1,0:T(8,128)(2,1)S(1)}, u32[]{:S(2)}, u32[]{:S(2)}) %all-to-all-start.1) | async-done | bytes 1048608 | tf_op jit(solution)/shard_map/all_to_all | solution.py:371
  87.6 1.0 copy-done.3
  88.9 0.7 hold.6
  89.6 5.7 %all-to-all-start.2 = ((bf16[16,2,64,256]{3,2,1,0:T(8,128)(2,1)}), bf16[16,2,64,256]{3,2,1,0:T(8,128)(2,1)S(1)}, u32[]{:S(2)}, u32[]{:S(2)}) async-start(bf16[16,2,64,256]{3,2,1,0:T(8,128)(2,1)} %hold.6), calls=%async_computation.2 | async-start | bytes 2097152 | tf_op jit(solution)/shard_map/all_to_all | solution.py:372
  95.3 32.0 %all-to-all-done.2.q_ref.refs_1_ = bf16[16,2,64,256]{3,2,1,0:T(8,128)(2,1)S(1)} async-done(((bf16[16,2,64,256]{3,2,1,0:T(8,128)(2,1)}), bf16[16,2,64,256]{3,2,1,0:T(8,128)(2,1)S(1)}, u32[]{:S(2)}, u32[]{:S(2)}) %all-to-all-start.2) | async-done | bytes 1048608 | tf_op jit(solution)/shard_map/all_to_all | solution.py:372
  127.3 1.0 copy-done.1
  128.2 0.7 hold.8
  128.9 2.0 last_frame.1
  130.9 2.4 collective-permute-start.7
  133.4 13.5 %collective-permute-done.7.refs_2_.base_ref = bf16[1,64,5120]{2,1,0:T(8,128)(2,1)} collective-permute-done((bf16[1,64,5120]{2,1,0:T(8,128)(2,1)}, bf16[1,64,5120]{2,1,0:T(8,128)(2,1)}, u32[]{:S(2)}, u32[]{:S(2)}) %collective-permute-start.7) | collective-permute-done | bytes 655392 | tf_op jit(solution)/shard_map/ppermute | solution.py:373
  146.9 0.7 hold.7.own_ref
  147.5 4.4 %collective-permute-start.8 = (bf16[16,2,2,64,128]{4,3,2,1,0:T(8,128)(2,1)}, bf16[16,2,2,64,128]{4,3,2,1,0:T(8,128)(2,1)S(1)}, u32[]{:S(2)}, u32[]{:S(2)}) collective-permute-start(bf16[16,2,2,64,128]{4,3,2,1,0:T(8,128)(2,1)} %hold.7.own_ref), channel_id=1, source_target_pairs={{0,16},{16,32},{32,48},{48,64},{64,80},{80,96},{96,112},{1,17},{17... | collective-permute-start | bytes 3145736 | tf_op jit(solution)/shard_map/ppermute | solution.py:375
  152.0 1.3 collective-permute-start.9
  153.3 17.6 %attend.3 = (bf16[16,2,64,128]{3,2,1,0:T(8,128)(2,1)S(1)}, f32[8,128]{1,0:T(8,128)S(1)}) custom-call(s32[1]{0:T(128)} %bitcast.pos_ref, bf16[16,2,64,256]{3,2,1,0:T(8,128)(2,1)S(1)} %copy-done.2, bf16[16,2,2,64,128]{4,3,2,1,0:T(8,128)(2,1)S(1)} %copy-done.8, bf16[16,2,2,64,128]{4,3,2,1,0:T(8,128)(2,1)S(1)} %copy-done.6, ...), custom_call_target="tpu_custom_call" | custom-call | flops 10737418240 | bytes 4194304 | tf_op jit(solution)/shard_map/attend/pallas_call | solution.py:174
  171.0 32.9 %all_to_all.40.rest_1_.refs_0_ = bf16[16,2,64,128]{3,2,1,0:T(8,128)(2,1)S(1)} all-to-all(bf16[16,2,64,128]{3,2,1,0:T(8,128)(2,1)S(1)} %get-tuple-element.17), channel_id=1, replica_groups=mesh['queue'=8,'spatial'=16] {'spatial'}, dimensions={0} | all-to-all | bytes 1048576 | tf_op jit(solution)/shard_map/all_to_all | solution.py:383
  203.9 2.4 collective-permute-start.3
  206.3 0.9 collective-permute-start.4
  207.1 7.6 %attend.4 = (bf16[16,1,64,128]{3,2,1,0:T(8,128)(2,1)S(1)}, f32[8,128]{1,0:T(8,128)S(1)}) custom-call(s32[1]{0:T(128)} %bitcast.pos_ref, bf16[16,2,64,256]{3,2,1,0:T(8,128)(2,1)S(1)} %copy-done.2, bf16[16,2,2,64,128]{4,3,2,1,0:T(8,128)(2,1)S(1)} %copy-done.4, bf16[16,2,2,64,128]{4,3,2,1,0:T(8,128)(2,1)S(1)} %collective-permute-done.8.before_ref, ...), custom_call_target="tpu_custom_call" | custom-call | flops 5368709120 | bytes 4194304 | tf_op jit(solution)/shard_map/attend/pallas_call | solution.py:174
  214.8 3.8 %collective-permute-done.3.rest_1_.refs_1_ = bf16[16,2,64,128]{3,2,1,0:T(8,128)(2,1)S(1)} collective-permute-done((bf16[16,2,64,128]{3,2,1,0:T(8,128)(2,1)S(1)}, bf16[16,2,64,128]{3,2,1,0:T(8,128)(2,1)S(1)}, u32[]{:S(2)}, u32[]{:S(2)}) %collective-permute-start.3) | collective-permute-done | bytes 524320 | tf_op jit(solution)/shard_map/ppermute | solution.py:384
  218.6 0.9 collective-permute-done.4.rest_2_.refs_2_
  219.5 8.4 %attend.5 = (bf16[16,1,64,128]{3,2,1,0:T(8,128)(2,1)}, f32[8,128]{1,0:T(8,128)S(1)}) custom-call(s32[1]{0:T(128)} %bitcast.pos_ref, bf16[16,2,64,256]{3,2,1,0:T(8,128)(2,1)S(1)} %copy-done.2, bf16[16,2,2,64,128]{4,3,2,1,0:T(8,128)(2,1)S(1)} %copy-done.4, bf16[16,2,2,64,128]{4,3,2,1,0:T(8,128)(2,1)S(1)} %collective-permute-done.8.before_ref, ...), custom_call_target="tpu_custom_call" | custom-call | flops 5368709120 | bytes 4194304 | tf_op jit(solution)/shard_map/attend/pallas_call | solution.py:174
  228.5 0.7 hold.9.refs_10_
  229.2 15.8 %all_to_all.41.refs_5_ = bf16[16,1,64,128]{3,2,1,0:T(8,128)(2,1)S(1)} all-to-all(bf16[16,1,64,128]{3,2,1,0:T(8,128)(2,1)S(1)} %get-tuple-element.22), channel_id=1, replica_groups=mesh['queue'=8,'spatial'=16] {'spatial'}, dimensions={0} | all-to-all | bytes 524288 | tf_op jit(solution)/shard_map/all_to_all | solution.py:383
  245.2 3.0 collective-permute-start.16
  248.3 0.7 slice.33
  249.0 3.2 collective-permute-start.6
  252.2 3.2 collective-permute-done.15.refs_6_
  255.5 0.6 copy-done.10
  256.1 0.7 slice.37
  256.8 2.6 collective-permute-start.18
  259.5 3.8 %all-to-all-start.4 = ((bf16[16,1,64,128]{3,2,1,0:T(8,128)(2,1)}), bf16[16,1,64,128]{3,2,1,0:T(8,128)(2,1)S(1)}, u32[]{:S(2)}, u32[]{:S(2)}) async-start(bf16[16,1,64,128]{3,2,1,0:T(8,128)(2,1)} %get-tuple-element.20), calls=%async_computation.4 | async-start | bytes 524288 | tf_op jit(solution)/shard_map/all_to_all | solution.py:383
  263.3 0.6 copy-done.14
  264.0 0.7 copy-done.16
  264.7 0.9 copy-done.11
  265.6 0.9 copy-done.13
  266.6 0.9 copy-done.15
  267.5 0.9 copy-done.17
  268.4 9.9 %project.3 = bf16[4,2,64,640]{3,2,1,0:T(8,128)(2,1)S(1)} custom-call(s32[2]{0:T(128)S(1)} %pad_add_fusion.place_ref, bf16[16,2,64,128]{3,2,1,0:T(8,128)(2,1)S(1)} %all_to_all.40.rest_1_.refs_0_, bf16[16,2,64,128]{3,2,1,0:T(8,128)(2,1)S(1)} %collective-permute-done.3.rest_1_.refs_1_, bf16[16,2,64,128]{3,2,1,0:T(8,128)(2,1)S(1)} %collective-permute-done.4.rest_2_.refs_2_, ...), custom_call_target="tpu_custom_call" | custom-call | flops 2684354560 | bytes 12582912 | tf_op jit(solution)/shard_map/project/pallas_call | solution.py:260
  278.3 0.7 slice.38
  279.0 1.9 collective-permute-start.19
  281.0 3.2 collective-permute-start.11
  284.6 1.8 pad_maximum_fusion
  286.4 3.5 %all-to-all-start.7 = ((bf16[4,2,64,640]{3,2,1,0:T(8,128)(2,1)}), bf16[4,2,64,640]{3,2,1,0:T(8,128)(2,1)S(1)}, u32[]{:S(2)}, u32[]{:S(2)}) async-start(bf16[4,2,64,640]{3,2,1,0:T(8,128)(2,1)} %pad_maximum_fusion), calls=%async_computation.7 | async-start | bytes 1310720 | tf_op jit(solution)/shard_map/all_to_all | solution.py:407
  290.5 1.5 collective-permute-start.12
  291.9 0.9 slice.35
  292.9 1.9 collective-permute-start.13
  294.7 8.5 %collective-permute-done.12.refs_8_ = bf16[8,1,64,128]{3,2,1,0:T(8,128)(2,1)S(1)} collective-permute-done((bf16[8,1,64,128]{3,2,1,0:T(8,128)(2,1)S(1)}, bf16[8,1,64,128]{3,2,1,0:T(8,128)(2,1)S(1)}, u32[]{:S(2)}, u32[]{:S(2)}) %collective-permute-start.12) | collective-permute-done | bytes 131104 | tf_op jit(solution)/shard_map/ppermute | solution.py:386
  303.2 10.8 %project.2 = bf16[4,2,64,640]{3,2,1,0:T(8,128)(2,1)} custom-call(s32[2]{0:T(128)S(1)} %pad_add_fusion.place_ref, bf16[16,2,64,128]{3,2,1,0:T(8,128)(2,1)S(1)} %all_to_all.40.rest_1_.refs_0_, bf16[16,2,64,128]{3,2,1,0:T(8,128)(2,1)S(1)} %collective-permute-done.3.rest_1_.refs_1_, bf16[16,2,64,128]{3,2,1,0:T(8,128)(2,1)S(1)} %collective-permute-done.4.rest_2_.refs_2_, ...), custom_call_target="tpu_custom_call" | custom-call | flops 2684354560 | bytes 12582912 | tf_op jit(solution)/shard_map/project/pallas_call | solution.py:260
  314.0 0.9 copy-done.20
  314.9 3.5 %all-to-all-start.5 = ((bf16[4,2,64,640]{3,2,1,0:T(8,128)(2,1)}), bf16[4,2,64,640]{3,2,1,0:T(8,128)(2,1)S(1)}, u32[]{:S(2)}, u32[]{:S(2)}) async-start(bf16[4,2,64,640]{3,2,1,0:T(8,128)(2,1)} %project.2), calls=%async_computation.5 | async-start | bytes 1310720 | tf_op jit(solution)/shard_map/all_to_all | solution.py:409
  318.4 2.6 add_branch.2.rest_0_
  320.9 6.9 %all-to-all-done.5.b_ref = bf16[4,2,64,640]{3,2,1,0:T(8,128)(2,1)S(1)} async-done(((bf16[4,2,64,640]{3,2,1,0:T(8,128)(2,1)}), bf16[4,2,64,640]{3,2,1,0:T(8,128)(2,1)S(1)}, u32[]{:S(2)}, u32[]{:S(2)}) %all-to-all-start.5) | async-done | bytes 655392 | tf_op jit(solution)/shard_map/all_to_all | solution.py:409
  327.8 0.8 copy-done.19
  328.7 2.3 add_branch.3
  (66 shorter events, 2.9 us)
Async XLA Ops:
  6.5 12.6 %copy-start = (f32[50,640]{1,0:T(8,128)S(1)}, f32[50,640]{1,0:T(8,128)}, u32[]{:S(2)}) copy-start(f32[50,640]{1,0:T(8,128)} %param.13) | copy-start | bytes 384004
  10.8 8.3 %copy-start.21 = (s32[16]{0:T(128)S(1)}, s32[16]{0:T(128)}, u32[]{:S(2)}) copy-start(s32[16]{0:T(128)} %param.14) | copy-start | bytes 196
  10.8 26.7 %all-to-all-start = ((bf16[16,2,2,64,128]{4,3,2,1,0:T(8,128)(2,1)}), bf16[16,2,2,64,128]{4,3,2,1,0:T(8,128)(2,1)S(1)}, u32[]{:S(2)}, u32[]{:S(2)}) async-start(bf16[16,2,2,64,128]{4,3,2,1,0:T(8,128)(2,1)} %get-tuple-element.16), calls=%async_computation | async-start | bytes 2097152 | tf_op jit(solution)/shard_map/all_to_all | solution.py:369
  19.3 22.9 %collective-permute-start = (f32[16,640]{1,0:T(8,128)S(1)}, f32[16,640]{1,0:T(8,128)S(1)}, u32[]{:S(2)}, u32[]{:S(2)}) collective-permute-start(f32[16,640]{1,0:T(8,128)S(1)} %fusion.3), channel_id=1, source_target_pairs={{0,64},{16,80},{32,96},{48,112},{64,0},{80,16},{96,32},{112,48},{1... | collective-permute-start | bytes 122888 | tf_op jit(solution)/shard_map/ppermute | solution.py:364
  37.5 5.4 %copy-start.7 = (bf16[16,2,2,64,128]{4,3,2,1,0:T(8,128)(2,1)}, bf16[16,2,2,64,128]{4,3,2,1,0:T(8,128)(2,1)S(1)}, u32[]{:S(2)}) copy-start(bf16[16,2,2,64,128]{4,3,2,1,0:T(8,128)(2,1)S(1)} %all-to-all-done.refs_1_.own_ref) | copy-start | bytes 3145732
  37.5 50.0 %collective-permute-start.1 = (bf16[16,2,2,64,128]{4,3,2,1,0:T(8,128)(2,1)S(1)}, bf16[16,2,2,64,128]{4,3,2,1,0:T(8,128)(2,1)S(1)}, u32[]{:S(2)}, u32[]{:S(2)}) collective-permute-start(bf16[16,2,2,64,128]{4,3,2,1,0:T(8,128)(2,1)S(1)} %all-to-all-done.refs_1_.own_ref), channel_id=1, source_target_pairs={{0,16},{16,32},{32,48},{48,64},{64,80},{80,96},{96,112},{1,17},{17... | collective-permute-start | bytes 3145736 | tf_op jit(solution)/shard_map/ppermute | solution.py:370
  41.0 46.6 %collective-permute-start.2 = (bf16[16,2,2,64,128]{4,3,2,1,0:T(8,128)(2,1)S(1)}, bf16[16,2,2,64,128]{4,3,2,1,0:T(8,128)(2,1)}, u32[]{:S(2)}, u32[]{:S(2)}) collective-permute-start(bf16[16,2,2,64,128]{4,3,2,1,0:T(8,128)(2,1)S(1)} %all-to-all-done.refs_1_.own_ref), channel_id=1, source_target_pairs={{16,0},{32,16},{48,32},{64,48},{80,64},{96,80},{112,96},{17,1},{33... | collective-permute-start | bytes 3145736 | tf_op jit(solution)/shard_map/ppermute | solution.py:370
  43.6 43.9 %all-to-all-start.1 = ((bf16[16,2,2,64,128]{4,3,2,1,0:T(8,128)(2,1)}), bf16[16,2,2,64,128]{4,3,2,1,0:T(8,128)(2,1)S(1)}, u32[]{:S(2)}, u32[]{:S(2)}) async-start(bf16[16,2,2,64,128]{4,3,2,1,0:T(8,128)(2,1)} %hold.5), calls=%async_computation.1 | async-start | bytes 2097152 | tf_op jit(solution)/shard_map/all_to_all | solution.py:371
  47.3 48.0 %all-gather.5.cloned.1.call-start = ((), (), s32[]{:S(2)}) async-start(), calls=%async_computation.8 | async-start | bytes 1638400 | tf_op jit(solution)/shard_map/all_gather | solution.py:377
  87.5 1.0 copy-start.3
  87.5 1.3 copy-start.5
  89.6 37.7 %all-to-all-start.2 = ((bf16[16,2,64,256]{3,2,1,0:T(8,128)(2,1)}), bf16[16,2,64,256]{3,2,1,0:T(8,128)(2,1)S(1)}, u32[]{:S(2)}, u32[]{:S(2)}) async-start(bf16[16,2,64,256]{3,2,1,0:T(8,128)(2,1)} %hold.6), calls=%async_computation.2 | async-start | bytes 2097152 | tf_op jit(solution)/shard_map/all_to_all | solution.py:372
  95.2 133.2 %all-gather.7.cloned.1.call-start = ((), (), s32[]{:S(2)}) async-start(), calls=%async_computation.9 | async-start | bytes 6553600 | tf_op jit(solution)/shard_map/all_gather | solution.py:379
  127.3 1.0 copy-start.1
  130.9 22.4 %copy-start.2 = (bf16[16,2,64,256]{3,2,1,0:T(8,128)(2,1)S(1)}, bf16[16,2,64,256]{3,2,1,0:T(8,128)(2,1)}, u32[]{:S(2)}) copy-start(bf16[16,2,64,256]{3,2,1,0:T(8,128)(2,1)} %copy-done.1) | copy-start | bytes 3145732
  130.9 22.4 %copy-start.6 = (bf16[16,2,2,64,128]{4,3,2,1,0:T(8,128)(2,1)S(1)}, bf16[16,2,2,64,128]{4,3,2,1,0:T(8,128)(2,1)}, u32[]{:S(2)}) copy-start(bf16[16,2,2,64,128]{4,3,2,1,0:T(8,128)(2,1)} %copy-done.5) | copy-start | bytes 3145732
  130.9 22.4 %copy-start.8 = (bf16[16,2,2,64,128]{4,3,2,1,0:T(8,128)(2,1)S(1)}, bf16[16,2,2,64,128]{4,3,2,1,0:T(8,128)(2,1)}, u32[]{:S(2)}) copy-start(bf16[16,2,2,64,128]{4,3,2,1,0:T(8,128)(2,1)} %copy-done.7) | copy-start | bytes 3145732
  130.9 15.9 %collective-permute-start.7 = (bf16[1,64,5120]{2,1,0:T(8,128)(2,1)}, bf16[1,64,5120]{2,1,0:T(8,128)(2,1)}, u32[]{:S(2)}, u32[]{:S(2)}) collective-permute-start(bf16[1,64,5120]{2,1,0:T(8,128)(2,1)} %last_frame.1), channel_id=1, source_target_pairs={{0,16},{16,32},{32,48},{48,64},{64,80},{80,96},{96,112},{1,17},{17... | collective-permute-start | bytes 1966088 | tf_op jit(solution)/shard_map/ppermute | solution.py:373
  147.5 59.6 %collective-permute-start.8 = (bf16[16,2,2,64,128]{4,3,2,1,0:T(8,128)(2,1)}, bf16[16,2,2,64,128]{4,3,2,1,0:T(8,128)(2,1)S(1)}, u32[]{:S(2)}, u32[]{:S(2)}) collective-permute-start(bf16[16,2,2,64,128]{4,3,2,1,0:T(8,128)(2,1)} %hold.7.own_ref), channel_id=1, source_target_pairs={{0,16},{16,32},{32,48},{48,64},{64,80},{80,96},{96,112},{1,17},{17... | collective-permute-start | bytes 3145736 | tf_op jit(solution)/shard_map/ppermute | solution.py:375
  152.0 55.1 %collective-permute-start.9 = (bf16[16,2,2,64,128]{4,3,2,1,0:T(8,128)(2,1)}, bf16[16,2,2,64,128]{4,3,2,1,0:T(8,128)(2,1)S(1)}, u32[]{:S(2)}, u32[]{:S(2)}) collective-permute-start(bf16[16,2,2,64,128]{4,3,2,1,0:T(8,128)(2,1)} %hold.7.own_ref), channel_id=1, source_target_pairs={{16,0},{32,16},{48,32},{64,48},{80,64},{96,80},{112,96},{17,1},{33... | collective-permute-start | bytes 3145736 | tf_op jit(solution)/shard_map/ppermute | solution.py:375
  153.3 53.8 %copy-start.4 = (bf16[16,2,2,64,128]{4,3,2,1,0:T(8,128)(2,1)S(1)}, bf16[16,2,2,64,128]{4,3,2,1,0:T(8,128)(2,1)}, u32[]{:S(2)}) copy-start(bf16[16,2,2,64,128]{4,3,2,1,0:T(8,128)(2,1)} %hold.7.own_ref) | copy-start | bytes 3145732
  203.9 14.7 %collective-permute-start.3 = (bf16[16,2,64,128]{3,2,1,0:T(8,128)(2,1)S(1)}, bf16[16,2,64,128]{3,2,1,0:T(8,128)(2,1)S(1)}, u32[]{:S(2)}, u32[]{:S(2)}) collective-permute-start(bf16[16,2,64,128]{3,2,1,0:T(8,128)(2,1)S(1)} %all_to_all.40.rest_1_.refs_0_), channel_id=1, source_target_pairs={{0,16},{16,32},{32,48},{48,0},{64,80},{80,96},{96,112},{112,64},{1... | collective-permute-start | bytes 1572872 | tf_op jit(solution)/shard_map/ppermute | solution.py:384
  206.3 13.2 %collective-permute-start.4 = (bf16[16,2,64,128]{3,2,1,0:T(8,128)(2,1)S(1)}, bf16[16,2,64,128]{3,2,1,0:T(8,128)(2,1)S(1)}, u32[]{:S(2)}, u32[]{:S(2)}) collective-permute-start(bf16[16,2,64,128]{3,2,1,0:T(8,128)(2,1)S(1)} %all_to_all.40.rest_1_.refs_0_), channel_id=1, source_target_pairs={{16,0},{32,16},{48,32},{0,48},{80,64},{96,80},{112,96},{64,112},{1... | collective-permute-start | bytes 1572872 | tf_op jit(solution)/shard_map/ppermute | solution.py:385
  227.9 0.6 copy-start.18
  229.2 35.5 %collective-permute-start.14 = (bf16[4,2,2,256,640]{4,3,2,1,0:T(8,128)(2,1)}, bf16[4,2,2,256,640]{4,3,2,1,0:T(8,128)(2,1)}, u32[]{:S(2)}, u32[]{:S(2)}) collective-permute-start(bf16[4,2,2,256,640]{4,3,2,1,0:T(8,128)(2,1)} %hold.9.refs_10_), channel_id=1, source_target_pairs={{0,1},{1,0},{2,3},{3,2},{4,5},{5,4},{6,7},{7,6},{8,9},{9,8},{10,11... | collective-permute-start | bytes 15728648 | tf_op jit(solution)/shard_map/ppermute | solution.py:398
  229.2 35.5 %copy-start.9 = (f32[2,8,640]{2,1,0:T(8,128)S(1)}, f32[2,8,640]{2,1,0:T(8,128)}, u32[]{:S(2)}) copy-start(f32[2,8,640]{2,1,0:T(8,128)} %fusion.1.refs_2_.refs_12_) | copy-start | bytes 122884
  244.9 10.5 %collective-permute-start.15 = (bf16[16,1,64,128]{3,2,1,0:T(8,128)(2,1)S(1)}, bf16[16,1,64,128]{3,2,1,0:T(8,128)(2,1)S(1)}, u32[]{:S(2)}, u32[]{:S(2)}) collective-permute-start(bf16[16,1,64,128]{3,2,1,0:T(8,128)(2,1)S(1)} %all_to_all.41.refs_5_), channel_id=1, source_target_pairs={{0,16},{16,32},{32,48},{48,0},{64,80},{80,96},{96,112},{112,64},{1... | collective-permute-start | bytes 786440 | tf_op jit(solution)/shard_map/ppermute | solution.py:384
  245.2 10.3 %collective-permute-start.16 = (bf16[16,1,64,128]{3,2,1,0:T(8,128)(2,1)S(1)}, bf16[16,1,64,128]{3,2,1,0:T(8,128)(2,1)S(1)}, u32[]{:S(2)}, u32[]{:S(2)}) collective-permute-start(bf16[16,1,64,128]{3,2,1,0:T(8,128)(2,1)S(1)} %all_to_all.41.refs_5_), channel_id=1, source_target_pairs={{16,0},{32,16},{48,32},{0,48},{80,64},{96,80},{112,96},{64,112},{1... | collective-permute-start | bytes 786440 | tf_op jit(solution)/shard_map/ppermute | solution.py:385
  248.2 15.1 %collective-permute-start.5 = (bf16[8,2,64,128]{3,2,1,0:T(8,128)(2,1)S(1)}, bf16[8,2,64,128]{3,2,1,0:T(8,128)(2,1)S(1)}, u32[]{:S(2)}, u32[]{:S(2)}) collective-permute-start(bf16[8,2,64,128]{3,2,1,0:T(8,128)(2,1)S(1)} %slice.32), channel_id=1, source_target_pairs={{0,16},{16,32},{32,48},{48,0},{64,80},{80,96},{96,112},{112,64},{1... | collective-permute-start | bytes 786440 | tf_op jit(solution)/shard_map/ppermute | solution.py:386
  249.0 14.3 %collective-permute-start.6 = (bf16[8,2,64,128]{3,2,1,0:T(8,128)(2,1)}, bf16[8,2,64,128]{3,2,1,0:T(8,128)(2,1)S(1)}, u32[]{:S(2)}, u32[]{:S(2)}) collective-permute-start(bf16[8,2,64,128]{3,2,1,0:T(8,128)(2,1)} %slice.33), channel_id=1, source_target_pairs={{16,0},{32,16},{48,32},{0,48},{80,64},{96,80},{112,96},{64,112},{1... | collective-permute-start | bytes 786440 | tf_op jit(solution)/shard_map/ppermute | solution.py:387
  255.4 0.7 copy-start.10
  255.4 7.9 %collective-permute-start.17 = (bf16[8,1,64,128]{3,2,1,0:T(8,128)(2,1)S(1)}, bf16[8,1,64,128]{3,2,1,0:T(8,128)(2,1)S(1)}, u32[]{:S(2)}, u32[]{:S(2)}) collective-permute-start(bf16[8,1,64,128]{3,2,1,0:T(8,128)(2,1)S(1)} %slice.36), channel_id=1, source_target_pairs={{0,16},{16,32},{32,48},{48,0},{64,80},{80,96},{96,112},{112,64},{1... | collective-permute-start | bytes 393224 | tf_op jit(solution)/shard_map/ppermute | solution.py:386
  256.1 0.8 copy-start.12
  256.8 7.1 %collective-permute-start.18 = (bf16[8,1,64,128]{3,2,1,0:T(8,128)(2,1)}, bf16[8,1,64,128]{3,2,1,0:T(8,128)(2,1)S(1)}, u32[]{:S(2)}, u32[]{:S(2)}) collective-permute-start(bf16[8,1,64,128]{3,2,1,0:T(8,128)(2,1)} %slice.37), channel_id=1, source_target_pairs={{16,0},{32,16},{48,32},{0,48},{80,64},{96,80},{112,96},{64,112},{1... | collective-permute-start | bytes 393224 | tf_op jit(solution)/shard_map/ppermute | solution.py:387
  259.5 21.4 %all-to-all-start.4 = ((bf16[16,1,64,128]{3,2,1,0:T(8,128)(2,1)}), bf16[16,1,64,128]{3,2,1,0:T(8,128)(2,1)S(1)}, u32[]{:S(2)}, u32[]{:S(2)}) async-start(bf16[16,1,64,128]{3,2,1,0:T(8,128)(2,1)} %get-tuple-element.20), calls=%async_computation.4 | async-start | bytes 524288 | tf_op jit(solution)/shard_map/all_to_all | solution.py:383
  263.3 0.7 copy-start.14
  264.0 0.7 copy-start.16
  264.7 1.0 copy-start.11
  265.6 0.9 copy-start.13
  266.6 0.9 copy-start.15
  267.5 0.9 copy-start.17
  279.0 5.6 %collective-permute-start.19 = (bf16[1,2,64,640]{3,2,1,0:T(8,128)(2,1)}, bf16[1,2,64,640]{3,2,1,0:T(8,128)(2,1)}, u32[]{:S(2)}, u32[]{:S(2)}) collective-permute-start(bf16[1,2,64,640]{3,2,1,0:T(8,128)(2,1)} %slice.38), channel_id=1, source_target_pairs={{0,64},{16,80},{32,96},{48,112},{1,65},{17,81},{33,97},{49,113},{2... | collective-permute-start | bytes 491528 | tf_op jit(solution)/shard_map/ppermute | solution.py:402
  281.0 9.5 %collective-permute-start.10 = (bf16[16,1,64,128]{3,2,1,0:T(8,128)(2,1)S(1)}, bf16[16,1,64,128]{3,2,1,0:T(8,128)(2,1)S(1)}, u32[]{:S(2)}, u32[]{:S(2)}) collective-permute-start(bf16[16,1,64,128]{3,2,1,0:T(8,128)(2,1)S(1)} %all-to-all-done.4.refs_5_), channel_id=1, source_target_pairs={{0,16},{16,32},{32,48},{48,0},{64,80},{80,96},{96,112},{112,64},{1... | collective-permute-start | bytes 786440 | tf_op jit(solution)/shard_map/ppermute | solution.py:384
  281.0 11.0 %collective-permute-start.11 = (bf16[16,1,64,128]{3,2,1,0:T(8,128)(2,1)S(1)}, bf16[16,1,64,128]{3,2,1,0:T(8,128)(2,1)}, u32[]{:S(2)}, u32[]{:S(2)}) collective-permute-start(bf16[16,1,64,128]{3,2,1,0:T(8,128)(2,1)S(1)} %all-to-all-done.4.refs_5_), channel_id=1, source_target_pairs={{16,0},{32,16},{48,32},{0,48},{80,64},{96,80},{112,96},{64,112},{1... | collective-permute-start | bytes 786440 | tf_op jit(solution)/shard_map/ppermute | solution.py:385
  286.4 27.6 %all-to-all-start.7 = ((bf16[4,2,64,640]{3,2,1,0:T(8,128)(2,1)}), bf16[4,2,64,640]{3,2,1,0:T(8,128)(2,1)S(1)}, u32[]{:S(2)}, u32[]{:S(2)}) async-start(bf16[4,2,64,640]{3,2,1,0:T(8,128)(2,1)} %pad_maximum_fusion), calls=%async_computation.7 | async-start | bytes 1310720 | tf_op jit(solution)/shard_map/all_to_all | solution.py:407
  290.5 12.8 %collective-permute-start.12 = (bf16[8,1,64,128]{3,2,1,0:T(8,128)(2,1)S(1)}, bf16[8,1,64,128]{3,2,1,0:T(8,128)(2,1)S(1)}, u32[]{:S(2)}, u32[]{:S(2)}) collective-permute-start(bf16[8,1,64,128]{3,2,1,0:T(8,128)(2,1)S(1)} %slice.34), channel_id=1, source_target_pairs={{0,16},{16,32},{32,48},{48,0},{64,80},{80,96},{96,112},{112,64},{1... | collective-permute-start | bytes 393224 | tf_op jit(solution)/shard_map/ppermute | solution.py:386
  292.9 10.4 %collective-permute-start.13 = (bf16[8,1,64,128]{3,2,1,0:T(8,128)(2,1)S(1)}, bf16[8,1,64,128]{3,2,1,0:T(8,128)(2,1)S(1)}, u32[]{:S(2)}, u32[]{:S(2)}) collective-permute-start(bf16[8,1,64,128]{3,2,1,0:T(8,128)(2,1)S(1)} %slice.35), channel_id=1, source_target_pairs={{16,0},{32,16},{48,32},{0,48},{80,64},{96,80},{112,96},{64,112},{1... | collective-permute-start | bytes 393224 | tf_op jit(solution)/shard_map/ppermute | solution.py:387
  314.0 0.9 copy-start.20
  314.9 12.9 %all-to-all-start.5 = ((bf16[4,2,64,640]{3,2,1,0:T(8,128)(2,1)}), bf16[4,2,64,640]{3,2,1,0:T(8,128)(2,1)S(1)}, u32[]{:S(2)}, u32[]{:S(2)}) async-start(bf16[4,2,64,640]{3,2,1,0:T(8,128)(2,1)} %project.2), calls=%async_computation.5 | async-start | bytes 1310720 | tf_op jit(solution)/shard_map/all_to_all | solution.py:409
  327.8 0.9 copy-start.19
Sparse Core Ops, SparseCore 0:
  49.8 40.7 all-gather.4
  129.1 79.4 all-gather.6

commit v3 on v1

--- a/solution.py
+++ b/solution.py
@@ -356,9 +356,19 @@
         lax.all_to_all, axis_name="spatial", split_axis=0, concat_axis=0, tiled=True
     )
 
+    selector = (levels[:, None] == jnp.arange(gate_table.shape[0], dtype=jnp.int32)[None, :]).astype(
+        jnp.float32
+    )
+    gates = jnp.dot(
+        selector, gate_table, precision=lax.Precision.HIGHEST, preferred_element_type=jnp.float32
+    )
+    other_gates = lax.ppermute(gates, "queue", swap_low)
+    gates = jnp.where(y_low == 0, jnp.stack((gates, other_gates)), jnp.stack((other_gates, gates)))
+    gates = lax.dynamic_slice_in_dim(gates, y_low * RING * frames, RING * frames, axis=1)
+
     kv0, kv1, query = pack(queries, keys, values)
     kv0 = to_heads(kv0)
-    kv1 = to_heads(hold(kv1, kv0))
+    kv1 = to_heads(hold(kv1, kv0, gates))
     kv0 = hold(kv0, kv1)
     kv0_before, kv0_after = lax.ppermute(kv0, "queue", up), lax.ppermute(kv0, "queue", down)
     query = to_heads(hold(query, kv1))
@@ -369,16 +379,6 @@
     weight = hold(weight, query)
     weight = lax.all_gather(weight, "spatial", axis_index_groups=along_z, axis=0)
     weight = weight.reshape(-1, 2, 2, *out_weight.shape)
-
-    selector = (levels[:, None] == jnp.arange(gate_table.shape[0], dtype=jnp.int32)[None, :]).astype(
-        jnp.float32
-    )
-    gates = jnp.dot(
-        selector, gate_table, precision=lax.Precision.HIGHEST, preferred_element_type=jnp.float32
-    )
-    other_gates = lax.ppermute(gates, "queue", swap_low)
-    gates = jnp.where(y_low == 0, jnp.stack((gates, other_gates)), jnp.stack((other_gates, gates)))
-    gates = lax.dynamic_slice_in_dim(gates, y_low * RING * frames, RING * frames, axis=1)
 
     def spread(attended):
         mine = to_heads(attended)
@@ -391,16 +391,16 @@
     head0 = (position_now, query, kv0, kv0_before, kv0_after)
     head1 = (position_now, query, kv1, kv1_before, kv1_after)
     odd, token = attend(1, 0, *head0, None)
-    even, token = attend(0, 0, *head0, None, token, gates)
     shifted = lax.ppermute(last_frame(hidden, token), "queue", up)
+    even, token = attend(0, 0, *head0, None, token)
     odd, token = attend(1, 1, *head1, odd, token)
     odd_sources = spread(odd)
-    even, token = attend(0, 1, *head1, even, token)
-    even_sources = spread(even)
     weight_own = hold(weight, token)
     weight_pair = lax.ppermute(weight_own, "spatial", swap_core)
-
-    branch = project(1, 1, place, odd_sources, weight_own, weight_pair, gates, shifted)
+    even, token = attend(0, 1, *head1, even, token, shifted)
+    even_sources = spread(even)
+
+    branch = project(1, 1, place, odd_sources, weight_own, weight_pair, gates)
     crossing = lax.ppermute(branch[:1], "queue", [(p, p + RING) for p in range(QUEUE - RING)])
     branch = jnp.concatenate((crossing, branch[1:]))
     to_positions = functools.partial(

time: 291 us -> 276 us (0.948)
  blocking collectives: 42.8 us -> 26.9 us
  waiting for transfers between devices: 103 us -> 88.2 us
  local copies, waits for them, and re-layouts: 7.16 us -> 16.2 us
  starting transfers between devices: 50.8 us -> 58.4 us
    all_to_all x1 -> x0, blocking collectives: 26.2 us -> none  [body(): kv0 = to_heads(kv0)]
    ppermute x1, waiting for transfers between devices: 38.3 us -> 13.3 us  [body(): other_gates = lax.ppermute(gates, 'queue', swap_low)]
    ppermute x1, waiting for transfers between devices: 0.01 us -> 15.9 us  [body(): lax.ppermute(kv0, 'queue', up)]
    all_to_all x1, blocking collectives: 16.6 us -> 26.9 us  [spread(): mine = to_heads(attended)]
    all_to_all x1 -> x2, starting transfers between devices: 3.65 us -> 12.3 us  [the longest x1 8.26 us: body(): kv0 = to_heads(kv0)]
    all_to_all x1, waiting for transfers between devices: 14.9 us -> 6.69 us  [spread(): mine = to_heads(attended)]
    unnamed x32 -> x50, local copies, waits for them, and re-layouts: 5.61 us -> 13.7 us
    ppermute x2, waiting for transfers between devices: 6.41 us -> 0.01 us  [spread(): left = lax.ppermute(mine, 'queue', ring_up)]
  transfers between devices with their start and end apart: 23 -> 24, of which waited for: 9 -> 10; matrix products, arithmetic and copies ran while one was open for 1% -> 2% of each run, Pallas kernels for 21% -> 22%
where the time goes in v3:
time: 276 us; the launch traced here: 274 us
  waiting for transfers between devices  88.2 us (32%)
  Pallas kernels  69.2 us (25%)
  starting transfers between devices  58.4 us (21%)
  blocking collectives  26.9 us (10%)
  local copies, waits for them, and re-layouts  16.2 us (6%)
  between operations  13.7 us (5%)
    pallas_call x4, Pallas kernels, attend(): pl.pallas_call(kernel, grid_spec=pltpu.PrefetchScalarGridSpec(num_scalar_...  33.7 us
    all_to_all x1, blocking collectives, spread(): mine = to_heads(attended)  26.9 us
    pallas_call x2, Pallas kernels, project(): pl.pallas_call(kernel, grid_spec=pltpu.PrefetchScalarGridSpec(num_scalar_...  20.3 us
    all_to_all x1, waiting for transfers between devices, body(): kv1 = to_heads(hold(kv1, kv0, gates))  17.3 us
    all_gather x1, waiting for transfers between devices, body(): lax.all_gather(out_weight, ('queue', 'spatial'), axis_index_groups=along_...  16.8 us
    ppermute x1, waiting for transfers between devices, body(): lax.ppermute(kv0, 'queue', up)  15.9 us
    unnamed x50, local copies, waits for them, and re-layouts  13.7 us
    ppermute x1, waiting for transfers between devices, body(): other_gates = lax.ppermute(gates, 'queue', swap_low)  13.3 us
  transfers between devices with their start and end apart: 24, of which 10 were waited for; matrix products, arithmetic and copies ran while one was open for 2% of the time, Pallas kernels for 22%

profile of v3, /device:TPU:0, one launch (start us, length us, event | category | flops | bytes accessed | tf_op | source)
XLA Modules:
  0.0 274.4 jit_solution(2414338814765920000)
XLA Ops:
  6.5 4.3 %pack.1 = (bf16[16,2,2,64,128]{4,3,2,1,0:T(8,128)(2,1)}, bf16[16,2,2,64,128]{4,3,2,1,0:T(8,128)(2,1)}, bf16[16,2,64,256]{3,2,1,0:T(8,128)(2,1)}) custom-call(bf16[2,64,4096]{2,1,0:T(8,128)(2,1)} %q_ref.1, bf16[2,64,4096]{2,1,0:T(8,128)(2,1)} %k_ref.1, bf16[2,64,4096]{2,1,0:T(8,128)(2,1)} %v_ref.1), custom_call_target="tpu_custom_call" | custom-call | tf_op jit(solution)/shard_map/pack/pallas_call | solution.py:50
  10.8 8.3 %all-to-all-start = ((bf16[16,2,2,64,128]{4,3,2,1,0:T(8,128)(2,1)}), bf16[16,2,2,64,128]{4,3,2,1,0:T(8,128)(2,1)S(1)}, u32[]{:S(2)}, u32[]{:S(2)}) async-start(bf16[16,2,2,64,128]{4,3,2,1,0:T(8,128)(2,1)} %get-tuple-element.17), calls=%async_computation | async-start | bytes 2097152 | tf_op jit(solution)/shard_map/all_to_all | solution.py:370
  19.1 0.2 fusion.3
  19.3 0.8 collective-permute-start
  20.1 13.3 %collective-permute-done = f32[16,640]{1,0:T(8,128)S(1)} collective-permute-done((f32[16,640]{1,0:T(8,128)S(1)}, f32[16,640]{1,0:T(8,128)S(1)}, u32[]{:S(2)}, u32[]{:S(2)}) %collective-permute-start) | collective-permute-done | bytes 40992 | tf_op jit(solution)/shard_map/ppermute | solution.py:365
  33.4 0.6 fusion.1.refs_2_.gates_ref
  34.0 3.5 %all-to-all-done.refs_1_.refs_0_ = bf16[16,2,2,64,128]{4,3,2,1,0:T(8,128)(2,1)S(1)} async-done(((bf16[16,2,2,64,128]{4,3,2,1,0:T(8,128)(2,1)}), bf16[16,2,2,64,128]{4,3,2,1,0:T(8,128)(2,1)S(1)}, u32[]{:S(2)}, u32[]{:S(2)}) %all-to-all-start) | async-done | bytes 1048608 | tf_op jit(solution)/shard_map/all_to_all | solution.py:370
  37.5 1.0 copy-done.3
  38.5 0.7 hold.6
  39.2 4.0 %all-to-all-start.1 = ((bf16[16,2,2,64,128]{4,3,2,1,0:T(8,128)(2,1)}), bf16[16,2,2,64,128]{4,3,2,1,0:T(8,128)(2,1)S(1)}, u32[]{:S(2)}, u32[]{:S(2)}) async-start(bf16[16,2,2,64,128]{4,3,2,1,0:T(8,128)(2,1)} %hold.6), calls=%async_computation.1 | async-start | bytes 2097152 | tf_op jit(solution)/shard_map/all_to_all | solution.py:371
  43.2 0.7 all-gather.5.cloned.1.call-update
  43.9 17.3 %all-to-all-done.1.refs_1_.refs_0_ = bf16[16,2,2,64,128]{4,3,2,1,0:T(8,128)(2,1)S(1)} async-done(((bf16[16,2,2,64,128]{4,3,2,1,0:T(8,128)(2,1)}), bf16[16,2,2,64,128]{4,3,2,1,0:T(8,128)(2,1)S(1)}, u32[]{:S(2)}, u32[]{:S(2)}) %all-to-all-start.1) | async-done | bytes 1048608 | tf_op jit(solution)/shard_map/all_to_all | solution.py:371
  61.2 1.0 copy-done.1
  62.2 0.7 hold.7
  62.9 3.7 %all-to-all-start.2 = ((bf16[16,2,64,256]{3,2,1,0:T(8,128)(2,1)}), bf16[16,2,64,256]{3,2,1,0:T(8,128)(2,1)S(1)}, u32[]{:S(2)}, u32[]{:S(2)}) async-start(bf16[16,2,64,256]{3,2,1,0:T(8,128)(2,1)} %hold.7), calls=%async_computation.2 | async-start | bytes 2097152 | tf_op jit(solution)/shard_map/all_to_all | solution.py:374
  66.6 16.8 %all-gather.5.cloned.1.call-done = bf16[1024,640]{1,0:T(8,128)(2,1)} async-done(((bf16[256,640]{1,0:T(8,128)(2,1)}), bf16[1024,640]{1,0:T(8,128)(2,1)}) %all-gather.5.cloned.1.call-update) | async-done | bytes 1310736 | tf_op jit(solution)/shard_map/all_gather | solution.py:378
  83.3 1.9 all-to-all-done.2.refs_1_.q_ref
  85.2 1.0 copy-done.5
  86.2 0.7 hold.10
  86.9 0.7 hold.9.own_ref
  87.6 3.6 %collective-permute-start.3 = (bf16[16,2,2,64,128]{4,3,2,1,0:T(8,128)(2,1)}, bf16[16,2,2,64,128]{4,3,2,1,0:T(8,128)(2,1)S(1)}, u32[]{:S(2)}, u32[]{:S(2)}) collective-permute-start(bf16[16,2,2,64,128]{4,3,2,1,0:T(8,128)(2,1)} %hold.9.own_ref), channel_id=1, source_target_pairs={{0,16},{16,32},{32,48},{48,64},{64,80},{80,96},{96,112},{1,17},{17... | collective-permute-start | bytes 3145736 | tf_op jit(solution)/shard_map/ppermute | solution.py:373
  91.2 1.3 collective-permute-start.4
  92.5 0.7 hold.8.own_ref
  93.1 4.6 %collective-permute-start.1 = (bf16[16,2,2,64,128]{4,3,2,1,0:T(8,128)(2,1)}, bf16[16,2,2,64,128]{4,3,2,1,0:T(8,128)(2,1)S(1)}, u32[]{:S(2)}, u32[]{:S(2)}) collective-permute-start(bf16[16,2,2,64,128]{4,3,2,1,0:T(8,128)(2,1)} %hold.8.own_ref), channel_id=1, source_target_pairs={{0,16},{16,32},{32,48},{48,64},{64,80},{80,96},{96,112},{1,17},{17... | collective-permute-start | bytes 3145736 | tf_op jit(solution)/shard_map/ppermute | solution.py:376
  97.7 1.3 collective-permute-start.2
  99.0 15.9 %collective-permute-done.3.before_ref = bf16[16,2,2,64,128]{4,3,2,1,0:T(8,128)(2,1)S(1)} collective-permute-done((bf16[16,2,2,64,128]{4,3,2,1,0:T(8,128)(2,1)}, bf16[16,2,2,64,128]{4,3,2,1,0:T(8,128)(2,1)S(1)}, u32[]{:S(2)}, u32[]{:S(2)}) %collective-permute-start.3) | collective-permute-done | bytes 1048608 | tf_op jit(solution)/shard_map/ppermute | solution.py:373
  115.0 4.5 %collective-permute-done.4.after_ref = bf16[16,2,2,64,128]{4,3,2,1,0:T(8,128)(2,1)} collective-permute-done((bf16[16,2,2,64,128]{4,3,2,1,0:T(8,128)(2,1)}, bf16[16,2,2,64,128]{4,3,2,1,0:T(8,128)(2,1)}, u32[]{:S(2)}, u32[]{:S(2)}) %collective-permute-start.4) | collective-permute-done | bytes 1048608 | tf_op jit(solution)/shard_map/ppermute | solution.py:373
  119.5 8.9 %attend.4 = (bf16[16,64,256]{2,1,0:T(8,128)(2,1)S(1)}, f32[8,128]{1,0:T(8,128)S(1)}) custom-call(s32[1]{0:T(128)} %bitcast.pos_ref, bf16[16,2,64,256]{3,2,1,0:T(8,128)(2,1)S(1)} %copy-done.6, bf16[16,2,2,64,128]{4,3,2,1,0:T(8,128)(2,1)S(1)} %copy-done.4, bf16[16,2,2,64,128]{4,3,2,1,0:T(8,128)(2,1)S(1)} %collective-permute-done.3.before_ref, ...), custom_call_target="tpu_custom_call" | custom-call | flops 5368709120 | bytes 4194304 | tf_op jit(solution)/shard_map/attend/pallas_call | solution.py:178
  128.3 1.2 copy-done.22
  129.6 8.8 %attend.5 = (bf16[16,64,256]{2,1,0:T(8,128)(2,1)S(1)}, f32[8,128]{1,0:T(8,128)S(1)}) custom-call(s32[1]{0:T(128)} %bitcast.pos_ref, bf16[16,2,64,256]{3,2,1,0:T(8,128)(2,1)S(1)} %copy-done.6, bf16[16,2,2,64,128]{4,3,2,1,0:T(8,128)(2,1)S(1)} %copy-done.4, bf16[16,2,2,64,128]{4,3,2,1,0:T(8,128)(2,1)S(1)} %copy-done.22, ...), custom_call_target="tpu_custom_call" | custom-call | flops 5368709120 | bytes 4194304 | tf_op jit(solution)/shard_map/attend/pallas_call | solution.py:178
  138.4 0.8 copy-done.9
  139.3 1.1 collective-permute-done.2.after_ref
  140.4 7.6 %attend.6 = (bf16[16,64,256]{2,1,0:T(8,128)(2,1)S(1)}, f32[8,128]{1,0:T(8,128)S(1)}) custom-call(s32[1]{0:T(128)} %bitcast.pos_ref, bf16[16,2,64,256]{3,2,1,0:T(8,128)(2,1)S(1)} %copy-done.6, bf16[16,2,2,64,128]{4,3,2,1,0:T(8,128)(2,1)S(1)} %copy-done.2, ...), custom_call_target="tpu_custom_call", output_to_operand_aliasing={{0}: (5, {})} | custom-call | flops 5368709120 | bytes 4194304 | tf_op jit(solution)/shard_map/attend/pallas_call | solution.py:178
  148.1 0.8 copy-done.12
  148.8 0.6 copy-done.14
  149.4 1.0 copy-done.17
  150.4 1.0 copy-done.19
  151.4 0.7 hold.11.wo_ref
  152.1 2.1 last_frame.1
  154.1 3.3 %collective-permute-start.5 = (bf16[1,64,5120]{2,1,0:T(8,128)(2,1)}, bf16[1,64,5120]{2,1,0:T(8,128)(2,1)S(1)}, u32[]{:S(2)}, u32[]{:S(2)}) collective-permute-start(bf16[1,64,5120]{2,1,0:T(8,128)(2,1)} %last_frame.1), channel_id=1, source_target_pairs={{0,16},{16,32},{32,48},{48,64},{64,80},{80,96},{96,112},{1,17},{17... | collective-permute-start | bytes 1966088 | tf_op jit(solution)/shard_map/ppermute | solution.py:394
  157.5 26.9 %all_to_all.35.mine_ref = bf16[16,64,256]{2,1,0:T(8,128)(2,1)S(1)} all-to-all(bf16[16,64,256]{2,1,0:T(8,128)(2,1)S(1)} %copy-done.13), channel_id=1, replica_groups=mesh['queue'=8,'spatial'=16] {'spatial'}, dimensions={0} | all-to-all | bytes 1048576 | tf_op jit(solution)/shard_map/all_to_all | solution.py:384
  184.4 3.2 %collective-permute-start.12 = (bf16[16,64,256]{2,1,0:T(8,128)(2,1)S(1)}, bf16[16,64,256]{2,1,0:T(8,128)(2,1)}, u32[]{:S(2)}, u32[]{:S(2)}) collective-permute-start(bf16[16,64,256]{2,1,0:T(8,128)(2,1)S(1)} %all_to_all.35.mine_ref), channel_id=1, source_target_pairs={{16,0},{32,16},{48,32},{0,48},{80,64},{96,80},{112,96},{64,112},{1... | collective-permute-start | bytes 1572872 | tf_op jit(solution)/shard_map/ppermute | solution.py:386
  187.7 1.3 copy-done.10
  188.9 1.2 copy-done.18
  190.2 1.2 copy-done.20
  191.4 8.3 %attend.7 = (bf16[16,64,256]{2,1,0:T(8,128)(2,1)S(1)}, f32[8,128]{1,0:T(8,128)}) custom-call(s32[1]{0:T(128)} %bitcast.pos_ref, bf16[16,2,64,256]{3,2,1,0:T(8,128)(2,1)S(1)} %copy-done.6, bf16[16,2,2,64,128]{4,3,2,1,0:T(8,128)(2,1)S(1)} %copy-done.2, bf16[16,2,2,64,128]{4,3,2,1,0:T(8,128)(2,1)S(1)} %copy-done.18, ...), custom_call_target="tpu_custom_call", output_to_operand_aliasing={{0}: (5, {})} | custom-call | flops 5368709120 | bytes 4194304 | tf_op jit(solution)/shard_map/attend/pallas_call | solution.py:178
  199.7 0.8 copy-done.11
  200.5 4.3 %all-to-all-start.3 = ((bf16[16,64,256]{2,1,0:T(8,128)(2,1)}), bf16[16,64,256]{2,1,0:T(8,128)(2,1)S(1)}, u32[]{:S(2)}, u32[]{:S(2)}) async-start(bf16[16,64,256]{2,1,0:T(8,128)(2,1)} %copy-done.11), calls=%async_computation.3 | async-start | bytes 1048576 | tf_op jit(solution)/shard_map/all_to_all | solution.py:384
  204.8 0.7 slice.26
  205.5 1.7 slice.27
  207.2 3.2 %collective-permute-start.14 = (bf16[8,64,256]{2,1,0:T(8,128)(2,1)}, bf16[8,64,256]{2,1,0:T(8,128)(2,1)S(1)}, u32[]{:S(2)}, u32[]{:S(2)}) collective-permute-start(bf16[8,64,256]{2,1,0:T(8,128)(2,1)} %slice.27), channel_id=1, source_target_pairs={{16,0},{32,16},{48,32},{0,48},{80,64},{96,80},{112,96},{64,112},{1... | collective-permute-start | bytes 786440 | tf_op jit(solution)/shard_map/ppermute | solution.py:388
  210.5 6.7 %all-to-all-done.3.mine_ref = bf16[16,64,256]{2,1,0:T(8,128)(2,1)S(1)} async-done(((bf16[16,64,256]{2,1,0:T(8,128)(2,1)}), bf16[16,64,256]{2,1,0:T(8,128)(2,1)S(1)}, u32[]{:S(2)}, u32[]{:S(2)}) %all-to-all-start.3) | async-done | bytes 524320 | tf_op jit(solution)/shard_map/all_to_all | solution.py:384
  217.1 3.2 %collective-permute-start.7 = (bf16[16,64,256]{2,1,0:T(8,128)(2,1)S(1)}, bf16[16,64,256]{2,1,0:T(8,128)(2,1)S(1)}, u32[]{:S(2)}, u32[]{:S(2)}) collective-permute-start(bf16[16,64,256]{2,1,0:T(8,128)(2,1)S(1)} %all-to-all-done.3.mine_ref), channel_id=1, source_target_pairs={{16,0},{32,16},{48,32},{0,48},{80,64},{96,80},{112,96},{64,112},{1... | collective-permute-start | bytes 1572872 | tf_op jit(solution)/shard_map/ppermute | solution.py:386
  220.5 9.9 %project.3 = bf16[4,2,64,640]{3,2,1,0:T(8,128)(2,1)S(1)} custom-call(s32[2]{0:T(128)S(1)} %pad_add_fusion.place_ref, bf16[16,64,256]{2,1,0:T(8,128)(2,1)S(1)} %all_to_all.35.mine_ref, bf16[16,64,256]{2,1,0:T(8,128)(2,1)S(1)} %collective-permute-done.11.left_ref, bf16[16,64,256]{2,1,0:T(8,128)(2,1)} %collective-permute-done.12.right_ref, ...), custom_call_target="tpu_custom_call" | custom-call | flops 2684354560 | bytes 12582912 | tf_op jit(solution)/shard_map/project/pallas_call | solution.py:264
  230.4 1.3 collective-permute-start.15
  231.9 3.3 %collective-permute-start.9 = (bf16[8,64,256]{2,1,0:T(8,128)(2,1)S(1)}, bf16[8,64,256]{2,1,0:T(8,128)(2,1)S(1)}, u32[]{:S(2)}, u32[]{:S(2)}) collective-permute-start(bf16[8,64,256]{2,1,0:T(8,128)(2,1)S(1)} %slice.25), channel_id=1, source_target_pairs={{16,0},{32,16},{48,32},{0,48},{80,64},{96,80},{112,96},{64,112},{1... | collective-permute-start | bytes 786440 | tf_op jit(solution)/shard_map/ppermute | solution.py:388
  235.3 0.9 pad_maximum_fusion
  236.2 4.2 %all-to-all-start.6 = ((bf16[4,2,64,640]{3,2,1,0:T(8,128)(2,1)}), bf16[4,2,64,640]{3,2,1,0:T(8,128)(2,1)}, u32[]{:S(2)}, u32[]{:S(2)}) async-start(bf16[4,2,64,640]{3,2,1,0:T(8,128)(2,1)} %pad_maximum_fusion), calls=%async_computation.6 | async-start | bytes 1310720 | tf_op jit(solution)/shard_map/all_to_all | solution.py:409
  240.3 10.3 %project.2 = bf16[4,2,64,640]{3,2,1,0:T(8,128)(2,1)} custom-call(s32[2]{0:T(128)S(1)} %pad_add_fusion.place_ref, bf16[16,64,256]{2,1,0:T(8,128)(2,1)S(1)} %all-to-all-done.3.mine_ref, bf16[16,64,256]{2,1,0:T(8,128)(2,1)S(1)} %collective-permute-done.6.left_ref, bf16[16,64,256]{2,1,0:T(8,128)(2,1)S(1)} %collective-permute-done.7.right_ref, ...), custom_call_target="tpu_custom_call" | custom-call | flops 2684354560 | bytes 12582912 | tf_op jit(solution)/shard_map/project/pallas_call | solution.py:264
  250.7 4.7 %all-to-all-start.4 = ((bf16[4,2,64,640]{3,2,1,0:T(8,128)(2,1)}), bf16[4,2,64,640]{3,2,1,0:T(8,128)(2,1)S(1)}, u32[]{:S(2)}, u32[]{:S(2)}) async-start(bf16[4,2,64,640]{3,2,1,0:T(8,128)(2,1)} %project.2), calls=%async_computation.4 | async-start | bytes 1310720 | tf_op jit(solution)/shard_map/all_to_all | solution.py:411
  255.4 2.6 add_branch.2.rest_0_
  258.0 6.5 %all-to-all-done.4.b_ref = bf16[4,2,64,640]{3,2,1,0:T(8,128)(2,1)S(1)} async-done(((bf16[4,2,64,640]{3,2,1,0:T(8,128)(2,1)}), bf16[4,2,64,640]{3,2,1,0:T(8,128)(2,1)S(1)}, u32[]{:S(2)}, u32[]{:S(2)}) %all-to-all-start.4) | async-done | bytes 655392 | tf_op jit(solution)/shard_map/all_to_all | solution.py:411
  264.4 0.9 copy-done.23
  265.3 2.3 add_branch.3
  (63 shorter events, 0.5 us)
Async XLA Ops:
  6.5 12.5 %copy-start = (f32[50,640]{1,0:T(8,128)S(1)}, f32[50,640]{1,0:T(8,128)}, u32[]{:S(2)}) copy-start(f32[50,640]{1,0:T(8,128)} %param.13) | copy-start | bytes 384004
  10.8 8.3 %copy-start.24 = (s32[16]{0:T(128)S(1)}, s32[16]{0:T(128)}, u32[]{:S(2)}) copy-start(s32[16]{0:T(128)} %param.14) | copy-start | bytes 196
  10.8 26.7 %all-to-all-start = ((bf16[16,2,2,64,128]{4,3,2,1,0:T(8,128)(2,1)}), bf16[16,2,2,64,128]{4,3,2,1,0:T(8,128)(2,1)S(1)}, u32[]{:S(2)}, u32[]{:S(2)}) async-start(bf16[16,2,2,64,128]{4,3,2,1,0:T(8,128)(2,1)} %get-tuple-element.17), calls=%async_computation | async-start | bytes 2097152 | tf_op jit(solution)/shard_map/all_to_all | solution.py:370
  19.3 14.0 %collective-permute-start = (f32[16,640]{1,0:T(8,128)S(1)}, f32[16,640]{1,0:T(8,128)S(1)}, u32[]{:S(2)}, u32[]{:S(2)}) collective-permute-start(f32[16,640]{1,0:T(8,128)S(1)} %fusion.3), channel_id=1, source_target_pairs={{0,64},{16,80},{32,96},{48,112},{64,0},{80,16},{96,32},{112,48},{1... | collective-permute-start | bytes 122888 | tf_op jit(solution)/shard_map/ppermute | solution.py:365
  37.5 1.0 copy-start.3
  39.2 22.0 %all-to-all-start.1 = ((bf16[16,2,2,64,128]{4,3,2,1,0:T(8,128)(2,1)}), bf16[16,2,2,64,128]{4,3,2,1,0:T(8,128)(2,1)S(1)}, u32[]{:S(2)}, u32[]{:S(2)}) async-start(bf16[16,2,2,64,128]{4,3,2,1,0:T(8,128)(2,1)} %hold.6), calls=%async_computation.1 | async-start | bytes 2097152 | tf_op jit(solution)/shard_map/all_to_all | solution.py:371
  43.2 40.1 %all-gather.5.cloned.1.call-start = ((), (), s32[]{:S(2)}) async-start(), calls=%async_computation.7 | async-start | bytes 1638400 | tf_op jit(solution)/shard_map/all_gather | solution.py:378
  61.2 1.0 copy-start.1
  62.9 22.3 %all-to-all-start.2 = ((bf16[16,2,64,256]{3,2,1,0:T(8,128)(2,1)}), bf16[16,2,64,256]{3,2,1,0:T(8,128)(2,1)S(1)}, u32[]{:S(2)}, u32[]{:S(2)}) async-start(bf16[16,2,64,256]{3,2,1,0:T(8,128)(2,1)} %hold.7), calls=%async_computation.2 | async-start | bytes 2097152 | tf_op jit(solution)/shard_map/all_to_all | solution.py:374
  66.5 84.9 %all-gather.7.cloned.1.call-start = ((), (), s32[]{:S(2)}) async-start(), calls=%async_computation.8 | async-start | bytes 6553600 | tf_op jit(solution)/shard_map/all_gather | solution.py:380
  85.2 1.0 copy-start.5
  87.6 31.9 %copy-start.4 = (bf16[16,2,2,64,128]{4,3,2,1,0:T(8,128)(2,1)S(1)}, bf16[16,2,2,64,128]{4,3,2,1,0:T(8,128)(2,1)}, u32[]{:S(2)}) copy-start(bf16[16,2,2,64,128]{4,3,2,1,0:T(8,128)(2,1)} %hold.9.own_ref) | copy-start | bytes 3145732
  87.6 31.9 %copy-start.6 = (bf16[16,2,64,256]{3,2,1,0:T(8,128)(2,1)S(1)}, bf16[16,2,64,256]{3,2,1,0:T(8,128)(2,1)}, u32[]{:S(2)}) copy-start(bf16[16,2,64,256]{3,2,1,0:T(8,128)(2,1)} %copy-done.5) | copy-start | bytes 3145732
  87.6 27.4 %collective-permute-start.3 = (bf16[16,2,2,64,128]{4,3,2,1,0:T(8,128)(2,1)}, bf16[16,2,2,64,128]{4,3,2,1,0:T(8,128)(2,1)S(1)}, u32[]{:S(2)}, u32[]{:S(2)}) collective-permute-start(bf16[16,2,2,64,128]{4,3,2,1,0:T(8,128)(2,1)} %hold.9.own_ref), channel_id=1, source_target_pairs={{0,16},{16,32},{32,48},{48,64},{64,80},{80,96},{96,112},{1,17},{17... | collective-permute-start | bytes 3145736 | tf_op jit(solution)/shard_map/ppermute | solution.py:373
  91.2 28.3 %collective-permute-start.4 = (bf16[16,2,2,64,128]{4,3,2,1,0:T(8,128)(2,1)}, bf16[16,2,2,64,128]{4,3,2,1,0:T(8,128)(2,1)}, u32[]{:S(2)}, u32[]{:S(2)}) collective-permute-start(bf16[16,2,2,64,128]{4,3,2,1,0:T(8,128)(2,1)} %hold.9.own_ref), channel_id=1, source_target_pairs={{16,0},{32,16},{48,32},{64,48},{80,64},{96,80},{112,96},{17,1},{33... | collective-permute-start | bytes 3145736 | tf_op jit(solution)/shard_map/ppermute | solution.py:373
  93.1 46.1 %collective-permute-start.1 = (bf16[16,2,2,64,128]{4,3,2,1,0:T(8,128)(2,1)}, bf16[16,2,2,64,128]{4,3,2,1,0:T(8,128)(2,1)S(1)}, u32[]{:S(2)}, u32[]{:S(2)}) collective-permute-start(bf16[16,2,2,64,128]{4,3,2,1,0:T(8,128)(2,1)} %hold.8.own_ref), channel_id=1, source_target_pairs={{0,16},{16,32},{32,48},{48,64},{64,80},{80,96},{96,112},{1,17},{17... | collective-permute-start | bytes 3145736 | tf_op jit(solution)/shard_map/ppermute | solution.py:376
  97.7 42.6 %collective-permute-start.2 = (bf16[16,2,2,64,128]{4,3,2,1,0:T(8,128)(2,1)}, bf16[16,2,2,64,128]{4,3,2,1,0:T(8,128)(2,1)S(1)}, u32[]{:S(2)}, u32[]{:S(2)}) collective-permute-start(bf16[16,2,2,64,128]{4,3,2,1,0:T(8,128)(2,1)} %hold.8.own_ref), channel_id=1, source_target_pairs={{16,0},{32,16},{48,32},{64,48},{80,64},{96,80},{112,96},{17,1},{33... | collective-permute-start | bytes 3145736 | tf_op jit(solution)/shard_map/ppermute | solution.py:376
  115.0 13.4 %copy-start.21 = (bf16[16,2,2,64,128]{4,3,2,1,0:T(8,128)(2,1)}, bf16[16,2,2,64,128]{4,3,2,1,0:T(8,128)(2,1)S(1)}, u32[]{:S(2)}) copy-start(bf16[16,2,2,64,128]{4,3,2,1,0:T(8,128)(2,1)S(1)} %collective-permute-done.3.before_ref) | copy-start | bytes 3145732
  128.3 10.1 %copy-start.16 = (f32[8,128]{1,0:T(8,128)}, f32[8,128]{1,0:T(8,128)S(1)}, u32[]{:S(2)}) copy-start(f32[8,128]{1,0:T(8,128)S(1)} %get-tuple-element.18.rest_0_) | copy-start | bytes 12292
  128.3 1.2 copy-start.22
  129.6 10.8 %copy-start.2 = (bf16[16,2,2,64,128]{4,3,2,1,0:T(8,128)(2,1)S(1)}, bf16[16,2,2,64,128]{4,3,2,1,0:T(8,128)(2,1)}, u32[]{:S(2)}) copy-start(bf16[16,2,2,64,128]{4,3,2,1,0:T(8,128)(2,1)} %hold.8.own_ref) | copy-start | bytes 3145732
  138.4 0.8 copy-start.9
  148.0 0.8 copy-start.12
  148.8 0.6 copy-start.14
  149.4 1.0 copy-start.17
  150.4 1.0 copy-start.19
  152.1 5.4 %copy-start.13 = (bf16[16,64,256]{2,1,0:T(8,128)(2,1)S(1)}, bf16[16,64,256]{2,1,0:T(8,128)(2,1)}, u32[]{:S(2)}) copy-start(bf16[16,64,256]{2,1,0:T(8,128)(2,1)} %copy-done.12) | copy-start | bytes 1572868
  152.1 35.6 %copy-start.15 = (f32[8,128]{1,0:T(8,128)S(1)}, f32[8,128]{1,0:T(8,128)}, u32[]{:S(2)}) copy-start(f32[8,128]{1,0:T(8,128)} %copy-done.14) | copy-start | bytes 12292
  152.1 68.4 %collective-permute-start.10 = (bf16[4,2,2,256,640]{4,3,2,1,0:T(8,128)(2,1)}, bf16[4,2,2,256,640]{4,3,2,1,0:T(8,128)(2,1)}, u32[]{:S(2)}, u32[]{:S(2)}) collective-permute-start(bf16[4,2,2,256,640]{4,3,2,1,0:T(8,128)(2,1)} %hold.11.wo_ref), channel_id=1, source_target_pairs={{0,1},{1,0},{2,3},{3,2},{4,5},{5,4},{6,7},{7,6},{8,9},{9,8},{10,11... | collective-permute-start | bytes 15728648 | tf_op jit(solution)/shard_map/ppermute | solution.py:399
  154.1 33.5 %collective-permute-start.5 = (bf16[1,64,5120]{2,1,0:T(8,128)(2,1)}, bf16[1,64,5120]{2,1,0:T(8,128)(2,1)S(1)}, u32[]{:S(2)}, u32[]{:S(2)}) collective-permute-start(bf16[1,64,5120]{2,1,0:T(8,128)(2,1)} %last_frame.1), channel_id=1, source_target_pairs={{0,16},{16,32},{32,48},{48,64},{64,80},{80,96},{96,112},{1,17},{17... | collective-permute-start | bytes 1966088 | tf_op jit(solution)/shard_map/ppermute | solution.py:394
  184.4 20.4 %collective-permute-start.11 = (bf16[16,64,256]{2,1,0:T(8,128)(2,1)S(1)}, bf16[16,64,256]{2,1,0:T(8,128)(2,1)S(1)}, u32[]{:S(2)}, u32[]{:S(2)}) collective-permute-start(bf16[16,64,256]{2,1,0:T(8,128)(2,1)S(1)} %all_to_all.35.mine_ref), channel_id=1, source_target_pairs={{0,16},{16,32},{32,48},{48,0},{64,80},{80,96},{96,112},{112,64},{1... | collective-permute-start | bytes 1572872 | tf_op jit(solution)/shard_map/ppermute | solution.py:385
  184.4 21.1 %collective-permute-start.12 = (bf16[16,64,256]{2,1,0:T(8,128)(2,1)S(1)}, bf16[16,64,256]{2,1,0:T(8,128)(2,1)}, u32[]{:S(2)}, u32[]{:S(2)}) collective-permute-start(bf16[16,64,256]{2,1,0:T(8,128)(2,1)S(1)} %all_to_all.35.mine_ref), channel_id=1, source_target_pairs={{16,0},{32,16},{48,32},{0,48},{80,64},{96,80},{112,96},{64,112},{1... | collective-permute-start | bytes 1572872 | tf_op jit(solution)/shard_map/ppermute | solution.py:386
  187.6 12.1 %copy-start.7 = (bf16[1,64,5120]{2,1,0:T(8,128)(2,1)}, bf16[1,64,5120]{2,1,0:T(8,128)(2,1)S(1)}, u32[]{:S(2)}) copy-start(bf16[1,64,5120]{2,1,0:T(8,128)(2,1)S(1)} %collective-permute-done.5.rest_2_.base_ref) | copy-start | bytes 1966084
  187.6 1.3 copy-start.10
  188.9 1.2 copy-start.18
  190.2 1.2 copy-start.20
  199.7 0.8 copy-start.11
  200.5 20.0 %copy-start.8 = (f32[2,8,640]{2,1,0:T(8,128)S(1)}, f32[2,8,640]{2,1,0:T(8,128)}, u32[]{:S(2)}) copy-start(f32[2,8,640]{2,1,0:T(8,128)} %fusion.1.refs_2_.gates_ref) | copy-start | bytes 122884
  200.5 16.6 %all-to-all-start.3 = ((bf16[16,64,256]{2,1,0:T(8,128)(2,1)}), bf16[16,64,256]{2,1,0:T(8,128)(2,1)S(1)}, u32[]{:S(2)}, u32[]{:S(2)}) async-start(bf16[16,64,256]{2,1,0:T(8,128)(2,1)} %copy-done.11), calls=%async_computation.3 | async-start | bytes 1048576 | tf_op jit(solution)/shard_map/all_to_all | solution.py:384
  205.5 14.9 %collective-permute-start.13 = (bf16[8,64,256]{2,1,0:T(8,128)(2,1)}, bf16[8,64,256]{2,1,0:T(8,128)(2,1)S(1)}, u32[]{:S(2)}, u32[]{:S(2)}) collective-permute-start(bf16[8,64,256]{2,1,0:T(8,128)(2,1)} %slice.26), channel_id=1, source_target_pairs={{0,16},{16,32},{32,48},{48,0},{64,80},{80,96},{96,112},{112,64},{1... | collective-permute-start | bytes 786440 | tf_op jit(solution)/shard_map/ppermute | solution.py:387
  207.2 13.2 %collective-permute-start.14 = (bf16[8,64,256]{2,1,0:T(8,128)(2,1)}, bf16[8,64,256]{2,1,0:T(8,128)(2,1)S(1)}, u32[]{:S(2)}, u32[]{:S(2)}) collective-permute-start(bf16[8,64,256]{2,1,0:T(8,128)(2,1)} %slice.27), channel_id=1, source_target_pairs={{16,0},{32,16},{48,32},{0,48},{80,64},{96,80},{112,96},{64,112},{1... | collective-permute-start | bytes 786440 | tf_op jit(solution)/shard_map/ppermute | solution.py:388
  217.1 14.6 %collective-permute-start.6 = (bf16[16,64,256]{2,1,0:T(8,128)(2,1)S(1)}, bf16[16,64,256]{2,1,0:T(8,128)(2,1)S(1)}, u32[]{:S(2)}, u32[]{:S(2)}) collective-permute-start(bf16[16,64,256]{2,1,0:T(8,128)(2,1)S(1)} %all-to-all-done.3.mine_ref), channel_id=1, source_target_pairs={{0,16},{16,32},{32,48},{48,0},{64,80},{80,96},{96,112},{112,64},{1... | collective-permute-start | bytes 1572872 | tf_op jit(solution)/shard_map/ppermute | solution.py:385
  217.1 14.7 %collective-permute-start.7 = (bf16[16,64,256]{2,1,0:T(8,128)(2,1)S(1)}, bf16[16,64,256]{2,1,0:T(8,128)(2,1)S(1)}, u32[]{:S(2)}, u32[]{:S(2)}) collective-permute-start(bf16[16,64,256]{2,1,0:T(8,128)(2,1)S(1)} %all-to-all-done.3.mine_ref), channel_id=1, source_target_pairs={{16,0},{32,16},{48,32},{0,48},{80,64},{96,80},{112,96},{64,112},{1... | collective-permute-start | bytes 1572872 | tf_op jit(solution)/shard_map/ppermute | solution.py:386
  230.4 4.8 %collective-permute-start.15 = (bf16[1,2,64,640]{3,2,1,0:T(8,128)(2,1)S(1)}, bf16[1,2,64,640]{3,2,1,0:T(8,128)(2,1)S(1)}, u32[]{:S(2)}, u32[]{:S(2)}) collective-permute-start(bf16[1,2,64,640]{3,2,1,0:T(8,128)(2,1)S(1)} %slice.28), channel_id=1, source_target_pairs={{0,64},{16,80},{32,96},{48,112},{1,65},{17,81},{33,97},{49,113},{2... | collective-permute-start | bytes 491528 | tf_op jit(solution)/shard_map/ppermute | solution.py:404
  231.8 8.5 %collective-permute-start.8 = (bf16[8,64,256]{2,1,0:T(8,128)(2,1)S(1)}, bf16[8,64,256]{2,1,0:T(8,128)(2,1)S(1)}, u32[]{:S(2)}, u32[]{:S(2)}) collective-permute-start(bf16[8,64,256]{2,1,0:T(8,128)(2,1)S(1)} %slice.24), channel_id=1, source_target_pairs={{0,16},{16,32},{32,48},{48,0},{64,80},{80,96},{96,112},{112,64},{1... | collective-permute-start | bytes 786440 | tf_op jit(solution)/shard_map/ppermute | solution.py:387
  231.9 8.4 %collective-permute-start.9 = (bf16[8,64,256]{2,1,0:T(8,128)(2,1)S(1)}, bf16[8,64,256]{2,1,0:T(8,128)(2,1)S(1)}, u32[]{:S(2)}, u32[]{:S(2)}) collective-permute-start(bf16[8,64,256]{2,1,0:T(8,128)(2,1)S(1)} %slice.25), channel_id=1, source_target_pairs={{16,0},{32,16},{48,32},{0,48},{80,64},{96,80},{112,96},{64,112},{1... | collective-permute-start | bytes 786440 | tf_op jit(solution)/shard_map/ppermute | solution.py:388
  236.2 14.5 %all-to-all-start.6 = ((bf16[4,2,64,640]{3,2,1,0:T(8,128)(2,1)}), bf16[4,2,64,640]{3,2,1,0:T(8,128)(2,1)}, u32[]{:S(2)}, u32[]{:S(2)}) async-start(bf16[4,2,64,640]{3,2,1,0:T(8,128)(2,1)} %pad_maximum_fusion), calls=%async_computation.6 | async-start | bytes 1310720 | tf_op jit(solution)/shard_map/all_to_all | solution.py:409
  250.7 13.7 %all-to-all-start.4 = ((bf16[4,2,64,640]{3,2,1,0:T(8,128)(2,1)}), bf16[4,2,64,640]{3,2,1,0:T(8,128)(2,1)S(1)}, u32[]{:S(2)}, u32[]{:S(2)}) async-start(bf16[4,2,64,640]{3,2,1,0:T(8,128)(2,1)} %project.2), calls=%async_computation.4 | async-start | bytes 1310720 | tf_op jit(solution)/shard_map/all_to_all | solution.py:411
  264.4 0.9 copy-start.23
Sparse Core Ops, SparseCore 0:
  45.7 37.5 all-gather.4
  87.0 56.4 all-gather.6

commit v4 on v2

v4 whole, which is shorter than its diff:
```python
import functools

import jax
import jax.numpy as jnp
from jax import lax
from jax.experimental import pallas as pl
from jax.experimental.pallas import tpu as pltpu
from jax.sharding import PartitionSpec as P

HEADS = 32
HD = 128
WMAX = 2
NEG_FILL = -1e30
SCALE_LOG2 = (HD ** -0.5) * 1.4426950408889634
BLOCK_Q = 512
VMEM = 48 * 1024 * 1024
QUEUE = 8
RING = 4
SPATIAL = 16
CORES = 2
PACK = 4
SPAN = 2 * WMAX + 1
ANY = pl.BlockSpec(memory_space=pl.ANY)
TOKEN = (8, 128)


def corner(array):
    rows = 8 if array.dtype == jnp.float32 else 16
    block = (1,) * (array.ndim - 2) + (rows, 128)
    return pl.BlockSpec(block, lambda *at: (0,) * array.ndim)


def pack(queries, keys, values):
    frames, tok, width = keys.shape
    group = width // SPATIAL
    piece = width // PACK
    count = SPATIAL // PACK

    def kernel(q_ref, k_ref, v_ref, *out_refs):
        for i in range(count):
            for head, out_ref in enumerate(out_refs):
                cols = slice(i * group + head * HD, i * group + (head + 1) * HD)
                for at, ref in enumerate((q_ref, k_ref, v_ref)):
                    out_ref[i, at] = ref[:, :, cols]

    heads = group // HD
    return pl.pallas_call(
        kernel,
        grid=(PACK,),
        in_specs=[pl.BlockSpec((frames, tok, piece), lambda s: (0, 0, s))] * 3,
        out_specs=[pl.BlockSpec((count, 3, frames, tok, HD), lambda s: (s, 0, 0, 0, 0))] * heads,
        out_shape=[jax.ShapeDtypeStruct((SPATIAL, 3, frames, tok, HD), keys.dtype)] * heads,
        name="pack",
    )(queries, keys, values)


def last_frame(hidden, *earlier):
    frames, tok, width = hidden.shape

    def kernel(hidden_ref, *rest):
        rest[-1][...] = hidden_ref[...]

    return pl.pallas_call(
        kernel,
        grid=(1,),
        in_specs=[pl.BlockSpec((1, tok, width), lambda i: (frames - 1, 0, 0))]
        + [corner(e) for e in earlier],
        out_specs=pl.BlockSpec((1, tok, width), lambda i: (0, 0, 0)),
        out_shape=jax.ShapeDtypeStruct((1, tok, width), hidden.dtype),
        name="last_frame",
    )(hidden, *earlier)


def hold(array, *earlier):
    def kernel(*refs):
        pass

    return pl.pallas_call(
        kernel,
        grid=(1,),
        in_specs=[ANY] + [corner(e) for e in earlier],
        out_specs=ANY,
        out_shape=jax.ShapeDtypeStruct(array.shape, array.dtype),
        input_output_aliases={0: 0},
        name="hold",
    )(array, *earlier)


def attend(frame, position, own, before, after, *earlier):
    groups, _, frames, tok, width = own.shape
    row_count = groups * tok
    groups_block = BLOCK_Q // tok
    blocks = row_count // BLOCK_Q
    asked = range(frames) if frame is None else (frame,)
    before_from = min(asked)
    before_count = frames - before_from
    after_count = max(asked) + 1
    loaded = before_count + frames + after_count

    def kernel(pos_ref, q_ref, own_ref, before_ref, after_ref, *rest):
        out_ref, token_ref, kt_ref, vx_ref = rest[-4:]
        sources = (
            [(before_ref, 0, f) for f in range(before_count)]
            + [(own_ref, 1, f) for f in range(frames)]
            + [(after_ref, 0, f) for f in range(after_count)]
        )
        turn_frame = pl.program_id(0)

        @pl.when((turn_frame == 0) & (pl.program_id(1) == 0))
        def _():
            for at, (ref, key, f) in enumerate(sources):
                rows = slice(at * row_count, (at + 1) * row_count)
                turned = ref[:, key, f].reshape(row_count, width).T
                kt_ref[:width, rows] = turned
                kt_ref[width:, rows] = turned
                vx_ref[rows, :width] = ref[:, key + 1, f].reshape(row_count, width)
                vx_ref[rows, width:] = jnp.ones((row_count, width), vx_ref.dtype)

        q = q_ref[:, 0, 0].reshape(BLOCK_Q, width).astype(jnp.float32) * SCALE_LOG2
        high = q.astype(jnp.bfloat16)
        low = (q - high.astype(jnp.float32)).astype(jnp.bfloat16)
        q = jnp.concatenate((high, low), axis=1)
        position_now = pos_ref[0]

        def rows_of(step):
            start = (turn_frame + step) * row_count
            return pl.ds(pl.multiple_of(start, row_count), row_count)

        def scores(step):
            return jnp.dot(q, kt_ref[:, rows_of(step)], preferred_element_type=jnp.float32)

        top = jnp.full((BLOCK_Q, 1), NEG_FILL, jnp.float32)
        total = jnp.zeros((BLOCK_Q, 2 * width), jnp.float32)
        order = (2, 1, 3, 0, 4)
        ahead = scores(order[0])
        for turn, step in enumerate(order):
            s = ahead
            if turn + 1 < SPAN:
                ahead = scores(order[turn + 1])
            at = turn_frame + step
            absent = ((position_now == 0) & (at < before_count)) | (
                (position_now == QUEUE - 1) & (at >= before_count + frames)
            )
            peak = jnp.max(s, axis=1, keepdims=True)
            peak = jnp.where(absent, NEG_FILL, peak)
            lifted_top = jnp.maximum(top, peak)
            less = jnp.where(absent, -NEG_FILL, lifted_top)
            weights = jnp.exp2(s - less).astype(jnp.bfloat16)
            part = jnp.dot(weights, vx_ref[rows_of(step)], preferred_element_type=jnp.float32)
            total = total * jnp.exp2(top - lifted_top) + part
            top = lifted_top
        result = total[:, :width] / total[:, width:]
        out_ref[:, 0] = result.astype(out_ref.dtype).reshape(groups_block, tok, width)
        token_ref[...] = jnp.zeros_like(token_ref)

    first = asked[0]
    in_specs = [
        pl.BlockSpec((groups_block, 1, 1, tok, width), lambda f, b, pos: (b, 0, first + f, 0, 0)),
        pl.BlockSpec(own.shape, lambda f, b, pos: (0, 0, 0, 0, 0)),
        pl.BlockSpec(
            (groups, 2, before_count, tok, width),
            lambda f, b, pos: (0, 0, before_from // before_count, 0, 0),
        ),
        pl.BlockSpec((groups, 2, after_count, tok, width), lambda f, b, pos: (0, 0, 0, 0, 0)),
    ]
    return pl.pallas_call(
        kernel,
        grid_spec=pltpu.PrefetchScalarGridSpec(
            num_scalar_prefetch=1,
            grid=(len(asked), blocks),
            in_specs=in_specs + [corner(e) for e in earlier],
            out_specs=[
                pl.BlockSpec((groups_block, 1, tok, width), lambda f, b, pos: (b, f, 0, 0)),
                pl.BlockSpec(TOKEN, lambda f, b, pos: (0, 0)),
            ],
            scratch_shapes=[
                pltpu.VMEM((2 * width, loaded * row_count), jnp.bfloat16),
                pltpu.VMEM((loaded * row_count, 2 * width), jnp.bfloat16),
            ],
        ),
        out_shape=[
            jax.ShapeDtypeStruct((groups, len(asked), tok, width), own.dtype),
            jax.ShapeDtypeStruct(TOKEN, jnp.float32),
        ],
        compiler_params=pltpu.CompilerParams(vmem_limit_bytes=VMEM),
        cost_estimate=pl.CostEstimate(
            flops=len(asked) * row_count * SPAN * row_count * width * 8,
            bytes_accessed=4 * 1024 * 1024,
            transcendentals=len(asked) * row_count * SPAN * row_count,
        ),
        name="attend",
    )(position, own, own, before, after, *earlier)


def project(head, place, sources, weight_own, weight_pair, partial, gates, *earlier):
    mine = sources[0]
    groups, frames, tok, width = mine.shape
    steps, sides, halves, rows_dev, cols_dev = weight_own.shape
    half = steps * sides
    rows = frames * tok
    last = partial is not None

    def kernel(place_ref, mine_ref, left_ref, right_ref, low_ref, high_ref, wo_ref, wp_ref, *rest):
        out_ref, a_ref = rest[-2:]
        x, core = place_ref[0], place_ref[1]

        @pl.when(pl.program_id(0) == 0)
        def _():
            for i in range(half):
                z, side = i // sides, i % sides
                for part in range(CORES):
                    group = side * half + CORES * z + (core if part == 0 else 1 - core)
                    cols = slice((part * half + i) * width, (part * half + i + 1) * width)
                    far = high_ref[group - half] if side else low_ref[group]
                    a_ref[0:rows, cols] = mine_ref[group].reshape(rows, width)
                    a_ref[rows : 2 * rows, cols] = right_ref[group].reshape(rows, width)
                    a_ref[2 * rows : 3 * rows, cols] = far.reshape(rows, width)
                    a_ref[3 * rows :, cols] = left_ref[group].reshape(rows, width)

        total = jnp.dot(
            a_ref[:, : half * width],
            wo_ref[:, :, 0].reshape(half * width, cols_dev),
            preferred_element_type=jnp.float32,
        )
        total += jnp.dot(
            a_ref[:, half * width :],
            wp_ref[:, :, 0].reshape(half * width, cols_dev),
            preferred_element_type=jnp.float32,
        )
        if not last:
            out_ref[0] = total
            return
        total += rest[0][0]
        gates_ref = rest[1]
        for source in range(RING):
            at = lax.rem(x + source, RING)
            for f in range(frames):
                gate = gates_ref[0, pl.ds(at * frames + f, 1), :]
                start = source * rows + f * tok
                slot = at * frames + 1 if f == 0 else lax.rem(at + 1, RING) * frames
                out_ref[slot, 0] = (gate * total[start : start + tok]).astype(out_ref.dtype)

    def whole(array):
        return pl.BlockSpec(array.shape, lambda n, place: (0,) * array.ndim)

    weight = pl.BlockSpec(
        (steps, sides, 1, width, cols_dev), lambda n, place: (0, 0, n, head, 0)
    )
    partial_spec = pl.BlockSpec((1, RING * rows, cols_dev), lambda n, place: (n, 0, 0))
    in_specs = [*map(whole, sources), weight, weight]
    operands = [*sources, weight_own, weight_pair]
    if last:
        in_specs += [partial_spec, pl.BlockSpec((1,) + gates.shape[1:], lambda n, place: (n, 0, 0))]
        operands += [partial, gates]
        out_spec = pl.BlockSpec((RING * frames, 1, tok, cols_dev), lambda n, place: (0, n, 0, 0))
        out_shape = jax.ShapeDtypeStruct((RING * frames, halves, tok, cols_dev), jnp.bfloat16)
    else:
        out_spec = partial_spec
        out_shape = jax.ShapeDtypeStruct((halves, RING * rows, cols_dev), jnp.float32)
    return pl.pallas_call(
        kernel,
        grid_spec=pltpu.PrefetchScalarGridSpec(
            num_scalar_prefetch=1,
            grid=(halves,),
            in_specs=in_specs + [corner(e) for e in earlier],
            out_specs=out_spec,
            scratch_shapes=[pltpu.VMEM((RING * rows, groups * width), jnp.bfloat16)],
        ),
        out_shape=out_shape,
        compiler_params=pltpu.CompilerParams(vmem_limit_bytes=VMEM),
        cost_estimate=pl.CostEstimate(
            flops=2 * RING * rows * groups * width * halves * cols_dev,
            bytes_accessed=8 * 1024 * 1024,
            transcendentals=0,
        ),
        name="project_last" if last else "project_first",
    )(place, *operands, *earlier)


def add_branch(position, branch, hidden, shifted, entering):
    sources, frames, halves, tok, cols = branch.shape
    width = hidden.shape[-1]

    def kernel(pos_ref, b_ref, hidden_ref, shifted_ref, entering_ref, out_ref):
        def add(base_ref, replaced):
            for half in range(halves):
                for source in range(sources):
                    start = (half * sources + source) * cols
                    at = slice(start, start + cols)
                    value = base_ref[0, :, at].astype(jnp.float32)
                    value += b_ref[source, 0, half].astype(jnp.float32)
                    if replaced:
                        value = jnp.where(
                            pos_ref[0] == 0, entering_ref[:, at].astype(jnp.float32), value
                        )
                    out_ref[0, :, at] = value.astype(out_ref.dtype)

        @pl.when(pl.program_id(0) == 0)
        def _():
            add(shifted_ref, True)

        @pl.when(pl.program_id(0) == 1)
        def _():
            add(hidden_ref, False)

    frame_spec = pl.BlockSpec((1, tok, width), lambda i, pos: (0, 0, 0))
    return pl.pallas_call(
        kernel,
        grid_spec=pltpu.PrefetchScalarGridSpec(
            num_scalar_prefetch=1,
            grid=(frames,),
            in_specs=[
                pl.BlockSpec((sources, 1, halves, tok, cols), lambda i, pos: (0, i, 0, 0, 0)),
                frame_spec,
                frame_spec,
                pl.BlockSpec((tok, width), lambda i, pos: (0, 0)),
            ],
            out_specs=pl.BlockSpec((1, tok, width), lambda i, pos: (i, 0, 0)),
        ),
        out_shape=jax.ShapeDtypeStruct((frames, tok, width), hidden.dtype),
        name="add_branch",
    )(position, branch, hidden, shifted, entering)


def body(hidden, queries, keys, values, out_weight, gate_table, levels, entering):
    frames = queries.shape[0]
    position = lax.axis_index("queue")
    spatial = lax.axis_index("spatial")
    y_low, x = position // RING, position % RING
    core = spatial % CORES
    position_now = position.astype(jnp.int32)[None]
    place = jnp.stack((x, core)).astype(jnp.int32)

    up = [(p, p + 1) for p in range(QUEUE - 1)]
    down = [(p + 1, p) for p in range(QUEUE - 1)]
    ring = [[r * RING + i for i in range(RING)] for r in range(QUEUE // RING)]
    ring_up = [(g[i], g[(i + 1) % RING]) for g in ring for i in range(RING)]
    ring_down = [(g[(i + 1) % RING], g[i]) for g in ring for i in range(RING)]
    swap_low = [(p, (p + RING) % QUEUE) for p in range(QUEUE)]
    swap_core = [(s, s ^ 1) for s in range(SPATIAL)]
    along_y = [
        [(low * RING + i) * SPATIAL + side * (SPATIAL // 2) + r for side in range(2) for low in range(2)]
        for i in range(RING)
        for r in range(SPATIAL // 2)
    ]
    along_z = [
        [side * (SPATIAL // 2) + z * CORES + c for z in range(SPATIAL // 2 // CORES)]
        for side in range(2)
        for c in range(CORES)
    ]

    to_heads = functools.partial(
        lax.all_to_all, axis_name="spatial", split_axis=0, concat_axis=0, tiled=True
    )

    selector = (levels[:, None] == jnp.arange(gate_table.shape[0], dtype=jnp.int32)[None, :]).astype(
        jnp.float32
    )
    gates = jnp.dot(
        selector, gate_table, precision=lax.Precision.HIGHEST, preferred_element_type=jnp.float32
    )
    other_gates = lax.ppermute(gates, "queue", swap_low)
    gates = jnp.where(y_low == 0, jnp.stack((gates, other_gates)), jnp.stack((other_gates, gates)))
    count = RING * frames
    is_last = (jnp.arange(count, dtype=jnp.int32) == count - 1)[None, :, None] & (y_low == 1)
    gates = jnp.where(
        is_last,
        gates[:, count - 1 : count],
        lax.dynamic_slice_in_dim(gates, y_low * count, count, axis=1),
    )

    first, second = pack(queries, keys, values)
    first = to_heads(first)
    first_kv = first[:, 1:]
    first_sides = lax.ppermute(first_kv, "queue", up), lax.ppermute(first_kv, "queue", down)
    second = to_heads(hold(second, *first_sides, gates))
    second_kv = second[:, 1:]
    second_sides = lax.ppermute(second_kv, "queue", up), lax.ppermute(second_kv, "queue", down)

    weight = lax.all_gather(out_weight, ("queue", "spatial"), axis_index_groups=along_y, axis=0)
    weight = hold(weight, first)
    weight = lax.all_gather(weight, "spatial", axis_index_groups=along_z, axis=0)
    weight = weight.reshape(-1, 2, 2, *out_weight.shape)

    def spread(even, odd):
        crossing = lax.ppermute(odd, "queue", [(RING - 1, QUEUE - 1)])
        odd = jnp.where(position == QUEUE - 1, crossing, odd)
        mine = to_heads(jnp.concatenate((even, odd), axis=1))
        left = lax.ppermute(mine, "queue", ring_up)
        right = lax.ppermute(mine, "queue", ring_down)
        far_low = lax.ppermute(left[: SPATIAL // 2], "queue", ring_up)
        far_high = lax.ppermute(right[SPATIAL // 2 :], "queue", ring_down)
        return mine, left, right, far_low, far_high

    both, token = attend(None, position_now, first, *first_sides)
    shifted = lax.ppermute(last_frame(hidden, *second_sides), "queue", up)
    first_sources = spread(both[:, :1], both[:, 1:])
    odd, token = attend(1, position_now, second, *second_sides, token)
    weight_own = hold(weight, token)
    weight_pair = lax.ppermute(weight_own, "spatial", swap_core)
    even, token = attend(0, position_now, second, *second_sides, token, first_sources[0])
    second_sources = spread(even, odd)

    partial = project(0, place, first_sources, weight_own, weight_pair, None, None, shifted)
    branch = project(1, place, second_sources, weight_own, weight_pair, partial, gates)
    branch = lax.all_to_all(
        branch, "queue", split_axis=0, concat_axis=0, axis_index_groups=ring, tiled=True
    )
    branch = branch.reshape(RING, frames, *branch.shape[1:])
    return add_branch(position_now, branch, hidden, shifted, entering)


def solution(mesh):
    return jax.shard_map(
        body,
        mesh=mesh,
        in_specs=(
            P("queue", "spatial", None),
            P("queue", "spatial", None),
            P("queue", "spatial", None),
            P("queue", "spatial", None),
            P("spatial", "queue"),
            P(None, "queue"),
            P(),
            P("spatial", None),
        ),
        out_specs=P("queue", "spatial", None),
        check_vma=False,
    )
```

time: 341 us -> 305 us (0.89)
  waiting for transfers between devices: 127 us -> 70.2 us
  blocking collectives: 48.7 us -> 91.9 us
  Pallas kernels: 68.9 us -> 58.2 us
  starting transfers between devices: 63.1 us -> 55.9 us
    all_to_all x6 -> x2, waiting for transfers between devices: 95.8 us -> 12.7 us  [spread(): mine = to_heads(jnp.concatenate((even, odd), axis=1))]
    all_to_all x2 -> x3, blocking collectives: 48.7 us -> 91.9 us  [the longest x1 42.4 us: body(): first = to_heads(first)]
    ppermute x1, waiting for transfers between devices: 0.01 us -> 24 us  [body(): other_gates = lax.ppermute(gates, 'queue', swap_low)]
    all_to_all x6 -> x2, starting transfers between devices: 28.3 us -> 9.78 us  [spread(): mine = to_heads(jnp.concatenate((even, odd), axis=1))]
    ppermute x3 -> x2, waiting for transfers between devices: 7.55 us -> 22.8 us  [spread(): left = lax.ppermute(mine, 'queue', ring_up)]
    ppermute x3 -> x2, starting transfers between devices: 7.07 us -> 22.2 us  [spread(): right = lax.ppermute(mine, 'queue', ring_down)]
    ppermute x6 -> x7, waiting for transfers between devices: 13.8 us -> 4.65 us  [the longest x1 3.46 us: body(): lax.ppermute(second_kv, 'queue', down)]
    pallas_call x2, Pallas kernels: 20.7 us -> 13.4 us  [project(): pl.pallas_call(kernel, grid_spec=pltpu.PrefetchScalarGridSpec(num_scalar_...]
  transfers between devices with their start and end apart: 28 -> 21, of which waited for: 11 -> 8; matrix products, arithmetic and copies ran while one was open for 2% -> 2% of each run, Pallas kernels for 18% -> 15%
where the time goes in v4:
time: 305 us; the launch traced here: 304 us
  blocking collectives  91.9 us (30%)
  waiting for transfers between devices  70.2 us (23%)
  Pallas kernels  58.2 us (19%)
  starting transfers between devices  55.9 us (18%)
  between operations  13.7 us (4%)
  local copies, waits for them, and re-layouts  11.3 us (4%)
    all_to_all x1, blocking collectives, body(): first = to_heads(first)  42.4 us
    pallas_call x3, Pallas kernels, attend(): pl.pallas_call(kernel, grid_spec=pltpu.PrefetchScalarGridSpec(num_scalar_...  33.2 us
    all_to_all x1, blocking collectives, body(): second = to_heads(hold(second, *first_sides, gates))  31.9 us
    ppermute x1, waiting for transfers between devices, body(): other_gates = lax.ppermute(gates, 'queue', swap_low)  24 us
    ppermute x2, waiting for transfers between devices, spread(): left = lax.ppermute(mine, 'queue', ring_up)  22.8 us
    ppermute x2, starting transfers between devices, spread(): right = lax.ppermute(mine, 'queue', ring_down)  22.2 us
    all_to_all x1, blocking collectives, body(): lax.all_to_all(branch, 'queue', split_axis=0, concat_axis=0, axis_index_g...  17.7 us
    pallas_call x2, Pallas kernels, project(): pl.pallas_call(kernel, grid_spec=pltpu.PrefetchScalarGridSpec(num_scalar_...  13.4 us
  transfers between devices with their start and end apart: 21, of which 8 were waited for; matrix products, arithmetic and copies ran while one was open for 2% of the time, Pallas kernels for 15%

profile of v4, /device:TPU:0, one launch (start us, length us, event | category | flops | bytes accessed | tf_op | source)
XLA Modules:
  0.0 303.9 jit_solution(6296792648144138547)
XLA Ops:
  6.5 0.7 all-gather.5.cloned.1.call-update
  7.3 0.0 all-gather.7.cloned.1.call-start
  7.3 4.4 %pack.1 = (bf16[16,3,2,64,128]{4,3,2,1,0:T(8,128)(2,1)}, bf16[16,3,2,64,128]{4,3,2,1,0:T(8,128)(2,1)}) custom-call(bf16[2,64,4096]{2,1,0:T(8,128)(2,1)} %q_ref.1, bf16[2,64,4096]{2,1,0:T(8,128)(2,1)} %k_ref.1, bf16[2,64,4096]{2,1,0:T(8,128)(2,1)} %v_ref.1), custom_call_target="tpu_custom_call" | custom-call | tf_op jit(solution)/shard_map/pack/pallas_call | solution.py:47
  11.7 42.4 %all_to_all.25.q_ref.own_ref.refs_1_ = bf16[16,3,2,64,128]{4,3,2,1,0:T(8,128)(2,1)} all-to-all(bf16[16,3,2,64,128]{4,3,2,1,0:T(8,128)(2,1)} %get-tuple-element.13), channel_id=1, replica_groups=mesh['queue'=8,'spatial'=16] {'spatial'}, dimensions={0} | all-to-all | bytes 3145728 | tf_op jit(solution)/shard_map/all_to_all | solution.py:373
  54.1 0.8 hold.4
  54.9 0.0 all-gather.7.cloned.1.call-update
  54.9 0.6 copy-done.1
  55.5 1.0 slice.36
  56.5 1.3 collective-permute-start.1
  57.8 5.6 %collective-permute-start = (bf16[16,2,2,64,128]{4,3,2,1,0:T(8,128)(2,1)}, bf16[16,2,2,64,128]{4,3,2,1,0:T(8,128)(2,1)}, u32[]{:S(2)}, u32[]{:S(2)}) collective-permute-start(bf16[16,2,2,64,128]{4,3,2,1,0:T(8,128)(2,1)} %slice.36), channel_id=1, source_target_pairs={{0,16},{16,32},{32,48},{48,64},{64,80},{80,96},{96,112},{1,17},{17... | collective-permute-start | bytes 3145736 | tf_op jit(solution)/shard_map/ppermute | solution.py:375
  63.4 0.2 fusion
  63.6 1.3 collective-permute-start.2
  64.9 24.0 %collective-permute-done.2 = f32[16,640]{1,0:T(8,128)S(1)} collective-permute-done((f32[16,640]{1,0:T(8,128)S(1)}, f32[16,640]{1,0:T(8,128)S(1)}, u32[]{:S(2)}, u32[]{:S(2)}) %collective-permute-start.2) | collective-permute-done | bytes 40992 | tf_op jit(solution)/shard_map/ppermute | solution.py:362
  89.0 0.7 dynamic-slice_select_fusion.refs_3_.rest_1_
  89.7 1.0 copy-done.5
  90.7 0.7 hold.3
  91.4 31.9 %all_to_all.26.q_ref.own_ref = bf16[16,3,2,64,128]{4,3,2,1,0:T(8,128)(2,1)S(1)} all-to-all(bf16[16,3,2,64,128]{4,3,2,1,0:T(8,128)(2,1)} %hold.3), channel_id=1, replica_groups=mesh['queue'=8,'spatial'=16] {'spatial'}, dimensions={0} | all-to-all | bytes 3145728 | tf_op jit(solution)/shard_map/all_to_all | solution.py:376
  123.3 0.1 slice.38
  123.3 1.4 collective-permute-start.4
  124.8 4.6 %collective-permute-start.3 = (bf16[16,2,2,64,128]{4,3,2,1,0:T(8,128)(2,1)S(1)}, bf16[16,2,2,64,128]{4,3,2,1,0:T(8,128)(2,1)S(1)}, u32[]{:S(2)}, u32[]{:S(2)}) collective-permute-start(bf16[16,2,2,64,128]{4,3,2,1,0:T(8,128)(2,1)S(1)} %slice.38), channel_id=1, source_target_pairs={{0,16},{16,32},{32,48},{48,64},{64,80},{80,96},{96,112},{1,17},{17... | collective-permute-start | bytes 3145736 | tf_op jit(solution)/shard_map/ppermute | solution.py:378
  129.4 17.4 %attend.3 = (bf16[16,2,64,128]{3,2,1,0:T(8,128)(2,1)S(1)}, f32[8,128]{1,0:T(8,128)S(1)}) custom-call(s32[1]{0:T(128)} %bitcast.pos_ref, bf16[16,3,2,64,128]{4,3,2,1,0:T(8,128)(2,1)S(1)} %copy-done.1, bf16[16,3,2,64,128]{4,3,2,1,0:T(8,128)(2,1)S(1)} %copy-done.1, bf16[16,2,2,64,128]{4,3,2,1,0:T(8,128)(2,1)} %collective-permute-done.refs_1_.before_ref, ...), custom_call_target="tpu_custom_call" | custom-call | flops 10737418240 | bytes 4194304 | tf_op jit(solution)/shard_map/attend/pallas_call | solution.py:166
  146.8 0.8 copy-done.3
  147.6 3.5 %collective-permute-done.4.after_ref.rest_1_ = bf16[16,2,2,64,128]{4,3,2,1,0:T(8,128)(2,1)S(1)} collective-permute-done((bf16[16,2,2,64,128]{4,3,2,1,0:T(8,128)(2,1)S(1)}, bf16[16,2,2,64,128]{4,3,2,1,0:T(8,128)(2,1)S(1)}, u32[]{:S(2)}, u32[]{:S(2)}) %collective-permute-start.4) | collective-permute-done | bytes 1048608 | tf_op jit(solution)/shard_map/ppermute | solution.py:378
  151.1 1.2 collective-permute-done.3.before_ref.rest_0_
  152.3 7.6 %attend.4 = (bf16[16,1,64,128]{3,2,1,0:T(8,128)(2,1)S(1)}, f32[8,128]{1,0:T(8,128)S(1)}) custom-call(s32[1]{0:T(128)} %bitcast.pos_ref, bf16[16,3,2,64,128]{4,3,2,1,0:T(8,128)(2,1)S(1)} %all_to_all.26.q_ref.own_ref, bf16[16,3,2,64,128]{4,3,2,1,0:T(8,128)(2,1)S(1)} %all_to_all.26.q_ref.own_ref, ...), custom_call_target="tpu_custom_call" | custom-call | flops 5368709120 | bytes 4194304 | tf_op jit(solution)/shard_map/attend/pallas_call | solution.py:166
  159.9 1.0 copy-done.7
  160.8 1.0 copy-done.9
  161.8 0.6 copy-done.12
  162.4 0.7 hold.5.wo_ref
  163.1 0.3 copy-done.4
  163.5 0.7 collective-permute-start.5
  164.2 0.0 collective-permute-done.5
  164.2 0.9 pad_maximum_fusion
  165.1 6.2 %all-to-all-start.2 = ((bf16[16,2,64,128]{3,2,1,0:T(8,128)(2,1)}), bf16[16,2,64,128]{3,2,1,0:T(8,128)(2,1)S(1)}, u32[]{:S(2)}, u32[]{:S(2)}) async-start(bf16[16,2,64,128]{3,2,1,0:T(8,128)(2,1)} %pad_maximum_fusion), calls=%async_computation.2 | async-start | bytes 1048576 | tf_op jit(solution)/shard_map/all_to_all | solution.py:388
  171.3 0.9 collective-permute-start.6
  172.2 11.5 %all-to-all-done.2.rest_1_.mine_ref = bf16[16,2,64,128]{3,2,1,0:T(8,128)(2,1)S(1)} async-done(((bf16[16,2,64,128]{3,2,1,0:T(8,128)(2,1)}), bf16[16,2,64,128]{3,2,1,0:T(8,128)(2,1)S(1)}, u32[]{:S(2)}, u32[]{:S(2)}) %all-to-all-start.2) | async-done | bytes 524320 | tf_op jit(solution)/shard_map/all_to_all | solution.py:388
  183.7 1.2 copy-done.8
  184.9 1.2 copy-done.10
  186.1 8.2 %attend.5 = (bf16[16,1,64,128]{3,2,1,0:T(8,128)(2,1)S(1)}, f32[8,128]{1,0:T(8,128)}) custom-call(s32[1]{0:T(128)} %bitcast.pos_ref, bf16[16,3,2,64,128]{4,3,2,1,0:T(8,128)(2,1)S(1)} %all_to_all.26.q_ref.own_ref, bf16[16,3,2,64,128]{4,3,2,1,0:T(8,128)(2,1)S(1)} %all_to_all.26.q_ref.own_ref, bf16[16,2,2,64,128]{4,3,2,1,0:T(8,128)(2,1)S(1)} %copy-done.10, ...), custom_call_target="tpu_custom_call" | custom-call | flops 5368709120 | bytes 4194304 | tf_op jit(solution)/shard_map/attend/pallas_call | solution.py:166
  194.3 0.0 collective-permute-done.6
  194.4 0.9 pad_maximum_fusion.1
  195.2 3.6 %all-to-all-start.3 = ((bf16[16,2,64,128]{3,2,1,0:T(8,128)(2,1)}), bf16[16,2,64,128]{3,2,1,0:T(8,128)(2,1)S(1)}, u32[]{:S(2)}, u32[]{:S(2)}) async-start(bf16[16,2,64,128]{3,2,1,0:T(8,128)(2,1)} %pad_maximum_fusion.1), calls=%async_computation.3 | async-start | bytes 1048576 | tf_op jit(solution)/shard_map/all_to_all | solution.py:388
  198.8 11.1 %collective-permute-start.13 = (bf16[16,2,64,128]{3,2,1,0:T(8,128)(2,1)S(1)}, bf16[16,2,64,128]{3,2,1,0:T(8,128)(2,1)S(1)}, u32[]{:S(2)}, u32[]{:S(2)}) collective-permute-start(bf16[16,2,64,128]{3,2,1,0:T(8,128)(2,1)S(1)} %all-to-all-done.2.rest_1_.mine_ref), channel_id=1, source_target_pairs={{16,0},{32,16},{48,32},{0,48},{80,64},{96,80},{112,96},{64,112},{1... | collective-permute-start | bytes 1572872 | tf_op jit(solution)/shard_map/ppermute | solution.py:390
  209.9 0.0 collective-permute-start.12
  209.9 1.2 all-to-all-done.3.mine_ref
  211.1 11.1 %collective-permute-start.8 = (bf16[16,2,64,128]{3,2,1,0:T(8,128)(2,1)S(1)}, bf16[16,2,64,128]{3,2,1,0:T(8,128)(2,1)S(1)}, u32[]{:S(2)}, u32[]{:S(2)}) collective-permute-start(bf16[16,2,64,128]{3,2,1,0:T(8,128)(2,1)S(1)} %all-to-all-done.3.mine_ref), channel_id=1, source_target_pairs={{16,0},{32,16},{48,32},{0,48},{80,64},{96,80},{112,96},{64,112},{1... | collective-permute-start | bytes 1572872 | tf_op jit(solution)/shard_map/ppermute | solution.py:390
  222.2 2.0 last_frame.1
  224.2 1.3 collective-permute-start.16
  225.5 0.0 collective-permute-done.13.right_ref
  225.5 0.1 collective-permute-start.7
  225.6 0.7 slice.42
  226.3 4.7 %collective-permute-start.15 = (bf16[8,2,64,128]{3,2,1,0:T(8,128)(2,1)}, bf16[8,2,64,128]{3,2,1,0:T(8,128)(2,1)}, u32[]{:S(2)}, u32[]{:S(2)}) collective-permute-start(bf16[8,2,64,128]{3,2,1,0:T(8,128)(2,1)} %slice.42), channel_id=1, source_target_pairs={{16,0},{32,16},{48,32},{0,48},{80,64},{96,80},{112,96},{64,112},{1... | collective-permute-start | bytes 786440 | tf_op jit(solution)/shard_map/ppermute | solution.py:392
  231.0 0.7 slice.41
  231.7 2.8 collective-permute-done.8.right_ref
  234.6 0.0 collective-permute-start.14
  234.6 22.8 %collective-permute-done.7.left_ref = bf16[16,2,64,128]{3,2,1,0:T(8,128)(2,1)} collective-permute-done((bf16[16,2,64,128]{3,2,1,0:T(8,128)(2,1)S(1)}, bf16[16,2,64,128]{3,2,1,0:T(8,128)(2,1)}, u32[]{:S(2)}, u32[]{:S(2)}) %collective-permute-start.7) | collective-permute-done | bytes 524320 | tf_op jit(solution)/shard_map/ppermute | solution.py:389
  257.4 1.0 slice.39
  258.3 2.1 collective-permute-start.9
  260.4 0.1 pad_add_fusion.place_ref
  260.5 2.5 collective-permute-done.14.low_ref
  263.0 6.6 %project_first.1.rest_0_ = f32[2,512,640]{2,1,0:T(8,128)S(1)} custom-call(s32[2]{0:T(128)S(1)} %pad_add_fusion.place_ref, bf16[16,2,64,128]{3,2,1,0:T(8,128)(2,1)S(1)} %all-to-all-done.2.rest_1_.mine_ref, bf16[16,2,64,128]{3,2,1,0:T(8,128)(2,1)S(1)} %collective-permute-done.12.left_ref, bf16[16,2,64,128]{3,2,1,0:T(8,128)(2,1)S(1)} %collective-permute-done.13.right_ref, ...), custom_call_target="tpu_custom_call" | custom-call | flops 2684354560 | bytes 8388608 | tf_op jit(solution)/shard_map/project_first/pallas_call | solution.py:260
  269.6 6.8 %project_last.1 = bf16[8,2,64,640]{3,2,1,0:T(8,128)(2,1)S(1)} custom-call(s32[2]{0:T(128)S(1)} %pad_add_fusion.place_ref, bf16[16,2,64,128]{3,2,1,0:T(8,128)(2,1)S(1)} %all-to-all-done.3.mine_ref, bf16[16,2,64,128]{3,2,1,0:T(8,128)(2,1)} %collective-permute-done.7.left_ref, bf16[16,2,64,128]{3,2,1,0:T(8,128)(2,1)S(1)} %collective-permute-done.8.right_ref, ...), custom_call_target="tpu_custom_call" | custom-call | flops 2684354560 | bytes 8388608 | tf_op jit(solution)/shard_map/project_last/pallas_call | solution.py:260
  276.4 17.7 %all_to_all.27 = bf16[8,2,64,640]{3,2,1,0:T(8,128)(2,1)} all-to-all(bf16[8,2,64,640]{3,2,1,0:T(8,128)(2,1)S(1)} %project_last.1), channel_id=1, replica_groups={{0,16,32,48},{64,80,96,112},{1,17,33,49},{65,81,97,113},{2,18,34,50},{6..., dimensions={0} | all-to-all | bytes 2621440 | tf_op jit(solution)/shard_map/all_to_all | solution.py:406
  294.1 3.0 add_branch.1
  (42 shorter events, 0.2 us)
Async XLA Ops:
  6.5 56.9 %copy-start = (f32[50,640]{1,0:T(8,128)S(1)}, f32[50,640]{1,0:T(8,128)}, u32[]{:S(2)}) copy-start(f32[50,640]{1,0:T(8,128)} %param.13) | copy-start | bytes 384004
  6.5 47.5 %all-gather.5.cloned.1.call-start = ((), (), s32[]{:S(2)}) async-start(), calls=%async_computation.5 | async-start | bytes 1638400 | tf_op jit(solution)/shard_map/all_gather | solution.py:380
  7.3 155.1 %all-gather.7.cloned.1.call-start = ((), (), s32[]{:S(2)}) async-start(), calls=%async_computation.6 | async-start | bytes 6553600 | tf_op jit(solution)/shard_map/all_gather | solution.py:382
  54.1 1.4 copy-start.1
  54.9 8.5 %copy-start.14 = (s32[16]{0:T(128)S(1)}, s32[16]{0:T(128)}, u32[]{:S(2)}) copy-start(s32[16]{0:T(128)} %param.14) | copy-start | bytes 196
  56.5 33.1 %collective-permute-start.1 = (bf16[16,2,2,64,128]{4,3,2,1,0:T(8,128)(2,1)}, bf16[16,2,2,64,128]{4,3,2,1,0:T(8,128)(2,1)S(1)}, u32[]{:S(2)}, u32[]{:S(2)}) collective-permute-start(bf16[16,2,2,64,128]{4,3,2,1,0:T(8,128)(2,1)} %slice.36), channel_id=1, source_target_pairs={{16,0},{32,16},{48,32},{64,48},{80,64},{96,80},{112,96},{17,1},{33... | collective-permute-start | bytes 3145736 | tf_op jit(solution)/shard_map/ppermute | solution.py:375
  57.8 31.8 %collective-permute-start = (bf16[16,2,2,64,128]{4,3,2,1,0:T(8,128)(2,1)}, bf16[16,2,2,64,128]{4,3,2,1,0:T(8,128)(2,1)}, u32[]{:S(2)}, u32[]{:S(2)}) collective-permute-start(bf16[16,2,2,64,128]{4,3,2,1,0:T(8,128)(2,1)} %slice.36), channel_id=1, source_target_pairs={{0,16},{16,32},{32,48},{48,64},{64,80},{80,96},{96,112},{1,17},{17... | collective-permute-start | bytes 3145736 | tf_op jit(solution)/shard_map/ppermute | solution.py:375
  63.6 25.3 %collective-permute-start.2 = (f32[16,640]{1,0:T(8,128)S(1)}, f32[16,640]{1,0:T(8,128)S(1)}, u32[]{:S(2)}, u32[]{:S(2)}) collective-permute-start(f32[16,640]{1,0:T(8,128)S(1)} %fusion), channel_id=1, source_target_pairs={{0,64},{16,80},{32,96},{48,112},{64,0},{80,16},{96,32},{112,48},{1... | collective-permute-start | bytes 122888 | tf_op jit(solution)/shard_map/ppermute | solution.py:362
  89.7 1.0 copy-start.5
  123.3 6.1 %copy-start.6 = (bf16[16,2,2,64,128]{4,3,2,1,0:T(8,128)(2,1)S(1)}, bf16[16,2,2,64,128]{4,3,2,1,0:T(8,128)(2,1)}, u32[]{:S(2)}) copy-start(bf16[16,2,2,64,128]{4,3,2,1,0:T(8,128)(2,1)} %copy-done.5) | copy-start | bytes 3145732
  123.3 27.7 %collective-permute-start.4 = (bf16[16,2,2,64,128]{4,3,2,1,0:T(8,128)(2,1)S(1)}, bf16[16,2,2,64,128]{4,3,2,1,0:T(8,128)(2,1)S(1)}, u32[]{:S(2)}, u32[]{:S(2)}) collective-permute-start(bf16[16,2,2,64,128]{4,3,2,1,0:T(8,128)(2,1)S(1)} %slice.38), channel_id=1, source_target_pairs={{16,0},{32,16},{48,32},{64,48},{80,64},{96,80},{112,96},{17,1},{33... | collective-permute-start | bytes 3145736 | tf_op jit(solution)/shard_map/ppermute | solution.py:378
  124.8 27.5 %collective-permute-start.3 = (bf16[16,2,2,64,128]{4,3,2,1,0:T(8,128)(2,1)S(1)}, bf16[16,2,2,64,128]{4,3,2,1,0:T(8,128)(2,1)S(1)}, u32[]{:S(2)}, u32[]{:S(2)}) collective-permute-start(bf16[16,2,2,64,128]{4,3,2,1,0:T(8,128)(2,1)S(1)} %slice.38), channel_id=1, source_target_pairs={{0,16},{16,32},{32,48},{48,64},{64,80},{80,96},{96,112},{1,17},{17... | collective-permute-start | bytes 3145736 | tf_op jit(solution)/shard_map/ppermute | solution.py:378
  146.8 0.8 copy-start.3
  159.9 1.0 copy-start.7
  160.8 1.0 copy-start.9
  161.8 0.6 copy-start.12
  162.4 1.0 copy-start.4
  163.1 99.8 %collective-permute-start.11 = (bf16[4,2,2,256,640]{4,3,2,1,0:T(8,128)(2,1)}, bf16[4,2,2,256,640]{4,3,2,1,0:T(8,128)(2,1)}, u32[]{:S(2)}, u32[]{:S(2)}) collective-permute-start(bf16[4,2,2,256,640]{4,3,2,1,0:T(8,128)(2,1)} %hold.5.wo_ref), channel_id=1, source_target_pairs={{0,1},{1,0},{2,3},{3,2},{4,5},{5,4},{6,7},{7,6},{8,9},{9,8},{10,11... | collective-permute-start | bytes 15728648 | tf_op jit(solution)/shard_map/ppermute | solution.py:400
  163.5 0.7 collective-permute-start.5
  164.2 19.5 %copy-start.13 = (f32[8,128]{1,0:T(8,128)S(1)}, f32[8,128]{1,0:T(8,128)}, u32[]{:S(2)}) copy-start(f32[8,128]{1,0:T(8,128)} %copy-done.12) | copy-start | bytes 12292
  165.1 18.6 %all-to-all-start.2 = ((bf16[16,2,64,128]{3,2,1,0:T(8,128)(2,1)}), bf16[16,2,64,128]{3,2,1,0:T(8,128)(2,1)S(1)}, u32[]{:S(2)}, u32[]{:S(2)}) async-start(bf16[16,2,64,128]{3,2,1,0:T(8,128)(2,1)} %pad_maximum_fusion), calls=%async_computation.2 | async-start | bytes 1048576 | tf_op jit(solution)/shard_map/all_to_all | solution.py:388
  171.3 23.0 %collective-permute-start.6 = (bf16[16,1,64,128]{3,2,1,0:T(8,128)(2,1)S(1)}, bf16[16,1,64,128]{3,2,1,0:T(8,128)(2,1)S(1)}, u32[]{:S(2)}, u32[]{:S(2)}) collective-permute-start(bf16[16,1,64,128]{3,2,1,0:T(8,128)(2,1)S(1)} %get-tuple-element.18), channel_id=1, source_target_pairs={{48,112},{49,113},{50,114},{51,115},{52,116},{53,117},{54,118},{55... | collective-permute-start | bytes 786440 | tf_op jit(solution)/shard_map/ppermute | solution.py:386
  183.7 1.2 copy-start.8
  184.9 1.2 copy-start.10
  195.2 15.9 %all-to-all-start.3 = ((bf16[16,2,64,128]{3,2,1,0:T(8,128)(2,1)}), bf16[16,2,64,128]{3,2,1,0:T(8,128)(2,1)S(1)}, u32[]{:S(2)}, u32[]{:S(2)}) async-start(bf16[16,2,64,128]{3,2,1,0:T(8,128)(2,1)} %pad_maximum_fusion.1), calls=%async_computation.3 | async-start | bytes 1048576 | tf_op jit(solution)/shard_map/all_to_all | solution.py:388
  198.8 26.7 %collective-permute-start.13 = (bf16[16,2,64,128]{3,2,1,0:T(8,128)(2,1)S(1)}, bf16[16,2,64,128]{3,2,1,0:T(8,128)(2,1)S(1)}, u32[]{:S(2)}, u32[]{:S(2)}) collective-permute-start(bf16[16,2,64,128]{3,2,1,0:T(8,128)(2,1)S(1)} %all-to-all-done.2.rest_1_.mine_ref), channel_id=1, source_target_pairs={{16,0},{32,16},{48,32},{0,48},{80,64},{96,80},{112,96},{64,112},{1... | collective-permute-start | bytes 1572872 | tf_op jit(solution)/shard_map/ppermute | solution.py:390
  209.9 16.4 %collective-permute-start.12 = (bf16[16,2,64,128]{3,2,1,0:T(8,128)(2,1)S(1)}, bf16[16,2,64,128]{3,2,1,0:T(8,128)(2,1)S(1)}, u32[]{:S(2)}, u32[]{:S(2)}) collective-permute-start(bf16[16,2,64,128]{3,2,1,0:T(8,128)(2,1)S(1)} %all-to-all-done.2.rest_1_.mine_ref), channel_id=1, source_target_pairs={{0,16},{16,32},{32,48},{48,0},{64,80},{80,96},{96,112},{112,64},{1... | collective-permute-start | bytes 1572872 | tf_op jit(solution)/shard_map/ppermute | solution.py:389
  211.1 23.4 %collective-permute-start.8 = (bf16[16,2,64,128]{3,2,1,0:T(8,128)(2,1)S(1)}, bf16[16,2,64,128]{3,2,1,0:T(8,128)(2,1)S(1)}, u32[]{:S(2)}, u32[]{:S(2)}) collective-permute-start(bf16[16,2,64,128]{3,2,1,0:T(8,128)(2,1)S(1)} %all-to-all-done.3.mine_ref), channel_id=1, source_target_pairs={{16,0},{32,16},{48,32},{0,48},{80,64},{96,80},{112,96},{64,112},{1... | collective-permute-start | bytes 1572872 | tf_op jit(solution)/shard_map/ppermute | solution.py:390
  224.2 38.8 %collective-permute-start.16 = (bf16[1,64,5120]{2,1,0:T(8,128)(2,1)}, bf16[1,64,5120]{2,1,0:T(8,128)(2,1)S(1)}, u32[]{:S(2)}, u32[]{:S(2)}) collective-permute-start(bf16[1,64,5120]{2,1,0:T(8,128)(2,1)} %last_frame.1), channel_id=1, source_target_pairs={{0,16},{16,32},{32,48},{48,64},{64,80},{80,96},{96,112},{1,17},{17... | collective-permute-start | bytes 1966088 | tf_op jit(solution)/shard_map/ppermute | solution.py:396
  225.5 31.8 %collective-permute-start.7 = (bf16[16,2,64,128]{3,2,1,0:T(8,128)(2,1)S(1)}, bf16[16,2,64,128]{3,2,1,0:T(8,128)(2,1)}, u32[]{:S(2)}, u32[]{:S(2)}) collective-permute-start(bf16[16,2,64,128]{3,2,1,0:T(8,128)(2,1)S(1)} %all-to-all-done.3.mine_ref), channel_id=1, source_target_pairs={{0,16},{16,32},{32,48},{48,0},{64,80},{80,96},{96,112},{112,64},{1... | collective-permute-start | bytes 1572872 | tf_op jit(solution)/shard_map/ppermute | solution.py:389
  226.3 32.0 %collective-permute-start.15 = (bf16[8,2,64,128]{3,2,1,0:T(8,128)(2,1)}, bf16[8,2,64,128]{3,2,1,0:T(8,128)(2,1)}, u32[]{:S(2)}, u32[]{:S(2)}) collective-permute-start(bf16[8,2,64,128]{3,2,1,0:T(8,128)(2,1)} %slice.42), channel_id=1, source_target_pairs={{16,0},{32,16},{48,32},{0,48},{80,64},{96,80},{112,96},{64,112},{1... | collective-permute-start | bytes 786440 | tf_op jit(solution)/shard_map/ppermute | solution.py:392
  234.6 28.4 %collective-permute-start.14 = (bf16[8,2,64,128]{3,2,1,0:T(8,128)(2,1)}, bf16[8,2,64,128]{3,2,1,0:T(8,128)(2,1)}, u32[]{:S(2)}, u32[]{:S(2)}) collective-permute-start(bf16[8,2,64,128]{3,2,1,0:T(8,128)(2,1)} %slice.41), channel_id=1, source_target_pairs={{0,16},{16,32},{32,48},{48,0},{64,80},{80,96},{96,112},{112,64},{1... | collective-permute-start | bytes 786440 | tf_op jit(solution)/shard_map/ppermute | solution.py:391
  257.4 12.3 %collective-permute-start.10 = (bf16[8,2,64,128]{3,2,1,0:T(8,128)(2,1)S(1)}, bf16[8,2,64,128]{3,2,1,0:T(8,128)(2,1)S(1)}, u32[]{:S(2)}, u32[]{:S(2)}) collective-permute-start(bf16[8,2,64,128]{3,2,1,0:T(8,128)(2,1)S(1)} %slice.40), channel_id=1, source_target_pairs={{16,0},{32,16},{48,32},{0,48},{80,64},{96,80},{112,96},{64,112},{1... | collective-permute-start | bytes 786440 | tf_op jit(solution)/shard_map/ppermute | solution.py:392
  258.3 11.3 %collective-permute-start.9 = (bf16[8,2,64,128]{3,2,1,0:T(8,128)(2,1)S(1)}, bf16[8,2,64,128]{3,2,1,0:T(8,128)(2,1)S(1)}, u32[]{:S(2)}, u32[]{:S(2)}) collective-permute-start(bf16[8,2,64,128]{3,2,1,0:T(8,128)(2,1)S(1)} %slice.39), channel_id=1, source_target_pairs={{0,16},{16,32},{32,48},{48,0},{64,80},{80,96},{96,112},{112,64},{1... | collective-permute-start | bytes 786440 | tf_op jit(solution)/shard_map/ppermute | solution.py:391
  260.5 9.1 %copy-start.11 = (f32[2,8,640]{2,1,0:T(8,128)S(1)}, f32[2,8,640]{2,1,0:T(8,128)}, u32[]{:S(2)}) copy-start(f32[2,8,640]{2,1,0:T(8,128)} %dynamic-slice_select_fusion.refs_3_.rest_1_) | copy-start | bytes 122884
  263.0 6.6 %copy-start.2 = (bf16[1,64,5120]{2,1,0:T(8,128)(2,1)}, bf16[1,64,5120]{2,1,0:T(8,128)(2,1)S(1)}, u32[]{:S(2)}) copy-start(bf16[1,64,5120]{2,1,0:T(8,128)(2,1)S(1)} %collective-permute-done.16.rest_0_.shifted_ref) | copy-start | bytes 1966084
Sparse Core Ops, SparseCore 0:
  9.0 37.5 all-gather.4
  55.0 70.8 all-gather.6

commit v5 on v4

--- a/solution.py
+++ b/solution.py
@@ -36,22 +36,66 @@
     piece = width // PACK
     count = SPATIAL // PACK
 
-    def kernel(q_ref, k_ref, v_ref, *out_refs):
+    def kernel(q_ref, k_ref, v_ref, kv0_ref, kv1_ref, out_ref):
         for i in range(count):
-            for head, out_ref in enumerate(out_refs):
+            for head, kv_ref in enumerate((kv0_ref, kv1_ref)):
                 cols = slice(i * group + head * HD, i * group + (head + 1) * HD)
-                for at, ref in enumerate((q_ref, k_ref, v_ref)):
-                    out_ref[i, at] = ref[:, :, cols]
-
-    heads = group // HD
+                kv_ref[i, 0] = k_ref[:, :, cols]
+                kv_ref[i, 1] = v_ref[:, :, cols]
+            out_ref[i] = q_ref[:, :, i * group : (i + 1) * group]
+
+    spec = pl.BlockSpec((frames, tok, piece), lambda s: (0, 0, s))
+    kv_spec = pl.BlockSpec((count, 2, frames, tok, HD), lambda s: (s, 0, 0, 0, 0))
+    kv_shape = jax.ShapeDtypeStruct((SPATIAL, 2, frames, tok, HD), keys.dtype)
     return pl.pallas_call(
         kernel,
         grid=(PACK,),
-        in_specs=[pl.BlockSpec((frames, tok, piece), lambda s: (0, 0, s))] * 3,
-        out_specs=[pl.BlockSpec((count, 3, frames, tok, HD), lambda s: (s, 0, 0, 0, 0))] * heads,
-        out_shape=[jax.ShapeDtypeStruct((SPATIAL, 3, frames, tok, HD), keys.dtype)] * heads,
+        in_specs=[spec] * 3,
+        out_specs=[kv_spec, kv_spec, pl.BlockSpec((count, frames, tok, group), lambda s: (s, 0, 0, 0))],
+        out_shape=[
+            kv_shape,
+            kv_shape,
+            jax.ShapeDtypeStruct((SPATIAL, frames, tok, group), queries.dtype),
+        ],
         name="pack",
     )(queries, keys, values)
+
+
+def assemble(position, first, first_crossing, even, odd, odd_crossing, *earlier):
+    groups, frames, tok, width = first.shape
+    count = groups // PACK
+
+    def kernel(pos_ref, first_ref, crossing0_ref, even_ref, odd_ref, crossing1_ref, *rest):
+        out_ref = rest[-1]
+        out_ref[:, 0, :, :width] = first_ref[:, 0]
+        out_ref[:, 0, :, width:] = even_ref[:, 0]
+
+        @pl.when(pos_ref[0] != QUEUE - 1)
+        def _():
+            out_ref[:, 1, :, :width] = first_ref[:, 1]
+            out_ref[:, 1, :, width:] = odd_ref[:, 0]
+
+        @pl.when(pos_ref[0] == QUEUE - 1)
+        def _():
+            out_ref[:, 1, :, :width] = crossing0_ref[:, 0]
+            out_ref[:, 1, :, width:] = crossing1_ref[:, 0]
+
+    one = pl.BlockSpec((count, 1, tok, width), lambda s, pos: (s, 0, 0, 0))
+    return pl.pallas_call(
+        kernel,
+        grid_spec=pltpu.PrefetchScalarGridSpec(
+            num_scalar_prefetch=1,
+            grid=(PACK,),
+            in_specs=[
+                pl.BlockSpec((count, frames, tok, width), lambda s, pos: (s, 0, 0, 0)),
+                one, one, one, one,
+                *[corner(e) for e in earlier],
+            ],
+            out_specs=pl.BlockSpec((count, frames, tok, 2 * width), lambda s, pos: (s, 0, 0, 0)),
+        ),
+        out_shape=jax.ShapeDtypeStruct((groups, frames, tok, 2 * width), first.dtype),
+        name="assemble",
+    )(position, first, first_crossing, even, odd, odd_crossing, *earlier)
 
 
 def last_frame(hidden, *earlier):
@@ -86,8 +130,9 @@
     )(array, *earlier)
 
 
-def attend(frame, position, own, before, after, *earlier):
-    groups, _, frames, tok, width = own.shape
+def attend(frame, position, query, head, own, before, after, *earlier):
+    groups, frames, tok, both = query.shape
+    width = own.shape[-1]
     row_count = groups * tok
     groups_block = BLOCK_Q // tok
     blocks = row_count // BLOCK_Q
@@ -100,23 +145,23 @@
     def kernel(pos_ref, q_ref, own_ref, before_ref, after_ref, *rest):
         out_ref, token_ref, kt_ref, vx_ref = rest[-4:]
         sources = (
-            [(before_ref, 0, f) for f in range(before_count)]
-            + [(own_ref, 1, f) for f in range(frames)]
-            + [(after_ref, 0, f) for f in range(after_count)]
+            [(before_ref, f) for f in range(before_count)]
+            + [(own_ref, f) for f in range(frames)]
+            + [(after_ref, f) for f in range(after_count)]
         )
         turn_frame = pl.program_id(0)
 
         @pl.when((turn_frame == 0) & (pl.program_id(1) == 0))
         def _():
-            for at, (ref, key, f) in enumerate(sources):
+            for at, (ref, f) in enumerate(sources):
                 rows = slice(at * row_count, (at + 1) * row_count)
-                turned = ref[:, key, f].reshape(row_count, width).T
+                turned = ref[:, 0, f].reshape(row_count, width).T
                 kt_ref[:width, rows] = turned
                 kt_ref[width:, rows] = turned
-                vx_ref[rows, :width] = ref[:, key + 1, f].reshape(row_count, width)
+                vx_ref[rows, :width] = ref[:, 1, f].reshape(row_count, width)
                 vx_ref[rows, width:] = jnp.ones((row_count, width), vx_ref.dtype)
 
-        q = q_ref[:, 0, 0].reshape(BLOCK_Q, width).astype(jnp.float32) * SCALE_LOG2
+        q = q_ref[:, 0].reshape(BLOCK_Q, width).astype(jnp.float32) * SCALE_LOG2
         high = q.astype(jnp.bfloat16)
         low = (q - high.astype(jnp.float32)).astype(jnp.bfloat16)
         q = jnp.concatenate((high, low), axis=1)
@@ -155,7 +200,7 @@
 
     first = asked[0]
     in_specs = [
-        pl.BlockSpec((groups_block, 1, 1, tok, width), lambda f, b, pos: (b, 0, first + f, 0, 0)),
+        pl.BlockSpec((groups_block, 1, tok, width), lambda f, b, pos: (b, first + f, 0, head)),
         pl.BlockSpec(own.shape, lambda f, b, pos: (0, 0, 0, 0, 0)),
         pl.BlockSpec(
             (groups, 2, before_count, tok, width),
@@ -179,7 +224,7 @@
             ],
         ),
         out_shape=[
-            jax.ShapeDtypeStruct((groups, len(asked), tok, width), own.dtype),
+            jax.ShapeDtypeStruct((groups, len(asked), tok, width), query.dtype),
             jax.ShapeDtypeStruct(TOKEN, jnp.float32),
         ],
         compiler_params=pltpu.CompilerParams(vmem_limit_bytes=VMEM),
@@ -189,14 +234,14 @@
             transcendentals=len(asked) * row_count * SPAN * row_count,
         ),
         name="attend",
-    )(position, own, own, before, after, *earlier)
-
-
-def project(head, place, sources, weight_own, weight_pair, partial, gates, *earlier):
-    mine = sources[0]
-    groups, frames, tok, width = mine.shape
-    steps, sides, halves, rows_dev, cols_dev = weight_own.shape
-    half = steps * sides
+    )(position, query, own, before, after, *earlier)
+
+
+def project(side, place, sources, weight_own, weight_pair, partial, gates, *earlier):
+    groups, frames, tok, width = sources[1].shape
+    steps, _, halves, _, cols_dev = weight_own.shape
+    half = groups // CORES
+    quarter = groups // 2
     rows = frames * tok
     last = partial is not None
 
@@ -206,12 +251,11 @@
 
         @pl.when(pl.program_id(0) == 0)
         def _():
-            for i in range(half):
-                z, side = i // sides, i % sides
+            for z in range(steps):
                 for part in range(CORES):
-                    group = side * half + CORES * z + (core if part == 0 else 1 - core)
-                    cols = slice((part * half + i) * width, (part * half + i + 1) * width)
-                    far = high_ref[group - half] if side else low_ref[group]
+                    group = CORES * z + (core if part == 0 else 1 - core)
+                    cols = slice((part * half + z) * width, (part * half + z + 1) * width)
+                    far = low_ref[group] if CORES * z < quarter else high_ref[group - quarter]
                     a_ref[0:rows, cols] = mine_ref[group].reshape(rows, width)
                     a_ref[rows : 2 * rows, cols] = right_ref[group].reshape(rows, width)
                     a_ref[2 * rows : 3 * rows, cols] = far.reshape(rows, width)
@@ -219,12 +263,12 @@
 
         total = jnp.dot(
             a_ref[:, : half * width],
-            wo_ref[:, :, 0].reshape(half * width, cols_dev),
+            wo_ref[:, 0, 0].reshape(half * width, cols_dev),
             preferred_element_type=jnp.float32,
         )
         total += jnp.dot(
             a_ref[:, half * width :],
-            wp_ref[:, :, 0].reshape(half * width, cols_dev),
+            wp_ref[:, 0, 0].reshape(half * width, cols_dev),
             preferred_element_type=jnp.float32,
         )
         if not last:
@@ -244,10 +288,11 @@
         return pl.BlockSpec(array.shape, lambda n, place: (0,) * array.ndim)
 
     weight = pl.BlockSpec(
-        (steps, sides, 1, width, cols_dev), lambda n, place: (0, 0, n, head, 0)
+        (steps, 1, 1, width, cols_dev), lambda n, place: (0, side, n, 0, 0)
     )
     partial_spec = pl.BlockSpec((1, RING * rows, cols_dev), lambda n, place: (n, 0, 0))
-    in_specs = [*map(whole, sources), weight, weight]
+    mine_spec = pl.BlockSpec(sources[1].shape, lambda n, place: (side, 0, 0, 0))
+    in_specs = [mine_spec, *map(whole, sources[1:]), weight, weight]
     operands = [*sources, weight_own, weight_pair]
     if last:
         in_specs += [partial_spec, pl.BlockSpec((1,) + gates.shape[1:], lambda n, place: (n, 0, 0))]
@@ -369,39 +414,45 @@
         lax.dynamic_slice_in_dim(gates, y_low * count, count, axis=1),
     )
 
-    first, second = pack(queries, keys, values)
-    first = to_heads(first)
-    first_kv = first[:, 1:]
-    first_sides = lax.ppermute(first_kv, "queue", up), lax.ppermute(first_kv, "queue", down)
-    second = to_heads(hold(second, *first_sides, gates))
-    second_kv = second[:, 1:]
-    second_sides = lax.ppermute(second_kv, "queue", up), lax.ppermute(second_kv, "queue", down)
+    kv0, kv1, query = pack(queries, keys, values)
+    kv0 = to_heads(kv0)
+    kv0_before, kv0_after = lax.ppermute(kv0, "queue", up), lax.ppermute(kv0, "queue", down)
+    kv1 = to_heads(hold(kv1, kv0, gates))
+    query = to_heads(hold(query, kv1, kv0_before, kv0_after))
+    kv1 = hold(kv1, query)
+    kv1_before, kv1_after = lax.ppermute(kv1, "queue", up), lax.ppermute(kv1, "queue", down)
 
     weight = lax.all_gather(out_weight, ("queue", "spatial"), axis_index_groups=along_y, axis=0)
-    weight = hold(weight, first)
+    weight = hold(weight, kv0)
     weight = lax.all_gather(weight, "spatial", axis_index_groups=along_z, axis=0)
     weight = weight.reshape(-1, 2, 2, *out_weight.shape)
 
-    def spread(even, odd):
-        crossing = lax.ppermute(odd, "queue", [(RING - 1, QUEUE - 1)])
-        odd = jnp.where(position == QUEUE - 1, crossing, odd)
-        mine = to_heads(jnp.concatenate((even, odd), axis=1))
-        left = lax.ppermute(mine, "queue", ring_up)
-        right = lax.ppermute(mine, "queue", ring_down)
-        far_low = lax.ppermute(left[: SPATIAL // 2], "queue", ring_up)
-        far_high = lax.ppermute(right[SPATIAL // 2 :], "queue", ring_down)
-        return mine, left, right, far_low, far_high
-
-    both, token = attend(None, position_now, first, *first_sides)
-    shifted = lax.ppermute(last_frame(hidden, *second_sides), "queue", up)
-    first_sources = spread(both[:, :1], both[:, 1:])
-    odd, token = attend(1, position_now, second, *second_sides, token)
+    cross = [(RING - 1, QUEUE - 1)]
+    both, token = attend(None, position_now, query, 0, kv0, kv0_before, kv0_after)
+    first_crossing = lax.ppermute(both[:, 1:], "queue", cross)
+    shifted = lax.ppermute(last_frame(hidden, token), "queue", up)
+    head1 = (position_now, query, 1, kv1, kv1_before, kv1_after)
+    odd, token = attend(1, *head1, token)
+    odd_crossing = lax.ppermute(odd, "queue", cross)
     weight_own = hold(weight, token)
     weight_pair = lax.ppermute(weight_own, "spatial", swap_core)
-    even, token = attend(0, position_now, second, *second_sides, token, first_sources[0])
-    second_sources = spread(even, odd)
-
-    partial = project(0, place, first_sources, weight_own, weight_pair, None, None, shifted)
+    even, _ = attend(0, *head1, token, first_crossing)
+    mine = to_heads(
+        assemble(position_now, both, first_crossing, even, odd, odd_crossing, shifted)
+    )
+
+    def spread(side):
+        half = SPATIAL // 2
+        part = mine[side * half : (side + 1) * half]
+        left = lax.ppermute(part, "queue", ring_up)
+        right = lax.ppermute(part, "queue", ring_down)
+        far_low = lax.ppermute(left[: half // 2], "queue", ring_up)
+        far_high = lax.ppermute(right[half // 2 :], "queue", ring_down)
+        return mine, left, right, far_low, far_high
+
+    first_sources = spread(0)
+    second_sources = spread(1)
+    partial = project(0, place, first_sources, weight_own, weight_pair, None, None)
     branch = project(1, place, second_sources, weight_own, weight_pair, partial, gates)
     branch = lax.all_to_all(
         branch, "queue", split_axis=0, concat_axis=0, axis_index_groups=ring, tiled=True

time: 305 us -> 296 us (0.970)
  blocking collectives: 91.9 us -> 138 us
  waiting for transfers between devices: 70.2 us -> 31.5 us
  starting transfers between devices: 55.9 us -> 31.5 us
  local copies, waits for them, and re-layouts: 11.3 us -> 16.9 us
  Pallas kernels: 58.2 us -> 61.4 us
    all_to_all x2 -> x4, blocking collectives: 74.3 us -> 119 us  [the longest x1 36.8 us: body(): kv0 = to_heads(kv0)]
    ppermute x1, waiting for transfers between devices: 24 us -> 3.35 us  [body(): other_gates = lax.ppermute(gates, 'queue', swap_low)]
    ppermute x15, starting transfers between devices: 44.8 us -> 30.7 us  [the longest x2 11.3 us: spread(): right = lax.ppermute(part, 'queue', ring_down)]
    all_to_all x2 -> x0, waiting for transfers between devices: 12.7 us -> none  [spread(): mine = to_heads(jnp.concatenate((even, odd), axis=1))]
    all_to_all x2 -> x0, starting transfers between devices: 9.78 us -> none  [spread(): mine = to_heads(jnp.concatenate((even, odd), axis=1))]
    unnamed x31 -> x53, local copies, waits for them, and re-layouts: 7.68 us -> 13.8 us
    ppermute x15, waiting for transfers between devices: 32.7 us -> 27.4 us  [the longest x2 16.1 us: spread(): left = lax.ppermute(part, 'queue', ring_up)]
    pallas_call x1 -> x2, Pallas kernels: 4.41 us -> 7.77 us  [the longest x1 4.24 us: pack(): pl.pallas_call(kernel, grid=(PACK,), in_specs=[spec] * 3, out_specs=[kv_s...]
  transfers between devices with their start and end apart: 21 -> 19, of which waited for: 8 -> 7; matrix products, arithmetic and copies ran while one was open for 2% -> 1% of each run, Pallas kernels for 15% -> 17%
where the time goes in v5:
time: 296 us; the launch traced here: 294 us
  blocking collectives  138 us (47%)
  Pallas kernels  61.4 us (21%)
  starting transfers between devices  31.5 us (11%)
  waiting for transfers between devices  31.5 us (11%)
  local copies, waits for them, and re-layouts  16.9 us (6%)
  between operations  13.7 us (5%)
    all_to_all x1, blocking collectives, body(): kv0 = to_heads(kv0)  36.8 us
    all_to_all x1, blocking collectives, body(): kv1 = to_heads(hold(kv1, kv0, gates))  33.5 us
    pallas_call x3, Pallas kernels, attend(): pl.pallas_call(kernel, grid_spec=pltpu.PrefetchScalarGridSpec(num_scalar_...  32.1 us
    all_to_all x1, blocking collectives, body(): query = to_heads(hold(query, kv1, kv0_before, kv0_after))  24.6 us
    all_to_all x1, blocking collectives, body(): to_heads(assemble(position_now, both, first_crossing, even, odd, odd_cros...  24.1 us
    all_to_all x1, blocking collectives, body(): lax.all_to_all(branch, 'queue', split_axis=0, concat_axis=0, axis_index_g...  19.3 us
    ppermute x2, waiting for transfers between devices, spread(): left = lax.ppermute(part, 'queue', ring_up)  16.1 us
    unnamed x53, local copies, waits for them, and re-layouts  13.8 us
  transfers between devices with their start and end apart: 19, of which 7 were waited for; matrix products, arithmetic and copies ran while one was open for 1% of the time, Pallas kernels for 17%

profile of v5, /device:TPU:0, one launch (start us, length us, event | category | flops | bytes accessed | tf_op | source)
XLA Modules:
  0.0 294.3 jit_solution(17289340374232758258)
XLA Ops:
  6.5 0.7 all-gather.5.cloned.1.call-update
  7.3 4.2 %pack.1 = (bf16[16,2,2,64,128]{4,3,2,1,0:T(8,128)(2,1)}, bf16[16,2,2,64,128]{4,3,2,1,0:T(8,128)(2,1)}, bf16[16,2,64,256]{3,2,1,0:T(8,128)(2,1)}) custom-call(bf16[2,64,4096]{2,1,0:T(8,128)(2,1)} %q_ref.1, bf16[2,64,4096]{2,1,0:T(8,128)(2,1)} %k_ref.1, bf16[2,64,4096]{2,1,0:T(8,128)(2,1)} %v_ref.1), custom_call_target="tpu_custom_call" | custom-call | tf_op jit(solution)/shard_map/pack/pallas_call | solution.py:50
  11.5 36.8 %all_to_all.25.refs_1_.own_ref = bf16[16,2,2,64,128]{4,3,2,1,0:T(8,128)(2,1)} all-to-all(bf16[16,2,2,64,128]{4,3,2,1,0:T(8,128)(2,1)} %get-tuple-element.15), channel_id=1, replica_groups=mesh['queue'=8,'spatial'=16] {'spatial'}, dimensions={0} | all-to-all | bytes 2097152 | tf_op jit(solution)/shard_map/all_to_all | solution.py:418
  48.3 0.7 hold.8
  49.0 0.6 copy-done.25
  49.6 0.2 fusion
  49.9 0.7 collective-permute-start
  50.6 3.4 %collective-permute-done = f32[16,640]{1,0:T(8,128)S(1)} collective-permute-done((f32[16,640]{1,0:T(8,128)S(1)}, f32[16,640]{1,0:T(8,128)S(1)}, u32[]{:S(2)}, u32[]{:S(2)}) %collective-permute-start) | collective-permute-done | bytes 40992 | tf_op jit(solution)/shard_map/ppermute | solution.py:407
  54.0 3.5 %collective-permute-start.1 = (bf16[16,2,2,64,128]{4,3,2,1,0:T(8,128)(2,1)S(1)}, bf16[16,2,2,64,128]{4,3,2,1,0:T(8,128)(2,1)S(1)}, u32[]{:S(2)}, u32[]{:S(2)}) collective-permute-start(bf16[16,2,2,64,128]{4,3,2,1,0:T(8,128)(2,1)S(1)} %copy-done.2), channel_id=1, source_target_pairs={{0,16},{16,32},{32,48},{48,64},{64,80},{80,96},{96,112},{1,17},{17... | collective-permute-start | bytes 3145736 | tf_op jit(solution)/shard_map/ppermute | solution.py:419
  57.5 1.3 collective-permute-start.2
  58.8 0.7 dynamic-slice_select_fusion.refs_2_.rest_1_
  59.4 0.7 hold.5
  60.2 33.5 %all_to_all.26.refs_1_.refs_0_ = bf16[16,2,2,64,128]{4,3,2,1,0:T(8,128)(2,1)} all-to-all(bf16[16,2,2,64,128]{4,3,2,1,0:T(8,128)(2,1)} %hold.5), channel_id=1, replica_groups=mesh['queue'=8,'spatial'=16] {'spatial'}, dimensions={0} | all-to-all | bytes 2097152 | tf_op jit(solution)/shard_map/all_to_all | solution.py:420
  93.6 1.0 copy-done.8
  94.6 0.4 copy-done.10
  94.9 0.7 hold.6
  95.6 24.6 %all_to_all.27.q_ref.refs_1_ = bf16[16,2,64,256]{3,2,1,0:T(8,128)(2,1)} all-to-all(bf16[16,2,64,256]{3,2,1,0:T(8,128)(2,1)} %hold.6), channel_id=1, replica_groups=mesh['queue'=8,'spatial'=16] {'spatial'}, dimensions={0} | all-to-all | bytes 2097152 | tf_op jit(solution)/shard_map/all_to_all | solution.py:421
  120.2 0.8 hold.7.own_ref
  121.1 1.3 collective-permute-start.4
  122.4 1.3 collective-permute-start.5
  123.7 1.2 copy-done.9
  125.0 1.2 copy-done.11
  126.2 16.2 %attend.3 = (bf16[16,2,64,128]{3,2,1,0:T(8,128)(2,1)S(1)}, f32[8,128]{1,0:T(8,128)S(1)}) custom-call(s32[1]{0:T(128)} %bitcast.pos_ref, bf16[16,2,64,256]{3,2,1,0:T(8,128)(2,1)S(1)} %copy-done.5, bf16[16,2,2,64,128]{4,3,2,1,0:T(8,128)(2,1)S(1)} %copy-done.3, bf16[16,2,2,64,128]{4,3,2,1,0:T(8,128)(2,1)S(1)} %copy-done.9, ...), custom_call_target="tpu_custom_call" | custom-call | flops 10737418240 | bytes 4194304 | tf_op jit(solution)/shard_map/attend/pallas_call | solution.py:211
  142.4 0.8 copy-done.6
  143.2 2.8 collective-permute-done.4.before_ref
  146.1 4.1 %collective-permute-done.5.after_ref = bf16[16,2,2,64,128]{4,3,2,1,0:T(8,128)(2,1)S(1)} collective-permute-done((bf16[16,2,2,64,128]{4,3,2,1,0:T(8,128)(2,1)}, bf16[16,2,2,64,128]{4,3,2,1,0:T(8,128)(2,1)S(1)}, u32[]{:S(2)}, u32[]{:S(2)}) %collective-permute-start.5) | collective-permute-done | bytes 1048608 | tf_op jit(solution)/shard_map/ppermute | solution.py:423
  150.1 7.6 %attend.4 = (bf16[16,1,64,128]{3,2,1,0:T(8,128)(2,1)S(1)}, f32[8,128]{1,0:T(8,128)S(1)}) custom-call(s32[1]{0:T(128)} %bitcast.pos_ref, bf16[16,2,64,256]{3,2,1,0:T(8,128)(2,1)S(1)} %copy-done.5, bf16[16,2,2,64,128]{4,3,2,1,0:T(8,128)(2,1)S(1)} %copy-done.4, bf16[16,2,2,64,128]{4,3,2,1,0:T(8,128)(2,1)S(1)} %collective-permute-done.4.before_ref, ...), custom_call_target="tpu_custom_call" | custom-call | flops 5368709120 | bytes 4194304 | tf_op jit(solution)/shard_map/attend/pallas_call | solution.py:211
  157.8 0.6 copy-done.16
  158.4 1.0 copy-done.19
  159.3 1.0 copy-done.21
  160.3 0.8 hold.9.wo_ref
  161.1 0.4 copy-done.7
  161.4 0.7 slice.25
  162.2 0.7 collective-permute-start.3
  162.8 2.0 last_frame.1
  164.8 1.6 collective-permute-start.7
  166.4 0.9 collective-permute-start.6
  167.3 1.2 copy-done.20
  168.6 1.2 copy-done.22
  169.8 8.2 %attend.5 = (bf16[16,1,64,128]{3,2,1,0:T(8,128)(2,1)S(1)}, f32[8,128]{1,0:T(8,128)}) custom-call(s32[1]{0:T(128)} %bitcast.pos_ref, bf16[16,2,64,256]{3,2,1,0:T(8,128)(2,1)S(1)} %copy-done.5, bf16[16,2,2,64,128]{4,3,2,1,0:T(8,128)(2,1)S(1)} %copy-done.4, bf16[16,2,2,64,128]{4,3,2,1,0:T(8,128)(2,1)S(1)} %copy-done.20, ...), custom_call_target="tpu_custom_call" | custom-call | flops 5368709120 | bytes 4194304 | tf_op jit(solution)/shard_map/attend/pallas_call | solution.py:211
  178.0 0.7 copy-done.15
  178.7 2.3 collective-permute-done.7.rest_0_.shifted_ref
  181.0 0.7 copy-done.24
  181.7 0.2 copy-done.23
  181.9 3.5 %assemble.1 = bf16[16,2,64,256]{3,2,1,0:T(8,128)(2,1)} custom-call(s32[1]{0:T(128)} %bitcast.pos_ref, bf16[16,2,64,128]{3,2,1,0:T(8,128)(2,1)} %copy-done.6, bf16[16,1,64,128]{3,2,1,0:T(8,128)(2,1)} %copy-done.14, bf16[16,1,64,128]{3,2,1,0:T(8,128)(2,1)} %copy-done.15, bf16[16,1,64,128]{3,2,1,0:T(8,128)(2,1)} %copy-done.13, ...), custom_call_target="tpu_custom_call" | custom-call | tf_op jit(solution)/shard_map/assemble/pallas_call | solution.py:84
  185.4 24.1 %all_to_all.28.mine_ref = bf16[16,2,64,256]{3,2,1,0:T(8,128)(2,1)S(1)} all-to-all(bf16[16,2,64,256]{3,2,1,0:T(8,128)(2,1)} %assemble.1), channel_id=1, replica_groups=mesh['queue'=8,'spatial'=16] {'spatial'}, dimensions={0} | all-to-all | bytes 2097152 | tf_op jit(solution)/shard_map/all_to_all | solution.py:440
  209.6 0.9 fusion.2
  210.5 2.4 collective-permute-start.13
  212.8 8.0 %collective-permute-start.14 = (bf16[8,2,64,256]{3,2,1,0:T(8,128)(2,1)S(1)}, bf16[8,2,64,256]{3,2,1,0:T(8,128)(2,1)S(1)}, u32[]{:S(2)}, u32[]{:S(2)}) collective-permute-start(bf16[8,2,64,256]{3,2,1,0:T(8,128)(2,1)S(1)} %get-tuple-element.21), channel_id=1, source_target_pairs={{16,0},{32,16},{48,32},{0,48},{80,64},{96,80},{112,96},{64,112},{1... | collective-permute-start | bytes 1572872 | tf_op jit(solution)/shard_map/ppermute | solution.py:448
  220.9 3.2 %collective-permute-start.9 = (bf16[8,2,64,256]{3,2,1,0:T(8,128)(2,1)}, bf16[8,2,64,256]{3,2,1,0:T(8,128)(2,1)S(1)}, u32[]{:S(2)}, u32[]{:S(2)}) collective-permute-start(bf16[8,2,64,256]{3,2,1,0:T(8,128)(2,1)} %get-tuple-element.22), channel_id=1, source_target_pairs={{16,0},{32,16},{48,32},{0,48},{80,64},{96,80},{112,96},{64,112},{1... | collective-permute-start | bytes 1572872 | tf_op jit(solution)/shard_map/ppermute | solution.py:448
  224.1 9.6 %collective-permute-done.13.left_ref = bf16[8,2,64,256]{3,2,1,0:T(8,128)(2,1)S(1)} collective-permute-done((bf16[8,2,64,256]{3,2,1,0:T(8,128)(2,1)S(1)}, bf16[8,2,64,256]{3,2,1,0:T(8,128)(2,1)S(1)}, u32[]{:S(2)}, u32[]{:S(2)}) %collective-permute-start.13) | collective-permute-done | bytes 524320 | tf_op jit(solution)/shard_map/ppermute | solution.py:447
  233.7 0.7 slice.37
  234.4 0.7 slice.38
  235.1 3.2 %collective-permute-start.16 = (bf16[4,2,64,256]{3,2,1,0:T(8,128)(2,1)}, bf16[4,2,64,256]{3,2,1,0:T(8,128)(2,1)}, u32[]{:S(2)}, u32[]{:S(2)}) collective-permute-start(bf16[4,2,64,256]{3,2,1,0:T(8,128)(2,1)} %slice.38), channel_id=1, source_target_pairs={{16,0},{32,16},{48,32},{0,48},{80,64},{96,80},{112,96},{64,112},{1... | collective-permute-start | bytes 786440 | tf_op jit(solution)/shard_map/ppermute | solution.py:450
  238.4 6.6 %collective-permute-done.8.left_ref = bf16[8,2,64,256]{3,2,1,0:T(8,128)(2,1)S(1)} collective-permute-done((bf16[8,2,64,256]{3,2,1,0:T(8,128)(2,1)}, bf16[8,2,64,256]{3,2,1,0:T(8,128)(2,1)S(1)}, u32[]{:S(2)}, u32[]{:S(2)}) %collective-permute-start.8) | collective-permute-done | bytes 524320 | tf_op jit(solution)/shard_map/ppermute | solution.py:447
  244.9 0.1 collective-permute-start.10
  245.1 3.3 %collective-permute-start.11 = (bf16[4,2,64,256]{3,2,1,0:T(8,128)(2,1)S(1)}, bf16[4,2,64,256]{3,2,1,0:T(8,128)(2,1)S(1)}, u32[]{:S(2)}, u32[]{:S(2)}) collective-permute-start(bf16[4,2,64,256]{3,2,1,0:T(8,128)(2,1)S(1)} %slice.35), channel_id=1, source_target_pairs={{16,0},{32,16},{48,32},{0,48},{80,64},{96,80},{112,96},{64,112},{1... | collective-permute-start | bytes 786440 | tf_op jit(solution)/shard_map/ppermute | solution.py:450
  248.3 0.1 pad_add_fusion.place_ref
  248.4 2.1 collective-permute-done.15.low_ref
  250.5 6.2 %project_first.1.rest_0_ = f32[2,512,640]{2,1,0:T(8,128)S(1)} custom-call(s32[2]{0:T(128)S(1)} %pad_add_fusion.place_ref, bf16[16,2,64,256]{3,2,1,0:T(8,128)(2,1)S(1)} %all_to_all.28.mine_ref, bf16[8,2,64,256]{3,2,1,0:T(8,128)(2,1)S(1)} %collective-permute-done.13.left_ref, bf16[8,2,64,256]{3,2,1,0:T(8,128)(2,1)S(1)} %collective-permute-done.14.right_ref, ...), custom_call_target="tpu_custom_call" | custom-call | flops 2684354560 | bytes 8388608 | tf_op jit(solution)/shard_map/project_first/pallas_call | solution.py:305
  256.8 1.6 copy-done.1
  258.4 6.7 %project_last.1 = bf16[8,2,64,640]{3,2,1,0:T(8,128)(2,1)S(1)} custom-call(s32[2]{0:T(128)S(1)} %pad_add_fusion.place_ref, bf16[16,2,64,256]{3,2,1,0:T(8,128)(2,1)S(1)} %all_to_all.28.mine_ref, bf16[8,2,64,256]{3,2,1,0:T(8,128)(2,1)S(1)} %collective-permute-done.8.left_ref, bf16[8,2,64,256]{3,2,1,0:T(8,128)(2,1)S(1)} %collective-permute-done.9.right_ref, ...), custom_call_target="tpu_custom_call" | custom-call | flops 2684354560 | bytes 8388608 | tf_op jit(solution)/shard_map/project_last/pallas_call | solution.py:305
  265.1 19.3 %all_to_all.29 = bf16[8,2,64,640]{3,2,1,0:T(8,128)(2,1)} all-to-all(bf16[8,2,64,640]{3,2,1,0:T(8,128)(2,1)S(1)} %project_last.1), channel_id=1, replica_groups={{0,16,32,48},{64,80,96,112},{1,17,33,49},{65,81,97,113},{2,18,34,50},{6..., dimensions={0} | all-to-all | bytes 2621440 | tf_op jit(solution)/shard_map/all_to_all | solution.py:457
  284.5 3.0 %add_branch.1 = bf16[2,64,5120]{2,1,0:T(8,128)(2,1)} custom-call(s32[1]{0:T(128)} %bitcast.pos_ref, bf16[4,2,2,64,640]{4,3,2,1,0:T(8,128)(2,1)} %bitcast.14, bf16[2,64,5120]{2,1,0:T(8,128)(2,1)} %hidden_ref.3, bf16[1,64,5120]{2,1,0:T(8,128)(2,1)} %copy-done.23, bf16[64,5120]{1,0:T(8,128)(2,1)} %entering_ref.1), custom_call_target="tpu_custom_call" | custom-call | tf_op jit(solution)/shard_map/add_branch/pallas_call | solution.py:352
  (60 shorter events, 0.2 us)
Async XLA Ops:
  6.5 42.5 %copy-start = (f32[50,640]{1,0:T(8,128)S(1)}, f32[50,640]{1,0:T(8,128)}, u32[]{:S(2)}) copy-start(f32[50,640]{1,0:T(8,128)} %param.13) | copy-start | bytes 384004
  6.5 41.8 %all-gather.5.cloned.1.call-start = ((), (), s32[]{:S(2)}) async-start(), calls=%async_computation.5 | async-start | bytes 1638400 | tf_op jit(solution)/shard_map/all_gather | solution.py:425
  7.3 153.0 %all-gather.7.cloned.1.call-start = ((), (), s32[]{:S(2)}) async-start(), calls=%async_computation.6 | async-start | bytes 6553600 | tf_op jit(solution)/shard_map/all_gather | solution.py:427
  49.0 0.7 copy-start.25
  49.0 5.0 %copy-start.2 = (bf16[16,2,2,64,128]{4,3,2,1,0:T(8,128)(2,1)S(1)}, bf16[16,2,2,64,128]{4,3,2,1,0:T(8,128)(2,1)}, u32[]{:S(2)}) copy-start(bf16[16,2,2,64,128]{4,3,2,1,0:T(8,128)(2,1)} %all_to_all.25.refs_1_.own_ref) | copy-start | bytes 3145732
  49.9 4.1 %collective-permute-start = (f32[16,640]{1,0:T(8,128)S(1)}, f32[16,640]{1,0:T(8,128)S(1)}, u32[]{:S(2)}, u32[]{:S(2)}) collective-permute-start(f32[16,640]{1,0:T(8,128)S(1)} %fusion), channel_id=1, source_target_pairs={{0,64},{16,80},{32,96},{48,112},{64,0},{80,16},{96,32},{112,48},{1... | collective-permute-start | bytes 122888 | tf_op jit(solution)/shard_map/ppermute | solution.py:407
  54.0 39.6 %collective-permute-start.1 = (bf16[16,2,2,64,128]{4,3,2,1,0:T(8,128)(2,1)S(1)}, bf16[16,2,2,64,128]{4,3,2,1,0:T(8,128)(2,1)S(1)}, u32[]{:S(2)}, u32[]{:S(2)}) collective-permute-start(bf16[16,2,2,64,128]{4,3,2,1,0:T(8,128)(2,1)S(1)} %copy-done.2), channel_id=1, source_target_pairs={{0,16},{16,32},{32,48},{48,64},{64,80},{80,96},{96,112},{1,17},{17... | collective-permute-start | bytes 3145736 | tf_op jit(solution)/shard_map/ppermute | solution.py:419
  57.5 36.2 %collective-permute-start.2 = (bf16[16,2,2,64,128]{4,3,2,1,0:T(8,128)(2,1)S(1)}, bf16[16,2,2,64,128]{4,3,2,1,0:T(8,128)(2,1)S(1)}, u32[]{:S(2)}, u32[]{:S(2)}) collective-permute-start(bf16[16,2,2,64,128]{4,3,2,1,0:T(8,128)(2,1)S(1)} %copy-done.2), channel_id=1, source_target_pairs={{16,0},{32,16},{48,32},{64,48},{80,64},{96,80},{112,96},{17,1},{33... | collective-permute-start | bytes 3145736 | tf_op jit(solution)/shard_map/ppermute | solution.py:419
  93.6 1.0 copy-start.8
  93.6 1.3 copy-start.10
  120.2 3.5 %copy-start.3 = (bf16[16,2,2,64,128]{4,3,2,1,0:T(8,128)(2,1)S(1)}, bf16[16,2,2,64,128]{4,3,2,1,0:T(8,128)(2,1)}, u32[]{:S(2)}) copy-start(bf16[16,2,2,64,128]{4,3,2,1,0:T(8,128)(2,1)} %all_to_all.25.refs_1_.own_ref) | copy-start | bytes 3145732
  120.2 3.5 %copy-start.5 = (bf16[16,2,64,256]{3,2,1,0:T(8,128)(2,1)S(1)}, bf16[16,2,64,256]{3,2,1,0:T(8,128)(2,1)}, u32[]{:S(2)}) copy-start(bf16[16,2,64,256]{3,2,1,0:T(8,128)(2,1)} %all_to_all.27.q_ref.refs_1_) | copy-start | bytes 3145732
  121.1 25.0 %collective-permute-start.4 = (bf16[16,2,2,64,128]{4,3,2,1,0:T(8,128)(2,1)}, bf16[16,2,2,64,128]{4,3,2,1,0:T(8,128)(2,1)S(1)}, u32[]{:S(2)}, u32[]{:S(2)}) collective-permute-start(bf16[16,2,2,64,128]{4,3,2,1,0:T(8,128)(2,1)} %hold.7.own_ref), channel_id=1, source_target_pairs={{0,16},{16,32},{32,48},{48,64},{64,80},{80,96},{96,112},{1,17},{17... | collective-permute-start | bytes 3145736 | tf_op jit(solution)/shard_map/ppermute | solution.py:423
  122.4 27.7 %collective-permute-start.5 = (bf16[16,2,2,64,128]{4,3,2,1,0:T(8,128)(2,1)}, bf16[16,2,2,64,128]{4,3,2,1,0:T(8,128)(2,1)S(1)}, u32[]{:S(2)}, u32[]{:S(2)}) collective-permute-start(bf16[16,2,2,64,128]{4,3,2,1,0:T(8,128)(2,1)} %hold.7.own_ref), channel_id=1, source_target_pairs={{16,0},{32,16},{48,32},{64,48},{80,64},{96,80},{112,96},{17,1},{33... | collective-permute-start | bytes 3145736 | tf_op jit(solution)/shard_map/ppermute | solution.py:423
  123.7 1.2 copy-start.9
  125.0 1.2 copy-start.11
  126.2 23.9 %copy-start.4 = (bf16[16,2,2,64,128]{4,3,2,1,0:T(8,128)(2,1)S(1)}, bf16[16,2,2,64,128]{4,3,2,1,0:T(8,128)(2,1)}, u32[]{:S(2)}) copy-start(bf16[16,2,2,64,128]{4,3,2,1,0:T(8,128)(2,1)} %hold.7.own_ref) | copy-start | bytes 3145732
  142.4 0.8 copy-start.6
  143.2 14.5 %copy-start.18 = (f32[8,128]{1,0:T(8,128)}, f32[8,128]{1,0:T(8,128)S(1)}, u32[]{:S(2)}) copy-start(f32[8,128]{1,0:T(8,128)S(1)} %get-tuple-element.17.rest_0_) | copy-start | bytes 12292
  157.8 0.6 copy-start.16
  158.4 1.0 copy-start.19
  159.3 1.0 copy-start.21
  160.3 6.1 %copy-start.13 = (bf16[16,1,64,128]{3,2,1,0:T(8,128)(2,1)}, bf16[16,1,64,128]{3,2,1,0:T(8,128)(2,1)S(1)}, u32[]{:S(2)}) copy-start(bf16[16,1,64,128]{3,2,1,0:T(8,128)(2,1)S(1)} %get-tuple-element.20.odd_ref) | copy-start | bytes 786436
  160.3 1.1 copy-start.7
  161.1 6.3 %copy-start.17 = (f32[8,128]{1,0:T(8,128)S(1)}, f32[8,128]{1,0:T(8,128)}, u32[]{:S(2)}) copy-start(f32[8,128]{1,0:T(8,128)} %copy-done.16) | copy-start | bytes 12292
  161.1 89.5 %collective-permute-start.12 = (bf16[4,2,2,256,640]{4,3,2,1,0:T(8,128)(2,1)}, bf16[4,2,2,256,640]{4,3,2,1,0:T(8,128)(2,1)}, u32[]{:S(2)}, u32[]{:S(2)}) collective-permute-start(bf16[4,2,2,256,640]{4,3,2,1,0:T(8,128)(2,1)} %hold.9.wo_ref), channel_id=1, source_target_pairs={{0,1},{1,0},{2,3},{3,2},{4,5},{5,4},{6,7},{7,6},{8,9},{9,8},{10,11... | collective-permute-start | bytes 15728648 | tf_op jit(solution)/shard_map/ppermute | solution.py:438
  162.2 5.1 %collective-permute-start.3 = (bf16[16,1,64,128]{3,2,1,0:T(8,128)(2,1)}, bf16[16,1,64,128]{3,2,1,0:T(8,128)(2,1)S(1)}, u32[]{:S(2)}, u32[]{:S(2)}) collective-permute-start(bf16[16,1,64,128]{3,2,1,0:T(8,128)(2,1)} %slice.25), channel_id=1, source_target_pairs={{48,112},{49,113},{50,114},{51,115},{52,116},{53,117},{54,118},{55... | collective-permute-start | bytes 786440 | tf_op jit(solution)/shard_map/ppermute | solution.py:432
  164.8 16.2 %collective-permute-start.7 = (bf16[1,64,5120]{2,1,0:T(8,128)(2,1)}, bf16[1,64,5120]{2,1,0:T(8,128)(2,1)S(1)}, u32[]{:S(2)}, u32[]{:S(2)}) collective-permute-start(bf16[1,64,5120]{2,1,0:T(8,128)(2,1)} %last_frame.1), channel_id=1, source_target_pairs={{0,16},{16,32},{32,48},{48,64},{64,80},{80,96},{96,112},{1,17},{17... | collective-permute-start | bytes 1966088 | tf_op jit(solution)/shard_map/ppermute | solution.py:433
  166.4 14.6 %collective-permute-start.6 = (bf16[16,1,64,128]{3,2,1,0:T(8,128)(2,1)S(1)}, bf16[16,1,64,128]{3,2,1,0:T(8,128)(2,1)S(1)}, u32[]{:S(2)}, u32[]{:S(2)}) collective-permute-start(bf16[16,1,64,128]{3,2,1,0:T(8,128)(2,1)S(1)} %get-tuple-element.20.odd_ref), channel_id=1, source_target_pairs={{48,112},{49,113},{50,114},{51,115},{52,116},{53,117},{54,118},{55... | collective-permute-start | bytes 786440 | tf_op jit(solution)/shard_map/ppermute | solution.py:436
  167.3 1.2 copy-start.20
  168.6 1.2 copy-start.22
  169.8 8.2 %copy-start.14 = (bf16[16,1,64,128]{3,2,1,0:T(8,128)(2,1)}, bf16[16,1,64,128]{3,2,1,0:T(8,128)(2,1)S(1)}, u32[]{:S(2)}) copy-start(bf16[16,1,64,128]{3,2,1,0:T(8,128)(2,1)S(1)} %collective-permute-done.3.rest_1_.crossing0_ref) | copy-start | bytes 786436
  178.0 0.7 copy-start.15
  181.0 0.9 copy-start.23
  181.0 0.7 copy-start.24
  210.5 23.2 %collective-permute-start.13 = (bf16[8,2,64,256]{3,2,1,0:T(8,128)(2,1)S(1)}, bf16[8,2,64,256]{3,2,1,0:T(8,128)(2,1)S(1)}, u32[]{:S(2)}, u32[]{:S(2)}) collective-permute-start(bf16[8,2,64,256]{3,2,1,0:T(8,128)(2,1)S(1)} %get-tuple-element.21), channel_id=1, source_target_pairs={{0,16},{16,32},{32,48},{48,0},{64,80},{80,96},{96,112},{112,64},{1... | collective-permute-start | bytes 1572872 | tf_op jit(solution)/shard_map/ppermute | solution.py:447
  212.8 21.6 %collective-permute-start.14 = (bf16[8,2,64,256]{3,2,1,0:T(8,128)(2,1)S(1)}, bf16[8,2,64,256]{3,2,1,0:T(8,128)(2,1)S(1)}, u32[]{:S(2)}, u32[]{:S(2)}) collective-permute-start(bf16[8,2,64,256]{3,2,1,0:T(8,128)(2,1)S(1)} %get-tuple-element.21), channel_id=1, source_target_pairs={{16,0},{32,16},{48,32},{0,48},{80,64},{96,80},{112,96},{64,112},{1... | collective-permute-start | bytes 1572872 | tf_op jit(solution)/shard_map/ppermute | solution.py:448
  220.9 24.0 %collective-permute-start.8 = (bf16[8,2,64,256]{3,2,1,0:T(8,128)(2,1)}, bf16[8,2,64,256]{3,2,1,0:T(8,128)(2,1)S(1)}, u32[]{:S(2)}, u32[]{:S(2)}) collective-permute-start(bf16[8,2,64,256]{3,2,1,0:T(8,128)(2,1)} %get-tuple-element.22), channel_id=1, source_target_pairs={{0,16},{16,32},{32,48},{48,0},{64,80},{80,96},{96,112},{112,64},{1... | collective-permute-start | bytes 1572872 | tf_op jit(solution)/shard_map/ppermute | solution.py:447
  220.9 24.2 %collective-permute-start.9 = (bf16[8,2,64,256]{3,2,1,0:T(8,128)(2,1)}, bf16[8,2,64,256]{3,2,1,0:T(8,128)(2,1)S(1)}, u32[]{:S(2)}, u32[]{:S(2)}) collective-permute-start(bf16[8,2,64,256]{3,2,1,0:T(8,128)(2,1)} %get-tuple-element.22), channel_id=1, source_target_pairs={{16,0},{32,16},{48,32},{0,48},{80,64},{96,80},{112,96},{64,112},{1... | collective-permute-start | bytes 1572872 | tf_op jit(solution)/shard_map/ppermute | solution.py:448
  234.4 16.1 %collective-permute-start.15 = (bf16[4,2,64,256]{3,2,1,0:T(8,128)(2,1)}, bf16[4,2,64,256]{3,2,1,0:T(8,128)(2,1)S(1)}, u32[]{:S(2)}, u32[]{:S(2)}) collective-permute-start(bf16[4,2,64,256]{3,2,1,0:T(8,128)(2,1)} %slice.37), channel_id=1, source_target_pairs={{0,16},{16,32},{32,48},{48,0},{64,80},{80,96},{96,112},{112,64},{1... | collective-permute-start | bytes 786440 | tf_op jit(solution)/shard_map/ppermute | solution.py:449
  235.1 15.4 %collective-permute-start.16 = (bf16[4,2,64,256]{3,2,1,0:T(8,128)(2,1)}, bf16[4,2,64,256]{3,2,1,0:T(8,128)(2,1)}, u32[]{:S(2)}, u32[]{:S(2)}) collective-permute-start(bf16[4,2,64,256]{3,2,1,0:T(8,128)(2,1)} %slice.38), channel_id=1, source_target_pairs={{16,0},{32,16},{48,32},{0,48},{80,64},{96,80},{112,96},{64,112},{1... | collective-permute-start | bytes 786440 | tf_op jit(solution)/shard_map/ppermute | solution.py:450
  244.9 13.4 %collective-permute-start.10 = (bf16[4,2,64,256]{3,2,1,0:T(8,128)(2,1)S(1)}, bf16[4,2,64,256]{3,2,1,0:T(8,128)(2,1)S(1)}, u32[]{:S(2)}, u32[]{:S(2)}) collective-permute-start(bf16[4,2,64,256]{3,2,1,0:T(8,128)(2,1)S(1)} %slice.34), channel_id=1, source_target_pairs={{0,16},{16,32},{32,48},{48,0},{64,80},{80,96},{96,112},{112,64},{1... | collective-permute-start | bytes 786440 | tf_op jit(solution)/shard_map/ppermute | solution.py:449
  245.1 13.3 %collective-permute-start.11 = (bf16[4,2,64,256]{3,2,1,0:T(8,128)(2,1)S(1)}, bf16[4,2,64,256]{3,2,1,0:T(8,128)(2,1)S(1)}, u32[]{:S(2)}, u32[]{:S(2)}) collective-permute-start(bf16[4,2,64,256]{3,2,1,0:T(8,128)(2,1)S(1)} %slice.35), channel_id=1, source_target_pairs={{16,0},{32,16},{48,32},{0,48},{80,64},{96,80},{112,96},{64,112},{1... | collective-permute-start | bytes 786440 | tf_op jit(solution)/shard_map/ppermute | solution.py:450
  248.4 10.0 %copy-start.12 = (f32[2,8,640]{2,1,0:T(8,128)S(1)}, f32[2,8,640]{2,1,0:T(8,128)}, u32[]{:S(2)}) copy-start(f32[2,8,640]{2,1,0:T(8,128)} %dynamic-slice_select_fusion.refs_2_.rest_1_) | copy-start | bytes 122884
  256.8 1.6 copy-start.1
Sparse Core Ops, SparseCore 0:
  9.0 37.2 all-gather.4
  49.1 78.0 all-gather.6

commit v6 on v4

--- a/solution.py
+++ b/solution.py
@@ -36,20 +36,27 @@
     piece = width // PACK
     count = SPATIAL // PACK
 
-    def kernel(q_ref, k_ref, v_ref, *out_refs):
+    def kernel(q_ref, k_ref, v_ref, kv0_ref, kv1_ref, out_ref):
         for i in range(count):
-            for head, out_ref in enumerate(out_refs):
+            for head, kv_ref in enumerate((kv0_ref, kv1_ref)):
                 cols = slice(i * group + head * HD, i * group + (head + 1) * HD)
-                for at, ref in enumerate((q_ref, k_ref, v_ref)):
-                    out_ref[i, at] = ref[:, :, cols]
-
-    heads = group // HD
+                kv_ref[i, 0] = k_ref[:, :, cols]
+                kv_ref[i, 1] = v_ref[:, :, cols]
+            out_ref[i] = q_ref[:, :, i * group : (i + 1) * group]
+
+    spec = pl.BlockSpec((frames, tok, piece), lambda s: (0, 0, s))
+    kv_spec = pl.BlockSpec((count, 2, frames, tok, HD), lambda s: (s, 0, 0, 0, 0))
+    kv_shape = jax.ShapeDtypeStruct((SPATIAL, 2, frames, tok, HD), keys.dtype)
     return pl.pallas_call(
         kernel,
         grid=(PACK,),
-        in_specs=[pl.BlockSpec((frames, tok, piece), lambda s: (0, 0, s))] * 3,
-        out_specs=[pl.BlockSpec((count, 3, frames, tok, HD), lambda s: (s, 0, 0, 0, 0))] * heads,
-        out_shape=[jax.ShapeDtypeStruct((SPATIAL, 3, frames, tok, HD), keys.dtype)] * heads,
+        in_specs=[spec] * 3,
+        out_specs=[kv_spec, kv_spec, pl.BlockSpec((count, frames, tok, group), lambda s: (s, 0, 0, 0))],
+        out_shape=[
+            kv_shape,
+            kv_shape,
+            jax.ShapeDtypeStruct((SPATIAL, frames, tok, group), queries.dtype),
+        ],
         name="pack",
     )(queries, keys, values)
 
@@ -86,8 +93,9 @@
     )(array, *earlier)
 
 
-def attend(frame, position, own, before, after, *earlier):
-    groups, _, frames, tok, width = own.shape
+def attend(frame, position, query, head, own, before, after, *earlier):
+    groups, frames, tok, both = query.shape
+    width = own.shape[-1]
     row_count = groups * tok
     groups_block = BLOCK_Q // tok
     blocks = row_count // BLOCK_Q
@@ -100,23 +108,23 @@
     def kernel(pos_ref, q_ref, own_ref, before_ref, after_ref, *rest):
         out_ref, token_ref, kt_ref, vx_ref = rest[-4:]
         sources = (
-            [(before_ref, 0, f) for f in range(before_count)]
-            + [(own_ref, 1, f) for f in range(frames)]
-            + [(after_ref, 0, f) for f in range(after_count)]
+            [(before_ref, f) for f in range(before_count)]
+            + [(own_ref, f) for f in range(frames)]
+            + [(after_ref, f) for f in range(after_count)]
         )
         turn_frame = pl.program_id(0)
 
         @pl.when((turn_frame == 0) & (pl.program_id(1) == 0))
         def _():
-            for at, (ref, key, f) in enumerate(sources):
+            for at, (ref, f) in enumerate(sources):
                 rows = slice(at * row_count, (at + 1) * row_count)
-                turned = ref[:, key, f].reshape(row_count, width).T
+                turned = ref[:, 0, f].reshape(row_count, width).T
                 kt_ref[:width, rows] = turned
                 kt_ref[width:, rows] = turned
-                vx_ref[rows, :width] = ref[:, key + 1, f].reshape(row_count, width)
+                vx_ref[rows, :width] = ref[:, 1, f].reshape(row_count, width)
                 vx_ref[rows, width:] = jnp.ones((row_count, width), vx_ref.dtype)
 
-        q = q_ref[:, 0, 0].reshape(BLOCK_Q, width).astype(jnp.float32) * SCALE_LOG2
+        q = q_ref[:, 0].reshape(BLOCK_Q, width).astype(jnp.float32) * SCALE_LOG2
         high = q.astype(jnp.bfloat16)
         low = (q - high.astype(jnp.float32)).astype(jnp.bfloat16)
         q = jnp.concatenate((high, low), axis=1)
@@ -155,7 +163,7 @@
 
     first = asked[0]
     in_specs = [
-        pl.BlockSpec((groups_block, 1, 1, tok, width), lambda f, b, pos: (b, 0, first + f, 0, 0)),
+        pl.BlockSpec((groups_block, 1, tok, width), lambda f, b, pos: (b, first + f, 0, head)),
         pl.BlockSpec(own.shape, lambda f, b, pos: (0, 0, 0, 0, 0)),
         pl.BlockSpec(
             (groups, 2, before_count, tok, width),
@@ -179,7 +187,7 @@
             ],
         ),
         out_shape=[
-            jax.ShapeDtypeStruct((groups, len(asked), tok, width), own.dtype),
+            jax.ShapeDtypeStruct((groups, len(asked), tok, width), query.dtype),
             jax.ShapeDtypeStruct(TOKEN, jnp.float32),
         ],
         compiler_params=pltpu.CompilerParams(vmem_limit_bytes=VMEM),
@@ -189,7 +197,7 @@
             transcendentals=len(asked) * row_count * SPAN * row_count,
         ),
         name="attend",
-    )(position, own, own, before, after, *earlier)
+    )(position, query, own, before, after, *earlier)
 
 
 def project(head, place, sources, weight_own, weight_pair, partial, gates, *earlier):
@@ -369,39 +377,49 @@
         lax.dynamic_slice_in_dim(gates, y_low * count, count, axis=1),
     )
 
-    first, second = pack(queries, keys, values)
-    first = to_heads(first)
-    first_kv = first[:, 1:]
-    first_sides = lax.ppermute(first_kv, "queue", up), lax.ppermute(first_kv, "queue", down)
-    second = to_heads(hold(second, *first_sides, gates))
-    second_kv = second[:, 1:]
-    second_sides = lax.ppermute(second_kv, "queue", up), lax.ppermute(second_kv, "queue", down)
+    kv0, kv1, query = pack(queries, keys, values)
+    kv0 = to_heads(kv0)
+    kv1 = to_heads(hold(kv1, kv0, gates))
+    kv0 = hold(kv0, kv1)
+    kv0_before, kv0_after = lax.ppermute(kv0, "queue", up), lax.ppermute(kv0, "queue", down)
+    query = to_heads(hold(query, kv1))
+    kv1 = hold(kv1, query)
+    kv1_before, kv1_after = lax.ppermute(kv1, "queue", up), lax.ppermute(kv1, "queue", down)
 
     weight = lax.all_gather(out_weight, ("queue", "spatial"), axis_index_groups=along_y, axis=0)
-    weight = hold(weight, first)
+    weight = hold(weight, query)
     weight = lax.all_gather(weight, "spatial", axis_index_groups=along_z, axis=0)
     weight = weight.reshape(-1, 2, 2, *out_weight.shape)
 
-    def spread(even, odd):
-        crossing = lax.ppermute(odd, "queue", [(RING - 1, QUEUE - 1)])
+    cross = [(RING - 1, QUEUE - 1)]
+
+    def returned(even, odd, crossing):
         odd = jnp.where(position == QUEUE - 1, crossing, odd)
-        mine = to_heads(jnp.concatenate((even, odd), axis=1))
+        return to_heads(jnp.concatenate((even, odd), axis=1))
+
+    def spread(mine):
         left = lax.ppermute(mine, "queue", ring_up)
         right = lax.ppermute(mine, "queue", ring_down)
         far_low = lax.ppermute(left[: SPATIAL // 2], "queue", ring_up)
         far_high = lax.ppermute(right[SPATIAL // 2 :], "queue", ring_down)
         return mine, left, right, far_low, far_high
 
-    both, token = attend(None, position_now, first, *first_sides)
-    shifted = lax.ppermute(last_frame(hidden, *second_sides), "queue", up)
-    first_sources = spread(both[:, :1], both[:, 1:])
-    odd, token = attend(1, position_now, second, *second_sides, token)
+    head0 = (position_now, query, 0, kv0, kv0_before, kv0_after)
+    head1 = (position_now, query, 1, kv1, kv1_before, kv1_after)
+    odd0, token = attend(1, *head0)
+    odd0_crossing = lax.ppermute(odd0, "queue", cross)
+    even0, token = attend(0, *head0, token)
+    first = returned(even0, odd0, odd0_crossing)
+    odd1, token = attend(1, *head1, token, odd0_crossing)
+    odd1_crossing = lax.ppermute(odd1, "queue", cross)
+    shifted = lax.ppermute(last_frame(hidden, kv1_before, kv1_after), "queue", up)
     weight_own = hold(weight, token)
     weight_pair = lax.ppermute(weight_own, "spatial", swap_core)
-    even, token = attend(0, position_now, second, *second_sides, token, first_sources[0])
-    second_sources = spread(even, odd)
-
-    partial = project(0, place, first_sources, weight_own, weight_pair, None, None, shifted)
+    even1, token = attend(0, *head1, token)
+    first_sources = spread(hold(first, token, shifted))
+    second_sources = spread(returned(even1, odd1, odd1_crossing))
+
+    partial = project(0, place, first_sources, weight_own, weight_pair, None, None)
     branch = project(1, place, second_sources, weight_own, weight_pair, partial, gates)
     branch = lax.all_to_all(
         branch, "queue", split_axis=0, concat_axis=0, axis_index_groups=ring, tiled=True

time: 305 us -> 264 us (0.87)
  blocking collectives: 91.9 us -> 19.3 us
  waiting for transfers between devices: 70.2 us -> 95.1 us
    all_to_all x2 -> x0, blocking collectives: 74.3 us -> none  [the longest x1 42.4 us: body(): first = to_heads(first)]
    ppermute x2, waiting for transfers between devices: 22.8 us -> 1.48 us  [spread(): left = lax.ppermute(mine, 'queue', ring_up)]
    all_to_all x2 -> x5, starting transfers between devices: 9.78 us -> 28.4 us  [the longest x2 12.4 us: returned(): return to_heads(jnp.concatenate((even, odd), axis=1))]
    all_to_all x2 -> x5, waiting for transfers between devices: 12.7 us -> 31 us  [the longest x1 17.3 us: body(): kv1 = to_heads(hold(kv1, kv0, gates))]
    all_gather x1, waiting for transfers between devices: 0.01 us -> 16.8 us  [body(): lax.all_gather(out_weight, ('queue', 'spatial'), axis_index_groups=along_...]
    ppermute x2, starting transfers between devices: 22.2 us -> 5.48 us  [spread(): right = lax.ppermute(mine, 'queue', ring_down)]
    ppermute x7, waiting for transfers between devices: 4.65 us -> 20.9 us  [the longest x1 15.9 us: body(): lax.ppermute(kv0, 'queue', up)]
    ppermute x1, waiting for transfers between devices: 24 us -> 13.3 us  [body(): other_gates = lax.ppermute(gates, 'queue', swap_low)]
  transfers between devices with their start and end apart: 21 -> 24, of which waited for: 8 -> 12; matrix products, arithmetic and copies ran while one was open for 2% -> 2% of each run, Pallas kernels for 15% -> 17%
where the time goes in v6:
time: 264 us; the launch traced here: 262 us
  waiting for transfers between devices  95.1 us (36%)
  Pallas kernels  60.3 us (23%)
  starting transfers between devices  58.3 us (22%)
  blocking collectives  19.3 us (7%)
  between operations  13.8 us (5%)
  local copies, waits for them, and re-layouts  12.9 us (5%)
    pallas_call x4, Pallas kernels, attend(): pl.pallas_call(kernel, grid_spec=pltpu.PrefetchScalarGridSpec(num_scalar_...  33 us
    all_to_all x1, blocking collectives, body(): lax.all_to_all(branch, 'queue', split_axis=0, concat_axis=0, axis_index_g...  19.3 us
    all_to_all x1, waiting for transfers between devices, body(): kv1 = to_heads(hold(kv1, kv0, gates))  17.3 us
    all_gather x1, waiting for transfers between devices, body(): lax.all_gather(out_weight, ('queue', 'spatial'), axis_index_groups=along_...  16.8 us
    ppermute x1, waiting for transfers between devices, body(): lax.ppermute(kv0, 'queue', up)  15.9 us
    ppermute x1, waiting for transfers between devices, body(): other_gates = lax.ppermute(gates, 'queue', swap_low)  13.3 us
    pallas_call x2, Pallas kernels, project(): pl.pallas_call(kernel, grid_spec=pltpu.PrefetchScalarGridSpec(num_scalar_...  13.2 us
    all_to_all x2, starting transfers between devices, returned(): return to_heads(jnp.concatenate((even, odd), axis=1))  12.4 us
  transfers between devices with their start and end apart: 24, of which 12 were waited for; matrix products, arithmetic and copies ran while one was open for 2% of the time, Pallas kernels for 17%

profile of v6, /device:TPU:0, one launch (start us, length us, event | category | flops | bytes accessed | tf_op | source)
XLA Modules:
  0.0 262.4 jit_solution(457800113461793937)
XLA Ops:
  6.5 4.3 %pack.1 = (bf16[16,2,2,64,128]{4,3,2,1,0:T(8,128)(2,1)}, bf16[16,2,2,64,128]{4,3,2,1,0:T(8,128)(2,1)}, bf16[16,2,64,256]{3,2,1,0:T(8,128)(2,1)}) custom-call(bf16[2,64,4096]{2,1,0:T(8,128)(2,1)} %q_ref.1, bf16[2,64,4096]{2,1,0:T(8,128)(2,1)} %k_ref.1, bf16[2,64,4096]{2,1,0:T(8,128)(2,1)} %v_ref.1), custom_call_target="tpu_custom_call" | custom-call | tf_op jit(solution)/shard_map/pack/pallas_call | solution.py:50
  10.8 8.3 %all-to-all-start = ((bf16[16,2,2,64,128]{4,3,2,1,0:T(8,128)(2,1)}), bf16[16,2,2,64,128]{4,3,2,1,0:T(8,128)(2,1)S(1)}, u32[]{:S(2)}, u32[]{:S(2)}) async-start(bf16[16,2,2,64,128]{4,3,2,1,0:T(8,128)(2,1)} %get-tuple-element.18), calls=%async_computation | async-start | bytes 2097152 | tf_op jit(solution)/shard_map/all_to_all | solution.py:381
  19.3 0.8 collective-permute-start
  20.1 13.3 %collective-permute-done = f32[16,640]{1,0:T(8,128)S(1)} collective-permute-done((f32[16,640]{1,0:T(8,128)S(1)}, f32[16,640]{1,0:T(8,128)S(1)}, u32[]{:S(2)}, u32[]{:S(2)}) %collective-permute-start) | collective-permute-done | bytes 40992 | tf_op jit(solution)/shard_map/ppermute | solution.py:370
  33.4 0.7 dynamic-slice_select_fusion.refs_2_.rest_1_
  34.1 3.4 %all-to-all-done.refs_1_.refs_0_ = bf16[16,2,2,64,128]{4,3,2,1,0:T(8,128)(2,1)S(1)} async-done(((bf16[16,2,2,64,128]{4,3,2,1,0:T(8,128)(2,1)}), bf16[16,2,2,64,128]{4,3,2,1,0:T(8,128)(2,1)S(1)}, u32[]{:S(2)}, u32[]{:S(2)}) %all-to-all-start) | async-done | bytes 1048608 | tf_op jit(solution)/shard_map/all_to_all | solution.py:381
  37.5 1.0 copy-done.3
  38.5 0.7 hold.7
  39.2 4.1 %all-to-all-start.1 = ((bf16[16,2,2,64,128]{4,3,2,1,0:T(8,128)(2,1)}), bf16[16,2,2,64,128]{4,3,2,1,0:T(8,128)(2,1)S(1)}, u32[]{:S(2)}, u32[]{:S(2)}) async-start(bf16[16,2,2,64,128]{4,3,2,1,0:T(8,128)(2,1)} %hold.7), calls=%async_computation.1 | async-start | bytes 2097152 | tf_op jit(solution)/shard_map/all_to_all | solution.py:382
  43.4 0.7 all-gather.5.cloned.1.call-update
  44.1 17.3 %all-to-all-done.1.refs_1_.refs_0_ = bf16[16,2,2,64,128]{4,3,2,1,0:T(8,128)(2,1)S(1)} async-done(((bf16[16,2,2,64,128]{4,3,2,1,0:T(8,128)(2,1)}), bf16[16,2,2,64,128]{4,3,2,1,0:T(8,128)(2,1)S(1)}, u32[]{:S(2)}, u32[]{:S(2)}) %all-to-all-start.1) | async-done | bytes 1048608 | tf_op jit(solution)/shard_map/all_to_all | solution.py:382
  61.4 1.0 copy-done.1
  62.3 0.7 hold.8
  63.0 3.7 %all-to-all-start.2 = ((bf16[16,2,64,256]{3,2,1,0:T(8,128)(2,1)}), bf16[16,2,64,256]{3,2,1,0:T(8,128)(2,1)S(1)}, u32[]{:S(2)}, u32[]{:S(2)}) async-start(bf16[16,2,64,256]{3,2,1,0:T(8,128)(2,1)} %hold.8), calls=%async_computation.2 | async-start | bytes 2097152 | tf_op jit(solution)/shard_map/all_to_all | solution.py:385
  66.7 16.8 %all-gather.5.cloned.1.call-done = bf16[1024,640]{1,0:T(8,128)(2,1)} async-done(((bf16[256,640]{1,0:T(8,128)(2,1)}), bf16[1024,640]{1,0:T(8,128)(2,1)}) %all-gather.5.cloned.1.call-update) | async-done | bytes 1310736 | tf_op jit(solution)/shard_map/all_gather | solution.py:389
  83.5 1.9 all-to-all-done.2.refs_1_.q_ref
  85.3 1.0 copy-done.5
  86.3 0.7 hold.11
  87.0 0.7 hold.10.own_ref
  87.7 3.6 %collective-permute-start.3 = (bf16[16,2,2,64,128]{4,3,2,1,0:T(8,128)(2,1)}, bf16[16,2,2,64,128]{4,3,2,1,0:T(8,128)(2,1)S(1)}, u32[]{:S(2)}, u32[]{:S(2)}) collective-permute-start(bf16[16,2,2,64,128]{4,3,2,1,0:T(8,128)(2,1)} %hold.10.own_ref), channel_id=1, source_target_pairs={{0,16},{16,32},{32,48},{48,64},{64,80},{80,96},{96,112},{1,17},{17... | collective-permute-start | bytes 3145736 | tf_op jit(solution)/shard_map/ppermute | solution.py:384
  91.3 1.3 collective-permute-start.4
  92.6 0.7 hold.9.own_ref
  93.3 4.6 %collective-permute-start.1 = (bf16[16,2,2,64,128]{4,3,2,1,0:T(8,128)(2,1)}, bf16[16,2,2,64,128]{4,3,2,1,0:T(8,128)(2,1)S(1)}, u32[]{:S(2)}, u32[]{:S(2)}) collective-permute-start(bf16[16,2,2,64,128]{4,3,2,1,0:T(8,128)(2,1)} %hold.9.own_ref), channel_id=1, source_target_pairs={{0,16},{16,32},{32,48},{48,64},{64,80},{80,96},{96,112},{1,17},{17... | collective-permute-start | bytes 3145736 | tf_op jit(solution)/shard_map/ppermute | solution.py:387
  97.9 1.3 collective-permute-start.2
  99.2 15.9 %collective-permute-done.3.before_ref = bf16[16,2,2,64,128]{4,3,2,1,0:T(8,128)(2,1)S(1)} collective-permute-done((bf16[16,2,2,64,128]{4,3,2,1,0:T(8,128)(2,1)}, bf16[16,2,2,64,128]{4,3,2,1,0:T(8,128)(2,1)S(1)}, u32[]{:S(2)}, u32[]{:S(2)}) %collective-permute-start.3) | collective-permute-done | bytes 1048608 | tf_op jit(solution)/shard_map/ppermute | solution.py:384
  115.1 4.5 %collective-permute-done.4.after_ref = bf16[16,2,2,64,128]{4,3,2,1,0:T(8,128)(2,1)} collective-permute-done((bf16[16,2,2,64,128]{4,3,2,1,0:T(8,128)(2,1)}, bf16[16,2,2,64,128]{4,3,2,1,0:T(8,128)(2,1)}, u32[]{:S(2)}, u32[]{:S(2)}) %collective-permute-start.4) | collective-permute-done | bytes 1048608 | tf_op jit(solution)/shard_map/ppermute | solution.py:384
  119.6 8.8 %attend.4 = (bf16[16,1,64,128]{3,2,1,0:T(8,128)(2,1)S(1)}, f32[8,128]{1,0:T(8,128)S(1)}) custom-call(s32[1]{0:T(128)} %bitcast.pos_ref, bf16[16,2,64,256]{3,2,1,0:T(8,128)(2,1)S(1)} %copy-done.6, bf16[16,2,2,64,128]{4,3,2,1,0:T(8,128)(2,1)S(1)} %copy-done.4, bf16[16,2,2,64,128]{4,3,2,1,0:T(8,128)(2,1)S(1)} %collective-permute-done.3.before_ref, ...), custom_call_target="tpu_custom_call" | custom-call | flops 5368709120 | bytes 4194304 | tf_op jit(solution)/shard_map/attend/pallas_call | solution.py:174
  128.5 0.9 collective-permute-start.5
  129.3 1.2 copy-done.22
  130.5 8.8 %attend.5 = (bf16[16,1,64,128]{3,2,1,0:T(8,128)(2,1)S(1)}, f32[8,128]{1,0:T(8,128)S(1)}) custom-call(s32[1]{0:T(128)} %bitcast.pos_ref, bf16[16,2,64,256]{3,2,1,0:T(8,128)(2,1)S(1)} %copy-done.6, bf16[16,2,2,64,128]{4,3,2,1,0:T(8,128)(2,1)S(1)} %copy-done.4, bf16[16,2,2,64,128]{4,3,2,1,0:T(8,128)(2,1)S(1)} %copy-done.22, ...), custom_call_target="tpu_custom_call" | custom-call | flops 5368709120 | bytes 4194304 | tf_op jit(solution)/shard_map/attend/pallas_call | solution.py:174
  139.4 0.7 copy-done.16
  140.1 0.4 collective-permute-done.2.after_ref.rest_1_
  140.5 7.6 %attend.6 = (bf16[16,1,64,128]{3,2,1,0:T(8,128)(2,1)S(1)}, f32[8,128]{1,0:T(8,128)S(1)}) custom-call(s32[1]{0:T(128)} %bitcast.pos_ref, bf16[16,2,64,256]{3,2,1,0:T(8,128)(2,1)S(1)} %copy-done.6, bf16[16,2,2,64,128]{4,3,2,1,0:T(8,128)(2,1)S(1)} %copy-done.2, bf16[16,2,2,64,128]{4,3,2,1,0:T(8,128)(2,1)S(1)} %collective-permute-done.1.before_ref.rest_0_, ...), custom_call_target="tpu_custom_call" | custom-call | flops 5368709120 | bytes 4194304 | tf_op jit(solution)/shard_map/attend/pallas_call | solution.py:174
  148.2 1.0 copy-done.9
  149.1 1.0 copy-done.11
  150.1 0.7 copy-done.14
  150.8 0.6 copy-done.18
  151.4 0.7 hold.12.wo_ref
  152.5 0.9 pad_maximum_fusion.1
  153.3 5.1 %all-to-all-start.4 = ((bf16[16,2,64,128]{3,2,1,0:T(8,128)(2,1)}), bf16[16,2,64,128]{3,2,1,0:T(8,128)(2,1)S(1)}, u32[]{:S(2)}, u32[]{:S(2)}) async-start(bf16[16,2,64,128]{3,2,1,0:T(8,128)(2,1)} %pad_maximum_fusion.1), calls=%async_computation.4 | async-start | bytes 1048576 | tf_op jit(solution)/shard_map/all_to_all | solution.py:398
  158.5 2.0 last_frame.1
  160.5 4.2 %collective-permute-start.12 = (bf16[1,64,5120]{2,1,0:T(8,128)(2,1)}, bf16[1,64,5120]{2,1,0:T(8,128)(2,1)}, u32[]{:S(2)}, u32[]{:S(2)}) collective-permute-start(bf16[1,64,5120]{2,1,0:T(8,128)(2,1)} %last_frame.1), channel_id=1, source_target_pairs={{0,16},{16,32},{32,48},{48,64},{64,80},{80,96},{96,112},{1,17},{17... | collective-permute-start | bytes 1966088 | tf_op jit(solution)/shard_map/ppermute | solution.py:415
  164.7 0.9 collective-permute-start.6
  165.6 1.2 copy-done.10
  166.9 1.2 copy-done.12
  168.1 7.7 %attend.7 = (bf16[16,1,64,128]{3,2,1,0:T(8,128)(2,1)S(1)}, f32[8,128]{1,0:T(8,128)S(1)}) custom-call(s32[1]{0:T(128)} %bitcast.pos_ref, bf16[16,2,64,256]{3,2,1,0:T(8,128)(2,1)S(1)} %copy-done.6, bf16[16,2,2,64,128]{4,3,2,1,0:T(8,128)(2,1)S(1)} %copy-done.2, bf16[16,2,2,64,128]{4,3,2,1,0:T(8,128)(2,1)S(1)} %copy-done.10, ...), custom_call_target="tpu_custom_call" | custom-call | flops 5368709120 | bytes 4194304 | tf_op jit(solution)/shard_map/attend/pallas_call | solution.py:174
  175.9 0.5 copy-done.20
  176.4 0.8 pad_maximum_fusion
  177.3 7.2 %all-to-all-start.3 = ((bf16[16,2,64,128]{3,2,1,0:T(8,128)(2,1)}), bf16[16,2,64,128]{3,2,1,0:T(8,128)(2,1)S(1)}, u32[]{:S(2)}, u32[]{:S(2)}) async-start(bf16[16,2,64,128]{3,2,1,0:T(8,128)(2,1)} %pad_maximum_fusion), calls=%async_computation.3 | async-start | bytes 1048576 | tf_op jit(solution)/shard_map/all_to_all | solution.py:398
  184.5 0.7 hold.13.mine_ref
  185.5 2.9 %collective-permute-start.14 = (bf16[16,2,64,128]{3,2,1,0:T(8,128)(2,1)}, bf16[16,2,64,128]{3,2,1,0:T(8,128)(2,1)S(1)}, u32[]{:S(2)}, u32[]{:S(2)}) collective-permute-start(bf16[16,2,64,128]{3,2,1,0:T(8,128)(2,1)} %hold.13.mine_ref), channel_id=1, source_target_pairs={{16,0},{32,16},{48,32},{0,48},{80,64},{96,80},{112,96},{64,112},{1... | collective-permute-start | bytes 1572872 | tf_op jit(solution)/shard_map/ppermute | solution.py:402
  188.4 8.4 %all-to-all-done.3.mine_ref = bf16[16,2,64,128]{3,2,1,0:T(8,128)(2,1)S(1)} async-done(((bf16[16,2,64,128]{3,2,1,0:T(8,128)(2,1)}), bf16[16,2,64,128]{3,2,1,0:T(8,128)(2,1)S(1)}, u32[]{:S(2)}, u32[]{:S(2)}) %all-to-all-start.3) | async-done | bytes 524320 | tf_op jit(solution)/shard_map/all_to_all | solution.py:398
  196.9 2.5 collective-permute-start.8
  199.4 1.5 collective-permute-done.13.left_ref
  200.9 0.7 slice.23
  201.8 0.7 slice.24
  202.6 3.0 %collective-permute-start.16 = (bf16[8,2,64,128]{3,2,1,0:T(8,128)(2,1)}, bf16[8,2,64,128]{3,2,1,0:T(8,128)(2,1)}, u32[]{:S(2)}, u32[]{:S(2)}) collective-permute-start(bf16[8,2,64,128]{3,2,1,0:T(8,128)(2,1)} %slice.24), channel_id=1, source_target_pairs={{16,0},{32,16},{48,32},{0,48},{80,64},{96,80},{112,96},{64,112},{1... | collective-permute-start | bytes 786440 | tf_op jit(solution)/shard_map/ppermute | solution.py:404
  205.6 7.1 %collective-permute-done.8.right_ref = bf16[16,2,64,128]{3,2,1,0:T(8,128)(2,1)S(1)} collective-permute-done((bf16[16,2,64,128]{3,2,1,0:T(8,128)(2,1)S(1)}, bf16[16,2,64,128]{3,2,1,0:T(8,128)(2,1)S(1)}, u32[]{:S(2)}, u32[]{:S(2)}) %collective-permute-start.8) | collective-permute-done | bytes 524320 | tf_op jit(solution)/shard_map/ppermute | solution.py:402
  212.8 3.2 %collective-permute-start.10 = (bf16[8,2,64,128]{3,2,1,0:T(8,128)(2,1)S(1)}, bf16[8,2,64,128]{3,2,1,0:T(8,128)(2,1)S(1)}, u32[]{:S(2)}, u32[]{:S(2)}) collective-permute-start(bf16[8,2,64,128]{3,2,1,0:T(8,128)(2,1)S(1)} %slice.22), channel_id=1, source_target_pairs={{16,0},{32,16},{48,32},{0,48},{80,64},{96,80},{112,96},{64,112},{1... | collective-permute-start | bytes 786440 | tf_op jit(solution)/shard_map/ppermute | solution.py:404
  216.2 3.9 %collective-permute-done.15.low_ref = bf16[8,2,64,128]{3,2,1,0:T(8,128)(2,1)S(1)} collective-permute-done((bf16[8,2,64,128]{3,2,1,0:T(8,128)(2,1)}, bf16[8,2,64,128]{3,2,1,0:T(8,128)(2,1)S(1)}, u32[]{:S(2)}, u32[]{:S(2)}) %collective-permute-start.15) | collective-permute-done | bytes 262176 | tf_op jit(solution)/shard_map/ppermute | solution.py:403
  220.1 6.5 %project_first.1.rest_0_ = f32[2,512,640]{2,1,0:T(8,128)S(1)} custom-call(s32[2]{0:T(128)S(1)} %pad_add_fusion.place_ref, bf16[16,2,64,128]{3,2,1,0:T(8,128)(2,1)S(1)} %copy-done.8, bf16[16,2,64,128]{3,2,1,0:T(8,128)(2,1)S(1)} %collective-permute-done.13.left_ref, bf16[16,2,64,128]{3,2,1,0:T(8,128)(2,1)S(1)} %collective-permute-done.14.right_ref, ...), custom_call_target="tpu_custom_call" | custom-call | flops 2684354560 | bytes 8388608 | tf_op jit(solution)/shard_map/project_first/pallas_call | solution.py:268
  226.6 6.7 %project_last.1 = bf16[8,2,64,640]{3,2,1,0:T(8,128)(2,1)S(1)} custom-call(s32[2]{0:T(128)S(1)} %pad_add_fusion.place_ref, bf16[16,2,64,128]{3,2,1,0:T(8,128)(2,1)S(1)} %all-to-all-done.3.mine_ref, bf16[16,2,64,128]{3,2,1,0:T(8,128)(2,1)S(1)} %collective-permute-done.7.left_ref, bf16[16,2,64,128]{3,2,1,0:T(8,128)(2,1)S(1)} %collective-permute-done.8.right_ref, ...), custom_call_target="tpu_custom_call" | custom-call | flops 2684354560 | bytes 8388608 | tf_op jit(solution)/shard_map/project_last/pallas_call | solution.py:268
  233.3 19.3 %all_to_all.30 = bf16[8,2,64,640]{3,2,1,0:T(8,128)(2,1)} all-to-all(bf16[8,2,64,640]{3,2,1,0:T(8,128)(2,1)S(1)} %project_last.1), channel_id=1, replica_groups={{0,16,32,48},{64,80,96,112},{1,17,33,49},{65,81,97,113},{2,18,34,50},{6..., dimensions={0} | all-to-all | bytes 2621440 | tf_op jit(solution)/shard_map/all_to_all | solution.py:424
  252.6 3.0 %add_branch.1 = bf16[2,64,5120]{2,1,0:T(8,128)(2,1)} custom-call(s32[1]{0:T(128)} %bitcast.pos_ref, bf16[4,2,2,64,640]{4,3,2,1,0:T(8,128)(2,1)} %bitcast.14, bf16[2,64,5120]{2,1,0:T(8,128)(2,1)} %hidden_ref.3, bf16[1,64,5120]{2,1,0:T(8,128)(2,1)} %collective-permute-done.12.refs_2_.shifted_ref, bf16[64,5120]{1,0:T(8,128)(2,1)} %entering_ref.1), custom_call_target="tpu_custom_call" | custom-call | tf_op jit(solution)/shard_map/add_branch/pallas_call | solution.py:315
  (66 shorter events, 1.5 us)
Async XLA Ops:
  6.5 12.5 %copy-start = (f32[50,640]{1,0:T(8,128)S(1)}, f32[50,640]{1,0:T(8,128)}, u32[]{:S(2)}) copy-start(f32[50,640]{1,0:T(8,128)} %param.13) | copy-start | bytes 384004
  10.8 8.3 %copy-start.23 = (s32[16]{0:T(128)S(1)}, s32[16]{0:T(128)}, u32[]{:S(2)}) copy-start(s32[16]{0:T(128)} %param.14) | copy-start | bytes 196
  10.8 26.7 %all-to-all-start = ((bf16[16,2,2,64,128]{4,3,2,1,0:T(8,128)(2,1)}), bf16[16,2,2,64,128]{4,3,2,1,0:T(8,128)(2,1)S(1)}, u32[]{:S(2)}, u32[]{:S(2)}) async-start(bf16[16,2,2,64,128]{4,3,2,1,0:T(8,128)(2,1)} %get-tuple-element.18), calls=%async_computation | async-start | bytes 2097152 | tf_op jit(solution)/shard_map/all_to_all | solution.py:381
  19.3 14.0 %collective-permute-start = (f32[16,640]{1,0:T(8,128)S(1)}, f32[16,640]{1,0:T(8,128)S(1)}, u32[]{:S(2)}, u32[]{:S(2)}) collective-permute-start(f32[16,640]{1,0:T(8,128)S(1)} %fusion), channel_id=1, source_target_pairs={{0,64},{16,80},{32,96},{48,112},{64,0},{80,16},{96,32},{112,48},{1... | collective-permute-start | bytes 122888 | tf_op jit(solution)/shard_map/ppermute | solution.py:370
  37.5 1.0 copy-start.3
  39.2 22.2 %all-to-all-start.1 = ((bf16[16,2,2,64,128]{4,3,2,1,0:T(8,128)(2,1)}), bf16[16,2,2,64,128]{4,3,2,1,0:T(8,128)(2,1)S(1)}, u32[]{:S(2)}, u32[]{:S(2)}) async-start(bf16[16,2,2,64,128]{4,3,2,1,0:T(8,128)(2,1)} %hold.7), calls=%async_computation.1 | async-start | bytes 2097152 | tf_op jit(solution)/shard_map/all_to_all | solution.py:382
  43.3 40.1 %all-gather.5.cloned.1.call-start = ((), (), s32[]{:S(2)}) async-start(), calls=%async_computation.6 | async-start | bytes 1638400 | tf_op jit(solution)/shard_map/all_gather | solution.py:389
  61.4 1.0 copy-start.1
  63.0 22.3 %all-to-all-start.2 = ((bf16[16,2,64,256]{3,2,1,0:T(8,128)(2,1)}), bf16[16,2,64,256]{3,2,1,0:T(8,128)(2,1)S(1)}, u32[]{:S(2)}, u32[]{:S(2)}) async-start(bf16[16,2,64,256]{3,2,1,0:T(8,128)(2,1)} %hold.8), calls=%async_computation.2 | async-start | bytes 2097152 | tf_op jit(solution)/shard_map/all_to_all | solution.py:385
  66.7 84.8 %all-gather.7.cloned.1.call-start = ((), (), s32[]{:S(2)}) async-start(), calls=%async_computation.7 | async-start | bytes 6553600 | tf_op jit(solution)/shard_map/all_gather | solution.py:391
  85.3 1.0 copy-start.5
  87.7 31.9 %copy-start.4 = (bf16[16,2,2,64,128]{4,3,2,1,0:T(8,128)(2,1)S(1)}, bf16[16,2,2,64,128]{4,3,2,1,0:T(8,128)(2,1)}, u32[]{:S(2)}) copy-start(bf16[16,2,2,64,128]{4,3,2,1,0:T(8,128)(2,1)} %hold.10.own_ref) | copy-start | bytes 3145732
  87.7 31.9 %copy-start.6 = (bf16[16,2,64,256]{3,2,1,0:T(8,128)(2,1)S(1)}, bf16[16,2,64,256]{3,2,1,0:T(8,128)(2,1)}, u32[]{:S(2)}) copy-start(bf16[16,2,64,256]{3,2,1,0:T(8,128)(2,1)} %copy-done.5) | copy-start | bytes 3145732
  87.7 27.4 %collective-permute-start.3 = (bf16[16,2,2,64,128]{4,3,2,1,0:T(8,128)(2,1)}, bf16[16,2,2,64,128]{4,3,2,1,0:T(8,128)(2,1)S(1)}, u32[]{:S(2)}, u32[]{:S(2)}) collective-permute-start(bf16[16,2,2,64,128]{4,3,2,1,0:T(8,128)(2,1)} %hold.10.own_ref), channel_id=1, source_target_pairs={{0,16},{16,32},{32,48},{48,64},{64,80},{80,96},{96,112},{1,17},{17... | collective-permute-start | bytes 3145736 | tf_op jit(solution)/shard_map/ppermute | solution.py:384
  91.3 28.3 %collective-permute-start.4 = (bf16[16,2,2,64,128]{4,3,2,1,0:T(8,128)(2,1)}, bf16[16,2,2,64,128]{4,3,2,1,0:T(8,128)(2,1)}, u32[]{:S(2)}, u32[]{:S(2)}) collective-permute-start(bf16[16,2,2,64,128]{4,3,2,1,0:T(8,128)(2,1)} %hold.10.own_ref), channel_id=1, source_target_pairs={{16,0},{32,16},{48,32},{64,48},{80,64},{96,80},{112,96},{17,1},{33... | collective-permute-start | bytes 3145736 | tf_op jit(solution)/shard_map/ppermute | solution.py:384
  93.3 46.8 %collective-permute-start.1 = (bf16[16,2,2,64,128]{4,3,2,1,0:T(8,128)(2,1)}, bf16[16,2,2,64,128]{4,3,2,1,0:T(8,128)(2,1)S(1)}, u32[]{:S(2)}, u32[]{:S(2)}) collective-permute-start(bf16[16,2,2,64,128]{4,3,2,1,0:T(8,128)(2,1)} %hold.9.own_ref), channel_id=1, source_target_pairs={{0,16},{16,32},{32,48},{48,64},{64,80},{80,96},{96,112},{1,17},{17... | collective-permute-start | bytes 3145736 | tf_op jit(solution)/shard_map/ppermute | solution.py:387
  97.9 42.7 %collective-permute-start.2 = (bf16[16,2,2,64,128]{4,3,2,1,0:T(8,128)(2,1)}, bf16[16,2,2,64,128]{4,3,2,1,0:T(8,128)(2,1)S(1)}, u32[]{:S(2)}, u32[]{:S(2)}) collective-permute-start(bf16[16,2,2,64,128]{4,3,2,1,0:T(8,128)(2,1)} %hold.9.own_ref), channel_id=1, source_target_pairs={{16,0},{32,16},{48,32},{64,48},{80,64},{96,80},{112,96},{17,1},{33... | collective-permute-start | bytes 3145736 | tf_op jit(solution)/shard_map/ppermute | solution.py:387
  115.1 13.4 %copy-start.21 = (bf16[16,2,2,64,128]{4,3,2,1,0:T(8,128)(2,1)}, bf16[16,2,2,64,128]{4,3,2,1,0:T(8,128)(2,1)S(1)}, u32[]{:S(2)}) copy-start(bf16[16,2,2,64,128]{4,3,2,1,0:T(8,128)(2,1)S(1)} %collective-permute-done.3.before_ref) | copy-start | bytes 3145732
  128.5 11.6 %collective-permute-start.5 = (bf16[16,1,64,128]{3,2,1,0:T(8,128)(2,1)S(1)}, bf16[16,1,64,128]{3,2,1,0:T(8,128)(2,1)S(1)}, u32[]{:S(2)}, u32[]{:S(2)}) collective-permute-start(bf16[16,1,64,128]{3,2,1,0:T(8,128)(2,1)S(1)} %get-tuple-element.21), channel_id=1, source_target_pairs={{48,112},{49,113},{50,114},{51,115},{52,116},{53,117},{54,118},{55... | collective-permute-start | bytes 786440 | tf_op jit(solution)/shard_map/ppermute | solution.py:410
  129.3 1.2 copy-start.22
  130.5 10.0 %copy-start.2 = (bf16[16,2,2,64,128]{4,3,2,1,0:T(8,128)(2,1)S(1)}, bf16[16,2,2,64,128]{4,3,2,1,0:T(8,128)(2,1)}, u32[]{:S(2)}) copy-start(bf16[16,2,2,64,128]{4,3,2,1,0:T(8,128)(2,1)} %hold.9.own_ref) | copy-start | bytes 3145732
  139.4 0.7 copy-start.16
  148.2 1.0 copy-start.9
  149.1 1.0 copy-start.11
  150.1 0.7 copy-start.14
  150.8 0.6 copy-start.18
  151.4 1.0 copy-start.15
  151.4 1.0 copy-start.17
  152.2 67.9 %collective-permute-start.11 = (bf16[4,2,2,256,640]{4,3,2,1,0:T(8,128)(2,1)}, bf16[4,2,2,256,640]{4,3,2,1,0:T(8,128)(2,1)}, u32[]{:S(2)}, u32[]{:S(2)}) collective-permute-start(bf16[4,2,2,256,640]{4,3,2,1,0:T(8,128)(2,1)} %hold.12.wo_ref), channel_id=1, source_target_pairs={{0,1},{1,0},{2,3},{3,2},{4,5},{5,4},{6,7},{7,6},{8,9},{9,8},{10,11... | collective-permute-start | bytes 15728648 | tf_op jit(solution)/shard_map/ppermute | solution.py:417
  153.3 23.9 %all-to-all-start.4 = ((bf16[16,2,64,128]{3,2,1,0:T(8,128)(2,1)}), bf16[16,2,64,128]{3,2,1,0:T(8,128)(2,1)S(1)}, u32[]{:S(2)}, u32[]{:S(2)}) async-start(bf16[16,2,64,128]{3,2,1,0:T(8,128)(2,1)} %pad_maximum_fusion.1), calls=%async_computation.4 | async-start | bytes 1048576 | tf_op jit(solution)/shard_map/all_to_all | solution.py:398
  158.5 7.2 %copy-start.19 = (f32[8,128]{1,0:T(8,128)S(1)}, f32[8,128]{1,0:T(8,128)}, u32[]{:S(2)}) copy-start(f32[8,128]{1,0:T(8,128)} %copy-done.18) | copy-start | bytes 12292
  160.5 24.0 %collective-permute-start.12 = (bf16[1,64,5120]{2,1,0:T(8,128)(2,1)}, bf16[1,64,5120]{2,1,0:T(8,128)(2,1)}, u32[]{:S(2)}, u32[]{:S(2)}) collective-permute-start(bf16[1,64,5120]{2,1,0:T(8,128)(2,1)} %last_frame.1), channel_id=1, source_target_pairs={{0,16},{16,32},{32,48},{48,64},{64,80},{80,96},{96,112},{1,17},{17... | collective-permute-start | bytes 1966088 | tf_op jit(solution)/shard_map/ppermute | solution.py:415
  164.7 11.1 %collective-permute-start.6 = (bf16[16,1,64,128]{3,2,1,0:T(8,128)(2,1)S(1)}, bf16[16,1,64,128]{3,2,1,0:T(8,128)(2,1)S(1)}, u32[]{:S(2)}, u32[]{:S(2)}) collective-permute-start(bf16[16,1,64,128]{3,2,1,0:T(8,128)(2,1)S(1)} %get-tuple-element.24), channel_id=1, source_target_pairs={{48,112},{49,113},{50,114},{51,115},{52,116},{53,117},{54,118},{55... | collective-permute-start | bytes 786440 | tf_op jit(solution)/shard_map/ppermute | solution.py:414
  165.6 1.2 copy-start.10
  166.9 1.2 copy-start.12
  175.8 0.6 copy-start.20
  177.3 7.2 %copy-start.7 = (bf16[16,2,64,128]{3,2,1,0:T(8,128)(2,1)}, bf16[16,2,64,128]{3,2,1,0:T(8,128)(2,1)S(1)}, u32[]{:S(2)}) copy-start(bf16[16,2,64,128]{3,2,1,0:T(8,128)(2,1)S(1)} %all-to-all-done.4.refs_0_) | copy-start | bytes 1572868
  177.3 19.6 %all-to-all-start.3 = ((bf16[16,2,64,128]{3,2,1,0:T(8,128)(2,1)}), bf16[16,2,64,128]{3,2,1,0:T(8,128)(2,1)S(1)}, u32[]{:S(2)}, u32[]{:S(2)}) async-start(bf16[16,2,64,128]{3,2,1,0:T(8,128)(2,1)} %pad_maximum_fusion), calls=%async_computation.3 | async-start | bytes 1048576 | tf_op jit(solution)/shard_map/all_to_all | solution.py:398
  185.2 34.9 %copy-start.8 = (bf16[16,2,64,128]{3,2,1,0:T(8,128)(2,1)S(1)}, bf16[16,2,64,128]{3,2,1,0:T(8,128)(2,1)}, u32[]{:S(2)}) copy-start(bf16[16,2,64,128]{3,2,1,0:T(8,128)(2,1)} %hold.13.mine_ref) | copy-start | bytes 1572868
  185.2 15.7 %collective-permute-start.13 = (bf16[16,2,64,128]{3,2,1,0:T(8,128)(2,1)}, bf16[16,2,64,128]{3,2,1,0:T(8,128)(2,1)S(1)}, u32[]{:S(2)}, u32[]{:S(2)}) collective-permute-start(bf16[16,2,64,128]{3,2,1,0:T(8,128)(2,1)} %hold.13.mine_ref), channel_id=1, source_target_pairs={{0,16},{16,32},{32,48},{48,0},{64,80},{80,96},{96,112},{112,64},{1... | collective-permute-start | bytes 1572872 | tf_op jit(solution)/shard_map/ppermute | solution.py:401
  185.5 16.3 %collective-permute-start.14 = (bf16[16,2,64,128]{3,2,1,0:T(8,128)(2,1)}, bf16[16,2,64,128]{3,2,1,0:T(8,128)(2,1)S(1)}, u32[]{:S(2)}, u32[]{:S(2)}) collective-permute-start(bf16[16,2,64,128]{3,2,1,0:T(8,128)(2,1)} %hold.13.mine_ref), channel_id=1, source_target_pairs={{16,0},{32,16},{48,32},{0,48},{80,64},{96,80},{112,96},{64,112},{1... | collective-permute-start | bytes 1572872 | tf_op jit(solution)/shard_map/ppermute | solution.py:402
  196.9 15.9 %collective-permute-start.8 = (bf16[16,2,64,128]{3,2,1,0:T(8,128)(2,1)S(1)}, bf16[16,2,64,128]{3,2,1,0:T(8,128)(2,1)S(1)}, u32[]{:S(2)}, u32[]{:S(2)}) collective-permute-start(bf16[16,2,64,128]{3,2,1,0:T(8,128)(2,1)S(1)} %all-to-all-done.3.mine_ref), channel_id=1, source_target_pairs={{16,0},{32,16},{48,32},{0,48},{80,64},{96,80},{112,96},{64,112},{1... | collective-permute-start | bytes 1572872 | tf_op jit(solution)/shard_map/ppermute | solution.py:402
  199.4 16.6 %collective-permute-start.7 = (bf16[16,2,64,128]{3,2,1,0:T(8,128)(2,1)S(1)}, bf16[16,2,64,128]{3,2,1,0:T(8,128)(2,1)S(1)}, u32[]{:S(2)}, u32[]{:S(2)}) collective-permute-start(bf16[16,2,64,128]{3,2,1,0:T(8,128)(2,1)S(1)} %all-to-all-done.3.mine_ref), channel_id=1, source_target_pairs={{0,16},{16,32},{32,48},{48,0},{64,80},{80,96},{96,112},{112,64},{1... | collective-permute-start | bytes 1572872 | tf_op jit(solution)/shard_map/ppermute | solution.py:401
  201.6 18.5 %collective-permute-start.15 = (bf16[8,2,64,128]{3,2,1,0:T(8,128)(2,1)}, bf16[8,2,64,128]{3,2,1,0:T(8,128)(2,1)S(1)}, u32[]{:S(2)}, u32[]{:S(2)}) collective-permute-start(bf16[8,2,64,128]{3,2,1,0:T(8,128)(2,1)} %slice.23), channel_id=1, source_target_pairs={{0,16},{16,32},{32,48},{48,0},{64,80},{80,96},{96,112},{112,64},{1... | collective-permute-start | bytes 786440 | tf_op jit(solution)/shard_map/ppermute | solution.py:403
  202.6 17.5 %collective-permute-start.16 = (bf16[8,2,64,128]{3,2,1,0:T(8,128)(2,1)}, bf16[8,2,64,128]{3,2,1,0:T(8,128)(2,1)}, u32[]{:S(2)}, u32[]{:S(2)}) collective-permute-start(bf16[8,2,64,128]{3,2,1,0:T(8,128)(2,1)} %slice.24), channel_id=1, source_target_pairs={{16,0},{32,16},{48,32},{0,48},{80,64},{96,80},{112,96},{64,112},{1... | collective-permute-start | bytes 786440 | tf_op jit(solution)/shard_map/ppermute | solution.py:404
  212.8 13.9 %collective-permute-start.10 = (bf16[8,2,64,128]{3,2,1,0:T(8,128)(2,1)S(1)}, bf16[8,2,64,128]{3,2,1,0:T(8,128)(2,1)S(1)}, u32[]{:S(2)}, u32[]{:S(2)}) collective-permute-start(bf16[8,2,64,128]{3,2,1,0:T(8,128)(2,1)S(1)} %slice.22), channel_id=1, source_target_pairs={{16,0},{32,16},{48,32},{0,48},{80,64},{96,80},{112,96},{64,112},{1... | collective-permute-start | bytes 786440 | tf_op jit(solution)/shard_map/ppermute | solution.py:404
  216.0 10.6 %collective-permute-start.9 = (bf16[8,2,64,128]{3,2,1,0:T(8,128)(2,1)S(1)}, bf16[8,2,64,128]{3,2,1,0:T(8,128)(2,1)S(1)}, u32[]{:S(2)}, u32[]{:S(2)}) collective-permute-start(bf16[8,2,64,128]{3,2,1,0:T(8,128)(2,1)S(1)} %slice.21), channel_id=1, source_target_pairs={{0,16},{16,32},{32,48},{48,0},{64,80},{80,96},{96,112},{112,64},{1... | collective-permute-start | bytes 786440 | tf_op jit(solution)/shard_map/ppermute | solution.py:403
  216.2 10.5 %copy-start.13 = (f32[2,8,640]{2,1,0:T(8,128)S(1)}, f32[2,8,640]{2,1,0:T(8,128)}, u32[]{:S(2)}) copy-start(f32[2,8,640]{2,1,0:T(8,128)} %dynamic-slice_select_fusion.refs_2_.rest_1_) | copy-start | bytes 122884
Sparse Core Ops, SparseCore 0:
  45.8 37.5 all-gather.4
  87.2 56.4 all-gather.6

commit v7 on v6

--- a/solution.py
+++ b/solution.py
@@ -13,7 +13,9 @@
 NEG_FILL = -1e30
 SCALE_LOG2 = (HD ** -0.5) * 1.4426950408889634
 BLOCK_Q = 512
-VMEM = 48 * 1024 * 1024
+VMEM = 28 * 1024 * 1024
+SMALL = pltpu.CompilerParams(vmem_limit_bytes=1024 * 1024)
+MEDIUM = pltpu.CompilerParams(vmem_limit_bytes=12 * 1024 * 1024)
 QUEUE = 8
 RING = 4
 SPATIAL = 16
@@ -57,25 +59,9 @@
             kv_shape,
             jax.ShapeDtypeStruct((SPATIAL, frames, tok, group), queries.dtype),
         ],
+        compiler_params=MEDIUM,
         name="pack",
     )(queries, keys, values)
-
-
-def last_frame(hidden, *earlier):
-    frames, tok, width = hidden.shape
-
-    def kernel(hidden_ref, *rest):
-        rest[-1][...] = hidden_ref[...]
-
-    return pl.pallas_call(
-        kernel,
-        grid=(1,),
-        in_specs=[pl.BlockSpec((1, tok, width), lambda i: (frames - 1, 0, 0))]
-        + [corner(e) for e in earlier],
-        out_specs=pl.BlockSpec((1, tok, width), lambda i: (0, 0, 0)),
-        out_shape=jax.ShapeDtypeStruct((1, tok, width), hidden.dtype),
-        name="last_frame",
-    )(hidden, *earlier)
 
 
 def hold(array, *earlier):
@@ -89,6 +75,7 @@
         out_specs=ANY,
         out_shape=jax.ShapeDtypeStruct(array.shape, array.dtype),
         input_output_aliases={0: 0},
+        compiler_params=SMALL,
         name="hold",
     )(array, *earlier)
 
@@ -326,6 +313,7 @@
             out_specs=pl.BlockSpec((1, tok, width), lambda i, pos: (i, 0, 0)),
         ),
         out_shape=jax.ShapeDtypeStruct((frames, tok, width), hidden.dtype),
+        compiler_params=MEDIUM,
         name="add_branch",
     )(position, branch, hidden, shifted, entering)
 
@@ -412,7 +400,7 @@
     first = returned(even0, odd0, odd0_crossing)
     odd1, token = attend(1, *head1, token, odd0_crossing)
     odd1_crossing = lax.ppermute(odd1, "queue", cross)
-    shifted = lax.ppermute(last_frame(hidden, kv1_before, kv1_after), "queue", up)
+    shifted = lax.ppermute(hold(hidden[frames - 1 :], kv1_before), "queue", up)
     weight_own = hold(weight, token)
     weight_pair = lax.ppermute(weight_own, "spatial", swap_core)
     even1, token = attend(0, *head1, token)

time: 264 us -> 267 us (1.011)
  Pallas kernels: 60.3 us -> 48 us
  local copies, waits for them, and re-layouts: 12.9 us -> 24.6 us
  waiting for transfers between devices: 95.1 us -> 101 us
    unnamed x49 -> x53, local copies, waits for them, and re-layouts: 11.4 us -> 21 us
    all_to_all x1, waiting for transfers between devices: 1.88 us -> 10.3 us  [body(): query = to_heads(hold(query, kv1))]
    all_gather x1, waiting for transfers between devices: 16.8 us -> 8.93 us  [body(): lax.all_gather(out_weight, ('queue', 'spatial'), axis_index_groups=along_...]
    pallas_call x7 -> x8, Pallas kernels: 4.85 us -> 0.69 us  [hold(): pl.pallas_call(kernel, grid=(1,), in_specs=[ANY] + [corner(e) for e in ea...]
    ppermute x1, waiting for transfers between devices: 0.44 us -> 4.12 us  [body(): lax.ppermute(kv1, 'queue', down)]
    pallas_call x1, Pallas kernels: 4.26 us -> 0.75 us  [pack(): pl.pallas_call(kernel, grid=(PACK,), in_specs=[spec] * 3, out_specs=[kv_s...]
  transfers between devices with their start and end apart: 24 -> 24, of which waited for: 12 -> 12; matrix products, arithmetic and copies ran while one was open for 2% -> 2% of each run, Pallas kernels for 17% -> 14%
where the time goes in v7:
time: 267 us; the launch traced here: 266 us
  waiting for transfers between devices  101 us (38%)
  starting transfers between devices  57.6 us (22%)
  Pallas kernels  48 us (18%)
  local copies, waits for them, and re-layouts  24.6 us (9%)
  blocking collectives  18.1 us (7%)
  between operations  13.8 us (5%)
  other arithmetic  2.87 us (1%)
    pallas_call x4, Pallas kernels, attend(): pl.pallas_call(kernel, grid_spec=pltpu.PrefetchScalarGridSpec(num_scalar_...  31.4 us
    unnamed x53, local copies, waits for them, and re-layouts  21 us
    all_to_all x1, blocking collectives, body(): lax.all_to_all(branch, 'queue', split_axis=0, concat_axis=0, axis_index_g...  18.1 us
    all_to_all x1, waiting for transfers between devices, body(): kv1 = to_heads(hold(kv1, kv0, gates))  17.2 us
    ppermute x1, waiting for transfers between devices, body(): lax.ppermute(kv0, 'queue', up)  16.2 us
    ppermute x1, waiting for transfers between devices, body(): other_gates = lax.ppermute(gates, 'queue', swap_low)  13.3 us
    pallas_call x2, Pallas kernels, project(): pl.pallas_call(kernel, grid_spec=pltpu.PrefetchScalarGridSpec(num_scalar_...  12.7 us
    all_to_all x2, starting transfers between devices, returned(): return to_heads(jnp.concatenate((even, odd), axis=1))  12.1 us
  transfers between devices with their start and end apart: 24, of which 12 were waited for; matrix products, arithmetic and copies ran while one was open for 2% of the time, Pallas kernels for 14%

profile of v7, /device:TPU:0, one launch (start us, length us, event | category | flops | bytes accessed | tf_op | source)
XLA Modules:
  0.0 266.2 jit_solution(2745246924226632218)
XLA Ops:
  6.5 1.3 copy-done.9
  7.8 1.2 copy-done.10
  9.0 1.2 copy-done.11
  10.2 0.8 pack.1
  11.0 1.0 copy-done.12
  12.0 8.3 %all-to-all-start = ((bf16[16,2,2,64,128]{4,3,2,1,0:T(8,128)(2,1)}), bf16[16,2,2,64,128]{4,3,2,1,0:T(8,128)(2,1)S(1)}, u32[]{:S(2)}, u32[]{:S(2)}) async-start(bf16[16,2,2,64,128]{4,3,2,1,0:T(8,128)(2,1)} %copy-done.12), calls=%async_computation | async-start | bytes 2097152 | tf_op jit(solution)/shard_map/all_to_all | solution.py:369
  20.5 0.8 collective-permute-start
  21.3 13.3 %collective-permute-done = f32[16,640]{1,0:T(8,128)S(1)} collective-permute-done((f32[16,640]{1,0:T(8,128)S(1)}, f32[16,640]{1,0:T(8,128)S(1)}, u32[]{:S(2)}, u32[]{:S(2)}) %collective-permute-start) | collective-permute-done | bytes 40992 | tf_op jit(solution)/shard_map/ppermute | solution.py:358
  34.7 4.0 %all-to-all-done.refs_1_.refs_0_ = bf16[16,2,2,64,128]{4,3,2,1,0:T(8,128)(2,1)S(1)} async-done(((bf16[16,2,2,64,128]{4,3,2,1,0:T(8,128)(2,1)}), bf16[16,2,2,64,128]{4,3,2,1,0:T(8,128)(2,1)S(1)}, u32[]{:S(2)}, u32[]{:S(2)}) %all-to-all-start) | async-done | bytes 1048608 | tf_op jit(solution)/shard_map/all_to_all | solution.py:369
  38.7 1.0 copy-done.7
  39.6 3.7 %all-to-all-start.1 = ((bf16[16,2,2,64,128]{4,3,2,1,0:T(8,128)(2,1)}), bf16[16,2,2,64,128]{4,3,2,1,0:T(8,128)(2,1)S(1)}, u32[]{:S(2)}, u32[]{:S(2)}) async-start(bf16[16,2,2,64,128]{4,3,2,1,0:T(8,128)(2,1)} %copy-done.7), calls=%async_computation.1 | async-start | bytes 2097152 | tf_op jit(solution)/shard_map/all_to_all | solution.py:370
  43.4 0.7 all-gather.5.cloned.1.call-update
  44.0 17.2 %all-to-all-done.1.refs_1_.refs_0_ = bf16[16,2,2,64,128]{4,3,2,1,0:T(8,128)(2,1)S(1)} async-done(((bf16[16,2,2,64,128]{4,3,2,1,0:T(8,128)(2,1)}), bf16[16,2,2,64,128]{4,3,2,1,0:T(8,128)(2,1)S(1)}, u32[]{:S(2)}, u32[]{:S(2)}) %all-to-all-start.1) | async-done | bytes 1048608 | tf_op jit(solution)/shard_map/all_to_all | solution.py:370
  61.3 1.0 copy-done.6
  62.3 3.7 %all-to-all-start.2 = ((bf16[16,2,64,256]{3,2,1,0:T(8,128)(2,1)}), bf16[16,2,64,256]{3,2,1,0:T(8,128)(2,1)S(1)}, u32[]{:S(2)}, u32[]{:S(2)}) async-start(bf16[16,2,64,256]{3,2,1,0:T(8,128)(2,1)} %copy-done.6), calls=%async_computation.2 | async-start | bytes 2097152 | tf_op jit(solution)/shard_map/all_to_all | solution.py:373
  66.0 8.9 %all-gather.5.cloned.1.call-done = bf16[1024,640]{1,0:T(8,128)(2,1)} async-done(((bf16[256,640]{1,0:T(8,128)(2,1)}), bf16[1024,640]{1,0:T(8,128)(2,1)}) %all-gather.5.cloned.1.call-update) | async-done | bytes 1310736 | tf_op jit(solution)/shard_map/all_gather | solution.py:377
  74.9 10.3 %all-to-all-done.2.refs_1_.q_ref = bf16[16,2,64,256]{3,2,1,0:T(8,128)(2,1)S(1)} async-done(((bf16[16,2,64,256]{3,2,1,0:T(8,128)(2,1)}), bf16[16,2,64,256]{3,2,1,0:T(8,128)(2,1)S(1)}, u32[]{:S(2)}, u32[]{:S(2)}) %all-to-all-start.2) | async-done | bytes 1048608 | tf_op jit(solution)/shard_map/all_to_all | solution.py:373
  85.2 1.3 copy-done.4
  86.5 1.1 copy-done.5
  87.6 3.4 %collective-permute-start.3 = (bf16[16,2,2,64,128]{4,3,2,1,0:T(8,128)(2,1)S(1)}, bf16[16,2,2,64,128]{4,3,2,1,0:T(8,128)(2,1)S(1)}, u32[]{:S(2)}, u32[]{:S(2)}) collective-permute-start(bf16[16,2,2,64,128]{4,3,2,1,0:T(8,128)(2,1)S(1)} %hold.11.own_ref), channel_id=1, source_target_pairs={{0,16},{16,32},{32,48},{48,64},{64,80},{80,96},{96,112},{1,17},{17... | collective-permute-start | bytes 3145736 | tf_op jit(solution)/shard_map/ppermute | solution.py:372
  91.1 1.3 collective-permute-start.4
  92.4 4.6 %collective-permute-start.1 = (bf16[16,2,2,64,128]{4,3,2,1,0:T(8,128)(2,1)S(1)}, bf16[16,2,2,64,128]{4,3,2,1,0:T(8,128)(2,1)S(1)}, u32[]{:S(2)}, u32[]{:S(2)}) collective-permute-start(bf16[16,2,2,64,128]{4,3,2,1,0:T(8,128)(2,1)S(1)} %hold.10.own_ref), channel_id=1, source_target_pairs={{0,16},{16,32},{32,48},{48,64},{64,80},{80,96},{96,112},{1,17},{17... | collective-permute-start | bytes 3145736 | tf_op jit(solution)/shard_map/ppermute | solution.py:375
  97.0 1.3 collective-permute-start.2
  98.3 16.2 %collective-permute-done.3.before_ref = bf16[16,2,2,64,128]{4,3,2,1,0:T(8,128)(2,1)S(1)} collective-permute-done((bf16[16,2,2,64,128]{4,3,2,1,0:T(8,128)(2,1)S(1)}, bf16[16,2,2,64,128]{4,3,2,1,0:T(8,128)(2,1)S(1)}, u32[]{:S(2)}, u32[]{:S(2)}) %collective-permute-start.3) | collective-permute-done | bytes 1048608 | tf_op jit(solution)/shard_map/ppermute | solution.py:372
  114.5 4.5 %collective-permute-done.4.after_ref = bf16[16,2,2,64,128]{4,3,2,1,0:T(8,128)(2,1)S(1)} collective-permute-done((bf16[16,2,2,64,128]{4,3,2,1,0:T(8,128)(2,1)S(1)}, bf16[16,2,2,64,128]{4,3,2,1,0:T(8,128)(2,1)S(1)}, u32[]{:S(2)}, u32[]{:S(2)}) %collective-permute-start.4) | collective-permute-done | bytes 1048608 | tf_op jit(solution)/shard_map/ppermute | solution.py:372
  119.0 7.6 %attend.4 = (bf16[16,1,64,128]{3,2,1,0:T(8,128)(2,1)S(1)}, f32[8,128]{1,0:T(8,128)S(1)}) custom-call(s32[1]{0:T(128)} %bitcast.pos_ref, bf16[16,2,64,256]{3,2,1,0:T(8,128)(2,1)S(1)} %all-to-all-done.2.refs_1_.q_ref, bf16[16,2,2,64,128]{4,3,2,1,0:T(8,128)(2,1)S(1)} %hold.11.own_ref, bf16[16,2,2,64,128]{4,3,2,1,0:T(8,128)(2,1)S(1)} %collective-permute-done.3.before_ref, ...), custom_call_target="tpu_custom_call" | custom-call | flops 5368709120 | bytes 4194304 | tf_op jit(solution)/shard_map/attend/pallas_call | solution.py:161
  126.7 0.9 collective-permute-start.5
  127.6 7.8 %attend.5 = (bf16[16,1,64,128]{3,2,1,0:T(8,128)(2,1)S(1)}, f32[8,128]{1,0:T(8,128)S(1)}) custom-call(s32[1]{0:T(128)} %bitcast.pos_ref, bf16[16,2,64,256]{3,2,1,0:T(8,128)(2,1)S(1)} %all-to-all-done.2.refs_1_.q_ref, bf16[16,2,2,64,128]{4,3,2,1,0:T(8,128)(2,1)S(1)} %hold.11.own_ref, bf16[16,2,2,64,128]{4,3,2,1,0:T(8,128)(2,1)S(1)} %collective-permute-done.3.before_ref, ...), custom_call_target="tpu_custom_call" | custom-call | flops 5368709120 | bytes 4194304 | tf_op jit(solution)/shard_map/attend/pallas_call | solution.py:161
  135.3 0.7 copy-done.21
  136.0 4.1 %collective-permute-done.2.after_ref = bf16[16,2,2,64,128]{4,3,2,1,0:T(8,128)(2,1)S(1)} collective-permute-done((bf16[16,2,2,64,128]{4,3,2,1,0:T(8,128)(2,1)S(1)}, bf16[16,2,2,64,128]{4,3,2,1,0:T(8,128)(2,1)S(1)}, u32[]{:S(2)}, u32[]{:S(2)}) %collective-permute-start.2) | collective-permute-done | bytes 1048608 | tf_op jit(solution)/shard_map/ppermute | solution.py:375
  140.2 8.3 %attend.6 = (bf16[16,1,64,128]{3,2,1,0:T(8,128)(2,1)}, f32[8,128]{1,0:T(8,128)S(1)}) custom-call(s32[1]{0:T(128)} %bitcast.pos_ref, bf16[16,2,64,256]{3,2,1,0:T(8,128)(2,1)S(1)} %all-to-all-done.2.refs_1_.q_ref, bf16[16,2,2,64,128]{4,3,2,1,0:T(8,128)(2,1)S(1)} %hold.10.own_ref, bf16[16,2,2,64,128]{4,3,2,1,0:T(8,128)(2,1)S(1)} %collective-permute-done.1.before_ref.refs_1_, ...), custom_call_target="tpu_custom_call" | custom-call | flops 5368709120 | bytes 4194304 | tf_op jit(solution)/shard_map/attend/pallas_call | solution.py:161
  148.4 1.0 copy-done.13
  149.4 0.7 copy-done.19
  150.1 1.0 copy-done.23
  151.1 2.5 copy-done.1
  153.6 2.4 copy-done.2
  156.0 2.0 slice.21.refs_0_
  158.1 0.8 pad_maximum_fusion.1
  159.0 4.9 %all-to-all-start.4 = ((bf16[16,2,64,128]{3,2,1,0:T(8,128)(2,1)}), bf16[16,2,64,128]{3,2,1,0:T(8,128)(2,1)S(1)}, u32[]{:S(2)}, u32[]{:S(2)}) async-start(bf16[16,2,64,128]{3,2,1,0:T(8,128)(2,1)} %pad_maximum_fusion.1), calls=%async_computation.4 | async-start | bytes 1048576 | tf_op jit(solution)/shard_map/all_to_all | solution.py:386
  163.8 1.2 copy-done.14
  165.1 4.2 %collective-permute-start.12 = (bf16[1,64,5120]{2,1,0:T(8,128)(2,1)}, bf16[1,64,5120]{2,1,0:T(8,128)(2,1)}, u32[]{:S(2)}, u32[]{:S(2)}) collective-permute-start(bf16[1,64,5120]{2,1,0:T(8,128)(2,1)} %hold.14), channel_id=1, source_target_pairs={{0,16},{16,32},{32,48},{48,64},{64,80},{80,96},{96,112},{1,17},{17... | collective-permute-start | bytes 1966088 | tf_op jit(solution)/shard_map/ppermute | solution.py:403
  169.3 0.9 collective-permute-start.6
  170.2 7.8 %attend.7 = (bf16[16,1,64,128]{3,2,1,0:T(8,128)(2,1)S(1)}, f32[8,128]{1,0:T(8,128)S(1)}) custom-call(s32[1]{0:T(128)} %bitcast.pos_ref, bf16[16,2,64,256]{3,2,1,0:T(8,128)(2,1)S(1)} %all-to-all-done.2.refs_1_.q_ref, bf16[16,2,2,64,128]{4,3,2,1,0:T(8,128)(2,1)S(1)} %hold.10.own_ref, bf16[16,2,2,64,128]{4,3,2,1,0:T(8,128)(2,1)S(1)} %copy-done.15, ...), custom_call_target="tpu_custom_call" | custom-call | flops 5368709120 | bytes 4194304 | tf_op jit(solution)/shard_map/attend/pallas_call | solution.py:161
  178.0 1.0 broadcast_select_fusion.1
  179.0 0.8 pad_maximum_fusion
  179.8 7.2 %all-to-all-start.3 = ((bf16[16,2,64,128]{3,2,1,0:T(8,128)(2,1)}), bf16[16,2,64,128]{3,2,1,0:T(8,128)(2,1)S(1)}, u32[]{:S(2)}, u32[]{:S(2)}) async-start(bf16[16,2,64,128]{3,2,1,0:T(8,128)(2,1)} %pad_maximum_fusion), calls=%async_computation.3 | async-start | bytes 1048576 | tf_op jit(solution)/shard_map/all_to_all | solution.py:386
  187.1 0.7 hold.15.mine_ref
  187.8 0.3 collective-permute-start.13
  188.1 2.9 %collective-permute-start.14 = (bf16[16,2,64,128]{3,2,1,0:T(8,128)(2,1)S(1)}, bf16[16,2,64,128]{3,2,1,0:T(8,128)(2,1)S(1)}, u32[]{:S(2)}, u32[]{:S(2)}) collective-permute-start(bf16[16,2,64,128]{3,2,1,0:T(8,128)(2,1)S(1)} %hold.15.mine_ref), channel_id=1, source_target_pairs={{16,0},{32,16},{48,32},{0,48},{80,64},{96,80},{112,96},{64,112},{1... | collective-permute-start | bytes 1572872 | tf_op jit(solution)/shard_map/ppermute | solution.py:390
  191.0 8.4 %all-to-all-done.3.mine_ref = bf16[16,2,64,128]{3,2,1,0:T(8,128)(2,1)S(1)} async-done(((bf16[16,2,64,128]{3,2,1,0:T(8,128)(2,1)}), bf16[16,2,64,128]{3,2,1,0:T(8,128)(2,1)S(1)}, u32[]{:S(2)}, u32[]{:S(2)}) %all-to-all-start.3) | async-done | bytes 524320 | tf_op jit(solution)/shard_map/all_to_all | solution.py:386
  199.4 2.8 %collective-permute-start.8 = (bf16[16,2,64,128]{3,2,1,0:T(8,128)(2,1)S(1)}, bf16[16,2,64,128]{3,2,1,0:T(8,128)(2,1)S(1)}, u32[]{:S(2)}, u32[]{:S(2)}) collective-permute-start(bf16[16,2,64,128]{3,2,1,0:T(8,128)(2,1)S(1)} %all-to-all-done.3.mine_ref), channel_id=1, source_target_pairs={{16,0},{32,16},{48,32},{0,48},{80,64},{96,80},{112,96},{64,112},{1... | collective-permute-start | bytes 1572872 | tf_op jit(solution)/shard_map/ppermute | solution.py:390
  202.2 1.0 collective-permute-done.13.left_ref
  203.2 0.7 slice.27
  204.0 0.3 collective-permute-start.15
  204.3 0.7 slice.28
  205.0 2.9 %collective-permute-start.16 = (bf16[8,2,64,128]{3,2,1,0:T(8,128)(2,1)}, bf16[8,2,64,128]{3,2,1,0:T(8,128)(2,1)}, u32[]{:S(2)}, u32[]{:S(2)}) collective-permute-start(bf16[8,2,64,128]{3,2,1,0:T(8,128)(2,1)} %slice.28), channel_id=1, source_target_pairs={{16,0},{32,16},{48,32},{0,48},{80,64},{96,80},{112,96},{64,112},{1... | collective-permute-start | bytes 786440 | tf_op jit(solution)/shard_map/ppermute | solution.py:392
  207.9 7.3 %collective-permute-done.8.right_ref = bf16[16,2,64,128]{3,2,1,0:T(8,128)(2,1)S(1)} collective-permute-done((bf16[16,2,64,128]{3,2,1,0:T(8,128)(2,1)S(1)}, bf16[16,2,64,128]{3,2,1,0:T(8,128)(2,1)S(1)}, u32[]{:S(2)}, u32[]{:S(2)}) %collective-permute-start.8) | collective-permute-done | bytes 524320 | tf_op jit(solution)/shard_map/ppermute | solution.py:390
  215.3 3.1 %collective-permute-start.10 = (bf16[8,2,64,128]{3,2,1,0:T(8,128)(2,1)S(1)}, bf16[8,2,64,128]{3,2,1,0:T(8,128)(2,1)S(1)}, u32[]{:S(2)}, u32[]{:S(2)}) collective-permute-start(bf16[8,2,64,128]{3,2,1,0:T(8,128)(2,1)S(1)} %slice.26), channel_id=1, source_target_pairs={{16,0},{32,16},{48,32},{0,48},{80,64},{96,80},{112,96},{64,112},{1... | collective-permute-start | bytes 786440 | tf_op jit(solution)/shard_map/ppermute | solution.py:392
  218.6 5.0 %collective-permute-done.15.low_ref = bf16[8,2,64,128]{3,2,1,0:T(8,128)(2,1)} collective-permute-done((bf16[8,2,64,128]{3,2,1,0:T(8,128)(2,1)}, bf16[8,2,64,128]{3,2,1,0:T(8,128)(2,1)}, u32[]{:S(2)}, u32[]{:S(2)}) %collective-permute-start.15) | collective-permute-done | bytes 262176 | tf_op jit(solution)/shard_map/ppermute | solution.py:391
  223.6 2.5 copy-done.3
  226.0 6.3 %project_first.1.rest_0_ = f32[2,512,640]{2,1,0:T(8,128)S(1)} custom-call(s32[2]{0:T(128)S(1)} %pad_add_fusion.place_ref, bf16[16,2,64,128]{3,2,1,0:T(8,128)(2,1)S(1)} %hold.15.mine_ref, bf16[16,2,64,128]{3,2,1,0:T(8,128)(2,1)S(1)} %collective-permute-done.13.left_ref, bf16[16,2,64,128]{3,2,1,0:T(8,128)(2,1)S(1)} %collective-permute-done.14.right_ref, ...), custom_call_target="tpu_custom_call" | custom-call | flops 2684354560 | bytes 8388608 | tf_op jit(solution)/shard_map/project_first/pallas_call | solution.py:255
  232.4 6.4 %project_last.1 = bf16[8,2,64,640]{3,2,1,0:T(8,128)(2,1)S(1)} custom-call(s32[2]{0:T(128)S(1)} %pad_add_fusion.place_ref, bf16[16,2,64,128]{3,2,1,0:T(8,128)(2,1)S(1)} %all-to-all-done.3.mine_ref, bf16[16,2,64,128]{3,2,1,0:T(8,128)(2,1)S(1)} %collective-permute-done.7.left_ref, bf16[16,2,64,128]{3,2,1,0:T(8,128)(2,1)S(1)} %collective-permute-done.8.right_ref, ...), custom_call_target="tpu_custom_call" | custom-call | flops 2684354560 | bytes 8388608 | tf_op jit(solution)/shard_map/project_last/pallas_call | solution.py:255
  238.8 18.1 %all_to_all.30 = bf16[8,2,64,640]{3,2,1,0:T(8,128)(2,1)S(1)} all-to-all(bf16[8,2,64,640]{3,2,1,0:T(8,128)(2,1)S(1)} %project_last.1), channel_id=1, replica_groups={{0,16,32,48},{64,80,96,112},{1,17,33,49},{65,81,97,113},{2,18,34,50},{6..., dimensions={0} | all-to-all | bytes 2621440 | tf_op jit(solution)/shard_map/all_to_all | solution.py:412
  256.9 2.5 add_branch.1
  (71 shorter events, 0.7 us)
Async XLA Ops:
  6.5 13.7 %copy-start = (f32[50,640]{1,0:T(8,128)S(1)}, f32[50,640]{1,0:T(8,128)}, u32[]{:S(2)}) copy-start(f32[50,640]{1,0:T(8,128)} %param.13) | copy-start | bytes 384004
  6.5 1.3 copy-start.9
  7.8 1.2 copy-start.10
  9.0 1.2 copy-start.11
  11.0 1.0 copy-start.12
  12.0 8.3 %copy-start.25 = (s32[16]{0:T(128)S(1)}, s32[16]{0:T(128)}, u32[]{:S(2)}) copy-start(s32[16]{0:T(128)} %param.14) | copy-start | bytes 196
  12.0 26.7 %all-to-all-start = ((bf16[16,2,2,64,128]{4,3,2,1,0:T(8,128)(2,1)}), bf16[16,2,2,64,128]{4,3,2,1,0:T(8,128)(2,1)S(1)}, u32[]{:S(2)}, u32[]{:S(2)}) async-start(bf16[16,2,2,64,128]{4,3,2,1,0:T(8,128)(2,1)} %copy-done.12), calls=%async_computation | async-start | bytes 2097152 | tf_op jit(solution)/shard_map/all_to_all | solution.py:369
  20.5 14.0 %collective-permute-start = (f32[16,640]{1,0:T(8,128)S(1)}, f32[16,640]{1,0:T(8,128)S(1)}, u32[]{:S(2)}, u32[]{:S(2)}) collective-permute-start(f32[16,640]{1,0:T(8,128)S(1)} %fusion), channel_id=1, source_target_pairs={{0,64},{16,80},{32,96},{48,112},{64,0},{80,16},{96,32},{112,48},{1... | collective-permute-start | bytes 122888 | tf_op jit(solution)/shard_map/ppermute | solution.py:358
  38.7 1.0 copy-start.7
  39.6 21.7 %all-to-all-start.1 = ((bf16[16,2,2,64,128]{4,3,2,1,0:T(8,128)(2,1)}), bf16[16,2,2,64,128]{4,3,2,1,0:T(8,128)(2,1)S(1)}, u32[]{:S(2)}, u32[]{:S(2)}) async-start(bf16[16,2,2,64,128]{4,3,2,1,0:T(8,128)(2,1)} %copy-done.7), calls=%async_computation.1 | async-start | bytes 2097152 | tf_op jit(solution)/shard_map/all_to_all | solution.py:370
  43.3 31.6 %all-gather.5.cloned.1.call-start = ((), (), s32[]{:S(2)}) async-start(), calls=%async_computation.6 | async-start | bytes 1638400 | tf_op jit(solution)/shard_map/all_gather | solution.py:377
  61.3 1.0 copy-start.6
  62.3 22.9 %all-to-all-start.2 = ((bf16[16,2,64,256]{3,2,1,0:T(8,128)(2,1)}), bf16[16,2,64,256]{3,2,1,0:T(8,128)(2,1)S(1)}, u32[]{:S(2)}, u32[]{:S(2)}) async-start(bf16[16,2,64,256]{3,2,1,0:T(8,128)(2,1)} %copy-done.6), calls=%async_computation.2 | async-start | bytes 2097152 | tf_op jit(solution)/shard_map/all_to_all | solution.py:373
  65.9 85.2 %all-gather.7.cloned.1.call-start = ((), (), s32[]{:S(2)}) async-start(), calls=%async_computation.7 | async-start | bytes 6553600 | tf_op jit(solution)/shard_map/all_gather | solution.py:379
  85.2 1.3 copy-start.4
  86.5 1.1 copy-start.5
  87.6 26.9 %collective-permute-start.3 = (bf16[16,2,2,64,128]{4,3,2,1,0:T(8,128)(2,1)S(1)}, bf16[16,2,2,64,128]{4,3,2,1,0:T(8,128)(2,1)S(1)}, u32[]{:S(2)}, u32[]{:S(2)}) collective-permute-start(bf16[16,2,2,64,128]{4,3,2,1,0:T(8,128)(2,1)S(1)} %hold.11.own_ref), channel_id=1, source_target_pairs={{0,16},{16,32},{32,48},{48,64},{64,80},{80,96},{96,112},{1,17},{17... | collective-permute-start | bytes 3145736 | tf_op jit(solution)/shard_map/ppermute | solution.py:372
  91.1 28.0 %collective-permute-start.4 = (bf16[16,2,2,64,128]{4,3,2,1,0:T(8,128)(2,1)S(1)}, bf16[16,2,2,64,128]{4,3,2,1,0:T(8,128)(2,1)S(1)}, u32[]{:S(2)}, u32[]{:S(2)}) collective-permute-start(bf16[16,2,2,64,128]{4,3,2,1,0:T(8,128)(2,1)S(1)} %hold.11.own_ref), channel_id=1, source_target_pairs={{16,0},{32,16},{48,32},{64,48},{80,64},{96,80},{112,96},{17,1},{33... | collective-permute-start | bytes 3145736 | tf_op jit(solution)/shard_map/ppermute | solution.py:372
  92.4 43.7 %collective-permute-start.1 = (bf16[16,2,2,64,128]{4,3,2,1,0:T(8,128)(2,1)S(1)}, bf16[16,2,2,64,128]{4,3,2,1,0:T(8,128)(2,1)S(1)}, u32[]{:S(2)}, u32[]{:S(2)}) collective-permute-start(bf16[16,2,2,64,128]{4,3,2,1,0:T(8,128)(2,1)S(1)} %hold.10.own_ref), channel_id=1, source_target_pairs={{0,16},{16,32},{32,48},{48,64},{64,80},{80,96},{96,112},{1,17},{17... | collective-permute-start | bytes 3145736 | tf_op jit(solution)/shard_map/ppermute | solution.py:375
  97.0 43.2 %collective-permute-start.2 = (bf16[16,2,2,64,128]{4,3,2,1,0:T(8,128)(2,1)S(1)}, bf16[16,2,2,64,128]{4,3,2,1,0:T(8,128)(2,1)S(1)}, u32[]{:S(2)}, u32[]{:S(2)}) collective-permute-start(bf16[16,2,2,64,128]{4,3,2,1,0:T(8,128)(2,1)S(1)} %hold.10.own_ref), channel_id=1, source_target_pairs={{16,0},{32,16},{48,32},{64,48},{80,64},{96,80},{112,96},{17,1},{33... | collective-permute-start | bytes 3145736 | tf_op jit(solution)/shard_map/ppermute | solution.py:375
  126.7 8.7 %copy-start.17 = (bf16[16,1,64,128]{3,2,1,0:T(8,128)(2,1)}, bf16[16,1,64,128]{3,2,1,0:T(8,128)(2,1)S(1)}, u32[]{:S(2)}) copy-start(bf16[16,1,64,128]{3,2,1,0:T(8,128)(2,1)S(1)} %get-tuple-element.21) | copy-start | bytes 786436
  126.7 9.3 %collective-permute-start.5 = (bf16[16,1,64,128]{3,2,1,0:T(8,128)(2,1)S(1)}, bf16[16,1,64,128]{3,2,1,0:T(8,128)(2,1)S(1)}, u32[]{:S(2)}, u32[]{:S(2)}) collective-permute-start(bf16[16,1,64,128]{3,2,1,0:T(8,128)(2,1)S(1)} %get-tuple-element.21), channel_id=1, source_target_pairs={{48,112},{49,113},{50,114},{51,115},{52,116},{53,117},{54,118},{55... | collective-permute-start | bytes 786440 | tf_op jit(solution)/shard_map/ppermute | solution.py:398
  135.3 0.7 copy-start.21
  148.4 1.0 copy-start.13
  149.4 0.7 copy-start.19
  150.1 1.1 copy-start.23
  151.1 2.5 copy-start.1
  153.6 2.4 copy-start.2
  156.0 2.1 copy-start.18
  156.0 2.1 copy-start.20
  156.0 2.1 copy-start.22
  156.0 67.5 %collective-permute-start.11 = (bf16[4,2,2,256,640]{4,3,2,1,0:T(8,128)(2,1)}, bf16[4,2,2,256,640]{4,3,2,1,0:T(8,128)(2,1)}, u32[]{:S(2)}, u32[]{:S(2)}) collective-permute-start(bf16[4,2,2,256,640]{4,3,2,1,0:T(8,128)(2,1)} %copy-done.2), channel_id=1, source_target_pairs={{0,1},{1,0},{2,3},{3,2},{4,5},{5,4},{6,7},{7,6},{8,9},{9,8},{10,11... | collective-permute-start | bytes 15728648 | tf_op jit(solution)/shard_map/ppermute | solution.py:405
  159.0 20.9 %all-to-all-start.4 = ((bf16[16,2,64,128]{3,2,1,0:T(8,128)(2,1)}), bf16[16,2,64,128]{3,2,1,0:T(8,128)(2,1)S(1)}, u32[]{:S(2)}, u32[]{:S(2)}) async-start(bf16[16,2,64,128]{3,2,1,0:T(8,128)(2,1)} %pad_maximum_fusion.1), calls=%async_computation.4 | async-start | bytes 1048576 | tf_op jit(solution)/shard_map/all_to_all | solution.py:386
  163.8 1.2 copy-start.14
  165.1 5.1 %copy-start.15 = (bf16[16,2,2,64,128]{4,3,2,1,0:T(8,128)(2,1)S(1)}, bf16[16,2,2,64,128]{4,3,2,1,0:T(8,128)(2,1)}, u32[]{:S(2)}) copy-start(bf16[16,2,2,64,128]{4,3,2,1,0:T(8,128)(2,1)} %copy-done.13) | copy-start | bytes 3145732
  165.1 5.1 %copy-start.24 = (bf16[16,2,2,64,128]{4,3,2,1,0:T(8,128)(2,1)S(1)}, bf16[16,2,2,64,128]{4,3,2,1,0:T(8,128)(2,1)}, u32[]{:S(2)}) copy-start(bf16[16,2,2,64,128]{4,3,2,1,0:T(8,128)(2,1)} %copy-done.23) | copy-start | bytes 3145732
  165.1 22.0 %collective-permute-start.12 = (bf16[1,64,5120]{2,1,0:T(8,128)(2,1)}, bf16[1,64,5120]{2,1,0:T(8,128)(2,1)}, u32[]{:S(2)}, u32[]{:S(2)}) collective-permute-start(bf16[1,64,5120]{2,1,0:T(8,128)(2,1)} %hold.14), channel_id=1, source_target_pairs={{0,16},{16,32},{32,48},{48,64},{64,80},{80,96},{96,112},{1,17},{17... | collective-permute-start | bytes 1966088 | tf_op jit(solution)/shard_map/ppermute | solution.py:403
  169.3 8.7 %collective-permute-start.6 = (bf16[16,1,64,128]{3,2,1,0:T(8,128)(2,1)}, bf16[16,1,64,128]{3,2,1,0:T(8,128)(2,1)S(1)}, u32[]{:S(2)}, u32[]{:S(2)}) collective-permute-start(bf16[16,1,64,128]{3,2,1,0:T(8,128)(2,1)} %get-tuple-element.24), channel_id=1, source_target_pairs={{48,112},{49,113},{50,114},{51,115},{52,116},{53,117},{54,118},{55... | collective-permute-start | bytes 786440 | tf_op jit(solution)/shard_map/ppermute | solution.py:402
  179.8 19.6 %all-to-all-start.3 = ((bf16[16,2,64,128]{3,2,1,0:T(8,128)(2,1)}), bf16[16,2,64,128]{3,2,1,0:T(8,128)(2,1)S(1)}, u32[]{:S(2)}, u32[]{:S(2)}) async-start(bf16[16,2,64,128]{3,2,1,0:T(8,128)(2,1)} %pad_maximum_fusion), calls=%async_computation.3 | async-start | bytes 1048576 | tf_op jit(solution)/shard_map/all_to_all | solution.py:386
  187.8 15.5 %collective-permute-start.13 = (bf16[16,2,64,128]{3,2,1,0:T(8,128)(2,1)S(1)}, bf16[16,2,64,128]{3,2,1,0:T(8,128)(2,1)S(1)}, u32[]{:S(2)}, u32[]{:S(2)}) collective-permute-start(bf16[16,2,64,128]{3,2,1,0:T(8,128)(2,1)S(1)} %hold.15.mine_ref), channel_id=1, source_target_pairs={{0,16},{16,32},{32,48},{48,0},{64,80},{80,96},{96,112},{112,64},{1... | collective-permute-start | bytes 1572872 | tf_op jit(solution)/shard_map/ppermute | solution.py:389
  188.1 16.2 %collective-permute-start.14 = (bf16[16,2,64,128]{3,2,1,0:T(8,128)(2,1)S(1)}, bf16[16,2,64,128]{3,2,1,0:T(8,128)(2,1)S(1)}, u32[]{:S(2)}, u32[]{:S(2)}) collective-permute-start(bf16[16,2,64,128]{3,2,1,0:T(8,128)(2,1)S(1)} %hold.15.mine_ref), channel_id=1, source_target_pairs={{16,0},{32,16},{48,32},{0,48},{80,64},{96,80},{112,96},{64,112},{1... | collective-permute-start | bytes 1572872 | tf_op jit(solution)/shard_map/ppermute | solution.py:390
  199.4 15.8 %collective-permute-start.8 = (bf16[16,2,64,128]{3,2,1,0:T(8,128)(2,1)S(1)}, bf16[16,2,64,128]{3,2,1,0:T(8,128)(2,1)S(1)}, u32[]{:S(2)}, u32[]{:S(2)}) collective-permute-start(bf16[16,2,64,128]{3,2,1,0:T(8,128)(2,1)S(1)} %all-to-all-done.3.mine_ref), channel_id=1, source_target_pairs={{16,0},{32,16},{48,32},{0,48},{80,64},{96,80},{112,96},{64,112},{1... | collective-permute-start | bytes 1572872 | tf_op jit(solution)/shard_map/ppermute | solution.py:390
  202.2 16.2 %collective-permute-start.7 = (bf16[16,2,64,128]{3,2,1,0:T(8,128)(2,1)S(1)}, bf16[16,2,64,128]{3,2,1,0:T(8,128)(2,1)S(1)}, u32[]{:S(2)}, u32[]{:S(2)}) collective-permute-start(bf16[16,2,64,128]{3,2,1,0:T(8,128)(2,1)S(1)} %all-to-all-done.3.mine_ref), channel_id=1, source_target_pairs={{0,16},{16,32},{32,48},{48,0},{64,80},{80,96},{96,112},{112,64},{1... | collective-permute-start | bytes 1572872 | tf_op jit(solution)/shard_map/ppermute | solution.py:389
  204.0 19.6 %collective-permute-start.15 = (bf16[8,2,64,128]{3,2,1,0:T(8,128)(2,1)}, bf16[8,2,64,128]{3,2,1,0:T(8,128)(2,1)}, u32[]{:S(2)}, u32[]{:S(2)}) collective-permute-start(bf16[8,2,64,128]{3,2,1,0:T(8,128)(2,1)} %slice.27), channel_id=1, source_target_pairs={{0,16},{16,32},{32,48},{48,0},{64,80},{80,96},{96,112},{112,64},{1... | collective-permute-start | bytes 786440 | tf_op jit(solution)/shard_map/ppermute | solution.py:391
  205.0 18.5 %collective-permute-start.16 = (bf16[8,2,64,128]{3,2,1,0:T(8,128)(2,1)}, bf16[8,2,64,128]{3,2,1,0:T(8,128)(2,1)}, u32[]{:S(2)}, u32[]{:S(2)}) collective-permute-start(bf16[8,2,64,128]{3,2,1,0:T(8,128)(2,1)} %slice.28), channel_id=1, source_target_pairs={{16,0},{32,16},{48,32},{0,48},{80,64},{96,80},{112,96},{64,112},{1... | collective-permute-start | bytes 786440 | tf_op jit(solution)/shard_map/ppermute | solution.py:392
  215.3 17.1 %collective-permute-start.10 = (bf16[8,2,64,128]{3,2,1,0:T(8,128)(2,1)S(1)}, bf16[8,2,64,128]{3,2,1,0:T(8,128)(2,1)S(1)}, u32[]{:S(2)}, u32[]{:S(2)}) collective-permute-start(bf16[8,2,64,128]{3,2,1,0:T(8,128)(2,1)S(1)} %slice.26), channel_id=1, source_target_pairs={{16,0},{32,16},{48,32},{0,48},{80,64},{96,80},{112,96},{64,112},{1... | collective-permute-start | bytes 786440 | tf_op jit(solution)/shard_map/ppermute | solution.py:392
  218.4 14.0 %collective-permute-start.9 = (bf16[8,2,64,128]{3,2,1,0:T(8,128)(2,1)S(1)}, bf16[8,2,64,128]{3,2,1,0:T(8,128)(2,1)S(1)}, u32[]{:S(2)}, u32[]{:S(2)}) collective-permute-start(bf16[8,2,64,128]{3,2,1,0:T(8,128)(2,1)S(1)} %slice.25), channel_id=1, source_target_pairs={{0,16},{16,32},{32,48},{48,0},{64,80},{80,96},{96,112},{112,64},{1... | collective-permute-start | bytes 786440 | tf_op jit(solution)/shard_map/ppermute | solution.py:391
  223.6 2.5 copy-start.3
  238.8 18.1 %copy-start.8 = (bf16[2,64,5120]{2,1,0:T(8,128)(2,1)S(1)}, bf16[2,64,5120]{2,1,0:T(8,128)(2,1)}, u32[]{:S(2)}) copy-start(bf16[2,64,5120]{2,1,0:T(8,128)(2,1)} %hidden_ref.1) | copy-start | bytes 3932164
  238.8 18.1 %copy-start.16 = (bf16[64,5120]{1,0:T(8,128)(2,1)S(1)}, bf16[64,5120]{1,0:T(8,128)(2,1)}, u32[]{:S(2)}) copy-start(bf16[64,5120]{1,0:T(8,128)(2,1)} %entering_ref.1) | copy-start | bytes 1966084
Sparse Core Ops, SparseCore 0:
  45.8 29.0 all-gather.4
  87.7 56.1 all-gather.6

commit v8 on v7

--- a/solution.py
+++ b/solution.py
@@ -14,6 +14,7 @@
 SCALE_LOG2 = (HD ** -0.5) * 1.4426950408889634
 BLOCK_Q = 512
 VMEM = 28 * 1024 * 1024
+LARGE = pltpu.CompilerParams(vmem_limit_bytes=58 * 1024 * 1024)
 SMALL = pltpu.CompilerParams(vmem_limit_bytes=1024 * 1024)
 MEDIUM = pltpu.CompilerParams(vmem_limit_bytes=12 * 1024 * 1024)
 QUEUE = 8
@@ -37,29 +38,29 @@
     group = width // SPATIAL
     piece = width // PACK
     count = SPATIAL // PACK
-
-    def kernel(q_ref, k_ref, v_ref, kv0_ref, kv1_ref, out_ref):
+    heads = group // HD
+
+    def kernel(q_ref, k_ref, v_ref, *out_refs):
         for i in range(count):
-            for head, kv_ref in enumerate((kv0_ref, kv1_ref)):
+            for head in range(heads):
+                kv_ref, out_ref = out_refs[head], out_refs[heads + head]
                 cols = slice(i * group + head * HD, i * group + (head + 1) * HD)
                 kv_ref[i, 0] = k_ref[:, :, cols]
                 kv_ref[i, 1] = v_ref[:, :, cols]
-            out_ref[i] = q_ref[:, :, i * group : (i + 1) * group]
+                out_ref[i] = q_ref[:, :, cols]
 
     spec = pl.BlockSpec((frames, tok, piece), lambda s: (0, 0, s))
     kv_spec = pl.BlockSpec((count, 2, frames, tok, HD), lambda s: (s, 0, 0, 0, 0))
+    q_spec = pl.BlockSpec((count, frames, tok, HD), lambda s: (s, 0, 0, 0))
     kv_shape = jax.ShapeDtypeStruct((SPATIAL, 2, frames, tok, HD), keys.dtype)
+    q_shape = jax.ShapeDtypeStruct((SPATIAL, frames, tok, HD), queries.dtype)
     return pl.pallas_call(
         kernel,
         grid=(PACK,),
         in_specs=[spec] * 3,
-        out_specs=[kv_spec, kv_spec, pl.BlockSpec((count, frames, tok, group), lambda s: (s, 0, 0, 0))],
-        out_shape=[
-            kv_shape,
-            kv_shape,
-            jax.ShapeDtypeStruct((SPATIAL, frames, tok, group), queries.dtype),
-        ],
-        compiler_params=MEDIUM,
+        out_specs=[kv_spec] * heads + [q_spec] * heads,
+        out_shape=[kv_shape] * heads + [q_shape] * heads,
+        compiler_params=LARGE,
         name="pack",
     )(queries, keys, values)
 
@@ -80,8 +81,8 @@
     )(array, *earlier)
 
 
-def attend(frame, position, query, head, own, before, after, *earlier):
-    groups, frames, tok, both = query.shape
+def attend(frame, position, query, own, before, after, *earlier):
+    groups, frames, tok, _ = query.shape
     width = own.shape[-1]
     row_count = groups * tok
     groups_block = BLOCK_Q // tok
@@ -150,7 +151,7 @@
 
     first = asked[0]
     in_specs = [
-        pl.BlockSpec((groups_block, 1, tok, width), lambda f, b, pos: (b, first + f, 0, head)),
+        pl.BlockSpec((groups_block, 1, tok, width), lambda f, b, pos: (b, first + f, 0, 0)),
         pl.BlockSpec(own.shape, lambda f, b, pos: (0, 0, 0, 0, 0)),
         pl.BlockSpec(
             (groups, 2, before_count, tok, width),
@@ -262,7 +263,7 @@
             scratch_shapes=[pltpu.VMEM((RING * rows, groups * width), jnp.bfloat16)],
         ),
         out_shape=out_shape,
-        compiler_params=pltpu.CompilerParams(vmem_limit_bytes=VMEM),
+        compiler_params=LARGE,
         cost_estimate=pl.CostEstimate(
             flops=2 * RING * rows * groups * width * halves * cols_dev,
             bytes_accessed=8 * 1024 * 1024,
@@ -365,25 +366,26 @@
         lax.dynamic_slice_in_dim(gates, y_low * count, count, axis=1),
     )
 
-    kv0, kv1, query = pack(queries, keys, values)
+    kv0, kv1, q0, q1 = pack(queries, keys, values)
     kv0 = to_heads(kv0)
     kv1 = to_heads(hold(kv1, kv0, gates))
-    kv0 = hold(kv0, kv1)
+    q0 = to_heads(hold(q0, kv1))
+    kv0 = hold(kv0, q0)
     kv0_before, kv0_after = lax.ppermute(kv0, "queue", up), lax.ppermute(kv0, "queue", down)
-    query = to_heads(hold(query, kv1))
-    kv1 = hold(kv1, query)
+    q1 = to_heads(hold(q1, kv0_before, kv0_after))
+    kv1 = hold(kv1, kv0_before, kv0_after)
     kv1_before, kv1_after = lax.ppermute(kv1, "queue", up), lax.ppermute(kv1, "queue", down)
 
     weight = lax.all_gather(out_weight, ("queue", "spatial"), axis_index_groups=along_y, axis=0)
-    weight = hold(weight, query)
+    weight = hold(weight, q0)
     weight = lax.all_gather(weight, "spatial", axis_index_groups=along_z, axis=0)
     weight = weight.reshape(-1, 2, 2, *out_weight.shape)
 
     cross = [(RING - 1, QUEUE - 1)]
 
-    def returned(even, odd, crossing):
+    def with_crossing(even, odd, crossing):
         odd = jnp.where(position == QUEUE - 1, crossing, odd)
-        return to_heads(jnp.concatenate((even, odd), axis=1))
+        return jnp.concatenate((even, odd), axis=1)
 
     def spread(mine):
         left = lax.ppermute(mine, "queue", ring_up)
@@ -392,20 +394,21 @@
         far_high = lax.ppermute(right[SPATIAL // 2 :], "queue", ring_down)
         return mine, left, right, far_low, far_high
 
-    head0 = (position_now, query, 0, kv0, kv0_before, kv0_after)
-    head1 = (position_now, query, 1, kv1, kv1_before, kv1_after)
+    head0 = (position_now, q0, kv0, kv0_before, kv0_after)
+    head1 = (position_now, q1, kv1, kv1_before, kv1_after)
     odd0, token = attend(1, *head0)
     odd0_crossing = lax.ppermute(odd0, "queue", cross)
     even0, token = attend(0, *head0, token)
-    first = returned(even0, odd0, odd0_crossing)
-    odd1, token = attend(1, *head1, token, odd0_crossing)
+    first = with_crossing(even0, odd0, odd0_crossing)
+    odd1, token = attend(1, *head1, token, first)
     odd1_crossing = lax.ppermute(odd1, "queue", cross)
-    shifted = lax.ppermute(hold(hidden[frames - 1 :], kv1_before), "queue", up)
+    first_sources = spread(hold(to_heads(first), token))
+    shifted = lax.ppermute(hold(hidden[frames - 1 :], kv1_before, token), "queue", up)
     weight_own = hold(weight, token)
     weight_pair = lax.ppermute(weight_own, "spatial", swap_core)
     even1, token = attend(0, *head1, token)
-    first_sources = spread(hold(first, token, shifted))
-    second_sources = spread(returned(even1, odd1, odd1_crossing))
+    second = with_crossing(even1, odd1, odd1_crossing)
+    second_sources = spread(to_heads(hold(second, shifted)))
 
     partial = project(0, place, first_sources, weight_own, weight_pair, None, None)
     branch = project(1, place, second_sources, weight_own, weight_pair, partial, gates)

time: 267 us -> 284 us (1.064)
  blocking collectives: 18.1 us -> 42.3 us
  Pallas kernels: 48 us -> 61.2 us
  local copies, waits for them, and re-layouts: 24.6 us -> 16.4 us
  waiting for transfers between devices: 101 us -> 94.6 us
  starting transfers between devices: 57.6 us -> 51.2 us
    all_to_all x0 -> x1, blocking collectives: none -> 23.5 us  [body(): kv1 = to_heads(hold(kv1, kv0, gates))]
    ppermute x1, waiting for transfers between devices: 16.2 us -> 1.08 us  [body(): lax.ppermute(kv0, 'queue', up)]
    ppermute x1, waiting for transfers between devices: 4.5 us -> 19.6 us  [body(): lax.ppermute(kv0, 'queue', down)]
    all_gather x1, waiting for transfers between devices: 8.93 us -> 0.02 us  [body(): lax.all_gather(out_weight, ('queue', 'spatial'), axis_index_groups=along_...]
    unnamed x53 -> x49, local copies, waits for them, and re-layouts: 21 us -> 12.2 us
    ppermute x2, starting transfers between devices: 5.7 us -> 0.08 us  [spread(): right = lax.ppermute(mine, 'queue', ring_down)]
    pallas_call x4, Pallas kernels: 31.4 us -> 36.5 us  [attend(): pl.pallas_call(kernel, grid_spec=pltpu.PrefetchScalarGridSpec(num_scalar_...]
    all_to_all x4, waiting for transfers between devices: 36 us -> 40.6 us  [the longest x1 12.3 us: body(): q0 = to_heads(hold(q0, kv1))]
  transfers between devices with their start and end apart: 24 -> 24, of which waited for: 12 -> 12; matrix products, arithmetic and copies ran while one was open for 2% -> 2% of each run, Pallas kernels for 14% -> 17%
where the time goes in v8:
time: 284 us; the launch traced here: 282 us
  waiting for transfers between devices  94.6 us (33%)
  Pallas kernels  61.2 us (22%)
  starting transfers between devices  51.2 us (18%)
  blocking collectives  42.3 us (15%)
  local copies, waits for them, and re-layouts  16.4 us (6%)
  between operations  13.7 us (5%)
    pallas_call x4, Pallas kernels, attend(): pl.pallas_call(kernel, grid_spec=pltpu.PrefetchScalarGridSpec(num_scalar_...  36.5 us
    all_to_all x1, blocking collectives, body(): kv1 = to_heads(hold(kv1, kv0, gates))  23.5 us
    ppermute x1, waiting for transfers between devices, body(): lax.ppermute(kv0, 'queue', down)  19.6 us
    all_to_all x1, blocking collectives, body(): lax.all_to_all(branch, 'queue', split_axis=0, concat_axis=0, axis_index_g...  18.8 us
    pallas_call x2, Pallas kernels, project(): pl.pallas_call(kernel, grid_spec=pltpu.PrefetchScalarGridSpec(num_scalar_...  16.8 us
    ppermute x1, waiting for transfers between devices, body(): other_gates = lax.ppermute(gates, 'queue', swap_low)  12.5 us
    all_to_all x1, waiting for transfers between devices, body(): q0 = to_heads(hold(q0, kv1))  12.3 us
    unnamed x49, local copies, waits for them, and re-layouts  12.2 us
  transfers between devices with their start and end apart: 24, of which 12 were waited for; matrix products, arithmetic and copies ran while one was open for 2% of the time, Pallas kernels for 17%

profile of v8, /device:TPU:0, one launch (start us, length us, event | category | flops | bytes accessed | tf_op | source)
XLA Modules:
  0.0 282.1 jit_solution(17874942975342617559)
XLA Ops:
  6.5 4.3 %pack.1 = (bf16[16,2,2,64,128]{4,3,2,1,0:T(8,128)(2,1)}, bf16[16,2,2,64,128]{4,3,2,1,0:T(8,128)(2,1)}, bf16[16,2,64,128]{3,2,1,0:T(8,128)(2,1)}, bf16[16,2,64,128]{3,2,1,0:T(8,128)(2,1)}) custom-call(bf16[2,64,4096]{2,1,0:T(8,128)(2,1)} %q_ref.1, bf16[2,64,4096]{2,1,0:T(8,128)(2,1)} %k_ref.1, bf16[2,64,4096]{2,1,0:T(8,128)(2,1)} %v_ref.1), custom_call_target="tpu_custom_call" | custom-call | tf_op jit(solution)/shard_map/pack/pallas_call | solution.py:57
  10.9 8.3 %all-to-all-start = ((bf16[16,2,2,64,128]{4,3,2,1,0:T(8,128)(2,1)}), bf16[16,2,2,64,128]{4,3,2,1,0:T(8,128)(2,1)S(1)}, u32[]{:S(2)}, u32[]{:S(2)}) async-start(bf16[16,2,2,64,128]{4,3,2,1,0:T(8,128)(2,1)} %get-tuple-element.17), calls=%async_computation | async-start | bytes 2097152 | tf_op jit(solution)/shard_map/all_to_all | solution.py:370
  19.2 0.7 all-gather.5.cloned.1.call-update
  19.9 0.2 fusion
  20.2 0.8 collective-permute-start
  20.9 12.5 %collective-permute-done = f32[16,640]{1,0:T(8,128)S(1)} collective-permute-done((f32[16,640]{1,0:T(8,128)S(1)}, f32[16,640]{1,0:T(8,128)S(1)}, u32[]{:S(2)}, u32[]{:S(2)}) %collective-permute-start) | collective-permute-done | bytes 40992 | tf_op jit(solution)/shard_map/ppermute | solution.py:359
  33.5 0.1 dynamic-slice_select_fusion.refs_2_.rest_1_
  33.6 4.0 %all-to-all-done.refs_1_.refs_0_ = bf16[16,2,2,64,128]{4,3,2,1,0:T(8,128)(2,1)S(1)} async-done(((bf16[16,2,2,64,128]{4,3,2,1,0:T(8,128)(2,1)}), bf16[16,2,2,64,128]{4,3,2,1,0:T(8,128)(2,1)S(1)}, u32[]{:S(2)}, u32[]{:S(2)}) %all-to-all-start) | async-done | bytes 1048608 | tf_op jit(solution)/shard_map/all_to_all | solution.py:370
  37.6 23.5 %all_to_all.35.refs_1_.refs_0_ = bf16[16,2,2,64,128]{4,3,2,1,0:T(8,128)(2,1)S(1)} all-to-all(bf16[16,2,2,64,128]{4,3,2,1,0:T(8,128)(2,1)S(1)} %hold.10), channel_id=1, replica_groups=mesh['queue'=8,'spatial'=16] {'spatial'}, dimensions={0} | all-to-all | bytes 2097152 | tf_op jit(solution)/shard_map/all_to_all | solution.py:371
  61.1 0.8 copy-done.11
  61.9 4.2 %all-to-all-start.2 = ((bf16[16,2,64,128]{3,2,1,0:T(8,128)(2,1)}), bf16[16,2,64,128]{3,2,1,0:T(8,128)(2,1)S(1)}, u32[]{:S(2)}, u32[]{:S(2)}) async-start(bf16[16,2,64,128]{3,2,1,0:T(8,128)(2,1)} %copy-done.11), calls=%async_computation.2 | async-start | bytes 1048576 | tf_op jit(solution)/shard_map/all_to_all | solution.py:372
  66.2 12.3 %all-to-all-done.2.refs_1_.q_ref = bf16[16,2,64,128]{3,2,1,0:T(8,128)(2,1)S(1)} async-done(((bf16[16,2,64,128]{3,2,1,0:T(8,128)(2,1)}), bf16[16,2,64,128]{3,2,1,0:T(8,128)(2,1)S(1)}, u32[]{:S(2)}, u32[]{:S(2)}) %all-to-all-start.2) | async-done | bytes 524320 | tf_op jit(solution)/shard_map/all_to_all | solution.py:372
  78.5 1.3 copy-done.3
  79.8 1.1 copy-done.4
  80.9 1.3 collective-permute-start.2
  82.2 5.6 %collective-permute-start.1 = (bf16[16,2,2,64,128]{4,3,2,1,0:T(8,128)(2,1)S(1)}, bf16[16,2,2,64,128]{4,3,2,1,0:T(8,128)(2,1)}, u32[]{:S(2)}, u32[]{:S(2)}) collective-permute-start(bf16[16,2,2,64,128]{4,3,2,1,0:T(8,128)(2,1)S(1)} %hold.12.own_ref), channel_id=1, source_target_pairs={{0,16},{16,32},{32,48},{48,64},{64,80},{80,96},{96,112},{1,17},{17... | collective-permute-start | bytes 3145736 | tf_op jit(solution)/shard_map/ppermute | solution.py:374
  87.8 19.6 %collective-permute-done.2.refs_2_.after_ref = bf16[16,2,2,64,128]{4,3,2,1,0:T(8,128)(2,1)} collective-permute-done((bf16[16,2,2,64,128]{4,3,2,1,0:T(8,128)(2,1)S(1)}, bf16[16,2,2,64,128]{4,3,2,1,0:T(8,128)(2,1)}, u32[]{:S(2)}, u32[]{:S(2)}) %collective-permute-start.2) | collective-permute-done | bytes 1048608 | tf_op jit(solution)/shard_map/ppermute | solution.py:374
  107.3 1.1 collective-permute-done.1.refs_1_.before_ref
  108.4 0.7 hold.14.own_ref
  109.1 1.3 collective-permute-start.4
  110.4 6.1 %collective-permute-start.3 = (bf16[16,2,2,64,128]{4,3,2,1,0:T(8,128)(2,1)S(1)}, bf16[16,2,2,64,128]{4,3,2,1,0:T(8,128)(2,1)}, u32[]{:S(2)}, u32[]{:S(2)}) collective-permute-start(bf16[16,2,2,64,128]{4,3,2,1,0:T(8,128)(2,1)S(1)} %hold.14.own_ref), channel_id=1, source_target_pairs={{0,16},{16,32},{32,48},{48,64},{64,80},{80,96},{96,112},{1,17},{17... | collective-permute-start | bytes 3145736 | tf_op jit(solution)/shard_map/ppermute | solution.py:377
  116.5 0.7 hold.13
  117.2 3.6 %all-to-all-start.3 = ((bf16[16,2,64,128]{3,2,1,0:T(8,128)(2,1)}), bf16[16,2,64,128]{3,2,1,0:T(8,128)(2,1)S(1)}, u32[]{:S(2)}, u32[]{:S(2)}) async-start(bf16[16,2,64,128]{3,2,1,0:T(8,128)(2,1)} %hold.13), calls=%async_computation.3 | async-start | bytes 1048576 | tf_op jit(solution)/shard_map/all_to_all | solution.py:375
  120.8 9.0 %attend.4 = (bf16[16,1,64,128]{3,2,1,0:T(8,128)(2,1)S(1)}, f32[8,128]{1,0:T(8,128)S(1)}) custom-call(s32[1]{0:T(128)} %bitcast.pos_ref, bf16[16,2,64,128]{3,2,1,0:T(8,128)(2,1)S(1)} %all-to-all-done.2.refs_1_.q_ref, bf16[16,2,2,64,128]{4,3,2,1,0:T(8,128)(2,1)S(1)} %hold.12.own_ref, bf16[16,2,2,64,128]{4,3,2,1,0:T(8,128)(2,1)} %collective-permute-done.1.refs_1_.before_ref, ...), custom_call_target="tpu_custom_call" | custom-call | flops 5368709120 | bytes 4194304 | tf_op jit(solution)/shard_map/attend/pallas_call | solution.py:162
  129.8 0.9 collective-permute-start.5
  130.6 9.0 %attend.5 = (bf16[16,1,64,128]{3,2,1,0:T(8,128)(2,1)S(1)}, f32[8,128]{1,0:T(8,128)S(1)}) custom-call(s32[1]{0:T(128)} %bitcast.pos_ref, bf16[16,2,64,128]{3,2,1,0:T(8,128)(2,1)S(1)} %all-to-all-done.2.refs_1_.q_ref, bf16[16,2,2,64,128]{4,3,2,1,0:T(8,128)(2,1)S(1)} %hold.12.own_ref, bf16[16,2,2,64,128]{4,3,2,1,0:T(8,128)(2,1)} %collective-permute-done.1.refs_1_.before_ref, ...), custom_call_target="tpu_custom_call" | custom-call | flops 5368709120 | bytes 4194304 | tf_op jit(solution)/shard_map/attend/pallas_call | solution.py:162
  139.8 0.5 copy-done.16
  140.3 0.8 pad_maximum_fusion.rest_1_
  141.1 10.5 %all-to-all-done.3.q_ref = bf16[16,2,64,128]{3,2,1,0:T(8,128)(2,1)S(1)} async-done(((bf16[16,2,64,128]{3,2,1,0:T(8,128)(2,1)}), bf16[16,2,64,128]{3,2,1,0:T(8,128)(2,1)S(1)}, u32[]{:S(2)}, u32[]{:S(2)}) %all-to-all-start.3) | async-done | bytes 524320 | tf_op jit(solution)/shard_map/all_to_all | solution.py:375
  151.6 0.7 copy-done.17
  152.3 8.9 %attend.6 = (bf16[16,1,64,128]{3,2,1,0:T(8,128)(2,1)S(1)}, f32[8,128]{1,0:T(8,128)S(1)}) custom-call(s32[1]{0:T(128)} %bitcast.pos_ref, bf16[16,2,64,128]{3,2,1,0:T(8,128)(2,1)S(1)} %all-to-all-done.3.q_ref, bf16[16,2,2,64,128]{4,3,2,1,0:T(8,128)(2,1)S(1)} %hold.14.own_ref, bf16[16,2,2,64,128]{4,3,2,1,0:T(8,128)(2,1)} %collective-permute-done.3.before_ref.refs_1_, ...), custom_call_target="tpu_custom_call" | custom-call | flops 5368709120 | bytes 4194304 | tf_op jit(solution)/shard_map/attend/pallas_call | solution.py:162
  161.2 0.7 copy-done.14
  161.9 2.5 copy-done.1
  164.4 2.3 copy-done.2
  166.8 0.9 slice.19.refs_0_
  167.7 4.9 %all-to-all-start.5 = ((bf16[16,2,64,128]{3,2,1,0:T(8,128)(2,1)}), bf16[16,2,64,128]{3,2,1,0:T(8,128)(2,1)S(1)}, u32[]{:S(2)}, u32[]{:S(2)}) async-start(bf16[16,2,64,128]{3,2,1,0:T(8,128)(2,1)} %pad_maximum_fusion.rest_1_), calls=%async_computation.5 | async-start | bytes 1048576 | tf_op jit(solution)/shard_map/all_to_all | solution.py:405
  172.6 0.7 collective-permute-start.6
  173.3 0.7 hold.15
  174.0 1.7 collective-permute-start.7
  175.7 9.6 %attend.7 = (bf16[16,1,64,128]{3,2,1,0:T(8,128)(2,1)S(1)}, f32[8,128]{1,0:T(8,128)}) custom-call(s32[1]{0:T(128)} %bitcast.pos_ref, bf16[16,2,64,128]{3,2,1,0:T(8,128)(2,1)S(1)} %all-to-all-done.3.q_ref, bf16[16,2,2,64,128]{4,3,2,1,0:T(8,128)(2,1)S(1)} %hold.14.own_ref, bf16[16,2,2,64,128]{4,3,2,1,0:T(8,128)(2,1)} %collective-permute-done.3.before_ref.refs_1_, ...), custom_call_target="tpu_custom_call" | custom-call | flops 5368709120 | bytes 4194304 | tf_op jit(solution)/shard_map/attend/pallas_call | solution.py:162
  185.3 0.9 pad_maximum_fusion.1.refs_0_
  186.1 4.4 %collective-permute-done.7.refs_1_.shifted_ref = bf16[1,64,5120]{2,1,0:T(8,128)(2,1)S(1)} collective-permute-done((bf16[1,64,5120]{2,1,0:T(8,128)(2,1)}, bf16[1,64,5120]{2,1,0:T(8,128)(2,1)S(1)}, u32[]{:S(2)}, u32[]{:S(2)}) %collective-permute-start.7) | collective-permute-done | bytes 655392 | tf_op jit(solution)/shard_map/ppermute | solution.py:406
  190.5 0.8 copy-done.8
  191.4 7.7 %all-to-all-done.5.refs_0_ = bf16[16,2,64,128]{3,2,1,0:T(8,128)(2,1)S(1)} async-done(((bf16[16,2,64,128]{3,2,1,0:T(8,128)(2,1)}), bf16[16,2,64,128]{3,2,1,0:T(8,128)(2,1)S(1)}, u32[]{:S(2)}, u32[]{:S(2)}) %all-to-all-start.5) | async-done | bytes 524320 | tf_op jit(solution)/shard_map/all_to_all | solution.py:405
  199.0 3.6 %all-to-all-start.4 = ((bf16[16,2,64,128]{3,2,1,0:T(8,128)(2,1)}), bf16[16,2,64,128]{3,2,1,0:T(8,128)(2,1)S(1)}, u32[]{:S(2)}, u32[]{:S(2)}) async-start(bf16[16,2,64,128]{3,2,1,0:T(8,128)(2,1)} %hold.16), calls=%async_computation.4 | async-start | bytes 1048576 | tf_op jit(solution)/shard_map/all_to_all | solution.py:411
  202.7 2.0 collective-permute-start.13
  204.7 10.2 %all-to-all-done.4.mine_ref = bf16[16,2,64,128]{3,2,1,0:T(8,128)(2,1)S(1)} async-done(((bf16[16,2,64,128]{3,2,1,0:T(8,128)(2,1)}), bf16[16,2,64,128]{3,2,1,0:T(8,128)(2,1)S(1)}, u32[]{:S(2)}, u32[]{:S(2)}) %all-to-all-start.4) | async-done | bytes 524320 | tf_op jit(solution)/shard_map/all_to_all | solution.py:411
  214.9 2.0 collective-permute-start.8
  217.0 1.7 slice.28
  218.6 1.4 collective-permute-start.16
  220.1 1.7 slice.27
  221.7 0.6 collective-permute-start.15
  222.3 7.5 %collective-permute-done.9.right_ref = bf16[16,2,64,128]{3,2,1,0:T(8,128)(2,1)S(1)} collective-permute-done((bf16[16,2,64,128]{3,2,1,0:T(8,128)(2,1)S(1)}, bf16[16,2,64,128]{3,2,1,0:T(8,128)(2,1)S(1)}, u32[]{:S(2)}, u32[]{:S(2)}) %collective-permute-start.9) | collective-permute-done | bytes 524320 | tf_op jit(solution)/shard_map/ppermute | solution.py:392
  229.8 1.3 collective-permute-start.11
  231.1 0.9 collective-permute-start.10
  232.0 0.6 pad_add_fusion.place_ref
  232.6 2.9 %collective-permute-done.16.high_ref = bf16[8,2,64,128]{3,2,1,0:T(8,128)(2,1)} collective-permute-done((bf16[8,2,64,128]{3,2,1,0:T(8,128)(2,1)}, bf16[8,2,64,128]{3,2,1,0:T(8,128)(2,1)}, u32[]{:S(2)}, u32[]{:S(2)}) %collective-permute-start.16) | collective-permute-done | bytes 262176 | tf_op jit(solution)/shard_map/ppermute | solution.py:394
  235.5 1.2 collective-permute-done.15.low_ref
  236.7 8.3 %project_first.1.rest_0_ = f32[2,512,640]{2,1,0:T(8,128)} custom-call(s32[2]{0:T(128)} %pad_add_fusion.place_ref, bf16[16,2,64,128]{3,2,1,0:T(8,128)(2,1)} %copy-done.5, bf16[16,2,64,128]{3,2,1,0:T(8,128)(2,1)} %collective-permute-done.13.left_ref, bf16[16,2,64,128]{3,2,1,0:T(8,128)(2,1)} %collective-permute-done.14.right_ref, ...), custom_call_target="tpu_custom_call" | custom-call | flops 2684354560 | bytes 8388608 | tf_op jit(solution)/shard_map/project_first/pallas_call | solution.py:256
  245.1 0.7 copy-done.21
  245.8 0.7 copy-done.22
  246.5 8.5 %project_last.1 = bf16[8,2,64,640]{3,2,1,0:T(8,128)(2,1)} custom-call(s32[2]{0:T(128)} %pad_add_fusion.place_ref, bf16[16,2,64,128]{3,2,1,0:T(8,128)(2,1)} %copy-done.18, bf16[16,2,64,128]{3,2,1,0:T(8,128)(2,1)} %copy-done.20, bf16[16,2,64,128]{3,2,1,0:T(8,128)(2,1)} %copy-done.19, bf16[8,2,64,128]{3,2,1,0:T(8,128)(2,1)} %copy-done.22, ...), custom_call_target="tpu_custom_call" | custom-call | flops 2684354560 | bytes 8388608 | tf_op jit(solution)/shard_map/project_last/pallas_call | solution.py:256
  255.0 18.8 %all_to_all.36 = bf16[8,2,64,640]{3,2,1,0:T(8,128)(2,1)S(1)} all-to-all(bf16[8,2,64,640]{3,2,1,0:T(8,128)(2,1)} %project_last.1), channel_id=1, replica_groups={{0,16,32,48},{64,80,96,112},{1,17,33,49},{65,81,97,113},{2,18,34,50},{6..., dimensions={0} | all-to-all | bytes 2621440 | tf_op jit(solution)/shard_map/all_to_all | solution.py:415
  273.8 1.4 add_branch.1
  (70 shorter events, 0.5 us)
Async XLA Ops:
  6.5 13.4 %copy-start = (f32[50,640]{1,0:T(8,128)S(1)}, f32[50,640]{1,0:T(8,128)}, u32[]{:S(2)}) copy-start(f32[50,640]{1,0:T(8,128)} %param.13) | copy-start | bytes 384004
  10.9 9.0 %copy-start.23 = (s32[16]{0:T(128)S(1)}, s32[16]{0:T(128)}, u32[]{:S(2)}) copy-start(s32[16]{0:T(128)} %param.14) | copy-start | bytes 196
  10.9 26.7 %copy-start.6 = (bf16[16,2,2,64,128]{4,3,2,1,0:T(8,128)(2,1)S(1)}, bf16[16,2,2,64,128]{4,3,2,1,0:T(8,128)(2,1)}, u32[]{:S(2)}) copy-start(bf16[16,2,2,64,128]{4,3,2,1,0:T(8,128)(2,1)} %get-tuple-element.19.refs_0_) | copy-start | bytes 3145732
  10.9 26.7 %all-to-all-start = ((bf16[16,2,2,64,128]{4,3,2,1,0:T(8,128)(2,1)}), bf16[16,2,2,64,128]{4,3,2,1,0:T(8,128)(2,1)S(1)}, u32[]{:S(2)}, u32[]{:S(2)}) async-start(bf16[16,2,2,64,128]{4,3,2,1,0:T(8,128)(2,1)} %get-tuple-element.17), calls=%async_computation | async-start | bytes 2097152 | tf_op jit(solution)/shard_map/all_to_all | solution.py:370
  19.2 47.0 %all-gather.5.cloned.1.call-start = ((), (), s32[]{:S(2)}) async-start(), calls=%async_computation.7 | async-start | bytes 1638400 | tf_op jit(solution)/shard_map/all_gather | solution.py:379
  20.2 13.3 %collective-permute-start = (f32[16,640]{1,0:T(8,128)S(1)}, f32[16,640]{1,0:T(8,128)S(1)}, u32[]{:S(2)}, u32[]{:S(2)}) collective-permute-start(f32[16,640]{1,0:T(8,128)S(1)} %fusion), channel_id=1, source_target_pairs={{0,64},{16,80},{32,96},{48,112},{64,0},{80,16},{96,32},{112,48},{1... | collective-permute-start | bytes 122888 | tf_op jit(solution)/shard_map/ppermute | solution.py:359
  33.6 4.0 %copy-start.13 = (f32[2,8,640]{2,1,0:T(8,128)}, f32[2,8,640]{2,1,0:T(8,128)S(1)}, u32[]{:S(2)}) copy-start(f32[2,8,640]{2,1,0:T(8,128)S(1)} %dynamic-slice_select_fusion.refs_2_.rest_1_) | copy-start | bytes 122884
  37.6 23.5 %copy-start.10 = (bf16[16,2,64,128]{3,2,1,0:T(8,128)(2,1)S(1)}, bf16[16,2,64,128]{3,2,1,0:T(8,128)(2,1)}, u32[]{:S(2)}) copy-start(bf16[16,2,64,128]{3,2,1,0:T(8,128)(2,1)} %get-tuple-element.18.refs_0_) | copy-start | bytes 1572868
  61.1 0.8 copy-start.11
  61.9 16.6 %all-to-all-start.2 = ((bf16[16,2,64,128]{3,2,1,0:T(8,128)(2,1)}), bf16[16,2,64,128]{3,2,1,0:T(8,128)(2,1)S(1)}, u32[]{:S(2)}, u32[]{:S(2)}) async-start(bf16[16,2,64,128]{3,2,1,0:T(8,128)(2,1)} %copy-done.11), calls=%async_computation.2 | async-start | bytes 1048576 | tf_op jit(solution)/shard_map/all_to_all | solution.py:372
  66.2 95.8 %all-gather.7.cloned.1.call-start = ((), (), s32[]{:S(2)}) async-start(), calls=%async_computation.8 | async-start | bytes 6553600 | tf_op jit(solution)/shard_map/all_gather | solution.py:381
  78.5 1.3 copy-start.3
  79.8 1.1 copy-start.4
  80.9 26.4 %collective-permute-start.2 = (bf16[16,2,2,64,128]{4,3,2,1,0:T(8,128)(2,1)S(1)}, bf16[16,2,2,64,128]{4,3,2,1,0:T(8,128)(2,1)}, u32[]{:S(2)}, u32[]{:S(2)}) collective-permute-start(bf16[16,2,2,64,128]{4,3,2,1,0:T(8,128)(2,1)S(1)} %hold.12.own_ref), channel_id=1, source_target_pairs={{16,0},{32,16},{48,32},{64,48},{80,64},{96,80},{112,96},{17,1},{33... | collective-permute-start | bytes 3145736 | tf_op jit(solution)/shard_map/ppermute | solution.py:374
  82.2 26.2 %collective-permute-start.1 = (bf16[16,2,2,64,128]{4,3,2,1,0:T(8,128)(2,1)S(1)}, bf16[16,2,2,64,128]{4,3,2,1,0:T(8,128)(2,1)}, u32[]{:S(2)}, u32[]{:S(2)}) collective-permute-start(bf16[16,2,2,64,128]{4,3,2,1,0:T(8,128)(2,1)S(1)} %hold.12.own_ref), channel_id=1, source_target_pairs={{0,16},{16,32},{32,48},{48,64},{64,80},{80,96},{96,112},{1,17},{17... | collective-permute-start | bytes 3145736 | tf_op jit(solution)/shard_map/ppermute | solution.py:374
  109.1 42.5 %collective-permute-start.4 = (bf16[16,2,2,64,128]{4,3,2,1,0:T(8,128)(2,1)S(1)}, bf16[16,2,2,64,128]{4,3,2,1,0:T(8,128)(2,1)}, u32[]{:S(2)}, u32[]{:S(2)}) collective-permute-start(bf16[16,2,2,64,128]{4,3,2,1,0:T(8,128)(2,1)S(1)} %hold.14.own_ref), channel_id=1, source_target_pairs={{16,0},{32,16},{48,32},{64,48},{80,64},{96,80},{112,96},{17,1},{33... | collective-permute-start | bytes 3145736 | tf_op jit(solution)/shard_map/ppermute | solution.py:377
  110.4 41.2 %collective-permute-start.3 = (bf16[16,2,2,64,128]{4,3,2,1,0:T(8,128)(2,1)S(1)}, bf16[16,2,2,64,128]{4,3,2,1,0:T(8,128)(2,1)}, u32[]{:S(2)}, u32[]{:S(2)}) collective-permute-start(bf16[16,2,2,64,128]{4,3,2,1,0:T(8,128)(2,1)S(1)} %hold.14.own_ref), channel_id=1, source_target_pairs={{0,16},{16,32},{32,48},{48,64},{64,80},{80,96},{96,112},{1,17},{17... | collective-permute-start | bytes 3145736 | tf_op jit(solution)/shard_map/ppermute | solution.py:377
  117.2 34.4 %all-to-all-start.3 = ((bf16[16,2,64,128]{3,2,1,0:T(8,128)(2,1)}), bf16[16,2,64,128]{3,2,1,0:T(8,128)(2,1)S(1)}, u32[]{:S(2)}, u32[]{:S(2)}) async-start(bf16[16,2,64,128]{3,2,1,0:T(8,128)(2,1)} %hold.13), calls=%async_computation.3 | async-start | bytes 1048576 | tf_op jit(solution)/shard_map/all_to_all | solution.py:375
  129.8 9.9 %collective-permute-start.5 = (bf16[16,1,64,128]{3,2,1,0:T(8,128)(2,1)S(1)}, bf16[16,1,64,128]{3,2,1,0:T(8,128)(2,1)S(1)}, u32[]{:S(2)}, u32[]{:S(2)}) collective-permute-start(bf16[16,1,64,128]{3,2,1,0:T(8,128)(2,1)S(1)} %get-tuple-element.23), channel_id=1, source_target_pairs={{48,112},{49,113},{50,114},{51,115},{52,116},{53,117},{54,118},{55... | collective-permute-start | bytes 786440 | tf_op jit(solution)/shard_map/ppermute | solution.py:400
  139.7 0.6 copy-start.16
  151.6 0.7 copy-start.17
  161.2 0.7 copy-start.14
  161.9 2.5 copy-start.1
  164.4 2.4 copy-start.7
  164.4 2.3 copy-start.2
  166.8 70.0 %collective-permute-start.12 = (bf16[4,2,2,256,640]{4,3,2,1,0:T(8,128)(2,1)}, bf16[4,2,2,256,640]{4,3,2,1,0:T(8,128)(2,1)}, u32[]{:S(2)}, u32[]{:S(2)}) collective-permute-start(bf16[4,2,2,256,640]{4,3,2,1,0:T(8,128)(2,1)} %copy-done.2), channel_id=1, source_target_pairs={{0,1},{1,0},{2,3},{3,2},{4,5},{5,4},{6,7},{7,6},{8,9},{9,8},{10,11... | collective-permute-start | bytes 15728648 | tf_op jit(solution)/shard_map/ppermute | solution.py:408
  167.7 31.3 %all-to-all-start.5 = ((bf16[16,2,64,128]{3,2,1,0:T(8,128)(2,1)}), bf16[16,2,64,128]{3,2,1,0:T(8,128)(2,1)S(1)}, u32[]{:S(2)}, u32[]{:S(2)}) async-start(bf16[16,2,64,128]{3,2,1,0:T(8,128)(2,1)} %pad_maximum_fusion.rest_1_), calls=%async_computation.5 | async-start | bytes 1048576 | tf_op jit(solution)/shard_map/all_to_all | solution.py:405
  172.6 12.6 %collective-permute-start.6 = (bf16[16,1,64,128]{3,2,1,0:T(8,128)(2,1)}, bf16[16,1,64,128]{3,2,1,0:T(8,128)(2,1)S(1)}, u32[]{:S(2)}, u32[]{:S(2)}) collective-permute-start(bf16[16,1,64,128]{3,2,1,0:T(8,128)(2,1)} %copy-done.14), channel_id=1, source_target_pairs={{48,112},{49,113},{50,114},{51,115},{52,116},{53,117},{54,118},{55... | collective-permute-start | bytes 786440 | tf_op jit(solution)/shard_map/ppermute | solution.py:404
  174.0 11.2 %copy-start.15 = (bf16[16,1,64,128]{3,2,1,0:T(8,128)(2,1)S(1)}, bf16[16,1,64,128]{3,2,1,0:T(8,128)(2,1)}, u32[]{:S(2)}) copy-start(bf16[16,1,64,128]{3,2,1,0:T(8,128)(2,1)} %copy-done.14) | copy-start | bytes 786436
  174.0 16.5 %collective-permute-start.7 = (bf16[1,64,5120]{2,1,0:T(8,128)(2,1)}, bf16[1,64,5120]{2,1,0:T(8,128)(2,1)S(1)}, u32[]{:S(2)}, u32[]{:S(2)}) collective-permute-start(bf16[1,64,5120]{2,1,0:T(8,128)(2,1)} %hold.15), channel_id=1, source_target_pairs={{0,16},{16,32},{32,48},{48,64},{64,80},{80,96},{96,112},{1,17},{17... | collective-permute-start | bytes 1966088 | tf_op jit(solution)/shard_map/ppermute | solution.py:406
  190.5 0.8 copy-start.8
  199.0 15.9 %all-to-all-start.4 = ((bf16[16,2,64,128]{3,2,1,0:T(8,128)(2,1)}), bf16[16,2,64,128]{3,2,1,0:T(8,128)(2,1)S(1)}, u32[]{:S(2)}, u32[]{:S(2)}) async-start(bf16[16,2,64,128]{3,2,1,0:T(8,128)(2,1)} %hold.16), calls=%async_computation.4 | async-start | bytes 1048576 | tf_op jit(solution)/shard_map/all_to_all | solution.py:411
  202.6 34.1 %copy-start.5 = (bf16[16,2,64,128]{3,2,1,0:T(8,128)(2,1)}, bf16[16,2,64,128]{3,2,1,0:T(8,128)(2,1)S(1)}, u32[]{:S(2)}) copy-start(bf16[16,2,64,128]{3,2,1,0:T(8,128)(2,1)S(1)} %hold.19.mine_ref) | copy-start | bytes 1572868
  202.6 14.3 %collective-permute-start.14 = (bf16[16,2,64,128]{3,2,1,0:T(8,128)(2,1)S(1)}, bf16[16,2,64,128]{3,2,1,0:T(8,128)(2,1)}, u32[]{:S(2)}, u32[]{:S(2)}) collective-permute-start(bf16[16,2,64,128]{3,2,1,0:T(8,128)(2,1)S(1)} %hold.19.mine_ref), channel_id=1, source_target_pairs={{16,0},{32,16},{48,32},{0,48},{80,64},{96,80},{112,96},{64,112},{1... | collective-permute-start | bytes 1572872 | tf_op jit(solution)/shard_map/ppermute | solution.py:392
  202.7 17.4 %collective-permute-start.13 = (bf16[16,2,64,128]{3,2,1,0:T(8,128)(2,1)S(1)}, bf16[16,2,64,128]{3,2,1,0:T(8,128)(2,1)}, u32[]{:S(2)}, u32[]{:S(2)}) collective-permute-start(bf16[16,2,64,128]{3,2,1,0:T(8,128)(2,1)S(1)} %hold.19.mine_ref), channel_id=1, source_target_pairs={{0,16},{16,32},{32,48},{48,0},{64,80},{80,96},{96,112},{112,64},{1... | collective-permute-start | bytes 1572872 | tf_op jit(solution)/shard_map/ppermute | solution.py:391
  214.9 30.1 %copy-start.18 = (bf16[16,2,64,128]{3,2,1,0:T(8,128)(2,1)}, bf16[16,2,64,128]{3,2,1,0:T(8,128)(2,1)S(1)}, u32[]{:S(2)}) copy-start(bf16[16,2,64,128]{3,2,1,0:T(8,128)(2,1)S(1)} %all-to-all-done.4.mine_ref) | copy-start | bytes 1572868
  214.9 14.9 %collective-permute-start.9 = (bf16[16,2,64,128]{3,2,1,0:T(8,128)(2,1)S(1)}, bf16[16,2,64,128]{3,2,1,0:T(8,128)(2,1)S(1)}, u32[]{:S(2)}, u32[]{:S(2)}) collective-permute-start(bf16[16,2,64,128]{3,2,1,0:T(8,128)(2,1)S(1)} %all-to-all-done.4.mine_ref), channel_id=1, source_target_pairs={{16,0},{32,16},{48,32},{0,48},{80,64},{96,80},{112,96},{64,112},{1... | collective-permute-start | bytes 1572872 | tf_op jit(solution)/shard_map/ppermute | solution.py:392
  214.9 16.1 %collective-permute-start.8 = (bf16[16,2,64,128]{3,2,1,0:T(8,128)(2,1)S(1)}, bf16[16,2,64,128]{3,2,1,0:T(8,128)(2,1)S(1)}, u32[]{:S(2)}, u32[]{:S(2)}) collective-permute-start(bf16[16,2,64,128]{3,2,1,0:T(8,128)(2,1)S(1)} %all-to-all-done.4.mine_ref), channel_id=1, source_target_pairs={{0,16},{16,32},{32,48},{48,0},{64,80},{80,96},{96,112},{112,64},{1... | collective-permute-start | bytes 1572872 | tf_op jit(solution)/shard_map/ppermute | solution.py:391
  218.6 16.9 %collective-permute-start.16 = (bf16[8,2,64,128]{3,2,1,0:T(8,128)(2,1)}, bf16[8,2,64,128]{3,2,1,0:T(8,128)(2,1)}, u32[]{:S(2)}, u32[]{:S(2)}) collective-permute-start(bf16[8,2,64,128]{3,2,1,0:T(8,128)(2,1)} %slice.28), channel_id=1, source_target_pairs={{16,0},{32,16},{48,32},{0,48},{80,64},{96,80},{112,96},{64,112},{1... | collective-permute-start | bytes 786440 | tf_op jit(solution)/shard_map/ppermute | solution.py:394
  221.7 15.0 %collective-permute-start.15 = (bf16[8,2,64,128]{3,2,1,0:T(8,128)(2,1)}, bf16[8,2,64,128]{3,2,1,0:T(8,128)(2,1)}, u32[]{:S(2)}, u32[]{:S(2)}) collective-permute-start(bf16[8,2,64,128]{3,2,1,0:T(8,128)(2,1)} %slice.27), channel_id=1, source_target_pairs={{0,16},{16,32},{32,48},{48,0},{64,80},{80,96},{96,112},{112,64},{1... | collective-permute-start | bytes 786440 | tf_op jit(solution)/shard_map/ppermute | solution.py:393
  229.8 15.3 %copy-start.19 = (bf16[16,2,64,128]{3,2,1,0:T(8,128)(2,1)}, bf16[16,2,64,128]{3,2,1,0:T(8,128)(2,1)S(1)}, u32[]{:S(2)}) copy-start(bf16[16,2,64,128]{3,2,1,0:T(8,128)(2,1)S(1)} %collective-permute-done.9.right_ref) | copy-start | bytes 1572868
  229.8 15.3 %collective-permute-start.11 = (bf16[8,2,64,128]{3,2,1,0:T(8,128)(2,1)S(1)}, bf16[8,2,64,128]{3,2,1,0:T(8,128)(2,1)S(1)}, u32[]{:S(2)}, u32[]{:S(2)}) collective-permute-start(bf16[8,2,64,128]{3,2,1,0:T(8,128)(2,1)S(1)} %slice.26), channel_id=1, source_target_pairs={{16,0},{32,16},{48,32},{0,48},{80,64},{96,80},{112,96},{64,112},{1... | collective-permute-start | bytes 786440 | tf_op jit(solution)/shard_map/ppermute | solution.py:394
  231.1 14.0 %copy-start.20 = (bf16[16,2,64,128]{3,2,1,0:T(8,128)(2,1)}, bf16[16,2,64,128]{3,2,1,0:T(8,128)(2,1)S(1)}, u32[]{:S(2)}) copy-start(bf16[16,2,64,128]{3,2,1,0:T(8,128)(2,1)S(1)} %collective-permute-done.8.left_ref) | copy-start | bytes 1572868
  231.1 14.0 %collective-permute-start.10 = (bf16[8,2,64,128]{3,2,1,0:T(8,128)(2,1)S(1)}, bf16[8,2,64,128]{3,2,1,0:T(8,128)(2,1)S(1)}, u32[]{:S(2)}, u32[]{:S(2)}) collective-permute-start(bf16[8,2,64,128]{3,2,1,0:T(8,128)(2,1)S(1)} %slice.25), channel_id=1, source_target_pairs={{0,16},{16,32},{32,48},{48,0},{64,80},{80,96},{96,112},{112,64},{1... | collective-permute-start | bytes 786440 | tf_op jit(solution)/shard_map/ppermute | solution.py:393
  245.1 0.7 copy-start.21
  245.8 0.7 copy-start.22
  255.0 18.8 %copy-start.9 = (bf16[1,64,5120]{2,1,0:T(8,128)(2,1)S(1)}, bf16[1,64,5120]{2,1,0:T(8,128)(2,1)}, u32[]{:S(2)}) copy-start(bf16[1,64,5120]{2,1,0:T(8,128)(2,1)} %copy-done.8) | copy-start | bytes 1966084
  255.0 18.8 %copy-start.12 = (bf16[64,5120]{1,0:T(8,128)(2,1)S(1)}, bf16[64,5120]{1,0:T(8,128)(2,1)}, u32[]{:S(2)}) copy-start(bf16[64,5120]{1,0:T(8,128)(2,1)} %entering_ref.1) | copy-start | bytes 1966084
Sparse Core Ops, SparseCore 0:
  21.7 29.4 all-gather.4
  81.0 57.1 all-gather.6

commit v9 on v7

--- a/solution.py
+++ b/solution.py
@@ -14,7 +14,7 @@
 SCALE_LOG2 = (HD ** -0.5) * 1.4426950408889634
 BLOCK_Q = 512
 VMEM = 28 * 1024 * 1024
-SMALL = pltpu.CompilerParams(vmem_limit_bytes=1024 * 1024)
+LARGE = pltpu.CompilerParams(vmem_limit_bytes=58 * 1024 * 1024)
 MEDIUM = pltpu.CompilerParams(vmem_limit_bytes=12 * 1024 * 1024)
 QUEUE = 8
 RING = 4
@@ -59,12 +59,12 @@
             kv_shape,
             jax.ShapeDtypeStruct((SPATIAL, frames, tok, group), queries.dtype),
         ],
-        compiler_params=MEDIUM,
+        compiler_params=LARGE,
         name="pack",
     )(queries, keys, values)
 
 
-def hold(array, *earlier):
+def hold(array, *earlier, room=1):
     def kernel(*refs):
         pass
 
@@ -75,7 +75,7 @@
         out_specs=ANY,
         out_shape=jax.ShapeDtypeStruct(array.shape, array.dtype),
         input_output_aliases={0: 0},
-        compiler_params=SMALL,
+        compiler_params=pltpu.CompilerParams(vmem_limit_bytes=room * 1024 * 1024),
         name="hold",
     )(array, *earlier)
 
@@ -262,7 +262,7 @@
             scratch_shapes=[pltpu.VMEM((RING * rows, groups * width), jnp.bfloat16)],
         ),
         out_shape=out_shape,
-        compiler_params=pltpu.CompilerParams(vmem_limit_bytes=VMEM),
+        compiler_params=pltpu.CompilerParams(vmem_limit_bytes=48 * 1024 * 1024),
         cost_estimate=pl.CostEstimate(
             flops=2 * RING * rows * groups * width * halves * cols_dev,
             bytes_accessed=8 * 1024 * 1024,
@@ -367,15 +367,15 @@
 
     kv0, kv1, query = pack(queries, keys, values)
     kv0 = to_heads(kv0)
-    kv1 = to_heads(hold(kv1, kv0, gates))
-    kv0 = hold(kv0, kv1)
+    kv1_heads = to_heads(hold(kv1, kv0, gates))
+    query = to_heads(hold(query, kv1_heads))
+    kv0 = hold(kv0, query)
     kv0_before, kv0_after = lax.ppermute(kv0, "queue", up), lax.ppermute(kv0, "queue", down)
-    query = to_heads(hold(query, kv1))
-    kv1 = hold(kv1, query)
+    kv1 = hold(kv1_heads, query)
     kv1_before, kv1_after = lax.ppermute(kv1, "queue", up), lax.ppermute(kv1, "queue", down)
 
     weight = lax.all_gather(out_weight, ("queue", "spatial"), axis_index_groups=along_y, axis=0)
-    weight = hold(weight, query)
+    weight = hold(weight, query, room=56)
     weight = lax.all_gather(weight, "spatial", axis_index_groups=along_z, axis=0)
     weight = weight.reshape(-1, 2, 2, *out_weight.shape)
 
@@ -401,7 +401,7 @@
     odd1, token = attend(1, *head1, token, odd0_crossing)
     odd1_crossing = lax.ppermute(odd1, "queue", cross)
     shifted = lax.ppermute(hold(hidden[frames - 1 :], kv1_before), "queue", up)
-    weight_own = hold(weight, token)
+    weight_own = hold(weight, token, room=56)
     weight_pair = lax.ppermute(weight_own, "spatial", swap_core)
     even1, token = attend(0, *head1, token)
     first_sources = spread(hold(first, token, shifted))

time: 267 us -> 267 us (level)
  local copies, waits for them, and re-layouts: 24.6 us -> 14.1 us
  Pallas kernels: 48 us -> 53.5 us
  waiting for transfers between devices: 101 us -> 105 us
  blocking collectives: 18.1 us -> 21.5 us
  starting transfers between devices: 57.6 us -> 54.4 us
    unnamed x53 -> x47, local copies, waits for them, and re-layouts: 21 us -> 10.5 us
    all_to_all x2, waiting for transfers between devices: 8.44 us -> 15.8 us  [returned(): return to_heads(jnp.concatenate((even, odd), axis=1))]
    pallas_call x1, Pallas kernels: 0.75 us -> 4.29 us  [pack(): pl.pallas_call(kernel, grid=(PACK,), in_specs=[spec] * 3, out_specs=[kv_s...]
    all_to_all x1, blocking collectives: 18.1 us -> 21.5 us  [body(): lax.all_to_all(branch, 'queue', split_axis=0, concat_axis=0, axis_index_g...]
    ppermute x2, waiting for transfers between devices: 4.97 us -> 1.7 us  [spread(): far_low = lax.ppermute(left[:SPATIAL // 2], 'queue', ring_up)]
    all_to_all x2, starting transfers between devices: 12.1 us -> 8.84 us  [returned(): return to_heads(jnp.concatenate((even, odd), axis=1))]
  transfers between devices with their start and end apart: 24 -> 24, of which waited for: 12 -> 14; matrix products, arithmetic and copies ran while one was open for 2% -> 3% of each run, Pallas kernels for 14% -> 15%
where the time goes in v9:
time: 267 us; the launch traced here: 266 us
  waiting for transfers between devices  105 us (39%)
  starting transfers between devices  54.4 us (20%)
  Pallas kernels  53.5 us (20%)
  blocking collectives  21.5 us (8%)
  local copies, waits for them, and re-layouts  14.1 us (5%)
  between operations  13.8 us (5%)
  other arithmetic  2.89 us (1%)
    pallas_call x4, Pallas kernels, attend(): pl.pallas_call(kernel, grid_spec=pltpu.PrefetchScalarGridSpec(num_scalar_...  31.4 us
    all_to_all x1, blocking collectives, body(): lax.all_to_all(branch, 'queue', split_axis=0, concat_axis=0, axis_index_g...  21.5 us
    all_to_all x1, waiting for transfers between devices, body(): kv1_heads = to_heads(hold(kv1, kv0, gates))  17.2 us
    ppermute x1, waiting for transfers between devices, body(): lax.ppermute(kv0, 'queue', up)  16.2 us
    all_to_all x2, waiting for transfers between devices, returned(): return to_heads(jnp.concatenate((even, odd), axis=1))  15.8 us
    ppermute x1, waiting for transfers between devices, body(): other_gates = lax.ppermute(gates, 'queue', swap_low)  13.3 us
    pallas_call x2, Pallas kernels, project(): pl.pallas_call(kernel, grid_spec=pltpu.PrefetchScalarGridSpec(num_scalar_...  13.3 us
    unnamed x47, local copies, waits for them, and re-layouts  10.5 us
  transfers between devices with their start and end apart: 24, of which 14 were waited for; matrix products, arithmetic and copies ran while one was open for 3% of the time, Pallas kernels for 15%

profile of v9, /device:TPU:0, one launch (start us, length us, event | category | flops | bytes accessed | tf_op | source)
XLA Modules:
  0.0 265.7 jit_solution(10751781406574231262)
XLA Ops:
  6.5 4.3 %pack.1 = (bf16[16,2,2,64,128]{4,3,2,1,0:T(8,128)(2,1)}, bf16[16,2,2,64,128]{4,3,2,1,0:T(8,128)(2,1)}, bf16[16,2,64,256]{3,2,1,0:T(8,128)(2,1)}) custom-call(bf16[2,64,4096]{2,1,0:T(8,128)(2,1)} %q_ref.1, bf16[2,64,4096]{2,1,0:T(8,128)(2,1)} %k_ref.1, bf16[2,64,4096]{2,1,0:T(8,128)(2,1)} %v_ref.1), custom_call_target="tpu_custom_call" | custom-call | tf_op jit(solution)/shard_map/pack/pallas_call | solution.py:52
  10.8 8.3 %all-to-all-start = ((bf16[16,2,2,64,128]{4,3,2,1,0:T(8,128)(2,1)}), bf16[16,2,2,64,128]{4,3,2,1,0:T(8,128)(2,1)S(1)}, u32[]{:S(2)}, u32[]{:S(2)}) async-start(bf16[16,2,2,64,128]{4,3,2,1,0:T(8,128)(2,1)} %get-tuple-element.18), calls=%async_computation | async-start | bytes 2097152 | tf_op jit(solution)/shard_map/all_to_all | solution.py:369
  19.1 0.2 fusion
  19.4 0.8 collective-permute-start
  20.1 13.3 %collective-permute-done = f32[16,640]{1,0:T(8,128)S(1)} collective-permute-done((f32[16,640]{1,0:T(8,128)S(1)}, f32[16,640]{1,0:T(8,128)S(1)}, u32[]{:S(2)}, u32[]{:S(2)}) %collective-permute-start) | collective-permute-done | bytes 40992 | tf_op jit(solution)/shard_map/ppermute | solution.py:358
  33.4 0.1 dynamic-slice_select_fusion.refs_2_.rest_1_
  33.5 4.0 %all-to-all-done.refs_1_.refs_0_ = bf16[16,2,2,64,128]{4,3,2,1,0:T(8,128)(2,1)S(1)} async-done(((bf16[16,2,2,64,128]{4,3,2,1,0:T(8,128)(2,1)}), bf16[16,2,2,64,128]{4,3,2,1,0:T(8,128)(2,1)S(1)}, u32[]{:S(2)}, u32[]{:S(2)}) %all-to-all-start) | async-done | bytes 1048608 | tf_op jit(solution)/shard_map/all_to_all | solution.py:369
  37.5 1.0 copy-done.6
  38.5 3.8 %all-to-all-start.1 = ((bf16[16,2,2,64,128]{4,3,2,1,0:T(8,128)(2,1)}), bf16[16,2,2,64,128]{4,3,2,1,0:T(8,128)(2,1)S(1)}, u32[]{:S(2)}, u32[]{:S(2)}) async-start(bf16[16,2,2,64,128]{4,3,2,1,0:T(8,128)(2,1)} %copy-done.6), calls=%async_computation.1 | async-start | bytes 2097152 | tf_op jit(solution)/shard_map/all_to_all | solution.py:370
  42.4 0.7 all-gather.5.cloned.1.call-update
  43.0 17.2 %all-to-all-done.1.refs_1_.refs_0_ = bf16[16,2,2,64,128]{4,3,2,1,0:T(8,128)(2,1)S(1)} async-done(((bf16[16,2,2,64,128]{4,3,2,1,0:T(8,128)(2,1)}), bf16[16,2,2,64,128]{4,3,2,1,0:T(8,128)(2,1)S(1)}, u32[]{:S(2)}, u32[]{:S(2)}) %all-to-all-start.1) | async-done | bytes 1048608 | tf_op jit(solution)/shard_map/all_to_all | solution.py:370
  60.3 1.0 copy-done.4
  61.3 3.7 %all-to-all-start.2 = ((bf16[16,2,64,256]{3,2,1,0:T(8,128)(2,1)}), bf16[16,2,64,256]{3,2,1,0:T(8,128)(2,1)S(1)}, u32[]{:S(2)}, u32[]{:S(2)}) async-start(bf16[16,2,64,256]{3,2,1,0:T(8,128)(2,1)} %copy-done.4), calls=%async_computation.2 | async-start | bytes 2097152 | tf_op jit(solution)/shard_map/all_to_all | solution.py:371
  65.0 8.9 %all-gather.5.cloned.1.call-done = bf16[1024,640]{1,0:T(8,128)(2,1)} async-done(((bf16[256,640]{1,0:T(8,128)(2,1)}), bf16[1024,640]{1,0:T(8,128)(2,1)}) %all-gather.5.cloned.1.call-update) | async-done | bytes 1310736 | tf_op jit(solution)/shard_map/all_gather | solution.py:377
  73.9 10.3 %all-to-all-done.2.refs_1_.q_ref = bf16[16,2,64,256]{3,2,1,0:T(8,128)(2,1)S(1)} async-done(((bf16[16,2,64,256]{3,2,1,0:T(8,128)(2,1)}), bf16[16,2,64,256]{3,2,1,0:T(8,128)(2,1)S(1)}, u32[]{:S(2)}, u32[]{:S(2)}) %all-to-all-start.2) | async-done | bytes 1048608 | tf_op jit(solution)/shard_map/all_to_all | solution.py:371
  84.2 1.0 copy-done.1
  85.2 0.7 hold.12
  85.9 1.2 copy-done.2
  87.1 3.4 %collective-permute-start.3 = (bf16[16,2,2,64,128]{4,3,2,1,0:T(8,128)(2,1)S(1)}, bf16[16,2,2,64,128]{4,3,2,1,0:T(8,128)(2,1)S(1)}, u32[]{:S(2)}, u32[]{:S(2)}) collective-permute-start(bf16[16,2,2,64,128]{4,3,2,1,0:T(8,128)(2,1)S(1)} %hold.11.own_ref), channel_id=1, source_target_pairs={{0,16},{16,32},{32,48},{48,64},{64,80},{80,96},{96,112},{1,17},{17... | collective-permute-start | bytes 3145736 | tf_op jit(solution)/shard_map/ppermute | solution.py:373
  90.5 1.3 collective-permute-start.4
  91.8 4.6 %collective-permute-start.1 = (bf16[16,2,2,64,128]{4,3,2,1,0:T(8,128)(2,1)S(1)}, bf16[16,2,2,64,128]{4,3,2,1,0:T(8,128)(2,1)S(1)}, u32[]{:S(2)}, u32[]{:S(2)}) collective-permute-start(bf16[16,2,2,64,128]{4,3,2,1,0:T(8,128)(2,1)S(1)} %hold.10.own_ref), channel_id=1, source_target_pairs={{0,16},{16,32},{32,48},{48,64},{64,80},{80,96},{96,112},{1,17},{17... | collective-permute-start | bytes 3145736 | tf_op jit(solution)/shard_map/ppermute | solution.py:375
  96.5 1.3 collective-permute-start.2
  97.8 16.2 %collective-permute-done.3.before_ref = bf16[16,2,2,64,128]{4,3,2,1,0:T(8,128)(2,1)S(1)} collective-permute-done((bf16[16,2,2,64,128]{4,3,2,1,0:T(8,128)(2,1)S(1)}, bf16[16,2,2,64,128]{4,3,2,1,0:T(8,128)(2,1)S(1)}, u32[]{:S(2)}, u32[]{:S(2)}) %collective-permute-start.3) | collective-permute-done | bytes 1048608 | tf_op jit(solution)/shard_map/ppermute | solution.py:373
  114.0 4.5 %collective-permute-done.4.after_ref = bf16[16,2,2,64,128]{4,3,2,1,0:T(8,128)(2,1)S(1)} collective-permute-done((bf16[16,2,2,64,128]{4,3,2,1,0:T(8,128)(2,1)S(1)}, bf16[16,2,2,64,128]{4,3,2,1,0:T(8,128)(2,1)S(1)}, u32[]{:S(2)}, u32[]{:S(2)}) %collective-permute-start.4) | collective-permute-done | bytes 1048608 | tf_op jit(solution)/shard_map/ppermute | solution.py:373
  118.5 7.6 %attend.4 = (bf16[16,1,64,128]{3,2,1,0:T(8,128)(2,1)S(1)}, f32[8,128]{1,0:T(8,128)S(1)}) custom-call(s32[1]{0:T(128)} %bitcast.pos_ref, bf16[16,2,64,256]{3,2,1,0:T(8,128)(2,1)S(1)} %copy-done.2, bf16[16,2,2,64,128]{4,3,2,1,0:T(8,128)(2,1)S(1)} %hold.11.own_ref, bf16[16,2,2,64,128]{4,3,2,1,0:T(8,128)(2,1)S(1)} %collective-permute-done.3.before_ref, ...), custom_call_target="tpu_custom_call" | custom-call | flops 5368709120 | bytes 4194304 | tf_op jit(solution)/shard_map/attend/pallas_call | solution.py:161
  126.2 0.9 collective-permute-start.5
  127.0 7.8 %attend.5 = (bf16[16,1,64,128]{3,2,1,0:T(8,128)(2,1)S(1)}, f32[8,128]{1,0:T(8,128)S(1)}) custom-call(s32[1]{0:T(128)} %bitcast.pos_ref, bf16[16,2,64,256]{3,2,1,0:T(8,128)(2,1)S(1)} %copy-done.2, bf16[16,2,2,64,128]{4,3,2,1,0:T(8,128)(2,1)S(1)} %hold.11.own_ref, bf16[16,2,2,64,128]{4,3,2,1,0:T(8,128)(2,1)S(1)} %collective-permute-done.3.before_ref, ...), custom_call_target="tpu_custom_call" | custom-call | flops 5368709120 | bytes 4194304 | tf_op jit(solution)/shard_map/attend/pallas_call | solution.py:161
  134.8 0.7 copy-done.16
  135.5 4.1 %collective-permute-done.2.after_ref = bf16[16,2,2,64,128]{4,3,2,1,0:T(8,128)(2,1)S(1)} collective-permute-done((bf16[16,2,2,64,128]{4,3,2,1,0:T(8,128)(2,1)S(1)}, bf16[16,2,2,64,128]{4,3,2,1,0:T(8,128)(2,1)S(1)}, u32[]{:S(2)}, u32[]{:S(2)}) %collective-permute-start.2) | collective-permute-done | bytes 1048608 | tf_op jit(solution)/shard_map/ppermute | solution.py:375
  139.6 8.3 %attend.6 = (bf16[16,1,64,128]{3,2,1,0:T(8,128)(2,1)}, f32[8,128]{1,0:T(8,128)S(1)}) custom-call(s32[1]{0:T(128)} %bitcast.pos_ref, bf16[16,2,64,256]{3,2,1,0:T(8,128)(2,1)S(1)} %copy-done.2, bf16[16,2,2,64,128]{4,3,2,1,0:T(8,128)(2,1)S(1)} %hold.10.own_ref, bf16[16,2,2,64,128]{4,3,2,1,0:T(8,128)(2,1)S(1)} %collective-permute-done.1.before_ref.refs_1_, ...), custom_call_target="tpu_custom_call" | custom-call | flops 5368709120 | bytes 4194304 | tf_op jit(solution)/shard_map/attend/pallas_call | solution.py:161
  147.9 1.0 copy-done.8
  148.9 0.7 copy-done.14
  149.6 0.6 copy-done.18
  150.2 1.0 copy-done.20
  151.1 0.7 hold.13.wo_ref
  151.8 2.1 slice.21.refs_0_
  154.0 4.3 %collective-permute-start.12 = (bf16[1,64,5120]{2,1,0:T(8,128)(2,1)}, bf16[1,64,5120]{2,1,0:T(8,128)(2,1)}, u32[]{:S(2)}, u32[]{:S(2)}) collective-permute-start(bf16[1,64,5120]{2,1,0:T(8,128)(2,1)} %hold.14), channel_id=1, source_target_pairs={{0,16},{16,32},{32,48},{48,64},{64,80},{80,96},{96,112},{1,17},{17... | collective-permute-start | bytes 1966088 | tf_op jit(solution)/shard_map/ppermute | solution.py:403
  158.3 0.9 pad_maximum_fusion.1
  159.2 4.8 %all-to-all-start.4 = ((bf16[16,2,64,128]{3,2,1,0:T(8,128)(2,1)}), bf16[16,2,64,128]{3,2,1,0:T(8,128)(2,1)S(1)}, u32[]{:S(2)}, u32[]{:S(2)}) async-start(bf16[16,2,64,128]{3,2,1,0:T(8,128)(2,1)} %pad_maximum_fusion.1), calls=%async_computation.4 | async-start | bytes 1048576 | tf_op jit(solution)/shard_map/all_to_all | solution.py:386
  164.0 0.9 collective-permute-start.6
  164.9 1.2 copy-done.10
  166.1 1.2 copy-done.21
  167.4 7.7 %attend.7 = (bf16[16,1,64,128]{3,2,1,0:T(8,128)(2,1)S(1)}, f32[8,128]{1,0:T(8,128)S(1)}) custom-call(s32[1]{0:T(128)} %bitcast.pos_ref, bf16[16,2,64,256]{3,2,1,0:T(8,128)(2,1)S(1)} %copy-done.2, bf16[16,2,2,64,128]{4,3,2,1,0:T(8,128)(2,1)S(1)} %hold.10.own_ref, bf16[16,2,2,64,128]{4,3,2,1,0:T(8,128)(2,1)S(1)} %copy-done.10, ...), custom_call_target="tpu_custom_call" | custom-call | flops 5368709120 | bytes 4194304 | tf_op jit(solution)/shard_map/attend/pallas_call | solution.py:161
  175.1 1.0 broadcast_select_fusion.1
  176.1 0.8 pad_maximum_fusion
  177.0 7.4 %all-to-all-done.4.refs_0_ = bf16[16,2,64,128]{3,2,1,0:T(8,128)(2,1)S(1)} async-done(((bf16[16,2,64,128]{3,2,1,0:T(8,128)(2,1)}), bf16[16,2,64,128]{3,2,1,0:T(8,128)(2,1)S(1)}, u32[]{:S(2)}, u32[]{:S(2)}) %all-to-all-start.4) | async-done | bytes 524320 | tf_op jit(solution)/shard_map/all_to_all | solution.py:386
  184.4 4.0 %all-to-all-start.3 = ((bf16[16,2,64,128]{3,2,1,0:T(8,128)(2,1)}), bf16[16,2,64,128]{3,2,1,0:T(8,128)(2,1)S(1)}, u32[]{:S(2)}, u32[]{:S(2)}) async-start(bf16[16,2,64,128]{3,2,1,0:T(8,128)(2,1)} %pad_maximum_fusion), calls=%async_computation.3 | async-start | bytes 1048576 | tf_op jit(solution)/shard_map/all_to_all | solution.py:386
  188.4 0.7 hold.15.mine_ref
  189.1 3.2 %collective-permute-start.14 = (bf16[16,2,64,128]{3,2,1,0:T(8,128)(2,1)S(1)}, bf16[16,2,64,128]{3,2,1,0:T(8,128)(2,1)S(1)}, u32[]{:S(2)}, u32[]{:S(2)}) collective-permute-start(bf16[16,2,64,128]{3,2,1,0:T(8,128)(2,1)S(1)} %hold.15.mine_ref), channel_id=1, source_target_pairs={{16,0},{32,16},{48,32},{0,48},{80,64},{96,80},{112,96},{64,112},{1... | collective-permute-start | bytes 1572872 | tf_op jit(solution)/shard_map/ppermute | solution.py:390
  192.3 8.4 %all-to-all-done.3.mine_ref = bf16[16,2,64,128]{3,2,1,0:T(8,128)(2,1)S(1)} async-done(((bf16[16,2,64,128]{3,2,1,0:T(8,128)(2,1)}), bf16[16,2,64,128]{3,2,1,0:T(8,128)(2,1)S(1)}, u32[]{:S(2)}, u32[]{:S(2)}) %all-to-all-start.3) | async-done | bytes 524320 | tf_op jit(solution)/shard_map/all_to_all | solution.py:386
  200.8 2.0 collective-permute-start.7
  202.8 2.2 collective-permute-done.13.left_ref
  205.0 0.7 slice.27
  205.8 0.7 slice.28
  206.5 3.2 %collective-permute-start.16 = (bf16[8,2,64,128]{3,2,1,0:T(8,128)(2,1)}, bf16[8,2,64,128]{3,2,1,0:T(8,128)(2,1)}, u32[]{:S(2)}, u32[]{:S(2)}) collective-permute-start(bf16[8,2,64,128]{3,2,1,0:T(8,128)(2,1)} %slice.28), channel_id=1, source_target_pairs={{16,0},{32,16},{48,32},{0,48},{80,64},{96,80},{112,96},{64,112},{1... | collective-permute-start | bytes 786440 | tf_op jit(solution)/shard_map/ppermute | solution.py:392
  209.7 6.1 %collective-permute-done.8.right_ref = bf16[16,2,64,128]{3,2,1,0:T(8,128)(2,1)S(1)} collective-permute-done((bf16[16,2,64,128]{3,2,1,0:T(8,128)(2,1)S(1)}, bf16[16,2,64,128]{3,2,1,0:T(8,128)(2,1)S(1)}, u32[]{:S(2)}, u32[]{:S(2)}) %collective-permute-start.8) | collective-permute-done | bytes 524320 | tf_op jit(solution)/shard_map/ppermute | solution.py:390
  215.9 3.8 %collective-permute-start.10 = (bf16[8,2,64,128]{3,2,1,0:T(8,128)(2,1)S(1)}, bf16[8,2,64,128]{3,2,1,0:T(8,128)(2,1)S(1)}, u32[]{:S(2)}, u32[]{:S(2)}) collective-permute-start(bf16[8,2,64,128]{3,2,1,0:T(8,128)(2,1)S(1)} %slice.26), channel_id=1, source_target_pairs={{16,0},{32,16},{48,32},{0,48},{80,64},{96,80},{112,96},{64,112},{1... | collective-permute-start | bytes 786440 | tf_op jit(solution)/shard_map/ppermute | solution.py:392
  219.7 0.1 collective-permute-start.9
  219.8 0.1 pad_add_fusion.place_ref
  219.8 1.7 collective-permute-done.15.low_ref
  221.6 6.6 %project_first.1.rest_0_ = f32[2,512,640]{2,1,0:T(8,128)S(1)} custom-call(s32[2]{0:T(128)S(1)} %pad_add_fusion.place_ref, bf16[16,2,64,128]{3,2,1,0:T(8,128)(2,1)S(1)} %hold.15.mine_ref, bf16[16,2,64,128]{3,2,1,0:T(8,128)(2,1)S(1)} %collective-permute-done.13.left_ref, bf16[16,2,64,128]{3,2,1,0:T(8,128)(2,1)S(1)} %collective-permute-done.14.right_ref, ...), custom_call_target="tpu_custom_call" | custom-call | flops 2684354560 | bytes 8388608 | tf_op jit(solution)/shard_map/project_first/pallas_call | solution.py:255
  228.2 6.7 %project_last.1 = bf16[8,2,64,640]{3,2,1,0:T(8,128)(2,1)S(1)} custom-call(s32[2]{0:T(128)S(1)} %pad_add_fusion.place_ref, bf16[16,2,64,128]{3,2,1,0:T(8,128)(2,1)S(1)} %all-to-all-done.3.mine_ref, bf16[16,2,64,128]{3,2,1,0:T(8,128)(2,1)S(1)} %collective-permute-done.7.left_ref, bf16[16,2,64,128]{3,2,1,0:T(8,128)(2,1)S(1)} %collective-permute-done.8.right_ref, ...), custom_call_target="tpu_custom_call" | custom-call | flops 2684354560 | bytes 8388608 | tf_op jit(solution)/shard_map/project_last/pallas_call | solution.py:255
  234.9 21.5 %all_to_all.30 = bf16[8,2,64,640]{3,2,1,0:T(8,128)(2,1)S(1)} all-to-all(bf16[8,2,64,640]{3,2,1,0:T(8,128)(2,1)S(1)} %project_last.1), channel_id=1, replica_groups={{0,16,32,48},{64,80,96,112},{1,17,33,49},{65,81,97,113},{2,18,34,50},{6..., dimensions={0} | all-to-all | bytes 2621440 | tf_op jit(solution)/shard_map/all_to_all | solution.py:412
  256.4 2.5 add_branch.1
  (65 shorter events, 0.4 us)
Async XLA Ops:
  6.5 12.6 %copy-start = (f32[50,640]{1,0:T(8,128)S(1)}, f32[50,640]{1,0:T(8,128)}, u32[]{:S(2)}) copy-start(f32[50,640]{1,0:T(8,128)} %param.13) | copy-start | bytes 384004
  10.8 8.3 %copy-start.22 = (s32[16]{0:T(128)S(1)}, s32[16]{0:T(128)}, u32[]{:S(2)}) copy-start(s32[16]{0:T(128)} %param.14) | copy-start | bytes 196
  10.8 26.7 %copy-start.5 = (bf16[16,2,2,64,128]{4,3,2,1,0:T(8,128)(2,1)S(1)}, bf16[16,2,2,64,128]{4,3,2,1,0:T(8,128)(2,1)}, u32[]{:S(2)}) copy-start(bf16[16,2,2,64,128]{4,3,2,1,0:T(8,128)(2,1)} %get-tuple-element.17.refs_0_) | copy-start | bytes 3145732
  10.8 26.7 %all-to-all-start = ((bf16[16,2,2,64,128]{4,3,2,1,0:T(8,128)(2,1)}), bf16[16,2,2,64,128]{4,3,2,1,0:T(8,128)(2,1)S(1)}, u32[]{:S(2)}, u32[]{:S(2)}) async-start(bf16[16,2,2,64,128]{4,3,2,1,0:T(8,128)(2,1)} %get-tuple-element.18), calls=%async_computation | async-start | bytes 2097152 | tf_op jit(solution)/shard_map/all_to_all | solution.py:369
  19.4 14.0 %collective-permute-start = (f32[16,640]{1,0:T(8,128)S(1)}, f32[16,640]{1,0:T(8,128)S(1)}, u32[]{:S(2)}, u32[]{:S(2)}) collective-permute-start(f32[16,640]{1,0:T(8,128)S(1)} %fusion), channel_id=1, source_target_pairs={{0,64},{16,80},{32,96},{48,112},{64,0},{80,16},{96,32},{112,48},{1... | collective-permute-start | bytes 122888 | tf_op jit(solution)/shard_map/ppermute | solution.py:358
  37.5 1.0 copy-start.6
  38.5 21.8 %copy-start.3 = (bf16[16,2,64,256]{3,2,1,0:T(8,128)(2,1)S(1)}, bf16[16,2,64,256]{3,2,1,0:T(8,128)(2,1)}, u32[]{:S(2)}) copy-start(bf16[16,2,64,256]{3,2,1,0:T(8,128)(2,1)} %get-tuple-element.16.refs_0_) | copy-start | bytes 3145732
  38.5 21.8 %all-to-all-start.1 = ((bf16[16,2,2,64,128]{4,3,2,1,0:T(8,128)(2,1)}), bf16[16,2,2,64,128]{4,3,2,1,0:T(8,128)(2,1)S(1)}, u32[]{:S(2)}, u32[]{:S(2)}) async-start(bf16[16,2,2,64,128]{4,3,2,1,0:T(8,128)(2,1)} %copy-done.6), calls=%async_computation.1 | async-start | bytes 2097152 | tf_op jit(solution)/shard_map/all_to_all | solution.py:370
  42.3 31.6 %all-gather.5.cloned.1.call-start = ((), (), s32[]{:S(2)}) async-start(), calls=%async_computation.6 | async-start | bytes 1638400 | tf_op jit(solution)/shard_map/all_gather | solution.py:377
  60.3 1.0 copy-start.4
  61.3 22.9 %all-to-all-start.2 = ((bf16[16,2,64,256]{3,2,1,0:T(8,128)(2,1)}), bf16[16,2,64,256]{3,2,1,0:T(8,128)(2,1)S(1)}, u32[]{:S(2)}, u32[]{:S(2)}) async-start(bf16[16,2,64,256]{3,2,1,0:T(8,128)(2,1)} %copy-done.4), calls=%async_computation.2 | async-start | bytes 2097152 | tf_op jit(solution)/shard_map/all_to_all | solution.py:371
  64.9 86.2 %all-gather.7.cloned.1.call-start = ((), (), s32[]{:S(2)}) async-start(), calls=%async_computation.7 | async-start | bytes 6553600 | tf_op jit(solution)/shard_map/all_gather | solution.py:379
  84.2 1.0 copy-start.1
  85.9 1.2 copy-start.2
  87.1 26.9 %collective-permute-start.3 = (bf16[16,2,2,64,128]{4,3,2,1,0:T(8,128)(2,1)S(1)}, bf16[16,2,2,64,128]{4,3,2,1,0:T(8,128)(2,1)S(1)}, u32[]{:S(2)}, u32[]{:S(2)}) collective-permute-start(bf16[16,2,2,64,128]{4,3,2,1,0:T(8,128)(2,1)S(1)} %hold.11.own_ref), channel_id=1, source_target_pairs={{0,16},{16,32},{32,48},{48,64},{64,80},{80,96},{96,112},{1,17},{17... | collective-permute-start | bytes 3145736 | tf_op jit(solution)/shard_map/ppermute | solution.py:373
  90.5 28.0 %collective-permute-start.4 = (bf16[16,2,2,64,128]{4,3,2,1,0:T(8,128)(2,1)S(1)}, bf16[16,2,2,64,128]{4,3,2,1,0:T(8,128)(2,1)S(1)}, u32[]{:S(2)}, u32[]{:S(2)}) collective-permute-start(bf16[16,2,2,64,128]{4,3,2,1,0:T(8,128)(2,1)S(1)} %hold.11.own_ref), channel_id=1, source_target_pairs={{16,0},{32,16},{48,32},{64,48},{80,64},{96,80},{112,96},{17,1},{33... | collective-permute-start | bytes 3145736 | tf_op jit(solution)/shard_map/ppermute | solution.py:373
  91.8 43.6 %collective-permute-start.1 = (bf16[16,2,2,64,128]{4,3,2,1,0:T(8,128)(2,1)S(1)}, bf16[16,2,2,64,128]{4,3,2,1,0:T(8,128)(2,1)S(1)}, u32[]{:S(2)}, u32[]{:S(2)}) collective-permute-start(bf16[16,2,2,64,128]{4,3,2,1,0:T(8,128)(2,1)S(1)} %hold.10.own_ref), channel_id=1, source_target_pairs={{0,16},{16,32},{32,48},{48,64},{64,80},{80,96},{96,112},{1,17},{17... | collective-permute-start | bytes 3145736 | tf_op jit(solution)/shard_map/ppermute | solution.py:375
  96.5 43.2 %collective-permute-start.2 = (bf16[16,2,2,64,128]{4,3,2,1,0:T(8,128)(2,1)S(1)}, bf16[16,2,2,64,128]{4,3,2,1,0:T(8,128)(2,1)S(1)}, u32[]{:S(2)}, u32[]{:S(2)}) collective-permute-start(bf16[16,2,2,64,128]{4,3,2,1,0:T(8,128)(2,1)S(1)} %hold.10.own_ref), channel_id=1, source_target_pairs={{16,0},{32,16},{48,32},{64,48},{80,64},{96,80},{112,96},{17,1},{33... | collective-permute-start | bytes 3145736 | tf_op jit(solution)/shard_map/ppermute | solution.py:375
  126.1 8.6 %copy-start.12 = (bf16[16,1,64,128]{3,2,1,0:T(8,128)(2,1)}, bf16[16,1,64,128]{3,2,1,0:T(8,128)(2,1)S(1)}, u32[]{:S(2)}) copy-start(bf16[16,1,64,128]{3,2,1,0:T(8,128)(2,1)S(1)} %get-tuple-element.21) | copy-start | bytes 786436
  126.2 13.5 %collective-permute-start.5 = (bf16[16,1,64,128]{3,2,1,0:T(8,128)(2,1)S(1)}, bf16[16,1,64,128]{3,2,1,0:T(8,128)(2,1)S(1)}, u32[]{:S(2)}, u32[]{:S(2)}) collective-permute-start(bf16[16,1,64,128]{3,2,1,0:T(8,128)(2,1)S(1)} %get-tuple-element.21), channel_id=1, source_target_pairs={{48,112},{49,113},{50,114},{51,115},{52,116},{53,117},{54,118},{55... | collective-permute-start | bytes 786440 | tf_op jit(solution)/shard_map/ppermute | solution.py:398
  134.8 0.7 copy-start.16
  147.9 1.0 copy-start.8
  148.9 0.7 copy-start.14
  149.6 0.6 copy-start.18
  150.2 1.0 copy-start.20
  151.8 2.1 copy-start.9
  151.8 69.8 %collective-permute-start.11 = (bf16[4,2,2,256,640]{4,3,2,1,0:T(8,128)(2,1)}, bf16[4,2,2,256,640]{4,3,2,1,0:T(8,128)(2,1)}, u32[]{:S(2)}, u32[]{:S(2)}) collective-permute-start(bf16[4,2,2,256,640]{4,3,2,1,0:T(8,128)(2,1)} %hold.13.wo_ref), channel_id=1, source_target_pairs={{0,1},{1,0},{2,3},{3,2},{4,5},{5,4},{6,7},{7,6},{8,9},{9,8},{10,11... | collective-permute-start | bytes 15728648 | tf_op jit(solution)/shard_map/ppermute | solution.py:405
  153.9 4.4 %copy-start.13 = (bf16[16,1,64,128]{3,2,1,0:T(8,128)(2,1)S(1)}, bf16[16,1,64,128]{3,2,1,0:T(8,128)(2,1)}, u32[]{:S(2)}) copy-start(bf16[16,1,64,128]{3,2,1,0:T(8,128)(2,1)} %copy-done.12) | copy-start | bytes 786436
  153.9 4.4 %copy-start.15 = (bf16[16,1,64,128]{3,2,1,0:T(8,128)(2,1)S(1)}, bf16[16,1,64,128]{3,2,1,0:T(8,128)(2,1)}, u32[]{:S(2)}) copy-start(bf16[16,1,64,128]{3,2,1,0:T(8,128)(2,1)} %copy-done.14) | copy-start | bytes 786436
  153.9 4.4 %copy-start.17 = (bf16[16,1,64,128]{3,2,1,0:T(8,128)(2,1)S(1)}, bf16[16,1,64,128]{3,2,1,0:T(8,128)(2,1)}, u32[]{:S(2)}) copy-start(bf16[16,1,64,128]{3,2,1,0:T(8,128)(2,1)} %copy-done.16) | copy-start | bytes 786436
  154.0 11.0 %copy-start.19 = (f32[8,128]{1,0:T(8,128)S(1)}, f32[8,128]{1,0:T(8,128)}, u32[]{:S(2)}) copy-start(f32[8,128]{1,0:T(8,128)} %copy-done.18) | copy-start | bytes 12292
  154.0 34.4 %collective-permute-start.12 = (bf16[1,64,5120]{2,1,0:T(8,128)(2,1)}, bf16[1,64,5120]{2,1,0:T(8,128)(2,1)}, u32[]{:S(2)}, u32[]{:S(2)}) collective-permute-start(bf16[1,64,5120]{2,1,0:T(8,128)(2,1)} %hold.14), channel_id=1, source_target_pairs={{0,16},{16,32},{32,48},{48,64},{64,80},{80,96},{96,112},{1,17},{17... | collective-permute-start | bytes 1966088 | tf_op jit(solution)/shard_map/ppermute | solution.py:403
  159.2 25.2 %all-to-all-start.4 = ((bf16[16,2,64,128]{3,2,1,0:T(8,128)(2,1)}), bf16[16,2,64,128]{3,2,1,0:T(8,128)(2,1)S(1)}, u32[]{:S(2)}, u32[]{:S(2)}) async-start(bf16[16,2,64,128]{3,2,1,0:T(8,128)(2,1)} %pad_maximum_fusion.1), calls=%async_computation.4 | async-start | bytes 1048576 | tf_op jit(solution)/shard_map/all_to_all | solution.py:386
  164.0 11.1 %collective-permute-start.6 = (bf16[16,1,64,128]{3,2,1,0:T(8,128)(2,1)}, bf16[16,1,64,128]{3,2,1,0:T(8,128)(2,1)S(1)}, u32[]{:S(2)}, u32[]{:S(2)}) collective-permute-start(bf16[16,1,64,128]{3,2,1,0:T(8,128)(2,1)} %get-tuple-element.24), channel_id=1, source_target_pairs={{48,112},{49,113},{50,114},{51,115},{52,116},{53,117},{54,118},{55... | collective-permute-start | bytes 786440 | tf_op jit(solution)/shard_map/ppermute | solution.py:402
  164.9 1.2 copy-start.10
  166.1 1.2 copy-start.21
  184.4 16.4 %all-to-all-start.3 = ((bf16[16,2,64,128]{3,2,1,0:T(8,128)(2,1)}), bf16[16,2,64,128]{3,2,1,0:T(8,128)(2,1)S(1)}, u32[]{:S(2)}, u32[]{:S(2)}) async-start(bf16[16,2,64,128]{3,2,1,0:T(8,128)(2,1)} %pad_maximum_fusion), calls=%async_computation.3 | async-start | bytes 1048576 | tf_op jit(solution)/shard_map/all_to_all | solution.py:386
  189.1 15.9 %collective-permute-start.13 = (bf16[16,2,64,128]{3,2,1,0:T(8,128)(2,1)S(1)}, bf16[16,2,64,128]{3,2,1,0:T(8,128)(2,1)S(1)}, u32[]{:S(2)}, u32[]{:S(2)}) collective-permute-start(bf16[16,2,64,128]{3,2,1,0:T(8,128)(2,1)S(1)} %hold.15.mine_ref), channel_id=1, source_target_pairs={{0,16},{16,32},{32,48},{48,0},{64,80},{80,96},{96,112},{112,64},{1... | collective-permute-start | bytes 1572872 | tf_op jit(solution)/shard_map/ppermute | solution.py:389
  189.1 16.7 %collective-permute-start.14 = (bf16[16,2,64,128]{3,2,1,0:T(8,128)(2,1)S(1)}, bf16[16,2,64,128]{3,2,1,0:T(8,128)(2,1)S(1)}, u32[]{:S(2)}, u32[]{:S(2)}) collective-permute-start(bf16[16,2,64,128]{3,2,1,0:T(8,128)(2,1)S(1)} %hold.15.mine_ref), channel_id=1, source_target_pairs={{16,0},{32,16},{48,32},{0,48},{80,64},{96,80},{112,96},{64,112},{1... | collective-permute-start | bytes 1572872 | tf_op jit(solution)/shard_map/ppermute | solution.py:390
  200.8 15.1 %collective-permute-start.8 = (bf16[16,2,64,128]{3,2,1,0:T(8,128)(2,1)S(1)}, bf16[16,2,64,128]{3,2,1,0:T(8,128)(2,1)S(1)}, u32[]{:S(2)}, u32[]{:S(2)}) collective-permute-start(bf16[16,2,64,128]{3,2,1,0:T(8,128)(2,1)S(1)} %all-to-all-done.3.mine_ref), channel_id=1, source_target_pairs={{16,0},{32,16},{48,32},{0,48},{80,64},{96,80},{112,96},{64,112},{1... | collective-permute-start | bytes 1572872 | tf_op jit(solution)/shard_map/ppermute | solution.py:390
  200.8 18.9 %collective-permute-start.7 = (bf16[16,2,64,128]{3,2,1,0:T(8,128)(2,1)S(1)}, bf16[16,2,64,128]{3,2,1,0:T(8,128)(2,1)S(1)}, u32[]{:S(2)}, u32[]{:S(2)}) collective-permute-start(bf16[16,2,64,128]{3,2,1,0:T(8,128)(2,1)S(1)} %all-to-all-done.3.mine_ref), channel_id=1, source_target_pairs={{0,16},{16,32},{32,48},{48,0},{64,80},{80,96},{96,112},{112,64},{1... | collective-permute-start | bytes 1572872 | tf_op jit(solution)/shard_map/ppermute | solution.py:389
  205.8 15.8 %collective-permute-start.15 = (bf16[8,2,64,128]{3,2,1,0:T(8,128)(2,1)}, bf16[8,2,64,128]{3,2,1,0:T(8,128)(2,1)}, u32[]{:S(2)}, u32[]{:S(2)}) collective-permute-start(bf16[8,2,64,128]{3,2,1,0:T(8,128)(2,1)} %slice.27), channel_id=1, source_target_pairs={{0,16},{16,32},{32,48},{48,0},{64,80},{80,96},{96,112},{112,64},{1... | collective-permute-start | bytes 786440 | tf_op jit(solution)/shard_map/ppermute | solution.py:391
  206.5 15.1 %collective-permute-start.16 = (bf16[8,2,64,128]{3,2,1,0:T(8,128)(2,1)}, bf16[8,2,64,128]{3,2,1,0:T(8,128)(2,1)}, u32[]{:S(2)}, u32[]{:S(2)}) collective-permute-start(bf16[8,2,64,128]{3,2,1,0:T(8,128)(2,1)} %slice.28), channel_id=1, source_target_pairs={{16,0},{32,16},{48,32},{0,48},{80,64},{96,80},{112,96},{64,112},{1... | collective-permute-start | bytes 786440 | tf_op jit(solution)/shard_map/ppermute | solution.py:392
  215.9 12.3 %collective-permute-start.10 = (bf16[8,2,64,128]{3,2,1,0:T(8,128)(2,1)S(1)}, bf16[8,2,64,128]{3,2,1,0:T(8,128)(2,1)S(1)}, u32[]{:S(2)}, u32[]{:S(2)}) collective-permute-start(bf16[8,2,64,128]{3,2,1,0:T(8,128)(2,1)S(1)} %slice.26), channel_id=1, source_target_pairs={{16,0},{32,16},{48,32},{0,48},{80,64},{96,80},{112,96},{64,112},{1... | collective-permute-start | bytes 786440 | tf_op jit(solution)/shard_map/ppermute | solution.py:392
  219.7 8.5 %collective-permute-start.9 = (bf16[8,2,64,128]{3,2,1,0:T(8,128)(2,1)S(1)}, bf16[8,2,64,128]{3,2,1,0:T(8,128)(2,1)S(1)}, u32[]{:S(2)}, u32[]{:S(2)}) collective-permute-start(bf16[8,2,64,128]{3,2,1,0:T(8,128)(2,1)S(1)} %slice.25), channel_id=1, source_target_pairs={{0,16},{16,32},{32,48},{48,0},{64,80},{80,96},{96,112},{112,64},{1... | collective-permute-start | bytes 786440 | tf_op jit(solution)/shard_map/ppermute | solution.py:391
  234.9 21.5 %copy-start.7 = (bf16[2,64,5120]{2,1,0:T(8,128)(2,1)S(1)}, bf16[2,64,5120]{2,1,0:T(8,128)(2,1)}, u32[]{:S(2)}) copy-start(bf16[2,64,5120]{2,1,0:T(8,128)(2,1)} %hidden_ref.1) | copy-start | bytes 3932164
  234.9 21.5 %copy-start.11 = (bf16[64,5120]{1,0:T(8,128)(2,1)S(1)}, bf16[64,5120]{1,0:T(8,128)(2,1)}, u32[]{:S(2)}) copy-start(bf16[64,5120]{1,0:T(8,128)(2,1)} %entering_ref.1) | copy-start | bytes 1966084
Sparse Core Ops, SparseCore 0:
  44.8 29.0 all-gather.4
  86.0 56.1 all-gather.6

commit v10 on v9

--- a/solution.py
+++ b/solution.py
@@ -32,13 +32,14 @@
     return pl.BlockSpec(block, lambda *at: (0,) * array.ndim)
 
 
-def pack(queries, keys, values):
+def pack(queries, keys, values, hidden):
     frames, tok, width = keys.shape
     group = width // SPATIAL
     piece = width // PACK
     count = SPATIAL // PACK
 
-    def kernel(q_ref, k_ref, v_ref, kv0_ref, kv1_ref, out_ref):
+    def kernel(q_ref, k_ref, v_ref, hidden_ref, kv0_ref, kv1_ref, out_ref, last_ref):
+        last_ref[...] = hidden_ref[...]
         for i in range(count):
             for head, kv_ref in enumerate((kv0_ref, kv1_ref)):
                 cols = slice(i * group + head * HD, i * group + (head + 1) * HD)
@@ -47,21 +48,28 @@
             out_ref[i] = q_ref[:, :, i * group : (i + 1) * group]
 
     spec = pl.BlockSpec((frames, tok, piece), lambda s: (0, 0, s))
+    part = hidden.shape[-1] // PACK
     kv_spec = pl.BlockSpec((count, 2, frames, tok, HD), lambda s: (s, 0, 0, 0, 0))
     kv_shape = jax.ShapeDtypeStruct((SPATIAL, 2, frames, tok, HD), keys.dtype)
     return pl.pallas_call(
         kernel,
         grid=(PACK,),
-        in_specs=[spec] * 3,
-        out_specs=[kv_spec, kv_spec, pl.BlockSpec((count, frames, tok, group), lambda s: (s, 0, 0, 0))],
+        in_specs=[spec] * 3 + [pl.BlockSpec((1, tok, part), lambda s: (frames - 1, 0, s))],
+        out_specs=[
+            kv_spec,
+            kv_spec,
+            pl.BlockSpec((count, frames, tok, group), lambda s: (s, 0, 0, 0)),
+            pl.BlockSpec((1, tok, part), lambda s: (0, 0, s)),
+        ],
         out_shape=[
             kv_shape,
             kv_shape,
             jax.ShapeDtypeStruct((SPATIAL, frames, tok, group), queries.dtype),
+            jax.ShapeDtypeStruct((1, *hidden.shape[1:]), hidden.dtype),
         ],
         compiler_params=LARGE,
         name="pack",
-    )(queries, keys, values)
+    )(queries, keys, values, hidden)
 
 
 def hold(array, *earlier, room=1):
@@ -365,7 +373,7 @@
         lax.dynamic_slice_in_dim(gates, y_low * count, count, axis=1),
     )
 
-    kv0, kv1, query = pack(queries, keys, values)
+    kv0, kv1, query, last_frame = pack(queries, keys, values, hidden)
     kv0 = to_heads(kv0)
     kv1_heads = to_heads(hold(kv1, kv0, gates))
     query = to_heads(hold(query, kv1_heads))
@@ -381,9 +389,9 @@
 
     cross = [(RING - 1, QUEUE - 1)]
 
-    def returned(even, odd, crossing):
+    def with_crossing(even, odd, crossing):
         odd = jnp.where(position == QUEUE - 1, crossing, odd)
-        return to_heads(jnp.concatenate((even, odd), axis=1))
+        return jnp.concatenate((even, odd), axis=1)
 
     def spread(mine):
         left = lax.ppermute(mine, "queue", ring_up)
@@ -397,15 +405,17 @@
     odd0, token = attend(1, *head0)
     odd0_crossing = lax.ppermute(odd0, "queue", cross)
     even0, token = attend(0, *head0, token)
-    first = returned(even0, odd0, odd0_crossing)
-    odd1, token = attend(1, *head1, token, odd0_crossing)
+    first = with_crossing(even0, odd0, odd0_crossing)
+    odd1, token = attend(1, *head1, token, first)
     odd1_crossing = lax.ppermute(odd1, "queue", cross)
-    shifted = lax.ppermute(hold(hidden[frames - 1 :], kv1_before), "queue", up)
+    first = hold(to_heads(first), token)
+    first_sources = spread(first)
+    shifted = lax.ppermute(hold(last_frame, kv1_before, token), "queue", up)
+    even1, token = attend(0, *head1, token, first)
     weight_own = hold(weight, token, room=56)
     weight_pair = lax.ppermute(weight_own, "spatial", swap_core)
-    even1, token = attend(0, *head1, token)
-    first_sources = spread(hold(first, token, shifted))
-    second_sources = spread(returned(even1, odd1, odd1_crossing))
+    second = to_heads(with_crossing(even1, odd1, odd1_crossing))
+    second_sources = spread(hold(second, shifted))
 
     partial = project(0, place, first_sources, weight_own, weight_pair, None, None)
     branch = project(1, place, second_sources, weight_own, weight_pair, partial, gates)

time: 267 us -> 264 us (0.989)
  starting transfers between devices: 54.4 us -> 60.1 us
  local copies, waits for them, and re-layouts: 14.1 us -> 8.81 us
  waiting for transfers between devices: 105 us -> 100 us
  Pallas kernels: 53.5 us -> 57.6 us
    ppermute x2, starting transfers between devices: 3.24 us -> 10.2 us  [spread(): right = lax.ppermute(mine, 'queue', ring_down)]
    ppermute x2, waiting for transfers between devices: 6.13 us -> 0.01 us  [spread(): right = lax.ppermute(mine, 'queue', ring_down)]
    ppermute x2, waiting for transfers between devices: 2.25 us -> 8.06 us  [spread(): left = lax.ppermute(mine, 'queue', ring_up)]
    pallas_call x4, Pallas kernels: 31.4 us -> 36.1 us  [attend(): pl.pallas_call(kernel, grid_spec=pltpu.PrefetchScalarGridSpec(num_scalar_...]
    unnamed x47 -> x31, local copies, waits for them, and re-layouts: 10.5 us -> 6.37 us
    ppermute x1, waiting for transfers between devices: 4.13 us -> 0.01 us  [body(): lax.ppermute(kv1, 'queue', down)]
  transfers between devices with their start and end apart: 24 -> 24, of which waited for: 14 -> 13; matrix products, arithmetic and copies ran while one was open for 3% -> 2% of each run, Pallas kernels for 15% -> 17%
where the time goes in v10:
time: 264 us; the launch traced here: 263 us
  waiting for transfers between devices  100 us (38%)
  starting transfers between devices  60.1 us (23%)
  Pallas kernels  57.6 us (22%)
  blocking collectives  20.2 us (8%)
  between operations  13.8 us (5%)
  local copies, waits for them, and re-layouts  8.81 us (3%)
    pallas_call x4, Pallas kernels, attend(): pl.pallas_call(kernel, grid_spec=pltpu.PrefetchScalarGridSpec(num_scalar_...  36.1 us
    all_to_all x1, blocking collectives, body(): lax.all_to_all(branch, 'queue', split_axis=0, concat_axis=0, axis_index_g...  20.2 us
    all_to_all x1, waiting for transfers between devices, body(): kv1_heads = to_heads(hold(kv1, kv0, gates))  17.2 us
    ppermute x1, waiting for transfers between devices, body(): lax.ppermute(kv0, 'queue', up)  14.4 us
    pallas_call x2, Pallas kernels, project(): pl.pallas_call(kernel, grid_spec=pltpu.PrefetchScalarGridSpec(num_scalar_...  13.4 us
    ppermute x1, waiting for transfers between devices, body(): other_gates = lax.ppermute(gates, 'queue', swap_low)  13.3 us
    all_to_all x1, waiting for transfers between devices, body(): second = to_heads(with_crossing(even1, odd1, odd1_crossing))  12.3 us
    all_to_all x1, waiting for transfers between devices, body(): query = to_heads(hold(query, kv1_heads))  10.3 us
  transfers between devices with their start and end apart: 24, of which 13 were waited for; matrix products, arithmetic and copies ran while one was open for 2% of the time, Pallas kernels for 17%

profile of v10, /device:TPU:0, one launch (start us, length us, event | category | flops | bytes accessed | tf_op | source)
XLA Modules:
  0.0 263.0 jit_solution(5085803023675903296)
XLA Ops:
  6.5 4.6 %pack.1 = (bf16[16,2,2,64,128]{4,3,2,1,0:T(8,128)(2,1)}, bf16[16,2,2,64,128]{4,3,2,1,0:T(8,128)(2,1)}, bf16[16,2,64,256]{3,2,1,0:T(8,128)(2,1)}, bf16[1,64,5120]{2,1,0:T(8,128)(2,1)}) custom-call(bf16[2,64,4096]{2,1,0:T(8,128)(2,1)} %q_ref.1, bf16[2,64,4096]{2,1,0:T(8,128)(2,1)} %k_ref.1, bf16[2,64,4096]{2,1,0:T(8,128)(2,1)} %v_ref.1, ...), custom_call_target="tpu_custom_call" | custom-call | tf_op jit(solution)/shard_map/pack/pallas_call | solution.py:54
  11.1 8.3 %all-to-all-start = ((bf16[16,2,2,64,128]{4,3,2,1,0:T(8,128)(2,1)}), bf16[16,2,2,64,128]{4,3,2,1,0:T(8,128)(2,1)S(1)}, u32[]{:S(2)}, u32[]{:S(2)}) async-start(bf16[16,2,2,64,128]{4,3,2,1,0:T(8,128)(2,1)} %get-tuple-element.19), calls=%async_computation | async-start | bytes 2097152 | tf_op jit(solution)/shard_map/all_to_all | solution.py:377
  19.4 0.2 fusion
  19.7 0.8 collective-permute-start
  20.4 13.3 %collective-permute-done = f32[16,640]{1,0:T(8,128)S(1)} collective-permute-done((f32[16,640]{1,0:T(8,128)S(1)}, f32[16,640]{1,0:T(8,128)S(1)}, u32[]{:S(2)}, u32[]{:S(2)}) %collective-permute-start) | collective-permute-done | bytes 40992 | tf_op jit(solution)/shard_map/ppermute | solution.py:366
  33.7 0.1 dynamic-slice_select_fusion.refs_2_.rest_1_
  33.8 4.0 %all-to-all-done.refs_1_.refs_0_ = bf16[16,2,2,64,128]{4,3,2,1,0:T(8,128)(2,1)S(1)} async-done(((bf16[16,2,2,64,128]{4,3,2,1,0:T(8,128)(2,1)}), bf16[16,2,2,64,128]{4,3,2,1,0:T(8,128)(2,1)S(1)}, u32[]{:S(2)}, u32[]{:S(2)}) %all-to-all-start) | async-done | bytes 1048608 | tf_op jit(solution)/shard_map/all_to_all | solution.py:377
  37.8 1.0 copy-done.7
  38.8 3.8 %all-to-all-start.1 = ((bf16[16,2,2,64,128]{4,3,2,1,0:T(8,128)(2,1)}), bf16[16,2,2,64,128]{4,3,2,1,0:T(8,128)(2,1)S(1)}, u32[]{:S(2)}, u32[]{:S(2)}) async-start(bf16[16,2,2,64,128]{4,3,2,1,0:T(8,128)(2,1)} %copy-done.7), calls=%async_computation.1 | async-start | bytes 2097152 | tf_op jit(solution)/shard_map/all_to_all | solution.py:378
  42.6 0.0 all-gather.5.cloned.1.call-start
  42.7 0.7 all-gather.5.cloned.1.call-update
  43.3 17.2 %all-to-all-done.1.refs_1_.refs_0_ = bf16[16,2,2,64,128]{4,3,2,1,0:T(8,128)(2,1)S(1)} async-done(((bf16[16,2,2,64,128]{4,3,2,1,0:T(8,128)(2,1)}), bf16[16,2,2,64,128]{4,3,2,1,0:T(8,128)(2,1)S(1)}, u32[]{:S(2)}, u32[]{:S(2)}) %all-to-all-start.1) | async-done | bytes 1048608 | tf_op jit(solution)/shard_map/all_to_all | solution.py:378
  60.6 1.0 copy-done.5
  61.6 3.7 %all-to-all-start.2 = ((bf16[16,2,64,256]{3,2,1,0:T(8,128)(2,1)}), bf16[16,2,64,256]{3,2,1,0:T(8,128)(2,1)S(1)}, u32[]{:S(2)}, u32[]{:S(2)}) async-start(bf16[16,2,64,256]{3,2,1,0:T(8,128)(2,1)} %copy-done.5), calls=%async_computation.2 | async-start | bytes 2097152 | tf_op jit(solution)/shard_map/all_to_all | solution.py:379
  65.2 0.0 all-gather.7.cloned.1.call-start
  65.3 8.9 %all-gather.5.cloned.1.call-done = bf16[1024,640]{1,0:T(8,128)(2,1)} async-done(((bf16[256,640]{1,0:T(8,128)(2,1)}), bf16[1024,640]{1,0:T(8,128)(2,1)}) %all-gather.5.cloned.1.call-update) | async-done | bytes 1310736 | tf_op jit(solution)/shard_map/all_gather | solution.py:385
  74.2 10.3 %all-to-all-done.2.refs_1_.q_ref = bf16[16,2,64,256]{3,2,1,0:T(8,128)(2,1)S(1)} async-done(((bf16[16,2,64,256]{3,2,1,0:T(8,128)(2,1)}), bf16[16,2,64,256]{3,2,1,0:T(8,128)(2,1)S(1)}, u32[]{:S(2)}, u32[]{:S(2)}) %all-to-all-start.2) | async-done | bytes 1048608 | tf_op jit(solution)/shard_map/all_to_all | solution.py:379
  84.5 1.0 copy-done.1
  85.5 0.7 hold.16
  86.2 0.0 all-gather.7.cloned.1.call-update
  86.2 1.2 copy-done.2
  87.4 4.4 %collective-permute-start.3 = (bf16[16,2,2,64,128]{4,3,2,1,0:T(8,128)(2,1)S(1)}, bf16[16,2,2,64,128]{4,3,2,1,0:T(8,128)(2,1)}, u32[]{:S(2)}, u32[]{:S(2)}) collective-permute-start(bf16[16,2,2,64,128]{4,3,2,1,0:T(8,128)(2,1)S(1)} %hold.12.own_ref), channel_id=1, source_target_pairs={{0,16},{16,32},{32,48},{48,64},{64,80},{80,96},{96,112},{1,17},{17... | collective-permute-start | bytes 3145736 | tf_op jit(solution)/shard_map/ppermute | solution.py:381
  91.7 1.3 collective-permute-start.4
  93.1 5.5 %collective-permute-start.1 = (bf16[16,2,2,64,128]{4,3,2,1,0:T(8,128)(2,1)S(1)}, bf16[16,2,2,64,128]{4,3,2,1,0:T(8,128)(2,1)}, u32[]{:S(2)}, u32[]{:S(2)}) collective-permute-start(bf16[16,2,2,64,128]{4,3,2,1,0:T(8,128)(2,1)S(1)} %hold.11.own_ref), channel_id=1, source_target_pairs={{0,16},{16,32},{32,48},{48,64},{64,80},{80,96},{96,112},{1,17},{17... | collective-permute-start | bytes 3145736 | tf_op jit(solution)/shard_map/ppermute | solution.py:383
  98.6 1.3 collective-permute-start.2
  99.9 14.4 %collective-permute-done.3.before_ref = bf16[16,2,2,64,128]{4,3,2,1,0:T(8,128)(2,1)} collective-permute-done((bf16[16,2,2,64,128]{4,3,2,1,0:T(8,128)(2,1)S(1)}, bf16[16,2,2,64,128]{4,3,2,1,0:T(8,128)(2,1)}, u32[]{:S(2)}, u32[]{:S(2)}) %collective-permute-start.3) | collective-permute-done | bytes 1048608 | tf_op jit(solution)/shard_map/ppermute | solution.py:381
  114.3 5.5 %collective-permute-done.4.after_ref = bf16[16,2,2,64,128]{4,3,2,1,0:T(8,128)(2,1)} collective-permute-done((bf16[16,2,2,64,128]{4,3,2,1,0:T(8,128)(2,1)S(1)}, bf16[16,2,2,64,128]{4,3,2,1,0:T(8,128)(2,1)}, u32[]{:S(2)}, u32[]{:S(2)}) %collective-permute-start.4) | collective-permute-done | bytes 1048608 | tf_op jit(solution)/shard_map/ppermute | solution.py:381
  119.8 9.0 %attend.4 = (bf16[16,1,64,128]{3,2,1,0:T(8,128)(2,1)S(1)}, f32[8,128]{1,0:T(8,128)S(1)}) custom-call(s32[1]{0:T(128)} %bitcast.pos_ref, bf16[16,2,64,256]{3,2,1,0:T(8,128)(2,1)S(1)} %copy-done.2, bf16[16,2,2,64,128]{4,3,2,1,0:T(8,128)(2,1)S(1)} %hold.12.own_ref, bf16[16,2,2,64,128]{4,3,2,1,0:T(8,128)(2,1)} %collective-permute-done.3.before_ref, ...), custom_call_target="tpu_custom_call" | custom-call | flops 5368709120 | bytes 4194304 | tf_op jit(solution)/shard_map/attend/pallas_call | solution.py:169
  128.8 0.7 collective-permute-start.5
  129.5 9.1 %attend.5 = (bf16[16,1,64,128]{3,2,1,0:T(8,128)(2,1)S(1)}, f32[8,128]{1,0:T(8,128)S(1)}) custom-call(s32[1]{0:T(128)} %bitcast.pos_ref, bf16[16,2,64,256]{3,2,1,0:T(8,128)(2,1)S(1)} %copy-done.2, bf16[16,2,2,64,128]{4,3,2,1,0:T(8,128)(2,1)S(1)} %hold.12.own_ref, bf16[16,2,2,64,128]{4,3,2,1,0:T(8,128)(2,1)} %collective-permute-done.3.before_ref, ...), custom_call_target="tpu_custom_call" | custom-call | flops 5368709120 | bytes 4194304 | tf_op jit(solution)/shard_map/attend/pallas_call | solution.py:169
  138.6 0.8 pad_maximum_fusion.rest_1_
  139.5 4.7 %all-to-all-start.3 = ((bf16[16,2,64,128]{3,2,1,0:T(8,128)(2,1)}), bf16[16,2,64,128]{3,2,1,0:T(8,128)(2,1)S(1)}, u32[]{:S(2)}, u32[]{:S(2)}) async-start(bf16[16,2,64,128]{3,2,1,0:T(8,128)(2,1)} %pad_maximum_fusion.rest_1_), calls=%async_computation.3 | async-start | bytes 1048576 | tf_op jit(solution)/shard_map/all_to_all | solution.py:411
  144.2 9.0 %attend.6 = (bf16[16,1,64,128]{3,2,1,0:T(8,128)(2,1)S(1)}, f32[8,128]{1,0:T(8,128)S(1)}) custom-call(s32[1]{0:T(128)} %bitcast.pos_ref, bf16[16,2,64,256]{3,2,1,0:T(8,128)(2,1)S(1)} %copy-done.2, bf16[16,2,2,64,128]{4,3,2,1,0:T(8,128)(2,1)S(1)} %hold.11.own_ref, bf16[16,2,2,64,128]{4,3,2,1,0:T(8,128)(2,1)} %collective-permute-done.1.before_ref.refs_1_, ...), custom_call_target="tpu_custom_call" | custom-call | flops 5368709120 | bytes 4194304 | tf_op jit(solution)/shard_map/attend/pallas_call | solution.py:169
  153.2 0.7 copy-done.9
  153.9 2.6 %all-to-all-done.3.refs_0_ = bf16[16,2,64,128]{3,2,1,0:T(8,128)(2,1)S(1)} async-done(((bf16[16,2,64,128]{3,2,1,0:T(8,128)(2,1)}), bf16[16,2,64,128]{3,2,1,0:T(8,128)(2,1)S(1)}, u32[]{:S(2)}, u32[]{:S(2)}) %all-to-all-start.3) | async-done | bytes 524320 | tf_op jit(solution)/shard_map/all_to_all | solution.py:411
  156.5 9.0 %attend.7 = (bf16[16,1,64,128]{3,2,1,0:T(8,128)(2,1)S(1)}, f32[8,128]{1,0:T(8,128)S(1)}) custom-call(s32[1]{0:T(128)} %bitcast.pos_ref, bf16[16,2,64,256]{3,2,1,0:T(8,128)(2,1)S(1)} %copy-done.2, bf16[16,2,2,64,128]{4,3,2,1,0:T(8,128)(2,1)S(1)} %hold.11.own_ref, bf16[16,2,2,64,128]{4,3,2,1,0:T(8,128)(2,1)} %collective-permute-done.1.before_ref.refs_1_, ...), custom_call_target="tpu_custom_call" | custom-call | flops 5368709120 | bytes 4194304 | tf_op jit(solution)/shard_map/attend/pallas_call | solution.py:169
  165.6 0.7 copy-done.11
  166.3 0.6 copy-done.13
  166.9 0.7 hold.17.wo_ref
  167.6 0.2 copy-done.10
  167.8 0.7 collective-permute-start.6
  168.5 0.7 hold.14
  169.2 2.4 collective-permute-start.7
  171.7 0.8 pad_maximum_fusion.1
  172.6 4.6 %all-to-all-start.4 = ((bf16[16,2,64,128]{3,2,1,0:T(8,128)(2,1)}), bf16[16,2,64,128]{3,2,1,0:T(8,128)(2,1)S(1)}, u32[]{:S(2)}, u32[]{:S(2)}) async-start(bf16[16,2,64,128]{3,2,1,0:T(8,128)(2,1)} %pad_maximum_fusion.1), calls=%async_computation.4 | async-start | bytes 1048576 | tf_op jit(solution)/shard_map/all_to_all | solution.py:417
  177.2 1.1 collective-permute-start.13
  178.3 6.9 %collective-permute-start.14 = (bf16[16,2,64,128]{3,2,1,0:T(8,128)(2,1)S(1)}, bf16[16,2,64,128]{3,2,1,0:T(8,128)(2,1)S(1)}, u32[]{:S(2)}, u32[]{:S(2)}) collective-permute-start(bf16[16,2,64,128]{3,2,1,0:T(8,128)(2,1)S(1)} %hold.13.rest_1_.mine_ref), channel_id=1, source_target_pairs={{16,0},{32,16},{48,32},{0,48},{80,64},{96,80},{112,96},{64,112},{1... | collective-permute-start | bytes 1572872 | tf_op jit(solution)/shard_map/ppermute | solution.py:398
  185.2 1.8 collective-permute-done.7.refs_1_.shifted_ref
  187.0 12.3 %all-to-all-done.4.refs_0_ = bf16[16,2,64,128]{3,2,1,0:T(8,128)(2,1)S(1)} async-done(((bf16[16,2,64,128]{3,2,1,0:T(8,128)(2,1)}), bf16[16,2,64,128]{3,2,1,0:T(8,128)(2,1)S(1)}, u32[]{:S(2)}, u32[]{:S(2)}) %all-to-all-start.4) | async-done | bytes 524320 | tf_op jit(solution)/shard_map/all_to_all | solution.py:417
  199.3 3.2 %collective-permute-start.9 = (bf16[16,2,64,128]{3,2,1,0:T(8,128)(2,1)S(1)}, bf16[16,2,64,128]{3,2,1,0:T(8,128)(2,1)}, u32[]{:S(2)}, u32[]{:S(2)}) collective-permute-start(bf16[16,2,64,128]{3,2,1,0:T(8,128)(2,1)S(1)} %hold.15.mine_ref), channel_id=1, source_target_pairs={{16,0},{32,16},{48,32},{0,48},{80,64},{96,80},{112,96},{64,112},{1... | collective-permute-start | bytes 1572872 | tf_op jit(solution)/shard_map/ppermute | solution.py:398
  202.6 0.1 collective-permute-done.13.left_ref
  202.6 0.7 slice.23
  203.4 0.7 slice.24
  204.1 3.2 %collective-permute-start.16 = (bf16[8,2,64,128]{3,2,1,0:T(8,128)(2,1)}, bf16[8,2,64,128]{3,2,1,0:T(8,128)(2,1)}, u32[]{:S(2)}, u32[]{:S(2)}) collective-permute-start(bf16[8,2,64,128]{3,2,1,0:T(8,128)(2,1)} %slice.24), channel_id=1, source_target_pairs={{16,0},{32,16},{48,32},{0,48},{80,64},{96,80},{112,96},{64,112},{1... | collective-permute-start | bytes 786440 | tf_op jit(solution)/shard_map/ppermute | solution.py:400
  207.3 8.0 %collective-permute-done.8.left_ref = bf16[16,2,64,128]{3,2,1,0:T(8,128)(2,1)S(1)} collective-permute-done((bf16[16,2,64,128]{3,2,1,0:T(8,128)(2,1)S(1)}, bf16[16,2,64,128]{3,2,1,0:T(8,128)(2,1)S(1)}, u32[]{:S(2)}, u32[]{:S(2)}) %collective-permute-start.8) | collective-permute-done | bytes 524320 | tf_op jit(solution)/shard_map/ppermute | solution.py:397
  215.3 0.3 collective-permute-start.10
  215.6 1.0 slice.22
  216.6 3.3 %collective-permute-start.11 = (bf16[8,2,64,128]{3,2,1,0:T(8,128)(2,1)S(1)}, bf16[8,2,64,128]{3,2,1,0:T(8,128)(2,1)S(1)}, u32[]{:S(2)}, u32[]{:S(2)}) collective-permute-start(bf16[8,2,64,128]{3,2,1,0:T(8,128)(2,1)S(1)} %slice.22), channel_id=1, source_target_pairs={{16,0},{32,16},{48,32},{0,48},{80,64},{96,80},{112,96},{64,112},{1... | collective-permute-start | bytes 786440 | tf_op jit(solution)/shard_map/ppermute | solution.py:400
  219.9 0.1 pad_add_fusion.place_ref
  220.0 1.1 collective-permute-done.15.low_ref
  221.0 6.6 %project_first.1.rest_0_ = f32[2,512,640]{2,1,0:T(8,128)S(1)} custom-call(s32[2]{0:T(128)S(1)} %pad_add_fusion.place_ref, bf16[16,2,64,128]{3,2,1,0:T(8,128)(2,1)S(1)} %hold.13.rest_1_.mine_ref, bf16[16,2,64,128]{3,2,1,0:T(8,128)(2,1)S(1)} %collective-permute-done.13.left_ref, bf16[16,2,64,128]{3,2,1,0:T(8,128)(2,1)S(1)} %collective-permute-done.14.right_ref, ...), custom_call_target="tpu_custom_call" | custom-call | flops 2684354560 | bytes 8388608 | tf_op jit(solution)/shard_map/project_first/pallas_call | solution.py:263
  227.7 6.8 %project_last.1 = bf16[8,2,64,640]{3,2,1,0:T(8,128)(2,1)S(1)} custom-call(s32[2]{0:T(128)S(1)} %pad_add_fusion.place_ref, bf16[16,2,64,128]{3,2,1,0:T(8,128)(2,1)S(1)} %hold.15.mine_ref, bf16[16,2,64,128]{3,2,1,0:T(8,128)(2,1)S(1)} %collective-permute-done.8.left_ref, bf16[16,2,64,128]{3,2,1,0:T(8,128)(2,1)} %collective-permute-done.9.right_ref, ...), custom_call_target="tpu_custom_call" | custom-call | flops 2684354560 | bytes 8388608 | tf_op jit(solution)/shard_map/project_last/pallas_call | solution.py:263
  234.5 20.2 %all_to_all.30 = bf16[8,2,64,640]{3,2,1,0:T(8,128)(2,1)S(1)} all-to-all(bf16[8,2,64,640]{3,2,1,0:T(8,128)(2,1)S(1)} %project_last.1), channel_id=1, replica_groups={{0,16,32,48},{64,80,96,112},{1,17,33,49},{65,81,97,113},{2,18,34,50},{6..., dimensions={0} | all-to-all | bytes 2621440 | tf_op jit(solution)/shard_map/all_to_all | solution.py:422
  254.7 1.4 add_branch.1
  (49 shorter events, 0.2 us)
Async XLA Ops:
  6.5 12.9 %copy-start = (f32[50,640]{1,0:T(8,128)S(1)}, f32[50,640]{1,0:T(8,128)}, u32[]{:S(2)}) copy-start(f32[50,640]{1,0:T(8,128)} %param.13) | copy-start | bytes 384004
  11.1 8.3 %copy-start.14 = (s32[16]{0:T(128)S(1)}, s32[16]{0:T(128)}, u32[]{:S(2)}) copy-start(s32[16]{0:T(128)} %param.14) | copy-start | bytes 196
  11.1 26.7 %copy-start.6 = (bf16[16,2,2,64,128]{4,3,2,1,0:T(8,128)(2,1)S(1)}, bf16[16,2,2,64,128]{4,3,2,1,0:T(8,128)(2,1)}, u32[]{:S(2)}) copy-start(bf16[16,2,2,64,128]{4,3,2,1,0:T(8,128)(2,1)} %get-tuple-element.18.refs_0_) | copy-start | bytes 3145732
  11.1 26.7 %all-to-all-start = ((bf16[16,2,2,64,128]{4,3,2,1,0:T(8,128)(2,1)}), bf16[16,2,2,64,128]{4,3,2,1,0:T(8,128)(2,1)S(1)}, u32[]{:S(2)}, u32[]{:S(2)}) async-start(bf16[16,2,2,64,128]{4,3,2,1,0:T(8,128)(2,1)} %get-tuple-element.19), calls=%async_computation | async-start | bytes 2097152 | tf_op jit(solution)/shard_map/all_to_all | solution.py:377
  19.7 14.0 %collective-permute-start = (f32[16,640]{1,0:T(8,128)S(1)}, f32[16,640]{1,0:T(8,128)S(1)}, u32[]{:S(2)}, u32[]{:S(2)}) collective-permute-start(f32[16,640]{1,0:T(8,128)S(1)} %fusion), channel_id=1, source_target_pairs={{0,64},{16,80},{32,96},{48,112},{64,0},{80,16},{96,32},{112,48},{1... | collective-permute-start | bytes 122888 | tf_op jit(solution)/shard_map/ppermute | solution.py:366
  37.8 1.0 copy-start.7
  38.8 21.8 %copy-start.4 = (bf16[16,2,64,256]{3,2,1,0:T(8,128)(2,1)S(1)}, bf16[16,2,64,256]{3,2,1,0:T(8,128)(2,1)}, u32[]{:S(2)}) copy-start(bf16[16,2,64,256]{3,2,1,0:T(8,128)(2,1)} %get-tuple-element.17.refs_0_) | copy-start | bytes 3145732
  38.8 21.8 %all-to-all-start.1 = ((bf16[16,2,2,64,128]{4,3,2,1,0:T(8,128)(2,1)}), bf16[16,2,2,64,128]{4,3,2,1,0:T(8,128)(2,1)S(1)}, u32[]{:S(2)}, u32[]{:S(2)}) async-start(bf16[16,2,2,64,128]{4,3,2,1,0:T(8,128)(2,1)} %copy-done.7), calls=%async_computation.1 | async-start | bytes 2097152 | tf_op jit(solution)/shard_map/all_to_all | solution.py:378
  42.6 31.6 %all-gather.5.cloned.1.call-start = ((), (), s32[]{:S(2)}) async-start(), calls=%async_computation.6 | async-start | bytes 1638400 | tf_op jit(solution)/shard_map/all_gather | solution.py:385
  60.6 1.0 copy-start.5
  61.6 22.9 %all-to-all-start.2 = ((bf16[16,2,64,256]{3,2,1,0:T(8,128)(2,1)}), bf16[16,2,64,256]{3,2,1,0:T(8,128)(2,1)S(1)}, u32[]{:S(2)}, u32[]{:S(2)}) async-start(bf16[16,2,64,256]{3,2,1,0:T(8,128)(2,1)} %copy-done.5), calls=%async_computation.2 | async-start | bytes 2097152 | tf_op jit(solution)/shard_map/all_to_all | solution.py:379
  65.2 101.6 %all-gather.7.cloned.1.call-start = ((), (), s32[]{:S(2)}) async-start(), calls=%async_computation.7 | async-start | bytes 6553600 | tf_op jit(solution)/shard_map/all_gather | solution.py:387
  84.5 1.0 copy-start.1
  86.2 1.2 copy-start.2
  87.4 26.9 %collective-permute-start.3 = (bf16[16,2,2,64,128]{4,3,2,1,0:T(8,128)(2,1)S(1)}, bf16[16,2,2,64,128]{4,3,2,1,0:T(8,128)(2,1)}, u32[]{:S(2)}, u32[]{:S(2)}) collective-permute-start(bf16[16,2,2,64,128]{4,3,2,1,0:T(8,128)(2,1)S(1)} %hold.12.own_ref), channel_id=1, source_target_pairs={{0,16},{16,32},{32,48},{48,64},{64,80},{80,96},{96,112},{1,17},{17... | collective-permute-start | bytes 3145736 | tf_op jit(solution)/shard_map/ppermute | solution.py:381
  91.7 28.1 %collective-permute-start.4 = (bf16[16,2,2,64,128]{4,3,2,1,0:T(8,128)(2,1)S(1)}, bf16[16,2,2,64,128]{4,3,2,1,0:T(8,128)(2,1)}, u32[]{:S(2)}, u32[]{:S(2)}) collective-permute-start(bf16[16,2,2,64,128]{4,3,2,1,0:T(8,128)(2,1)S(1)} %hold.12.own_ref), channel_id=1, source_target_pairs={{16,0},{32,16},{48,32},{64,48},{80,64},{96,80},{112,96},{17,1},{33... | collective-permute-start | bytes 3145736 | tf_op jit(solution)/shard_map/ppermute | solution.py:381
  93.1 51.1 %collective-permute-start.1 = (bf16[16,2,2,64,128]{4,3,2,1,0:T(8,128)(2,1)S(1)}, bf16[16,2,2,64,128]{4,3,2,1,0:T(8,128)(2,1)}, u32[]{:S(2)}, u32[]{:S(2)}) collective-permute-start(bf16[16,2,2,64,128]{4,3,2,1,0:T(8,128)(2,1)S(1)} %hold.11.own_ref), channel_id=1, source_target_pairs={{0,16},{16,32},{32,48},{48,64},{64,80},{80,96},{96,112},{1,17},{17... | collective-permute-start | bytes 3145736 | tf_op jit(solution)/shard_map/ppermute | solution.py:383
  98.6 45.6 %collective-permute-start.2 = (bf16[16,2,2,64,128]{4,3,2,1,0:T(8,128)(2,1)S(1)}, bf16[16,2,2,64,128]{4,3,2,1,0:T(8,128)(2,1)}, u32[]{:S(2)}, u32[]{:S(2)}) collective-permute-start(bf16[16,2,2,64,128]{4,3,2,1,0:T(8,128)(2,1)S(1)} %hold.11.own_ref), channel_id=1, source_target_pairs={{16,0},{32,16},{48,32},{64,48},{80,64},{96,80},{112,96},{17,1},{33... | collective-permute-start | bytes 3145736 | tf_op jit(solution)/shard_map/ppermute | solution.py:383
  128.8 9.8 %collective-permute-start.5 = (bf16[16,1,64,128]{3,2,1,0:T(8,128)(2,1)S(1)}, bf16[16,1,64,128]{3,2,1,0:T(8,128)(2,1)S(1)}, u32[]{:S(2)}, u32[]{:S(2)}) collective-permute-start(bf16[16,1,64,128]{3,2,1,0:T(8,128)(2,1)S(1)} %get-tuple-element.23), channel_id=1, source_target_pairs={{48,112},{49,113},{50,114},{51,115},{52,116},{53,117},{54,118},{55... | collective-permute-start | bytes 786440 | tf_op jit(solution)/shard_map/ppermute | solution.py:406
  139.5 17.1 %all-to-all-start.3 = ((bf16[16,2,64,128]{3,2,1,0:T(8,128)(2,1)}), bf16[16,2,64,128]{3,2,1,0:T(8,128)(2,1)S(1)}, u32[]{:S(2)}, u32[]{:S(2)}) async-start(bf16[16,2,64,128]{3,2,1,0:T(8,128)(2,1)} %pad_maximum_fusion.rest_1_), calls=%async_computation.3 | async-start | bytes 1048576 | tf_op jit(solution)/shard_map/all_to_all | solution.py:411
  153.2 0.7 copy-start.9
  165.6 0.7 copy-start.11
  166.3 0.6 copy-start.13
  166.9 1.0 copy-start.10
  167.6 53.4 %collective-permute-start.12 = (bf16[4,2,2,256,640]{4,3,2,1,0:T(8,128)(2,1)}, bf16[4,2,2,256,640]{4,3,2,1,0:T(8,128)(2,1)}, u32[]{:S(2)}, u32[]{:S(2)}) collective-permute-start(bf16[4,2,2,256,640]{4,3,2,1,0:T(8,128)(2,1)} %hold.17.wo_ref), channel_id=1, source_target_pairs={{0,1},{1,0},{2,3},{3,2},{4,5},{5,4},{6,7},{7,6},{8,9},{9,8},{10,11... | collective-permute-start | bytes 15728648 | tf_op jit(solution)/shard_map/ppermute | solution.py:416
  167.8 3.9 %collective-permute-start.6 = (bf16[16,1,64,128]{3,2,1,0:T(8,128)(2,1)S(1)}, bf16[16,1,64,128]{3,2,1,0:T(8,128)(2,1)S(1)}, u32[]{:S(2)}, u32[]{:S(2)}) collective-permute-start(bf16[16,1,64,128]{3,2,1,0:T(8,128)(2,1)S(1)} %copy-done.10), channel_id=1, source_target_pairs={{48,112},{49,113},{50,114},{51,115},{52,116},{53,117},{54,118},{55... | collective-permute-start | bytes 786440 | tf_op jit(solution)/shard_map/ppermute | solution.py:410
  168.5 3.2 %copy-start.12 = (bf16[16,1,64,128]{3,2,1,0:T(8,128)(2,1)S(1)}, bf16[16,1,64,128]{3,2,1,0:T(8,128)(2,1)}, u32[]{:S(2)}) copy-start(bf16[16,1,64,128]{3,2,1,0:T(8,128)(2,1)} %copy-done.11) | copy-start | bytes 786436
  169.2 17.8 %collective-permute-start.7 = (bf16[1,64,5120]{2,1,0:T(8,128)(2,1)}, bf16[1,64,5120]{2,1,0:T(8,128)(2,1)S(1)}, u32[]{:S(2)}, u32[]{:S(2)}) collective-permute-start(bf16[1,64,5120]{2,1,0:T(8,128)(2,1)} %hold.14), channel_id=1, source_target_pairs={{0,16},{16,32},{32,48},{48,64},{64,80},{80,96},{96,112},{1,17},{17... | collective-permute-start | bytes 1966088 | tf_op jit(solution)/shard_map/ppermute | solution.py:413
  172.6 26.7 %all-to-all-start.4 = ((bf16[16,2,64,128]{3,2,1,0:T(8,128)(2,1)}), bf16[16,2,64,128]{3,2,1,0:T(8,128)(2,1)S(1)}, u32[]{:S(2)}, u32[]{:S(2)}) async-start(bf16[16,2,64,128]{3,2,1,0:T(8,128)(2,1)} %pad_maximum_fusion.1), calls=%async_computation.4 | async-start | bytes 1048576 | tf_op jit(solution)/shard_map/all_to_all | solution.py:417
  177.2 25.5 %collective-permute-start.13 = (bf16[16,2,64,128]{3,2,1,0:T(8,128)(2,1)S(1)}, bf16[16,2,64,128]{3,2,1,0:T(8,128)(2,1)S(1)}, u32[]{:S(2)}, u32[]{:S(2)}) collective-permute-start(bf16[16,2,64,128]{3,2,1,0:T(8,128)(2,1)S(1)} %hold.13.rest_1_.mine_ref), channel_id=1, source_target_pairs={{0,16},{16,32},{32,48},{48,0},{64,80},{80,96},{96,112},{112,64},{1... | collective-permute-start | bytes 1572872 | tf_op jit(solution)/shard_map/ppermute | solution.py:397
  178.3 25.1 %collective-permute-start.14 = (bf16[16,2,64,128]{3,2,1,0:T(8,128)(2,1)S(1)}, bf16[16,2,64,128]{3,2,1,0:T(8,128)(2,1)S(1)}, u32[]{:S(2)}, u32[]{:S(2)}) collective-permute-start(bf16[16,2,64,128]{3,2,1,0:T(8,128)(2,1)S(1)} %hold.13.rest_1_.mine_ref), channel_id=1, source_target_pairs={{16,0},{32,16},{48,32},{0,48},{80,64},{96,80},{112,96},{64,112},{1... | collective-permute-start | bytes 1572872 | tf_op jit(solution)/shard_map/ppermute | solution.py:398
  199.3 16.0 %collective-permute-start.8 = (bf16[16,2,64,128]{3,2,1,0:T(8,128)(2,1)S(1)}, bf16[16,2,64,128]{3,2,1,0:T(8,128)(2,1)S(1)}, u32[]{:S(2)}, u32[]{:S(2)}) collective-permute-start(bf16[16,2,64,128]{3,2,1,0:T(8,128)(2,1)S(1)} %hold.15.mine_ref), channel_id=1, source_target_pairs={{0,16},{16,32},{32,48},{48,0},{64,80},{80,96},{96,112},{112,64},{1... | collective-permute-start | bytes 1572872 | tf_op jit(solution)/shard_map/ppermute | solution.py:397
  199.3 16.3 %collective-permute-start.9 = (bf16[16,2,64,128]{3,2,1,0:T(8,128)(2,1)S(1)}, bf16[16,2,64,128]{3,2,1,0:T(8,128)(2,1)}, u32[]{:S(2)}, u32[]{:S(2)}) collective-permute-start(bf16[16,2,64,128]{3,2,1,0:T(8,128)(2,1)S(1)} %hold.15.mine_ref), channel_id=1, source_target_pairs={{16,0},{32,16},{48,32},{0,48},{80,64},{96,80},{112,96},{64,112},{1... | collective-permute-start | bytes 1572872 | tf_op jit(solution)/shard_map/ppermute | solution.py:398
  203.4 17.7 %collective-permute-start.15 = (bf16[8,2,64,128]{3,2,1,0:T(8,128)(2,1)}, bf16[8,2,64,128]{3,2,1,0:T(8,128)(2,1)}, u32[]{:S(2)}, u32[]{:S(2)}) collective-permute-start(bf16[8,2,64,128]{3,2,1,0:T(8,128)(2,1)} %slice.23), channel_id=1, source_target_pairs={{0,16},{16,32},{32,48},{48,0},{64,80},{80,96},{96,112},{112,64},{1... | collective-permute-start | bytes 786440 | tf_op jit(solution)/shard_map/ppermute | solution.py:399
  204.1 16.9 %collective-permute-start.16 = (bf16[8,2,64,128]{3,2,1,0:T(8,128)(2,1)}, bf16[8,2,64,128]{3,2,1,0:T(8,128)(2,1)}, u32[]{:S(2)}, u32[]{:S(2)}) collective-permute-start(bf16[8,2,64,128]{3,2,1,0:T(8,128)(2,1)} %slice.24), channel_id=1, source_target_pairs={{16,0},{32,16},{48,32},{0,48},{80,64},{96,80},{112,96},{64,112},{1... | collective-permute-start | bytes 786440 | tf_op jit(solution)/shard_map/ppermute | solution.py:400
  215.3 12.3 %collective-permute-start.10 = (bf16[8,2,64,128]{3,2,1,0:T(8,128)(2,1)S(1)}, bf16[8,2,64,128]{3,2,1,0:T(8,128)(2,1)S(1)}, u32[]{:S(2)}, u32[]{:S(2)}) collective-permute-start(bf16[8,2,64,128]{3,2,1,0:T(8,128)(2,1)S(1)} %slice.21), channel_id=1, source_target_pairs={{0,16},{16,32},{32,48},{48,0},{64,80},{80,96},{96,112},{112,64},{1... | collective-permute-start | bytes 786440 | tf_op jit(solution)/shard_map/ppermute | solution.py:399
  216.6 11.0 %collective-permute-start.11 = (bf16[8,2,64,128]{3,2,1,0:T(8,128)(2,1)S(1)}, bf16[8,2,64,128]{3,2,1,0:T(8,128)(2,1)S(1)}, u32[]{:S(2)}, u32[]{:S(2)}) collective-permute-start(bf16[8,2,64,128]{3,2,1,0:T(8,128)(2,1)S(1)} %slice.22), channel_id=1, source_target_pairs={{16,0},{32,16},{48,32},{0,48},{80,64},{96,80},{112,96},{64,112},{1... | collective-permute-start | bytes 786440 | tf_op jit(solution)/shard_map/ppermute | solution.py:400
  234.5 20.3 %copy-start.3 = (bf16[2,64,5120]{2,1,0:T(8,128)(2,1)S(1)}, bf16[2,64,5120]{2,1,0:T(8,128)(2,1)}, u32[]{:S(2)}) copy-start(bf16[2,64,5120]{2,1,0:T(8,128)(2,1)} %hidden_ref.3) | copy-start | bytes 3932164
  234.5 20.3 %copy-start.8 = (bf16[64,5120]{1,0:T(8,128)(2,1)S(1)}, bf16[64,5120]{1,0:T(8,128)(2,1)}, u32[]{:S(2)}) copy-start(bf16[64,5120]{1,0:T(8,128)(2,1)} %entering_ref.1) | copy-start | bytes 1966084
Sparse Core Ops, SparseCore 0:
  45.1 29.0 all-gather.4
  86.3 56.1 all-gather.6

commit v11 on v10

--- a/solution.py
+++ b/solution.py
@@ -414,8 +414,9 @@
     even1, token = attend(0, *head1, token, first)
     weight_own = hold(weight, token, room=56)
     weight_pair = lax.ppermute(weight_own, "spatial", swap_core)
-    second = to_heads(with_crossing(even1, odd1, odd1_crossing))
-    second_sources = spread(hold(second, shifted))
+    second = with_crossing(even1, odd1, odd1_crossing)
+    second = to_heads(hold(second, *first_sources[1:3]))
+    second_sources = spread(hold(second, shifted, *first_sources[3:]))
 
     partial = project(0, place, first_sources, weight_own, weight_pair, None, None)
     branch = project(1, place, second_sources, weight_own, weight_pair, partial, gates)

time: 264 us -> 273 us (1.034)
  waiting for transfers between devices: 100 us -> 112 us
  starting transfers between devices: 60.1 us -> 56.1 us
    ppermute x2, waiting for transfers between devices: 8.06 us -> 21.5 us  [spread(): left = lax.ppermute(mine, 'queue', ring_up)]
    all_to_all x1, waiting for transfers between devices: 12.3 us -> 2.3 us  [body(): second = to_heads(hold(second, *first_sources[1:3]))]
    ppermute x2, waiting for transfers between devices: 1.05 us -> 10 us  [spread(): far_low = lax.ppermute(left[:SPATIAL // 2], 'queue', ring_up)]
    unnamed x31 -> x39, local copies, waits for them, and re-layouts: 6.37 us -> 9.68 us
  transfers between devices with their start and end apart: 24 -> 24, of which waited for: 13 -> 13; matrix products, arithmetic and copies ran while one was open for 2% -> 1% of each run, Pallas kernels for 17% -> 16%
where the time goes in v11:
time: 273 us; the launch traced here: 272 us
  waiting for transfers between devices  112 us (41%)
  Pallas kernels  57.5 us (21%)
  starting transfers between devices  56.1 us (21%)
  blocking collectives  19.6 us (7%)
  between operations  13.8 us (5%)
  local copies, waits for them, and re-layouts  10.7 us (4%)
    pallas_call x4, Pallas kernels, attend(): pl.pallas_call(kernel, grid_spec=pltpu.PrefetchScalarGridSpec(num_scalar_...  36.1 us
    ppermute x2, waiting for transfers between devices, spread(): left = lax.ppermute(mine, 'queue', ring_up)  21.5 us
    all_to_all x1, blocking collectives, body(): lax.all_to_all(branch, 'queue', split_axis=0, concat_axis=0, axis_index_g...  19.6 us
    all_to_all x1, waiting for transfers between devices, body(): kv1_heads = to_heads(hold(kv1, kv0, gates))  17.2 us
    ppermute x1, waiting for transfers between devices, body(): lax.ppermute(kv0, 'queue', up)  14.4 us
    ppermute x1, waiting for transfers between devices, body(): other_gates = lax.ppermute(gates, 'queue', swap_low)  13.3 us
    pallas_call x2, Pallas kernels, project(): pl.pallas_call(kernel, grid_spec=pltpu.PrefetchScalarGridSpec(num_scalar_...  13.3 us
    all_to_all x1, waiting for transfers between devices, body(): query = to_heads(hold(query, kv1_heads))  10.3 us
  transfers between devices with their start and end apart: 24, of which 13 were waited for; matrix products, arithmetic and copies ran while one was open for 1% of the time, Pallas kernels for 16%

profile of v11, /device:TPU:0, one launch (start us, length us, event | category | flops | bytes accessed | tf_op | source)
XLA Modules:
  0.0 272.1 jit_solution(4782831208945454656)
XLA Ops:
  6.5 4.6 %pack.1 = (bf16[16,2,2,64,128]{4,3,2,1,0:T(8,128)(2,1)}, bf16[16,2,2,64,128]{4,3,2,1,0:T(8,128)(2,1)}, bf16[16,2,64,256]{3,2,1,0:T(8,128)(2,1)}, bf16[1,64,5120]{2,1,0:T(8,128)(2,1)}) custom-call(bf16[2,64,4096]{2,1,0:T(8,128)(2,1)} %q_ref.1, bf16[2,64,4096]{2,1,0:T(8,128)(2,1)} %k_ref.1, bf16[2,64,4096]{2,1,0:T(8,128)(2,1)} %v_ref.1, ...), custom_call_target="tpu_custom_call" | custom-call | tf_op jit(solution)/shard_map/pack/pallas_call | solution.py:54
  11.1 8.3 %all-to-all-start = ((bf16[16,2,2,64,128]{4,3,2,1,0:T(8,128)(2,1)}), bf16[16,2,2,64,128]{4,3,2,1,0:T(8,128)(2,1)S(1)}, u32[]{:S(2)}, u32[]{:S(2)}) async-start(bf16[16,2,2,64,128]{4,3,2,1,0:T(8,128)(2,1)} %get-tuple-element.19), calls=%async_computation | async-start | bytes 2097152 | tf_op jit(solution)/shard_map/all_to_all | solution.py:377
  19.4 0.2 fusion
  19.7 0.8 collective-permute-start
  20.4 13.3 %collective-permute-done = f32[16,640]{1,0:T(8,128)S(1)} collective-permute-done((f32[16,640]{1,0:T(8,128)S(1)}, f32[16,640]{1,0:T(8,128)S(1)}, u32[]{:S(2)}, u32[]{:S(2)}) %collective-permute-start) | collective-permute-done | bytes 40992 | tf_op jit(solution)/shard_map/ppermute | solution.py:366
  33.7 0.1 dynamic-slice_select_fusion.refs_2_.rest_1_
  33.8 4.0 %all-to-all-done.refs_1_.refs_0_ = bf16[16,2,2,64,128]{4,3,2,1,0:T(8,128)(2,1)S(1)} async-done(((bf16[16,2,2,64,128]{4,3,2,1,0:T(8,128)(2,1)}), bf16[16,2,2,64,128]{4,3,2,1,0:T(8,128)(2,1)S(1)}, u32[]{:S(2)}, u32[]{:S(2)}) %all-to-all-start) | async-done | bytes 1048608 | tf_op jit(solution)/shard_map/all_to_all | solution.py:377
  37.8 1.0 copy-done.7
  38.8 3.8 %all-to-all-start.1 = ((bf16[16,2,2,64,128]{4,3,2,1,0:T(8,128)(2,1)}), bf16[16,2,2,64,128]{4,3,2,1,0:T(8,128)(2,1)S(1)}, u32[]{:S(2)}, u32[]{:S(2)}) async-start(bf16[16,2,2,64,128]{4,3,2,1,0:T(8,128)(2,1)} %copy-done.7), calls=%async_computation.1 | async-start | bytes 2097152 | tf_op jit(solution)/shard_map/all_to_all | solution.py:378
  42.7 0.7 all-gather.5.cloned.1.call-update
  43.3 17.2 %all-to-all-done.1.refs_1_.refs_0_ = bf16[16,2,2,64,128]{4,3,2,1,0:T(8,128)(2,1)S(1)} async-done(((bf16[16,2,2,64,128]{4,3,2,1,0:T(8,128)(2,1)}), bf16[16,2,2,64,128]{4,3,2,1,0:T(8,128)(2,1)S(1)}, u32[]{:S(2)}, u32[]{:S(2)}) %all-to-all-start.1) | async-done | bytes 1048608 | tf_op jit(solution)/shard_map/all_to_all | solution.py:378
  60.6 1.0 copy-done.5
  61.6 3.7 %all-to-all-start.2 = ((bf16[16,2,64,256]{3,2,1,0:T(8,128)(2,1)}), bf16[16,2,64,256]{3,2,1,0:T(8,128)(2,1)S(1)}, u32[]{:S(2)}, u32[]{:S(2)}) async-start(bf16[16,2,64,256]{3,2,1,0:T(8,128)(2,1)} %copy-done.5), calls=%async_computation.2 | async-start | bytes 2097152 | tf_op jit(solution)/shard_map/all_to_all | solution.py:379
  65.3 8.9 %all-gather.5.cloned.1.call-done = bf16[1024,640]{1,0:T(8,128)(2,1)} async-done(((bf16[256,640]{1,0:T(8,128)(2,1)}), bf16[1024,640]{1,0:T(8,128)(2,1)}) %all-gather.5.cloned.1.call-update) | async-done | bytes 1310736 | tf_op jit(solution)/shard_map/all_gather | solution.py:385
  74.2 10.3 %all-to-all-done.2.refs_1_.q_ref = bf16[16,2,64,256]{3,2,1,0:T(8,128)(2,1)S(1)} async-done(((bf16[16,2,64,256]{3,2,1,0:T(8,128)(2,1)}), bf16[16,2,64,256]{3,2,1,0:T(8,128)(2,1)S(1)}, u32[]{:S(2)}, u32[]{:S(2)}) %all-to-all-start.2) | async-done | bytes 1048608 | tf_op jit(solution)/shard_map/all_to_all | solution.py:379
  84.5 1.0 copy-done.1
  85.5 0.7 hold.18
  86.2 1.2 copy-done.2
  87.4 4.4 %collective-permute-start.3 = (bf16[16,2,2,64,128]{4,3,2,1,0:T(8,128)(2,1)S(1)}, bf16[16,2,2,64,128]{4,3,2,1,0:T(8,128)(2,1)}, u32[]{:S(2)}, u32[]{:S(2)}) collective-permute-start(bf16[16,2,2,64,128]{4,3,2,1,0:T(8,128)(2,1)S(1)} %hold.13.own_ref), channel_id=1, source_target_pairs={{0,16},{16,32},{32,48},{48,64},{64,80},{80,96},{96,112},{1,17},{17... | collective-permute-start | bytes 3145736 | tf_op jit(solution)/shard_map/ppermute | solution.py:381
  91.7 1.3 collective-permute-start.4
  93.1 5.5 %collective-permute-start.1 = (bf16[16,2,2,64,128]{4,3,2,1,0:T(8,128)(2,1)S(1)}, bf16[16,2,2,64,128]{4,3,2,1,0:T(8,128)(2,1)}, u32[]{:S(2)}, u32[]{:S(2)}) collective-permute-start(bf16[16,2,2,64,128]{4,3,2,1,0:T(8,128)(2,1)S(1)} %hold.12.own_ref), channel_id=1, source_target_pairs={{0,16},{16,32},{32,48},{48,64},{64,80},{80,96},{96,112},{1,17},{17... | collective-permute-start | bytes 3145736 | tf_op jit(solution)/shard_map/ppermute | solution.py:383
  98.6 1.3 collective-permute-start.2
  99.9 14.4 %collective-permute-done.3.before_ref = bf16[16,2,2,64,128]{4,3,2,1,0:T(8,128)(2,1)} collective-permute-done((bf16[16,2,2,64,128]{4,3,2,1,0:T(8,128)(2,1)S(1)}, bf16[16,2,2,64,128]{4,3,2,1,0:T(8,128)(2,1)}, u32[]{:S(2)}, u32[]{:S(2)}) %collective-permute-start.3) | collective-permute-done | bytes 1048608 | tf_op jit(solution)/shard_map/ppermute | solution.py:381
  114.3 5.5 %collective-permute-done.4.after_ref = bf16[16,2,2,64,128]{4,3,2,1,0:T(8,128)(2,1)} collective-permute-done((bf16[16,2,2,64,128]{4,3,2,1,0:T(8,128)(2,1)S(1)}, bf16[16,2,2,64,128]{4,3,2,1,0:T(8,128)(2,1)}, u32[]{:S(2)}, u32[]{:S(2)}) %collective-permute-start.4) | collective-permute-done | bytes 1048608 | tf_op jit(solution)/shard_map/ppermute | solution.py:381
  119.8 9.0 %attend.4 = (bf16[16,1,64,128]{3,2,1,0:T(8,128)(2,1)S(1)}, f32[8,128]{1,0:T(8,128)S(1)}) custom-call(s32[1]{0:T(128)} %bitcast.pos_ref, bf16[16,2,64,256]{3,2,1,0:T(8,128)(2,1)S(1)} %copy-done.2, bf16[16,2,2,64,128]{4,3,2,1,0:T(8,128)(2,1)S(1)} %hold.13.own_ref, bf16[16,2,2,64,128]{4,3,2,1,0:T(8,128)(2,1)} %collective-permute-done.3.before_ref, ...), custom_call_target="tpu_custom_call" | custom-call | flops 5368709120 | bytes 4194304 | tf_op jit(solution)/shard_map/attend/pallas_call | solution.py:169
  128.8 0.7 collective-permute-start.5
  129.5 9.1 %attend.5 = (bf16[16,1,64,128]{3,2,1,0:T(8,128)(2,1)S(1)}, f32[8,128]{1,0:T(8,128)S(1)}) custom-call(s32[1]{0:T(128)} %bitcast.pos_ref, bf16[16,2,64,256]{3,2,1,0:T(8,128)(2,1)S(1)} %copy-done.2, bf16[16,2,2,64,128]{4,3,2,1,0:T(8,128)(2,1)S(1)} %hold.13.own_ref, bf16[16,2,2,64,128]{4,3,2,1,0:T(8,128)(2,1)} %collective-permute-done.3.before_ref, ...), custom_call_target="tpu_custom_call" | custom-call | flops 5368709120 | bytes 4194304 | tf_op jit(solution)/shard_map/attend/pallas_call | solution.py:169
  138.6 0.8 pad_maximum_fusion.rest_1_
  139.5 4.7 %all-to-all-start.3 = ((bf16[16,2,64,128]{3,2,1,0:T(8,128)(2,1)}), bf16[16,2,64,128]{3,2,1,0:T(8,128)(2,1)S(1)}, u32[]{:S(2)}, u32[]{:S(2)}) async-start(bf16[16,2,64,128]{3,2,1,0:T(8,128)(2,1)} %pad_maximum_fusion.rest_1_), calls=%async_computation.3 | async-start | bytes 1048576 | tf_op jit(solution)/shard_map/all_to_all | solution.py:411
  144.2 9.0 %attend.6 = (bf16[16,1,64,128]{3,2,1,0:T(8,128)(2,1)S(1)}, f32[8,128]{1,0:T(8,128)S(1)}) custom-call(s32[1]{0:T(128)} %bitcast.pos_ref, bf16[16,2,64,256]{3,2,1,0:T(8,128)(2,1)S(1)} %copy-done.2, bf16[16,2,2,64,128]{4,3,2,1,0:T(8,128)(2,1)S(1)} %hold.12.own_ref, bf16[16,2,2,64,128]{4,3,2,1,0:T(8,128)(2,1)} %collective-permute-done.1.before_ref.refs_1_, ...), custom_call_target="tpu_custom_call" | custom-call | flops 5368709120 | bytes 4194304 | tf_op jit(solution)/shard_map/attend/pallas_call | solution.py:169
  153.2 0.7 copy-done.13
  153.9 2.6 all-to-all-done.3.refs_0_
  156.5 9.0 %attend.7 = (bf16[16,1,64,128]{3,2,1,0:T(8,128)(2,1)S(1)}, f32[8,128]{1,0:T(8,128)S(1)}) custom-call(s32[1]{0:T(128)} %bitcast.pos_ref, bf16[16,2,64,256]{3,2,1,0:T(8,128)(2,1)S(1)} %copy-done.2, bf16[16,2,2,64,128]{4,3,2,1,0:T(8,128)(2,1)S(1)} %hold.12.own_ref, bf16[16,2,2,64,128]{4,3,2,1,0:T(8,128)(2,1)} %collective-permute-done.1.before_ref.refs_1_, ...), custom_call_target="tpu_custom_call" | custom-call | flops 5368709120 | bytes 4194304 | tf_op jit(solution)/shard_map/attend/pallas_call | solution.py:169
  165.6 0.7 copy-done.15
  166.3 0.6 copy-done.17
  166.9 0.7 hold.19.wo_ref
  167.6 0.2 copy-done.14
  167.9 0.7 collective-permute-start.6
  168.5 0.5 collective-permute-start.7
  169.1 4.4 %collective-permute-start.8 = (bf16[16,2,64,128]{3,2,1,0:T(8,128)(2,1)S(1)}, bf16[16,2,64,128]{3,2,1,0:T(8,128)(2,1)S(1)}, u32[]{:S(2)}, u32[]{:S(2)}) collective-permute-start(bf16[16,2,64,128]{3,2,1,0:T(8,128)(2,1)S(1)} %hold.14.rest_1_.mine_ref), channel_id=1, source_target_pairs={{16,0},{32,16},{48,32},{0,48},{80,64},{96,80},{112,96},{64,112},{1... | collective-permute-start | bytes 1572872 | tf_op jit(solution)/shard_map/ppermute | solution.py:398
  173.5 0.7 hold.16
  174.2 1.3 collective-permute-start.9
  175.6 0.8 pad_maximum_fusion.1.refs_0_
  176.4 9.7 %collective-permute-done.7.refs_1_.left_ref = bf16[16,2,64,128]{3,2,1,0:T(8,128)(2,1)S(1)} collective-permute-done((bf16[16,2,64,128]{3,2,1,0:T(8,128)(2,1)S(1)}, bf16[16,2,64,128]{3,2,1,0:T(8,128)(2,1)S(1)}, u32[]{:S(2)}, u32[]{:S(2)}) %collective-permute-start.7) | collective-permute-done | bytes 524320 | tf_op jit(solution)/shard_map/ppermute | solution.py:397
  186.1 4.6 %all-to-all-start.4 = ((bf16[16,2,64,128]{3,2,1,0:T(8,128)(2,1)}), bf16[16,2,64,128]{3,2,1,0:T(8,128)(2,1)S(1)}, u32[]{:S(2)}, u32[]{:S(2)}) async-start(bf16[16,2,64,128]{3,2,1,0:T(8,128)(2,1)} %hold.15), calls=%async_computation.4 | async-start | bytes 1048576 | tf_op jit(solution)/shard_map/all_to_all | solution.py:418
  190.7 0.9 collective-permute-start.10
  191.6 2.5 collective-permute-start.11
  194.1 1.4 collective-permute-done.9.refs_1_.shifted_ref
  195.5 10.0 %collective-permute-done.10.refs_2_.low_ref = bf16[8,2,64,128]{3,2,1,0:T(8,128)(2,1)S(1)} collective-permute-done((bf16[8,2,64,128]{3,2,1,0:T(8,128)(2,1)S(1)}, bf16[8,2,64,128]{3,2,1,0:T(8,128)(2,1)S(1)}, u32[]{:S(2)}, u32[]{:S(2)}) %collective-permute-start.10) | collective-permute-done | bytes 262176 | tf_op jit(solution)/shard_map/ppermute | solution.py:399
  205.5 2.3 all-to-all-done.4.refs_0_
  207.8 0.7 copy-done.8
  208.5 0.7 copy-done.10
  209.2 3.2 %collective-permute-start.13 = (bf16[16,2,64,128]{3,2,1,0:T(8,128)(2,1)S(1)}, bf16[16,2,64,128]{3,2,1,0:T(8,128)(2,1)}, u32[]{:S(2)}, u32[]{:S(2)}) collective-permute-start(bf16[16,2,64,128]{3,2,1,0:T(8,128)(2,1)S(1)} %hold.17.mine_ref), channel_id=1, source_target_pairs={{16,0},{32,16},{48,32},{0,48},{80,64},{96,80},{112,96},{64,112},{1... | collective-permute-start | bytes 1572872 | tf_op jit(solution)/shard_map/ppermute | solution.py:398
  212.4 11.9 %collective-permute-done.12.left_ref = bf16[16,2,64,128]{3,2,1,0:T(8,128)(2,1)S(1)} collective-permute-done((bf16[16,2,64,128]{3,2,1,0:T(8,128)(2,1)S(1)}, bf16[16,2,64,128]{3,2,1,0:T(8,128)(2,1)S(1)}, u32[]{:S(2)}, u32[]{:S(2)}) %collective-permute-start.12) | collective-permute-done | bytes 524320 | tf_op jit(solution)/shard_map/ppermute | solution.py:397
  224.3 0.3 collective-permute-start.14
  224.7 1.0 slice.24
  225.6 3.3 %collective-permute-start.15 = (bf16[8,2,64,128]{3,2,1,0:T(8,128)(2,1)S(1)}, bf16[8,2,64,128]{3,2,1,0:T(8,128)(2,1)S(1)}, u32[]{:S(2)}, u32[]{:S(2)}) collective-permute-start(bf16[8,2,64,128]{3,2,1,0:T(8,128)(2,1)S(1)} %slice.24), channel_id=1, source_target_pairs={{16,0},{32,16},{48,32},{0,48},{80,64},{96,80},{112,96},{64,112},{1... | collective-permute-start | bytes 786440 | tf_op jit(solution)/shard_map/ppermute | solution.py:400
  228.9 0.1 pad_add_fusion.place_ref
  229.0 0.9 copy-done.9
  229.9 0.9 copy-done.11
  230.9 6.5 %project_first.1.rest_0_ = f32[2,512,640]{2,1,0:T(8,128)S(1)} custom-call(s32[2]{0:T(128)S(1)} %pad_add_fusion.place_ref, bf16[16,2,64,128]{3,2,1,0:T(8,128)(2,1)S(1)} %hold.14.rest_1_.mine_ref, bf16[16,2,64,128]{3,2,1,0:T(8,128)(2,1)S(1)} %collective-permute-done.7.refs_1_.left_ref, bf16[16,2,64,128]{3,2,1,0:T(8,128)(2,1)S(1)} %collective-permute-done.8.refs_2_.right_ref, ...), custom_call_target="tpu_custom_call" | custom-call | flops 2684354560 | bytes 8388608 | tf_op jit(solution)/shard_map/project_first/pallas_call | solution.py:263
  237.4 6.8 %project_last.1 = bf16[8,2,64,640]{3,2,1,0:T(8,128)(2,1)S(1)} custom-call(s32[2]{0:T(128)S(1)} %pad_add_fusion.place_ref, bf16[16,2,64,128]{3,2,1,0:T(8,128)(2,1)S(1)} %hold.17.mine_ref, bf16[16,2,64,128]{3,2,1,0:T(8,128)(2,1)S(1)} %collective-permute-done.12.left_ref, bf16[16,2,64,128]{3,2,1,0:T(8,128)(2,1)} %collective-permute-done.13.right_ref, ...), custom_call_target="tpu_custom_call" | custom-call | flops 2684354560 | bytes 8388608 | tf_op jit(solution)/shard_map/project_last/pallas_call | solution.py:263
  244.2 19.6 %all_to_all.30 = bf16[8,2,64,640]{3,2,1,0:T(8,128)(2,1)S(1)} all-to-all(bf16[8,2,64,640]{3,2,1,0:T(8,128)(2,1)S(1)} %project_last.1), channel_id=1, replica_groups={{0,16,32,48},{64,80,96,112},{1,17,33,49},{65,81,97,113},{2,18,34,50},{6..., dimensions={0} | all-to-all | bytes 2621440 | tf_op jit(solution)/shard_map/all_to_all | solution.py:423
  263.8 1.4 add_branch.1
  (58 shorter events, 0.3 us)
Async XLA Ops:
  6.5 12.9 %copy-start = (f32[50,640]{1,0:T(8,128)S(1)}, f32[50,640]{1,0:T(8,128)}, u32[]{:S(2)}) copy-start(f32[50,640]{1,0:T(8,128)} %param.13) | copy-start | bytes 384004
  11.1 8.3 %copy-start.18 = (s32[16]{0:T(128)S(1)}, s32[16]{0:T(128)}, u32[]{:S(2)}) copy-start(s32[16]{0:T(128)} %param.14) | copy-start | bytes 196
  11.1 26.7 %copy-start.6 = (bf16[16,2,2,64,128]{4,3,2,1,0:T(8,128)(2,1)S(1)}, bf16[16,2,2,64,128]{4,3,2,1,0:T(8,128)(2,1)}, u32[]{:S(2)}) copy-start(bf16[16,2,2,64,128]{4,3,2,1,0:T(8,128)(2,1)} %get-tuple-element.18.refs_0_) | copy-start | bytes 3145732
  11.1 26.7 %all-to-all-start = ((bf16[16,2,2,64,128]{4,3,2,1,0:T(8,128)(2,1)}), bf16[16,2,2,64,128]{4,3,2,1,0:T(8,128)(2,1)S(1)}, u32[]{:S(2)}, u32[]{:S(2)}) async-start(bf16[16,2,2,64,128]{4,3,2,1,0:T(8,128)(2,1)} %get-tuple-element.19), calls=%async_computation | async-start | bytes 2097152 | tf_op jit(solution)/shard_map/all_to_all | solution.py:377
  19.7 14.0 %collective-permute-start = (f32[16,640]{1,0:T(8,128)S(1)}, f32[16,640]{1,0:T(8,128)S(1)}, u32[]{:S(2)}, u32[]{:S(2)}) collective-permute-start(f32[16,640]{1,0:T(8,128)S(1)} %fusion), channel_id=1, source_target_pairs={{0,64},{16,80},{32,96},{48,112},{64,0},{80,16},{96,32},{112,48},{1... | collective-permute-start | bytes 122888 | tf_op jit(solution)/shard_map/ppermute | solution.py:366
  37.8 1.0 copy-start.7
  38.8 21.8 %copy-start.4 = (bf16[16,2,64,256]{3,2,1,0:T(8,128)(2,1)S(1)}, bf16[16,2,64,256]{3,2,1,0:T(8,128)(2,1)}, u32[]{:S(2)}) copy-start(bf16[16,2,64,256]{3,2,1,0:T(8,128)(2,1)} %get-tuple-element.17.refs_0_) | copy-start | bytes 3145732
  38.8 21.8 %all-to-all-start.1 = ((bf16[16,2,2,64,128]{4,3,2,1,0:T(8,128)(2,1)}), bf16[16,2,2,64,128]{4,3,2,1,0:T(8,128)(2,1)S(1)}, u32[]{:S(2)}, u32[]{:S(2)}) async-start(bf16[16,2,2,64,128]{4,3,2,1,0:T(8,128)(2,1)} %copy-done.7), calls=%async_computation.1 | async-start | bytes 2097152 | tf_op jit(solution)/shard_map/all_to_all | solution.py:378
  42.6 31.6 %all-gather.5.cloned.1.call-start = ((), (), s32[]{:S(2)}) async-start(), calls=%async_computation.6 | async-start | bytes 1638400 | tf_op jit(solution)/shard_map/all_gather | solution.py:385
  60.6 1.0 copy-start.5
  61.6 22.9 %all-to-all-start.2 = ((bf16[16,2,64,256]{3,2,1,0:T(8,128)(2,1)}), bf16[16,2,64,256]{3,2,1,0:T(8,128)(2,1)S(1)}, u32[]{:S(2)}, u32[]{:S(2)}) async-start(bf16[16,2,64,256]{3,2,1,0:T(8,128)(2,1)} %copy-done.5), calls=%async_computation.2 | async-start | bytes 2097152 | tf_op jit(solution)/shard_map/all_to_all | solution.py:379
  65.2 101.7 %all-gather.7.cloned.1.call-start = ((), (), s32[]{:S(2)}) async-start(), calls=%async_computation.7 | async-start | bytes 6553600 | tf_op jit(solution)/shard_map/all_gather | solution.py:387
  84.5 1.0 copy-start.1
  86.2 1.2 copy-start.2
  87.4 26.9 %collective-permute-start.3 = (bf16[16,2,2,64,128]{4,3,2,1,0:T(8,128)(2,1)S(1)}, bf16[16,2,2,64,128]{4,3,2,1,0:T(8,128)(2,1)}, u32[]{:S(2)}, u32[]{:S(2)}) collective-permute-start(bf16[16,2,2,64,128]{4,3,2,1,0:T(8,128)(2,1)S(1)} %hold.13.own_ref), channel_id=1, source_target_pairs={{0,16},{16,32},{32,48},{48,64},{64,80},{80,96},{96,112},{1,17},{17... | collective-permute-start | bytes 3145736 | tf_op jit(solution)/shard_map/ppermute | solution.py:381
  91.7 28.1 %collective-permute-start.4 = (bf16[16,2,2,64,128]{4,3,2,1,0:T(8,128)(2,1)S(1)}, bf16[16,2,2,64,128]{4,3,2,1,0:T(8,128)(2,1)}, u32[]{:S(2)}, u32[]{:S(2)}) collective-permute-start(bf16[16,2,2,64,128]{4,3,2,1,0:T(8,128)(2,1)S(1)} %hold.13.own_ref), channel_id=1, source_target_pairs={{16,0},{32,16},{48,32},{64,48},{80,64},{96,80},{112,96},{17,1},{33... | collective-permute-start | bytes 3145736 | tf_op jit(solution)/shard_map/ppermute | solution.py:381
  93.1 51.1 %collective-permute-start.1 = (bf16[16,2,2,64,128]{4,3,2,1,0:T(8,128)(2,1)S(1)}, bf16[16,2,2,64,128]{4,3,2,1,0:T(8,128)(2,1)}, u32[]{:S(2)}, u32[]{:S(2)}) collective-permute-start(bf16[16,2,2,64,128]{4,3,2,1,0:T(8,128)(2,1)S(1)} %hold.12.own_ref), channel_id=1, source_target_pairs={{0,16},{16,32},{32,48},{48,64},{64,80},{80,96},{96,112},{1,17},{17... | collective-permute-start | bytes 3145736 | tf_op jit(solution)/shard_map/ppermute | solution.py:383
  98.6 45.6 %collective-permute-start.2 = (bf16[16,2,2,64,128]{4,3,2,1,0:T(8,128)(2,1)S(1)}, bf16[16,2,2,64,128]{4,3,2,1,0:T(8,128)(2,1)}, u32[]{:S(2)}, u32[]{:S(2)}) collective-permute-start(bf16[16,2,2,64,128]{4,3,2,1,0:T(8,128)(2,1)S(1)} %hold.12.own_ref), channel_id=1, source_target_pairs={{16,0},{32,16},{48,32},{64,48},{80,64},{96,80},{112,96},{17,1},{33... | collective-permute-start | bytes 3145736 | tf_op jit(solution)/shard_map/ppermute | solution.py:383
  128.8 9.8 %collective-permute-start.5 = (bf16[16,1,64,128]{3,2,1,0:T(8,128)(2,1)S(1)}, bf16[16,1,64,128]{3,2,1,0:T(8,128)(2,1)S(1)}, u32[]{:S(2)}, u32[]{:S(2)}) collective-permute-start(bf16[16,1,64,128]{3,2,1,0:T(8,128)(2,1)S(1)} %get-tuple-element.23), channel_id=1, source_target_pairs={{48,112},{49,113},{50,114},{51,115},{52,116},{53,117},{54,118},{55... | collective-permute-start | bytes 786440 | tf_op jit(solution)/shard_map/ppermute | solution.py:406
  139.5 17.1 %all-to-all-start.3 = ((bf16[16,2,64,128]{3,2,1,0:T(8,128)(2,1)}), bf16[16,2,64,128]{3,2,1,0:T(8,128)(2,1)S(1)}, u32[]{:S(2)}, u32[]{:S(2)}) async-start(bf16[16,2,64,128]{3,2,1,0:T(8,128)(2,1)} %pad_maximum_fusion.rest_1_), calls=%async_computation.3 | async-start | bytes 1048576 | tf_op jit(solution)/shard_map/all_to_all | solution.py:411
  153.2 0.7 copy-start.13
  165.6 0.7 copy-start.15
  166.3 0.6 copy-start.17
  166.9 1.0 copy-start.14
  167.6 61.4 %collective-permute-start.16 = (bf16[4,2,2,256,640]{4,3,2,1,0:T(8,128)(2,1)}, bf16[4,2,2,256,640]{4,3,2,1,0:T(8,128)(2,1)}, u32[]{:S(2)}, u32[]{:S(2)}) collective-permute-start(bf16[4,2,2,256,640]{4,3,2,1,0:T(8,128)(2,1)} %hold.19.wo_ref), channel_id=1, source_target_pairs={{0,1},{1,0},{2,3},{3,2},{4,5},{5,4},{6,7},{7,6},{8,9},{9,8},{10,11... | collective-permute-start | bytes 15728648 | tf_op jit(solution)/shard_map/ppermute | solution.py:416
  167.9 7.7 %collective-permute-start.6 = (bf16[16,1,64,128]{3,2,1,0:T(8,128)(2,1)S(1)}, bf16[16,1,64,128]{3,2,1,0:T(8,128)(2,1)S(1)}, u32[]{:S(2)}, u32[]{:S(2)}) collective-permute-start(bf16[16,1,64,128]{3,2,1,0:T(8,128)(2,1)S(1)} %copy-done.14), channel_id=1, source_target_pairs={{48,112},{49,113},{50,114},{51,115},{52,116},{53,117},{54,118},{55... | collective-permute-start | bytes 786440 | tf_op jit(solution)/shard_map/ppermute | solution.py:410
  168.5 17.6 %collective-permute-start.7 = (bf16[16,2,64,128]{3,2,1,0:T(8,128)(2,1)S(1)}, bf16[16,2,64,128]{3,2,1,0:T(8,128)(2,1)S(1)}, u32[]{:S(2)}, u32[]{:S(2)}) collective-permute-start(bf16[16,2,64,128]{3,2,1,0:T(8,128)(2,1)S(1)} %hold.14.rest_1_.mine_ref), channel_id=1, source_target_pairs={{0,16},{16,32},{32,48},{48,0},{64,80},{80,96},{96,112},{112,64},{1... | collective-permute-start | bytes 1572872 | tf_op jit(solution)/shard_map/ppermute | solution.py:397
  169.1 17.0 %collective-permute-start.8 = (bf16[16,2,64,128]{3,2,1,0:T(8,128)(2,1)S(1)}, bf16[16,2,64,128]{3,2,1,0:T(8,128)(2,1)S(1)}, u32[]{:S(2)}, u32[]{:S(2)}) collective-permute-start(bf16[16,2,64,128]{3,2,1,0:T(8,128)(2,1)S(1)} %hold.14.rest_1_.mine_ref), channel_id=1, source_target_pairs={{16,0},{32,16},{48,32},{0,48},{80,64},{96,80},{112,96},{64,112},{1... | collective-permute-start | bytes 1572872 | tf_op jit(solution)/shard_map/ppermute | solution.py:398
  173.5 2.1 copy-start.16
  174.2 21.3 %collective-permute-start.9 = (bf16[1,64,5120]{2,1,0:T(8,128)(2,1)}, bf16[1,64,5120]{2,1,0:T(8,128)(2,1)S(1)}, u32[]{:S(2)}, u32[]{:S(2)}) collective-permute-start(bf16[1,64,5120]{2,1,0:T(8,128)(2,1)} %hold.16), channel_id=1, source_target_pairs={{0,16},{16,32},{32,48},{48,64},{64,80},{80,96},{96,112},{1,17},{17... | collective-permute-start | bytes 1966088 | tf_op jit(solution)/shard_map/ppermute | solution.py:413
  186.1 21.7 %all-to-all-start.4 = ((bf16[16,2,64,128]{3,2,1,0:T(8,128)(2,1)}), bf16[16,2,64,128]{3,2,1,0:T(8,128)(2,1)S(1)}, u32[]{:S(2)}, u32[]{:S(2)}) async-start(bf16[16,2,64,128]{3,2,1,0:T(8,128)(2,1)} %hold.15), calls=%async_computation.4 | async-start | bytes 1048576 | tf_op jit(solution)/shard_map/all_to_all | solution.py:418
  190.7 14.8 %collective-permute-start.10 = (bf16[8,2,64,128]{3,2,1,0:T(8,128)(2,1)S(1)}, bf16[8,2,64,128]{3,2,1,0:T(8,128)(2,1)S(1)}, u32[]{:S(2)}, u32[]{:S(2)}) collective-permute-start(bf16[8,2,64,128]{3,2,1,0:T(8,128)(2,1)S(1)} %slice.21), channel_id=1, source_target_pairs={{0,16},{16,32},{32,48},{48,0},{64,80},{80,96},{96,112},{112,64},{1... | collective-permute-start | bytes 786440 | tf_op jit(solution)/shard_map/ppermute | solution.py:399
  191.6 13.9 %collective-permute-start.11 = (bf16[8,2,64,128]{3,2,1,0:T(8,128)(2,1)S(1)}, bf16[8,2,64,128]{3,2,1,0:T(8,128)(2,1)S(1)}, u32[]{:S(2)}, u32[]{:S(2)}) collective-permute-start(bf16[8,2,64,128]{3,2,1,0:T(8,128)(2,1)S(1)} %slice.22), channel_id=1, source_target_pairs={{16,0},{32,16},{48,32},{0,48},{80,64},{96,80},{112,96},{64,112},{1... | collective-permute-start | bytes 786440 | tf_op jit(solution)/shard_map/ppermute | solution.py:400
  207.8 0.7 copy-start.8
  208.5 0.7 copy-start.10
  209.2 15.1 %collective-permute-start.12 = (bf16[16,2,64,128]{3,2,1,0:T(8,128)(2,1)S(1)}, bf16[16,2,64,128]{3,2,1,0:T(8,128)(2,1)S(1)}, u32[]{:S(2)}, u32[]{:S(2)}) collective-permute-start(bf16[16,2,64,128]{3,2,1,0:T(8,128)(2,1)S(1)} %hold.17.mine_ref), channel_id=1, source_target_pairs={{0,16},{16,32},{32,48},{48,0},{64,80},{80,96},{96,112},{112,64},{1... | collective-permute-start | bytes 1572872 | tf_op jit(solution)/shard_map/ppermute | solution.py:397
  209.2 15.4 %collective-permute-start.13 = (bf16[16,2,64,128]{3,2,1,0:T(8,128)(2,1)S(1)}, bf16[16,2,64,128]{3,2,1,0:T(8,128)(2,1)}, u32[]{:S(2)}, u32[]{:S(2)}) collective-permute-start(bf16[16,2,64,128]{3,2,1,0:T(8,128)(2,1)S(1)} %hold.17.mine_ref), channel_id=1, source_target_pairs={{16,0},{32,16},{48,32},{0,48},{80,64},{96,80},{112,96},{64,112},{1... | collective-permute-start | bytes 1572872 | tf_op jit(solution)/shard_map/ppermute | solution.py:398
  224.3 13.0 %collective-permute-start.14 = (bf16[8,2,64,128]{3,2,1,0:T(8,128)(2,1)S(1)}, bf16[8,2,64,128]{3,2,1,0:T(8,128)(2,1)S(1)}, u32[]{:S(2)}, u32[]{:S(2)}) collective-permute-start(bf16[8,2,64,128]{3,2,1,0:T(8,128)(2,1)S(1)} %slice.23), channel_id=1, source_target_pairs={{0,16},{16,32},{32,48},{48,0},{64,80},{80,96},{96,112},{112,64},{1... | collective-permute-start | bytes 786440 | tf_op jit(solution)/shard_map/ppermute | solution.py:399
  225.6 11.8 %collective-permute-start.15 = (bf16[8,2,64,128]{3,2,1,0:T(8,128)(2,1)S(1)}, bf16[8,2,64,128]{3,2,1,0:T(8,128)(2,1)S(1)}, u32[]{:S(2)}, u32[]{:S(2)}) collective-permute-start(bf16[8,2,64,128]{3,2,1,0:T(8,128)(2,1)S(1)} %slice.24), channel_id=1, source_target_pairs={{16,0},{32,16},{48,32},{0,48},{80,64},{96,80},{112,96},{64,112},{1... | collective-permute-start | bytes 786440 | tf_op jit(solution)/shard_map/ppermute | solution.py:400
  229.0 1.0 copy-start.9
  229.9 0.9 copy-start.11
  244.2 19.6 %copy-start.3 = (bf16[2,64,5120]{2,1,0:T(8,128)(2,1)S(1)}, bf16[2,64,5120]{2,1,0:T(8,128)(2,1)}, u32[]{:S(2)}) copy-start(bf16[2,64,5120]{2,1,0:T(8,128)(2,1)} %hidden_ref.3) | copy-start | bytes 3932164
  244.2 19.6 %copy-start.12 = (bf16[64,5120]{1,0:T(8,128)(2,1)S(1)}, bf16[64,5120]{1,0:T(8,128)(2,1)}, u32[]{:S(2)}) copy-start(bf16[64,5120]{1,0:T(8,128)(2,1)} %entering_ref.1) | copy-start | bytes 1966084
Sparse Core Ops, SparseCore 0:
  45.1 29.0 all-gather.4
  86.3 56.1 all-gather.6

commit v12 on v10

--- a/solution.py
+++ b/solution.py
@@ -414,8 +414,8 @@
     even1, token = attend(0, *head1, token, first)
     weight_own = hold(weight, token, room=56)
     weight_pair = lax.ppermute(weight_own, "spatial", swap_core)
-    second = to_heads(with_crossing(even1, odd1, odd1_crossing))
-    second_sources = spread(hold(second, shifted))
+    second = hold(with_crossing(even1, odd1, odd1_crossing), shifted)
+    second_sources = spread(to_heads(second))
 
     partial = project(0, place, first_sources, weight_own, weight_pair, None, None)
     branch = project(1, place, second_sources, weight_own, weight_pair, partial, gates)

time: 264 us -> 270 us (1.023)
  waiting for transfers between devices: 100 us -> 105 us
    ppermute x1, waiting for transfers between devices: 1.8 us -> 12.6 us  [body(): shifted = lax.ppermute(hold(last_frame, kv1_before, token), 'queue', up)]
    all_to_all x1, waiting for transfers between devices: 12.3 us -> 6 us  [body(): second_sources = spread(to_heads(second))]
    ppermute x2, starting transfers between devices: 1.14 us -> 5.03 us  [spread(): left = lax.ppermute(mine, 'queue', ring_up)]
    unnamed x31 -> x33, local copies, waits for them, and re-layouts: 6.37 us -> 5.87 us
  transfers between devices with their start and end apart: 24 -> 24, of which waited for: 13 -> 13; matrix products, arithmetic and copies ran while one was open for 2% -> 2% of each run, Pallas kernels for 17% -> 16%
where the time goes in v12:
time: 270 us; the launch traced here: 268 us
  waiting for transfers between devices  105 us (39%)
  starting transfers between devices  61.5 us (23%)
  Pallas kernels  57.7 us (21%)
  blocking collectives  19.3 us (7%)
  between operations  13.8 us (5%)
  local copies, waits for them, and re-layouts  8.31 us (3%)
    pallas_call x4, Pallas kernels, attend(): pl.pallas_call(kernel, grid_spec=pltpu.PrefetchScalarGridSpec(num_scalar_...  36.1 us
    all_to_all x1, blocking collectives, body(): lax.all_to_all(branch, 'queue', split_axis=0, concat_axis=0, axis_index_g...  19.3 us
    all_to_all x1, waiting for transfers between devices, body(): kv1_heads = to_heads(hold(kv1, kv0, gates))  17.2 us
    ppermute x1, waiting for transfers between devices, body(): lax.ppermute(kv0, 'queue', up)  14.4 us
    pallas_call x2, Pallas kernels, project(): pl.pallas_call(kernel, grid_spec=pltpu.PrefetchScalarGridSpec(num_scalar_...  13.4 us
    ppermute x1, waiting for transfers between devices, body(): other_gates = lax.ppermute(gates, 'queue', swap_low)  13.3 us
    ppermute x1, waiting for transfers between devices, body(): shifted = lax.ppermute(hold(last_frame, kv1_before, token), 'queue', up)  12.6 us
    all_to_all x1, waiting for transfers between devices, body(): query = to_heads(hold(query, kv1_heads))  10.3 us
  transfers between devices with their start and end apart: 24, of which 13 were waited for; matrix products, arithmetic and copies ran while one was open for 2% of the time, Pallas kernels for 16%

profile of v12, /device:TPU:0, one launch (start us, length us, event | category | flops | bytes accessed | tf_op | source)
XLA Modules:
  0.0 267.6 jit_solution(11694168272227013168)
XLA Ops:
  6.5 4.6 %pack.1 = (bf16[16,2,2,64,128]{4,3,2,1,0:T(8,128)(2,1)}, bf16[16,2,2,64,128]{4,3,2,1,0:T(8,128)(2,1)}, bf16[16,2,64,256]{3,2,1,0:T(8,128)(2,1)}, bf16[1,64,5120]{2,1,0:T(8,128)(2,1)}) custom-call(bf16[2,64,4096]{2,1,0:T(8,128)(2,1)} %q_ref.1, bf16[2,64,4096]{2,1,0:T(8,128)(2,1)} %k_ref.1, bf16[2,64,4096]{2,1,0:T(8,128)(2,1)} %v_ref.1, ...), custom_call_target="tpu_custom_call" | custom-call | tf_op jit(solution)/shard_map/pack/pallas_call | solution.py:54
  11.1 8.3 %all-to-all-start = ((bf16[16,2,2,64,128]{4,3,2,1,0:T(8,128)(2,1)}), bf16[16,2,2,64,128]{4,3,2,1,0:T(8,128)(2,1)S(1)}, u32[]{:S(2)}, u32[]{:S(2)}) async-start(bf16[16,2,2,64,128]{4,3,2,1,0:T(8,128)(2,1)} %get-tuple-element.19), calls=%async_computation | async-start | bytes 2097152 | tf_op jit(solution)/shard_map/all_to_all | solution.py:377
  19.4 0.2 fusion
  19.7 0.8 collective-permute-start
  20.4 13.3 %collective-permute-done = f32[16,640]{1,0:T(8,128)S(1)} collective-permute-done((f32[16,640]{1,0:T(8,128)S(1)}, f32[16,640]{1,0:T(8,128)S(1)}, u32[]{:S(2)}, u32[]{:S(2)}) %collective-permute-start) | collective-permute-done | bytes 40992 | tf_op jit(solution)/shard_map/ppermute | solution.py:366
  33.7 0.1 dynamic-slice_select_fusion.refs_2_.rest_1_
  33.8 4.0 %all-to-all-done.refs_1_.refs_0_ = bf16[16,2,2,64,128]{4,3,2,1,0:T(8,128)(2,1)S(1)} async-done(((bf16[16,2,2,64,128]{4,3,2,1,0:T(8,128)(2,1)}), bf16[16,2,2,64,128]{4,3,2,1,0:T(8,128)(2,1)S(1)}, u32[]{:S(2)}, u32[]{:S(2)}) %all-to-all-start) | async-done | bytes 1048608 | tf_op jit(solution)/shard_map/all_to_all | solution.py:377
  37.8 1.0 copy-done.7
  38.8 3.8 %all-to-all-start.1 = ((bf16[16,2,2,64,128]{4,3,2,1,0:T(8,128)(2,1)}), bf16[16,2,2,64,128]{4,3,2,1,0:T(8,128)(2,1)S(1)}, u32[]{:S(2)}, u32[]{:S(2)}) async-start(bf16[16,2,2,64,128]{4,3,2,1,0:T(8,128)(2,1)} %copy-done.7), calls=%async_computation.1 | async-start | bytes 2097152 | tf_op jit(solution)/shard_map/all_to_all | solution.py:378
  42.6 0.0 all-gather.5.cloned.1.call-start
  42.7 0.7 all-gather.5.cloned.1.call-update
  43.3 17.2 %all-to-all-done.1.refs_1_.refs_0_ = bf16[16,2,2,64,128]{4,3,2,1,0:T(8,128)(2,1)S(1)} async-done(((bf16[16,2,2,64,128]{4,3,2,1,0:T(8,128)(2,1)}), bf16[16,2,2,64,128]{4,3,2,1,0:T(8,128)(2,1)S(1)}, u32[]{:S(2)}, u32[]{:S(2)}) %all-to-all-start.1) | async-done | bytes 1048608 | tf_op jit(solution)/shard_map/all_to_all | solution.py:378
  60.6 1.0 copy-done.5
  61.6 3.7 %all-to-all-start.2 = ((bf16[16,2,64,256]{3,2,1,0:T(8,128)(2,1)}), bf16[16,2,64,256]{3,2,1,0:T(8,128)(2,1)S(1)}, u32[]{:S(2)}, u32[]{:S(2)}) async-start(bf16[16,2,64,256]{3,2,1,0:T(8,128)(2,1)} %copy-done.5), calls=%async_computation.2 | async-start | bytes 2097152 | tf_op jit(solution)/shard_map/all_to_all | solution.py:379
  65.2 0.0 all-gather.7.cloned.1.call-start
  65.3 8.9 %all-gather.5.cloned.1.call-done = bf16[1024,640]{1,0:T(8,128)(2,1)} async-done(((bf16[256,640]{1,0:T(8,128)(2,1)}), bf16[1024,640]{1,0:T(8,128)(2,1)}) %all-gather.5.cloned.1.call-update) | async-done | bytes 1310736 | tf_op jit(solution)/shard_map/all_gather | solution.py:385
  74.2 10.3 %all-to-all-done.2.refs_1_.q_ref = bf16[16,2,64,256]{3,2,1,0:T(8,128)(2,1)S(1)} async-done(((bf16[16,2,64,256]{3,2,1,0:T(8,128)(2,1)}), bf16[16,2,64,256]{3,2,1,0:T(8,128)(2,1)S(1)}, u32[]{:S(2)}, u32[]{:S(2)}) %all-to-all-start.2) | async-done | bytes 1048608 | tf_op jit(solution)/shard_map/all_to_all | solution.py:379
  84.5 1.0 copy-done.1
  85.5 0.7 hold.16
  86.2 0.0 all-gather.7.cloned.1.call-update
  86.2 1.2 copy-done.2
  87.4 4.3 %collective-permute-start.3 = (bf16[16,2,2,64,128]{4,3,2,1,0:T(8,128)(2,1)S(1)}, bf16[16,2,2,64,128]{4,3,2,1,0:T(8,128)(2,1)}, u32[]{:S(2)}, u32[]{:S(2)}) collective-permute-start(bf16[16,2,2,64,128]{4,3,2,1,0:T(8,128)(2,1)S(1)} %hold.12.own_ref), channel_id=1, source_target_pairs={{0,16},{16,32},{32,48},{48,64},{64,80},{80,96},{96,112},{1,17},{17... | collective-permute-start | bytes 3145736 | tf_op jit(solution)/shard_map/ppermute | solution.py:381
  91.7 1.3 collective-permute-start.4
  93.0 5.5 %collective-permute-start.1 = (bf16[16,2,2,64,128]{4,3,2,1,0:T(8,128)(2,1)S(1)}, bf16[16,2,2,64,128]{4,3,2,1,0:T(8,128)(2,1)}, u32[]{:S(2)}, u32[]{:S(2)}) collective-permute-start(bf16[16,2,2,64,128]{4,3,2,1,0:T(8,128)(2,1)S(1)} %hold.11.own_ref), channel_id=1, source_target_pairs={{0,16},{16,32},{32,48},{48,64},{64,80},{80,96},{96,112},{1,17},{17... | collective-permute-start | bytes 3145736 | tf_op jit(solution)/shard_map/ppermute | solution.py:383
  98.6 1.3 collective-permute-start.2
  99.9 14.4 %collective-permute-done.3.before_ref = bf16[16,2,2,64,128]{4,3,2,1,0:T(8,128)(2,1)} collective-permute-done((bf16[16,2,2,64,128]{4,3,2,1,0:T(8,128)(2,1)S(1)}, bf16[16,2,2,64,128]{4,3,2,1,0:T(8,128)(2,1)}, u32[]{:S(2)}, u32[]{:S(2)}) %collective-permute-start.3) | collective-permute-done | bytes 1048608 | tf_op jit(solution)/shard_map/ppermute | solution.py:381
  114.3 5.5 %collective-permute-done.4.after_ref = bf16[16,2,2,64,128]{4,3,2,1,0:T(8,128)(2,1)} collective-permute-done((bf16[16,2,2,64,128]{4,3,2,1,0:T(8,128)(2,1)S(1)}, bf16[16,2,2,64,128]{4,3,2,1,0:T(8,128)(2,1)}, u32[]{:S(2)}, u32[]{:S(2)}) %collective-permute-start.4) | collective-permute-done | bytes 1048608 | tf_op jit(solution)/shard_map/ppermute | solution.py:381
  119.8 9.0 %attend.4 = (bf16[16,1,64,128]{3,2,1,0:T(8,128)(2,1)S(1)}, f32[8,128]{1,0:T(8,128)S(1)}) custom-call(s32[1]{0:T(128)} %bitcast.pos_ref, bf16[16,2,64,256]{3,2,1,0:T(8,128)(2,1)S(1)} %copy-done.2, bf16[16,2,2,64,128]{4,3,2,1,0:T(8,128)(2,1)S(1)} %hold.12.own_ref, bf16[16,2,2,64,128]{4,3,2,1,0:T(8,128)(2,1)} %collective-permute-done.3.before_ref, ...), custom_call_target="tpu_custom_call" | custom-call | flops 5368709120 | bytes 4194304 | tf_op jit(solution)/shard_map/attend/pallas_call | solution.py:169
  128.8 0.7 collective-permute-start.5
  129.5 9.1 %attend.5 = (bf16[16,1,64,128]{3,2,1,0:T(8,128)(2,1)S(1)}, f32[8,128]{1,0:T(8,128)S(1)}) custom-call(s32[1]{0:T(128)} %bitcast.pos_ref, bf16[16,2,64,256]{3,2,1,0:T(8,128)(2,1)S(1)} %copy-done.2, bf16[16,2,2,64,128]{4,3,2,1,0:T(8,128)(2,1)S(1)} %hold.12.own_ref, bf16[16,2,2,64,128]{4,3,2,1,0:T(8,128)(2,1)} %collective-permute-done.3.before_ref, ...), custom_call_target="tpu_custom_call" | custom-call | flops 5368709120 | bytes 4194304 | tf_op jit(solution)/shard_map/attend/pallas_call | solution.py:169
  138.6 0.8 pad_maximum_fusion.rest_1_
  139.5 4.7 %all-to-all-start.3 = ((bf16[16,2,64,128]{3,2,1,0:T(8,128)(2,1)}), bf16[16,2,64,128]{3,2,1,0:T(8,128)(2,1)S(1)}, u32[]{:S(2)}, u32[]{:S(2)}) async-start(bf16[16,2,64,128]{3,2,1,0:T(8,128)(2,1)} %pad_maximum_fusion.rest_1_), calls=%async_computation.3 | async-start | bytes 1048576 | tf_op jit(solution)/shard_map/all_to_all | solution.py:411
  144.2 9.0 %attend.6 = (bf16[16,1,64,128]{3,2,1,0:T(8,128)(2,1)S(1)}, f32[8,128]{1,0:T(8,128)S(1)}) custom-call(s32[1]{0:T(128)} %bitcast.pos_ref, bf16[16,2,64,256]{3,2,1,0:T(8,128)(2,1)S(1)} %copy-done.2, bf16[16,2,2,64,128]{4,3,2,1,0:T(8,128)(2,1)S(1)} %hold.11.own_ref, bf16[16,2,2,64,128]{4,3,2,1,0:T(8,128)(2,1)} %collective-permute-done.1.before_ref.refs_1_, ...), custom_call_target="tpu_custom_call" | custom-call | flops 5368709120 | bytes 4194304 | tf_op jit(solution)/shard_map/attend/pallas_call | solution.py:169
  153.2 0.7 copy-done.10
  153.9 2.6 all-to-all-done.3.refs_0_
  156.5 9.0 %attend.7 = (bf16[16,1,64,128]{3,2,1,0:T(8,128)(2,1)S(1)}, f32[8,128]{1,0:T(8,128)S(1)}) custom-call(s32[1]{0:T(128)} %bitcast.pos_ref, bf16[16,2,64,256]{3,2,1,0:T(8,128)(2,1)S(1)} %copy-done.2, bf16[16,2,2,64,128]{4,3,2,1,0:T(8,128)(2,1)S(1)} %hold.11.own_ref, bf16[16,2,2,64,128]{4,3,2,1,0:T(8,128)(2,1)} %collective-permute-done.1.before_ref.refs_1_, ...), custom_call_target="tpu_custom_call" | custom-call | flops 5368709120 | bytes 4194304 | tf_op jit(solution)/shard_map/attend/pallas_call | solution.py:169
  165.6 0.6 copy-done.14
  166.2 0.8 hold.17.wo_ref
  167.0 0.4 copy-done.8
  167.4 0.7 hold.14
  168.1 2.4 collective-permute-start.7
  170.5 0.7 collective-permute-start.6
  171.3 0.8 pad_maximum_fusion.1.refs_0_
  172.1 12.6 %collective-permute-done.7.refs_1_.shifted_ref = bf16[1,64,5120]{2,1,0:T(8,128)(2,1)S(1)} collective-permute-done((bf16[1,64,5120]{2,1,0:T(8,128)(2,1)S(1)}, bf16[1,64,5120]{2,1,0:T(8,128)(2,1)S(1)}, u32[]{:S(2)}, u32[]{:S(2)}) %collective-permute-start.7) | collective-permute-done | bytes 655392 | tf_op jit(solution)/shard_map/ppermute | solution.py:413
  184.7 4.7 %all-to-all-start.4 = ((bf16[16,2,64,128]{3,2,1,0:T(8,128)(2,1)}), bf16[16,2,64,128]{3,2,1,0:T(8,128)(2,1)S(1)}, u32[]{:S(2)}, u32[]{:S(2)}) async-start(bf16[16,2,64,128]{3,2,1,0:T(8,128)(2,1)} %hold.15), calls=%async_computation.4 | async-start | bytes 1048576 | tf_op jit(solution)/shard_map/all_to_all | solution.py:418
  189.4 2.6 collective-permute-start.13
  191.9 3.8 %collective-permute-start.14 = (bf16[16,2,64,128]{3,2,1,0:T(8,128)(2,1)S(1)}, bf16[16,2,64,128]{3,2,1,0:T(8,128)(2,1)}, u32[]{:S(2)}, u32[]{:S(2)}) collective-permute-start(bf16[16,2,64,128]{3,2,1,0:T(8,128)(2,1)S(1)} %hold.13.rest_1_.mine_ref), channel_id=1, source_target_pairs={{16,0},{32,16},{48,32},{0,48},{80,64},{96,80},{112,96},{64,112},{1... | collective-permute-start | bytes 1572872 | tf_op jit(solution)/shard_map/ppermute | solution.py:398
  195.7 6.0 %all-to-all-done.4.mine_ref = bf16[16,2,64,128]{3,2,1,0:T(8,128)(2,1)S(1)} async-done(((bf16[16,2,64,128]{3,2,1,0:T(8,128)(2,1)}), bf16[16,2,64,128]{3,2,1,0:T(8,128)(2,1)S(1)}, u32[]{:S(2)}, u32[]{:S(2)}) %all-to-all-start.4) | async-done | bytes 524320 | tf_op jit(solution)/shard_map/all_to_all | solution.py:418
  201.7 2.5 collective-permute-start.8
  204.2 3.7 %collective-permute-start.9 = (bf16[16,2,64,128]{3,2,1,0:T(8,128)(2,1)S(1)}, bf16[16,2,64,128]{3,2,1,0:T(8,128)(2,1)S(1)}, u32[]{:S(2)}, u32[]{:S(2)}) collective-permute-start(bf16[16,2,64,128]{3,2,1,0:T(8,128)(2,1)S(1)} %all-to-all-done.4.mine_ref), channel_id=1, source_target_pairs={{16,0},{32,16},{48,32},{0,48},{80,64},{96,80},{112,96},{64,112},{1... | collective-permute-start | bytes 1572872 | tf_op jit(solution)/shard_map/ppermute | solution.py:398
  208.0 0.1 collective-permute-done.13.left_ref
  208.1 0.7 slice.23
  208.8 1.7 slice.24
  210.5 3.2 %collective-permute-start.16 = (bf16[8,2,64,128]{3,2,1,0:T(8,128)(2,1)}, bf16[8,2,64,128]{3,2,1,0:T(8,128)(2,1)}, u32[]{:S(2)}, u32[]{:S(2)}) collective-permute-start(bf16[8,2,64,128]{3,2,1,0:T(8,128)(2,1)} %slice.24), channel_id=1, source_target_pairs={{16,0},{32,16},{48,32},{0,48},{80,64},{96,80},{112,96},{64,112},{1... | collective-permute-start | bytes 786440 | tf_op jit(solution)/shard_map/ppermute | solution.py:400
  213.7 7.0 %collective-permute-done.8.left_ref = bf16[16,2,64,128]{3,2,1,0:T(8,128)(2,1)S(1)} collective-permute-done((bf16[16,2,64,128]{3,2,1,0:T(8,128)(2,1)S(1)}, bf16[16,2,64,128]{3,2,1,0:T(8,128)(2,1)S(1)}, u32[]{:S(2)}, u32[]{:S(2)}) %collective-permute-start.8) | collective-permute-done | bytes 524320 | tf_op jit(solution)/shard_map/ppermute | solution.py:397
  220.8 0.3 collective-permute-start.10
  221.1 3.3 %collective-permute-start.11 = (bf16[8,2,64,128]{3,2,1,0:T(8,128)(2,1)S(1)}, bf16[8,2,64,128]{3,2,1,0:T(8,128)(2,1)S(1)}, u32[]{:S(2)}, u32[]{:S(2)}) collective-permute-start(bf16[8,2,64,128]{3,2,1,0:T(8,128)(2,1)S(1)} %slice.22), channel_id=1, source_target_pairs={{16,0},{32,16},{48,32},{0,48},{80,64},{96,80},{112,96},{64,112},{1... | collective-permute-start | bytes 786440 | tf_op jit(solution)/shard_map/ppermute | solution.py:400
  224.4 0.1 pad_add_fusion.place_ref
  224.5 2.0 collective-permute-done.15.low_ref
  226.5 6.8 %project_first.1.rest_0_ = f32[2,512,640]{2,1,0:T(8,128)S(1)} custom-call(s32[2]{0:T(128)S(1)} %pad_add_fusion.place_ref, bf16[16,2,64,128]{3,2,1,0:T(8,128)(2,1)S(1)} %hold.13.rest_1_.mine_ref, bf16[16,2,64,128]{3,2,1,0:T(8,128)(2,1)S(1)} %collective-permute-done.13.left_ref, bf16[16,2,64,128]{3,2,1,0:T(8,128)(2,1)} %collective-permute-done.14.right_ref, ...), custom_call_target="tpu_custom_call" | custom-call | flops 2684354560 | bytes 8388608 | tf_op jit(solution)/shard_map/project_first/pallas_call | solution.py:263
  233.3 6.7 %project_last.1 = bf16[8,2,64,640]{3,2,1,0:T(8,128)(2,1)S(1)} custom-call(s32[2]{0:T(128)S(1)} %pad_add_fusion.place_ref, bf16[16,2,64,128]{3,2,1,0:T(8,128)(2,1)S(1)} %all-to-all-done.4.mine_ref, bf16[16,2,64,128]{3,2,1,0:T(8,128)(2,1)S(1)} %collective-permute-done.8.left_ref, bf16[16,2,64,128]{3,2,1,0:T(8,128)(2,1)S(1)} %collective-permute-done.9.right_ref, ...), custom_call_target="tpu_custom_call" | custom-call | flops 2684354560 | bytes 8388608 | tf_op jit(solution)/shard_map/project_last/pallas_call | solution.py:263
  240.0 0.0 copy-start.3
  240.0 19.3 %all_to_all.30 = bf16[8,2,64,640]{3,2,1,0:T(8,128)(2,1)S(1)} all-to-all(bf16[8,2,64,640]{3,2,1,0:T(8,128)(2,1)S(1)} %project_last.1), channel_id=1, replica_groups={{0,16,32,48},{64,80,96,112},{1,17,33,49},{65,81,97,113},{2,18,34,50},{6..., dimensions={0} | all-to-all | bytes 2621440 | tf_op jit(solution)/shard_map/all_to_all | solution.py:422
  259.3 1.4 add_branch.1
  (51 shorter events, 0.2 us)
Async XLA Ops:
  6.5 12.9 %copy-start = (f32[50,640]{1,0:T(8,128)S(1)}, f32[50,640]{1,0:T(8,128)}, u32[]{:S(2)}) copy-start(f32[50,640]{1,0:T(8,128)} %param.13) | copy-start | bytes 384004
  11.1 8.3 %copy-start.15 = (s32[16]{0:T(128)S(1)}, s32[16]{0:T(128)}, u32[]{:S(2)}) copy-start(s32[16]{0:T(128)} %param.14) | copy-start | bytes 196
  11.1 26.7 %copy-start.6 = (bf16[16,2,2,64,128]{4,3,2,1,0:T(8,128)(2,1)S(1)}, bf16[16,2,2,64,128]{4,3,2,1,0:T(8,128)(2,1)}, u32[]{:S(2)}) copy-start(bf16[16,2,2,64,128]{4,3,2,1,0:T(8,128)(2,1)} %get-tuple-element.18.refs_0_) | copy-start | bytes 3145732
  11.1 26.7 %all-to-all-start = ((bf16[16,2,2,64,128]{4,3,2,1,0:T(8,128)(2,1)}), bf16[16,2,2,64,128]{4,3,2,1,0:T(8,128)(2,1)S(1)}, u32[]{:S(2)}, u32[]{:S(2)}) async-start(bf16[16,2,2,64,128]{4,3,2,1,0:T(8,128)(2,1)} %get-tuple-element.19), calls=%async_computation | async-start | bytes 2097152 | tf_op jit(solution)/shard_map/all_to_all | solution.py:377
  19.7 14.0 %collective-permute-start = (f32[16,640]{1,0:T(8,128)S(1)}, f32[16,640]{1,0:T(8,128)S(1)}, u32[]{:S(2)}, u32[]{:S(2)}) collective-permute-start(f32[16,640]{1,0:T(8,128)S(1)} %fusion), channel_id=1, source_target_pairs={{0,64},{16,80},{32,96},{48,112},{64,0},{80,16},{96,32},{112,48},{1... | collective-permute-start | bytes 122888 | tf_op jit(solution)/shard_map/ppermute | solution.py:366
  37.8 1.0 copy-start.7
  38.8 21.8 %copy-start.4 = (bf16[16,2,64,256]{3,2,1,0:T(8,128)(2,1)S(1)}, bf16[16,2,64,256]{3,2,1,0:T(8,128)(2,1)}, u32[]{:S(2)}) copy-start(bf16[16,2,64,256]{3,2,1,0:T(8,128)(2,1)} %get-tuple-element.17.refs_0_) | copy-start | bytes 3145732
  38.8 21.8 %all-to-all-start.1 = ((bf16[16,2,2,64,128]{4,3,2,1,0:T(8,128)(2,1)}), bf16[16,2,2,64,128]{4,3,2,1,0:T(8,128)(2,1)S(1)}, u32[]{:S(2)}, u32[]{:S(2)}) async-start(bf16[16,2,2,64,128]{4,3,2,1,0:T(8,128)(2,1)} %copy-done.7), calls=%async_computation.1 | async-start | bytes 2097152 | tf_op jit(solution)/shard_map/all_to_all | solution.py:378
  42.6 31.6 %all-gather.5.cloned.1.call-start = ((), (), s32[]{:S(2)}) async-start(), calls=%async_computation.6 | async-start | bytes 1638400 | tf_op jit(solution)/shard_map/all_gather | solution.py:385
  60.6 1.0 copy-start.5
  61.6 22.9 %all-to-all-start.2 = ((bf16[16,2,64,256]{3,2,1,0:T(8,128)(2,1)}), bf16[16,2,64,256]{3,2,1,0:T(8,128)(2,1)S(1)}, u32[]{:S(2)}, u32[]{:S(2)}) async-start(bf16[16,2,64,256]{3,2,1,0:T(8,128)(2,1)} %copy-done.5), calls=%async_computation.2 | async-start | bytes 2097152 | tf_op jit(solution)/shard_map/all_to_all | solution.py:379
  65.2 101.0 %all-gather.7.cloned.1.call-start = ((), (), s32[]{:S(2)}) async-start(), calls=%async_computation.7 | async-start | bytes 6553600 | tf_op jit(solution)/shard_map/all_gather | solution.py:387
  84.5 1.0 copy-start.1
  86.2 1.2 copy-start.2
  87.4 26.9 %collective-permute-start.3 = (bf16[16,2,2,64,128]{4,3,2,1,0:T(8,128)(2,1)S(1)}, bf16[16,2,2,64,128]{4,3,2,1,0:T(8,128)(2,1)}, u32[]{:S(2)}, u32[]{:S(2)}) collective-permute-start(bf16[16,2,2,64,128]{4,3,2,1,0:T(8,128)(2,1)S(1)} %hold.12.own_ref), channel_id=1, source_target_pairs={{0,16},{16,32},{32,48},{48,64},{64,80},{80,96},{96,112},{1,17},{17... | collective-permute-start | bytes 3145736 | tf_op jit(solution)/shard_map/ppermute | solution.py:381
  91.7 28.1 %collective-permute-start.4 = (bf16[16,2,2,64,128]{4,3,2,1,0:T(8,128)(2,1)S(1)}, bf16[16,2,2,64,128]{4,3,2,1,0:T(8,128)(2,1)}, u32[]{:S(2)}, u32[]{:S(2)}) collective-permute-start(bf16[16,2,2,64,128]{4,3,2,1,0:T(8,128)(2,1)S(1)} %hold.12.own_ref), channel_id=1, source_target_pairs={{16,0},{32,16},{48,32},{64,48},{80,64},{96,80},{112,96},{17,1},{33... | collective-permute-start | bytes 3145736 | tf_op jit(solution)/shard_map/ppermute | solution.py:381
  93.0 51.1 %collective-permute-start.1 = (bf16[16,2,2,64,128]{4,3,2,1,0:T(8,128)(2,1)S(1)}, bf16[16,2,2,64,128]{4,3,2,1,0:T(8,128)(2,1)}, u32[]{:S(2)}, u32[]{:S(2)}) collective-permute-start(bf16[16,2,2,64,128]{4,3,2,1,0:T(8,128)(2,1)S(1)} %hold.11.own_ref), channel_id=1, source_target_pairs={{0,16},{16,32},{32,48},{48,64},{64,80},{80,96},{96,112},{1,17},{17... | collective-permute-start | bytes 3145736 | tf_op jit(solution)/shard_map/ppermute | solution.py:383
  98.6 45.6 %collective-permute-start.2 = (bf16[16,2,2,64,128]{4,3,2,1,0:T(8,128)(2,1)S(1)}, bf16[16,2,2,64,128]{4,3,2,1,0:T(8,128)(2,1)}, u32[]{:S(2)}, u32[]{:S(2)}) collective-permute-start(bf16[16,2,2,64,128]{4,3,2,1,0:T(8,128)(2,1)S(1)} %hold.11.own_ref), channel_id=1, source_target_pairs={{16,0},{32,16},{48,32},{64,48},{80,64},{96,80},{112,96},{17,1},{33... | collective-permute-start | bytes 3145736 | tf_op jit(solution)/shard_map/ppermute | solution.py:383
  128.8 9.8 %collective-permute-start.5 = (bf16[16,1,64,128]{3,2,1,0:T(8,128)(2,1)S(1)}, bf16[16,1,64,128]{3,2,1,0:T(8,128)(2,1)S(1)}, u32[]{:S(2)}, u32[]{:S(2)}) collective-permute-start(bf16[16,1,64,128]{3,2,1,0:T(8,128)(2,1)S(1)} %get-tuple-element.23), channel_id=1, source_target_pairs={{48,112},{49,113},{50,114},{51,115},{52,116},{53,117},{54,118},{55... | collective-permute-start | bytes 786440 | tf_op jit(solution)/shard_map/ppermute | solution.py:406
  139.5 17.1 %all-to-all-start.3 = ((bf16[16,2,64,128]{3,2,1,0:T(8,128)(2,1)}), bf16[16,2,64,128]{3,2,1,0:T(8,128)(2,1)S(1)}, u32[]{:S(2)}, u32[]{:S(2)}) async-start(bf16[16,2,64,128]{3,2,1,0:T(8,128)(2,1)} %pad_maximum_fusion.rest_1_), calls=%async_computation.3 | async-start | bytes 1048576 | tf_op jit(solution)/shard_map/all_to_all | solution.py:411
  153.2 0.7 copy-start.10
  165.6 0.6 copy-start.14
  166.2 0.8 copy-start.12
  166.2 1.2 copy-start.8
  167.0 3.6 %copy-start.11 = (bf16[16,1,64,128]{3,2,1,0:T(8,128)(2,1)S(1)}, bf16[16,1,64,128]{3,2,1,0:T(8,128)(2,1)}, u32[]{:S(2)}) copy-start(bf16[16,1,64,128]{3,2,1,0:T(8,128)(2,1)} %copy-done.10) | copy-start | bytes 786436
  167.0 59.5 %collective-permute-start.12 = (bf16[4,2,2,256,640]{4,3,2,1,0:T(8,128)(2,1)}, bf16[4,2,2,256,640]{4,3,2,1,0:T(8,128)(2,1)}, u32[]{:S(2)}, u32[]{:S(2)}) collective-permute-start(bf16[4,2,2,256,640]{4,3,2,1,0:T(8,128)(2,1)} %hold.17.wo_ref), channel_id=1, source_target_pairs={{0,1},{1,0},{2,3},{3,2},{4,5},{5,4},{6,7},{7,6},{8,9},{9,8},{10,11... | collective-permute-start | bytes 15728648 | tf_op jit(solution)/shard_map/ppermute | solution.py:416
  167.4 3.9 %copy-start.13 = (bf16[16,1,64,128]{3,2,1,0:T(8,128)(2,1)S(1)}, bf16[16,1,64,128]{3,2,1,0:T(8,128)(2,1)}, u32[]{:S(2)}) copy-start(bf16[16,1,64,128]{3,2,1,0:T(8,128)(2,1)} %copy-done.12) | copy-start | bytes 786436
  168.1 16.6 %collective-permute-start.7 = (bf16[1,64,5120]{2,1,0:T(8,128)(2,1)S(1)}, bf16[1,64,5120]{2,1,0:T(8,128)(2,1)S(1)}, u32[]{:S(2)}, u32[]{:S(2)}) collective-permute-start(bf16[1,64,5120]{2,1,0:T(8,128)(2,1)S(1)} %hold.14), channel_id=1, source_target_pairs={{0,16},{16,32},{32,48},{48,64},{64,80},{80,96},{96,112},{1,17},{17... | collective-permute-start | bytes 1966088 | tf_op jit(solution)/shard_map/ppermute | solution.py:413
  170.5 0.7 collective-permute-start.6
  184.7 17.0 %all-to-all-start.4 = ((bf16[16,2,64,128]{3,2,1,0:T(8,128)(2,1)}), bf16[16,2,64,128]{3,2,1,0:T(8,128)(2,1)S(1)}, u32[]{:S(2)}, u32[]{:S(2)}) async-start(bf16[16,2,64,128]{3,2,1,0:T(8,128)(2,1)} %hold.15), calls=%async_computation.4 | async-start | bytes 1048576 | tf_op jit(solution)/shard_map/all_to_all | solution.py:418
  189.4 18.7 %collective-permute-start.13 = (bf16[16,2,64,128]{3,2,1,0:T(8,128)(2,1)S(1)}, bf16[16,2,64,128]{3,2,1,0:T(8,128)(2,1)S(1)}, u32[]{:S(2)}, u32[]{:S(2)}) collective-permute-start(bf16[16,2,64,128]{3,2,1,0:T(8,128)(2,1)S(1)} %hold.13.rest_1_.mine_ref), channel_id=1, source_target_pairs={{0,16},{16,32},{32,48},{48,0},{64,80},{80,96},{96,112},{112,64},{1... | collective-permute-start | bytes 1572872 | tf_op jit(solution)/shard_map/ppermute | solution.py:397
  191.9 16.9 %collective-permute-start.14 = (bf16[16,2,64,128]{3,2,1,0:T(8,128)(2,1)S(1)}, bf16[16,2,64,128]{3,2,1,0:T(8,128)(2,1)}, u32[]{:S(2)}, u32[]{:S(2)}) collective-permute-start(bf16[16,2,64,128]{3,2,1,0:T(8,128)(2,1)S(1)} %hold.13.rest_1_.mine_ref), channel_id=1, source_target_pairs={{16,0},{32,16},{48,32},{0,48},{80,64},{96,80},{112,96},{64,112},{1... | collective-permute-start | bytes 1572872 | tf_op jit(solution)/shard_map/ppermute | solution.py:398
  201.7 19.0 %collective-permute-start.8 = (bf16[16,2,64,128]{3,2,1,0:T(8,128)(2,1)S(1)}, bf16[16,2,64,128]{3,2,1,0:T(8,128)(2,1)S(1)}, u32[]{:S(2)}, u32[]{:S(2)}) collective-permute-start(bf16[16,2,64,128]{3,2,1,0:T(8,128)(2,1)S(1)} %all-to-all-done.4.mine_ref), channel_id=1, source_target_pairs={{0,16},{16,32},{32,48},{48,0},{64,80},{80,96},{96,112},{112,64},{1... | collective-permute-start | bytes 1572872 | tf_op jit(solution)/shard_map/ppermute | solution.py:397
  204.2 16.9 %collective-permute-start.9 = (bf16[16,2,64,128]{3,2,1,0:T(8,128)(2,1)S(1)}, bf16[16,2,64,128]{3,2,1,0:T(8,128)(2,1)S(1)}, u32[]{:S(2)}, u32[]{:S(2)}) collective-permute-start(bf16[16,2,64,128]{3,2,1,0:T(8,128)(2,1)S(1)} %all-to-all-done.4.mine_ref), channel_id=1, source_target_pairs={{16,0},{32,16},{48,32},{0,48},{80,64},{96,80},{112,96},{64,112},{1... | collective-permute-start | bytes 1572872 | tf_op jit(solution)/shard_map/ppermute | solution.py:398
  208.8 17.7 %collective-permute-start.15 = (bf16[8,2,64,128]{3,2,1,0:T(8,128)(2,1)}, bf16[8,2,64,128]{3,2,1,0:T(8,128)(2,1)}, u32[]{:S(2)}, u32[]{:S(2)}) collective-permute-start(bf16[8,2,64,128]{3,2,1,0:T(8,128)(2,1)} %slice.23), channel_id=1, source_target_pairs={{0,16},{16,32},{32,48},{48,0},{64,80},{80,96},{96,112},{112,64},{1... | collective-permute-start | bytes 786440 | tf_op jit(solution)/shard_map/ppermute | solution.py:399
  210.5 16.0 %collective-permute-start.16 = (bf16[8,2,64,128]{3,2,1,0:T(8,128)(2,1)}, bf16[8,2,64,128]{3,2,1,0:T(8,128)(2,1)}, u32[]{:S(2)}, u32[]{:S(2)}) collective-permute-start(bf16[8,2,64,128]{3,2,1,0:T(8,128)(2,1)} %slice.24), channel_id=1, source_target_pairs={{16,0},{32,16},{48,32},{0,48},{80,64},{96,80},{112,96},{64,112},{1... | collective-permute-start | bytes 786440 | tf_op jit(solution)/shard_map/ppermute | solution.py:400
  220.8 12.5 %collective-permute-start.10 = (bf16[8,2,64,128]{3,2,1,0:T(8,128)(2,1)S(1)}, bf16[8,2,64,128]{3,2,1,0:T(8,128)(2,1)S(1)}, u32[]{:S(2)}, u32[]{:S(2)}) collective-permute-start(bf16[8,2,64,128]{3,2,1,0:T(8,128)(2,1)S(1)} %slice.21), channel_id=1, source_target_pairs={{0,16},{16,32},{32,48},{48,0},{64,80},{80,96},{96,112},{112,64},{1... | collective-permute-start | bytes 786440 | tf_op jit(solution)/shard_map/ppermute | solution.py:399
  221.1 12.2 %collective-permute-start.11 = (bf16[8,2,64,128]{3,2,1,0:T(8,128)(2,1)S(1)}, bf16[8,2,64,128]{3,2,1,0:T(8,128)(2,1)S(1)}, u32[]{:S(2)}, u32[]{:S(2)}) collective-permute-start(bf16[8,2,64,128]{3,2,1,0:T(8,128)(2,1)S(1)} %slice.22), channel_id=1, source_target_pairs={{16,0},{32,16},{48,32},{0,48},{80,64},{96,80},{112,96},{64,112},{1... | collective-permute-start | bytes 786440 | tf_op jit(solution)/shard_map/ppermute | solution.py:400
  240.0 19.3 %copy-start.3 = (bf16[2,64,5120]{2,1,0:T(8,128)(2,1)S(1)}, bf16[2,64,5120]{2,1,0:T(8,128)(2,1)}, u32[]{:S(2)}) copy-start(bf16[2,64,5120]{2,1,0:T(8,128)(2,1)} %hidden_ref.3) | copy-start | bytes 3932164
  240.0 19.3 %copy-start.9 = (bf16[64,5120]{1,0:T(8,128)(2,1)S(1)}, bf16[64,5120]{1,0:T(8,128)(2,1)}, u32[]{:S(2)}) copy-start(bf16[64,5120]{1,0:T(8,128)(2,1)} %entering_ref.1) | copy-start | bytes 1966084
Sparse Core Ops, SparseCore 0:
  45.1 29.0 all-gather.4
  86.3 56.1 all-gather.6

commit v13 on v10

--- a/solution.py
+++ b/solution.py
@@ -406,16 +406,16 @@
     odd0_crossing = lax.ppermute(odd0, "queue", cross)
     even0, token = attend(0, *head0, token)
     first = with_crossing(even0, odd0, odd0_crossing)
+    shifted = lax.ppermute(hold(last_frame, kv1_before, token), "queue", up)
     odd1, token = attend(1, *head1, token, first)
     odd1_crossing = lax.ppermute(odd1, "queue", cross)
     first = hold(to_heads(first), token)
     first_sources = spread(first)
-    shifted = lax.ppermute(hold(last_frame, kv1_before, token), "queue", up)
-    even1, token = attend(0, *head1, token, first)
+    even1, token = attend(0, *head1, token, first, shifted)
     weight_own = hold(weight, token, room=56)
     weight_pair = lax.ppermute(weight_own, "spatial", swap_core)
     second = to_heads(with_crossing(even1, odd1, odd1_crossing))
-    second_sources = spread(hold(second, shifted))
+    second_sources = spread(second)
 
     partial = project(0, place, first_sources, weight_own, weight_pair, None, None)
     branch = project(1, place, second_sources, weight_own, weight_pair, partial, gates)

time: 264 us -> 264 us (level)
  starting transfers between devices: 60.1 us -> 55.8 us
  waiting for transfers between devices: 100 us -> 103 us
    all_to_all x1, waiting for transfers between devices: 2.64 us -> 9.84 us  [body(): first = hold(to_heads(first), token)]
    ppermute x2, starting transfers between devices: 10.2 us -> 6.46 us  [spread(): right = lax.ppermute(mine, 'queue', ring_down)]
    all_to_all x1, waiting for transfers between devices: 12.3 us -> 9.06 us  [body(): second = to_heads(with_crossing(even1, odd1, odd1_crossing))]
  transfers between devices with their start and end apart: 24 -> 24, of which waited for: 13 -> 11; matrix products, arithmetic and copies ran while one was open for 2% -> 1% of each run, Pallas kernels for 17% -> 17%
where the time goes in v13:
time: 264 us; the launch traced here: 260 us
  waiting for transfers between devices  103 us (39%)
  Pallas kernels  58.5 us (22%)
  starting transfers between devices  55.8 us (21%)
  blocking collectives  19 us (7%)
  between operations  13.7 us (5%)
  local copies, waits for them, and re-layouts  7.79 us (3%)
    pallas_call x4, Pallas kernels, attend(): pl.pallas_call(kernel, grid_spec=pltpu.PrefetchScalarGridSpec(num_scalar_...  36.1 us
    all_to_all x1, blocking collectives, body(): lax.all_to_all(branch, 'queue', split_axis=0, concat_axis=0, axis_index_g...  19 us
    all_to_all x1, waiting for transfers between devices, body(): kv1_heads = to_heads(hold(kv1, kv0, gates))  17.2 us
    ppermute x1, waiting for transfers between devices, body(): lax.ppermute(kv0, 'queue', up)  14.4 us
    ppermute x1, waiting for transfers between devices, body(): other_gates = lax.ppermute(gates, 'queue', swap_low)  13.3 us
    pallas_call x2, Pallas kernels, project(): pl.pallas_call(kernel, grid_spec=pltpu.PrefetchScalarGridSpec(num_scalar_...  13.3 us
    all_to_all x1, waiting for transfers between devices, body(): query = to_heads(hold(query, kv1_heads))  10.3 us
    all_to_all x1, waiting for transfers between devices, body(): first = hold(to_heads(first), token)  9.84 us
  transfers between devices with their start and end apart: 24, of which 11 were waited for; matrix products, arithmetic and copies ran while one was open for 1% of the time, Pallas kernels for 17%

profile of v13, /device:TPU:0, one launch (start us, length us, event | category | flops | bytes accessed | tf_op | source)
XLA Modules:
  0.0 260.4 jit_solution(18351974813561797644)
XLA Ops:
  6.5 4.6 %pack.1 = (bf16[16,2,2,64,128]{4,3,2,1,0:T(8,128)(2,1)}, bf16[16,2,2,64,128]{4,3,2,1,0:T(8,128)(2,1)}, bf16[16,2,64,256]{3,2,1,0:T(8,128)(2,1)}, bf16[1,64,5120]{2,1,0:T(8,128)(2,1)}) custom-call(bf16[2,64,4096]{2,1,0:T(8,128)(2,1)} %q_ref.1, bf16[2,64,4096]{2,1,0:T(8,128)(2,1)} %k_ref.1, bf16[2,64,4096]{2,1,0:T(8,128)(2,1)} %v_ref.1, ...), custom_call_target="tpu_custom_call" | custom-call | tf_op jit(solution)/shard_map/pack/pallas_call | solution.py:54
  11.1 8.3 %all-to-all-start = ((bf16[16,2,2,64,128]{4,3,2,1,0:T(8,128)(2,1)}), bf16[16,2,2,64,128]{4,3,2,1,0:T(8,128)(2,1)S(1)}, u32[]{:S(2)}, u32[]{:S(2)}) async-start(bf16[16,2,2,64,128]{4,3,2,1,0:T(8,128)(2,1)} %get-tuple-element.19), calls=%async_computation | async-start | bytes 2097152 | tf_op jit(solution)/shard_map/all_to_all | solution.py:377
  19.4 0.2 fusion
  19.6 0.8 collective-permute-start
  20.4 13.3 %collective-permute-done = f32[16,640]{1,0:T(8,128)S(1)} collective-permute-done((f32[16,640]{1,0:T(8,128)S(1)}, f32[16,640]{1,0:T(8,128)S(1)}, u32[]{:S(2)}, u32[]{:S(2)}) %collective-permute-start) | collective-permute-done | bytes 40992 | tf_op jit(solution)/shard_map/ppermute | solution.py:366
  33.7 0.1 dynamic-slice_select_fusion.refs_2_.rest_1_
  33.8 4.0 %all-to-all-done.refs_1_.refs_0_ = bf16[16,2,2,64,128]{4,3,2,1,0:T(8,128)(2,1)S(1)} async-done(((bf16[16,2,2,64,128]{4,3,2,1,0:T(8,128)(2,1)}), bf16[16,2,2,64,128]{4,3,2,1,0:T(8,128)(2,1)S(1)}, u32[]{:S(2)}, u32[]{:S(2)}) %all-to-all-start) | async-done | bytes 1048608 | tf_op jit(solution)/shard_map/all_to_all | solution.py:377
  37.8 1.0 copy-done.7
  38.8 3.8 %all-to-all-start.1 = ((bf16[16,2,2,64,128]{4,3,2,1,0:T(8,128)(2,1)}), bf16[16,2,2,64,128]{4,3,2,1,0:T(8,128)(2,1)S(1)}, u32[]{:S(2)}, u32[]{:S(2)}) async-start(bf16[16,2,2,64,128]{4,3,2,1,0:T(8,128)(2,1)} %copy-done.7), calls=%async_computation.1 | async-start | bytes 2097152 | tf_op jit(solution)/shard_map/all_to_all | solution.py:378
  42.6 0.0 all-gather.5.cloned.1.call-start
  42.6 0.7 all-gather.5.cloned.1.call-update
  43.3 17.2 %all-to-all-done.1.refs_1_.refs_0_ = bf16[16,2,2,64,128]{4,3,2,1,0:T(8,128)(2,1)S(1)} async-done(((bf16[16,2,2,64,128]{4,3,2,1,0:T(8,128)(2,1)}), bf16[16,2,2,64,128]{4,3,2,1,0:T(8,128)(2,1)S(1)}, u32[]{:S(2)}, u32[]{:S(2)}) %all-to-all-start.1) | async-done | bytes 1048608 | tf_op jit(solution)/shard_map/all_to_all | solution.py:378
  60.6 1.0 copy-done.5
  61.5 3.7 %all-to-all-start.2 = ((bf16[16,2,64,256]{3,2,1,0:T(8,128)(2,1)}), bf16[16,2,64,256]{3,2,1,0:T(8,128)(2,1)S(1)}, u32[]{:S(2)}, u32[]{:S(2)}) async-start(bf16[16,2,64,256]{3,2,1,0:T(8,128)(2,1)} %copy-done.5), calls=%async_computation.2 | async-start | bytes 2097152 | tf_op jit(solution)/shard_map/all_to_all | solution.py:379
  65.2 0.0 all-gather.7.cloned.1.call-start
  65.3 8.9 %all-gather.5.cloned.1.call-done = bf16[1024,640]{1,0:T(8,128)(2,1)} async-done(((bf16[256,640]{1,0:T(8,128)(2,1)}), bf16[1024,640]{1,0:T(8,128)(2,1)}) %all-gather.5.cloned.1.call-update) | async-done | bytes 1310736 | tf_op jit(solution)/shard_map/all_gather | solution.py:385
  74.2 10.3 %all-to-all-done.2.refs_1_.q_ref = bf16[16,2,64,256]{3,2,1,0:T(8,128)(2,1)S(1)} async-done(((bf16[16,2,64,256]{3,2,1,0:T(8,128)(2,1)}), bf16[16,2,64,256]{3,2,1,0:T(8,128)(2,1)S(1)}, u32[]{:S(2)}, u32[]{:S(2)}) %all-to-all-start.2) | async-done | bytes 1048608 | tf_op jit(solution)/shard_map/all_to_all | solution.py:379
  84.5 1.0 copy-done.1
  85.5 0.7 hold.14
  86.2 0.0 all-gather.7.cloned.1.call-update
  86.2 1.2 copy-done.2
  87.4 4.3 %collective-permute-start.3 = (bf16[16,2,2,64,128]{4,3,2,1,0:T(8,128)(2,1)S(1)}, bf16[16,2,2,64,128]{4,3,2,1,0:T(8,128)(2,1)}, u32[]{:S(2)}, u32[]{:S(2)}) collective-permute-start(bf16[16,2,2,64,128]{4,3,2,1,0:T(8,128)(2,1)S(1)} %hold.11.own_ref), channel_id=1, source_target_pairs={{0,16},{16,32},{32,48},{48,64},{64,80},{80,96},{96,112},{1,17},{17... | collective-permute-start | bytes 3145736 | tf_op jit(solution)/shard_map/ppermute | solution.py:381
  91.7 1.3 collective-permute-start.4
  93.0 5.6 %collective-permute-start.1 = (bf16[16,2,2,64,128]{4,3,2,1,0:T(8,128)(2,1)S(1)}, bf16[16,2,2,64,128]{4,3,2,1,0:T(8,128)(2,1)}, u32[]{:S(2)}, u32[]{:S(2)}) collective-permute-start(bf16[16,2,2,64,128]{4,3,2,1,0:T(8,128)(2,1)S(1)} %hold.10.own_ref), channel_id=1, source_target_pairs={{0,16},{16,32},{32,48},{48,64},{64,80},{80,96},{96,112},{1,17},{17... | collective-permute-start | bytes 3145736 | tf_op jit(solution)/shard_map/ppermute | solution.py:383
  98.5 1.3 collective-permute-start.2
  99.8 14.4 %collective-permute-done.3.before_ref = bf16[16,2,2,64,128]{4,3,2,1,0:T(8,128)(2,1)} collective-permute-done((bf16[16,2,2,64,128]{4,3,2,1,0:T(8,128)(2,1)S(1)}, bf16[16,2,2,64,128]{4,3,2,1,0:T(8,128)(2,1)}, u32[]{:S(2)}, u32[]{:S(2)}) %collective-permute-start.3) | collective-permute-done | bytes 1048608 | tf_op jit(solution)/shard_map/ppermute | solution.py:381
  114.3 5.5 %collective-permute-done.4.after_ref = bf16[16,2,2,64,128]{4,3,2,1,0:T(8,128)(2,1)} collective-permute-done((bf16[16,2,2,64,128]{4,3,2,1,0:T(8,128)(2,1)S(1)}, bf16[16,2,2,64,128]{4,3,2,1,0:T(8,128)(2,1)}, u32[]{:S(2)}, u32[]{:S(2)}) %collective-permute-start.4) | collective-permute-done | bytes 1048608 | tf_op jit(solution)/shard_map/ppermute | solution.py:381
  119.8 9.0 %attend.4 = (bf16[16,1,64,128]{3,2,1,0:T(8,128)(2,1)S(1)}, f32[8,128]{1,0:T(8,128)S(1)}) custom-call(s32[1]{0:T(128)} %bitcast.pos_ref, bf16[16,2,64,256]{3,2,1,0:T(8,128)(2,1)S(1)} %copy-done.2, bf16[16,2,2,64,128]{4,3,2,1,0:T(8,128)(2,1)S(1)} %hold.11.own_ref, bf16[16,2,2,64,128]{4,3,2,1,0:T(8,128)(2,1)} %collective-permute-done.3.before_ref, ...), custom_call_target="tpu_custom_call" | custom-call | flops 5368709120 | bytes 4194304 | tf_op jit(solution)/shard_map/attend/pallas_call | solution.py:169
  128.7 0.7 collective-permute-start.5
  129.4 9.1 %attend.5 = (bf16[16,1,64,128]{3,2,1,0:T(8,128)(2,1)S(1)}, f32[8,128]{1,0:T(8,128)S(1)}) custom-call(s32[1]{0:T(128)} %bitcast.pos_ref, bf16[16,2,64,256]{3,2,1,0:T(8,128)(2,1)S(1)} %copy-done.2, bf16[16,2,2,64,128]{4,3,2,1,0:T(8,128)(2,1)S(1)} %hold.11.own_ref, bf16[16,2,2,64,128]{4,3,2,1,0:T(8,128)(2,1)} %collective-permute-done.3.before_ref, ...), custom_call_target="tpu_custom_call" | custom-call | flops 5368709120 | bytes 4194304 | tf_op jit(solution)/shard_map/attend/pallas_call | solution.py:169
  138.5 0.7 hold.13
  139.2 3.3 %collective-permute-start.6 = (bf16[1,64,5120]{2,1,0:T(8,128)(2,1)}, bf16[1,64,5120]{2,1,0:T(8,128)(2,1)}, u32[]{:S(2)}, u32[]{:S(2)}) collective-permute-start(bf16[1,64,5120]{2,1,0:T(8,128)(2,1)} %hold.13), channel_id=1, source_target_pairs={{0,16},{16,32},{32,48},{48,64},{64,80},{80,96},{96,112},{1,17},{17... | collective-permute-start | bytes 1966088 | tf_op jit(solution)/shard_map/ppermute | solution.py:409
  142.5 0.8 pad_maximum_fusion.rest_1_
  143.4 4.7 %all-to-all-start.3 = ((bf16[16,2,64,128]{3,2,1,0:T(8,128)(2,1)}), bf16[16,2,64,128]{3,2,1,0:T(8,128)(2,1)S(1)}, u32[]{:S(2)}, u32[]{:S(2)}) async-start(bf16[16,2,64,128]{3,2,1,0:T(8,128)(2,1)} %pad_maximum_fusion.rest_1_), calls=%async_computation.3 | async-start | bytes 1048576 | tf_op jit(solution)/shard_map/all_to_all | solution.py:412
  148.0 9.0 %attend.6 = (bf16[16,1,64,128]{3,2,1,0:T(8,128)(2,1)S(1)}, f32[8,128]{1,0:T(8,128)S(1)}) custom-call(s32[1]{0:T(128)} %bitcast.pos_ref, bf16[16,2,64,256]{3,2,1,0:T(8,128)(2,1)S(1)} %copy-done.2, bf16[16,2,2,64,128]{4,3,2,1,0:T(8,128)(2,1)S(1)} %hold.10.own_ref, bf16[16,2,2,64,128]{4,3,2,1,0:T(8,128)(2,1)} %collective-permute-done.1.before_ref.refs_1_, ...), custom_call_target="tpu_custom_call" | custom-call | flops 5368709120 | bytes 4194304 | tf_op jit(solution)/shard_map/attend/pallas_call | solution.py:169
  157.0 0.7 copy-done.9
  157.8 9.8 %all-to-all-done.3.refs_0_ = bf16[16,2,64,128]{3,2,1,0:T(8,128)(2,1)S(1)} async-done(((bf16[16,2,64,128]{3,2,1,0:T(8,128)(2,1)}), bf16[16,2,64,128]{3,2,1,0:T(8,128)(2,1)S(1)}, u32[]{:S(2)}, u32[]{:S(2)}) %all-to-all-start.3) | async-done | bytes 524320 | tf_op jit(solution)/shard_map/all_to_all | solution.py:412
  167.6 9.0 %attend.7 = (bf16[16,1,64,128]{3,2,1,0:T(8,128)(2,1)S(1)}, f32[8,128]{1,0:T(8,128)S(1)}) custom-call(s32[1]{0:T(128)} %bitcast.pos_ref, bf16[16,2,64,256]{3,2,1,0:T(8,128)(2,1)S(1)} %copy-done.2, bf16[16,2,2,64,128]{4,3,2,1,0:T(8,128)(2,1)S(1)} %hold.10.own_ref, bf16[16,2,2,64,128]{4,3,2,1,0:T(8,128)(2,1)} %collective-permute-done.1.before_ref.refs_1_, ...), custom_call_target="tpu_custom_call" | custom-call | flops 5368709120 | bytes 4194304 | tf_op jit(solution)/shard_map/attend/pallas_call | solution.py:169
  176.7 0.7 copy-done.11
  177.4 0.6 copy-done.13
  177.9 0.7 hold.15.wo_ref
  178.7 0.1 collective-permute-start.12
  178.7 0.2 copy-done.10
  178.9 0.7 collective-permute-start.7
  179.6 0.8 pad_maximum_fusion.1
  180.5 4.1 %all-to-all-start.4 = ((bf16[16,2,64,128]{3,2,1,0:T(8,128)(2,1)}), bf16[16,2,64,128]{3,2,1,0:T(8,128)(2,1)S(1)}, u32[]{:S(2)}, u32[]{:S(2)}) async-start(bf16[16,2,64,128]{3,2,1,0:T(8,128)(2,1)} %pad_maximum_fusion.1), calls=%async_computation.4 | async-start | bytes 1048576 | tf_op jit(solution)/shard_map/all_to_all | solution.py:417
  184.6 0.1 collective-permute-start.13
  184.7 3.2 %collective-permute-start.14 = (bf16[16,2,64,128]{3,2,1,0:T(8,128)(2,1)S(1)}, bf16[16,2,64,128]{3,2,1,0:T(8,128)(2,1)S(1)}, u32[]{:S(2)}, u32[]{:S(2)}) collective-permute-start(bf16[16,2,64,128]{3,2,1,0:T(8,128)(2,1)S(1)} %hold.12.rest_1_.mine_ref), channel_id=1, source_target_pairs={{16,0},{32,16},{48,32},{0,48},{80,64},{96,80},{112,96},{64,112},{1... | collective-permute-start | bytes 1572872 | tf_op jit(solution)/shard_map/ppermute | solution.py:398
  187.9 9.1 %all-to-all-done.4.mine_ref = bf16[16,2,64,128]{3,2,1,0:T(8,128)(2,1)S(1)} async-done(((bf16[16,2,64,128]{3,2,1,0:T(8,128)(2,1)}), bf16[16,2,64,128]{3,2,1,0:T(8,128)(2,1)S(1)}, u32[]{:S(2)}, u32[]{:S(2)}) %all-to-all-start.4) | async-done | bytes 524320 | tf_op jit(solution)/shard_map/all_to_all | solution.py:417
  197.0 3.2 %collective-permute-start.9 = (bf16[16,2,64,128]{3,2,1,0:T(8,128)(2,1)S(1)}, bf16[16,2,64,128]{3,2,1,0:T(8,128)(2,1)S(1)}, u32[]{:S(2)}, u32[]{:S(2)}) collective-permute-start(bf16[16,2,64,128]{3,2,1,0:T(8,128)(2,1)S(1)} %all-to-all-done.4.mine_ref), channel_id=1, source_target_pairs={{16,0},{32,16},{48,32},{0,48},{80,64},{96,80},{112,96},{64,112},{1... | collective-permute-start | bytes 1572872 | tf_op jit(solution)/shard_map/ppermute | solution.py:398
  200.2 0.0 collective-permute-done.13.left_ref
  200.2 0.7 slice.23
  200.9 0.7 slice.24
  201.7 3.2 %collective-permute-start.16 = (bf16[8,2,64,128]{3,2,1,0:T(8,128)(2,1)}, bf16[8,2,64,128]{3,2,1,0:T(8,128)(2,1)}, u32[]{:S(2)}, u32[]{:S(2)}) collective-permute-start(bf16[8,2,64,128]{3,2,1,0:T(8,128)(2,1)} %slice.24), channel_id=1, source_target_pairs={{16,0},{32,16},{48,32},{0,48},{80,64},{96,80},{112,96},{64,112},{1... | collective-permute-start | bytes 786440 | tf_op jit(solution)/shard_map/ppermute | solution.py:400
  204.9 8.1 %collective-permute-done.8.left_ref = bf16[16,2,64,128]{3,2,1,0:T(8,128)(2,1)S(1)} collective-permute-done((bf16[16,2,64,128]{3,2,1,0:T(8,128)(2,1)S(1)}, bf16[16,2,64,128]{3,2,1,0:T(8,128)(2,1)S(1)}, u32[]{:S(2)}, u32[]{:S(2)}) %collective-permute-start.8) | collective-permute-done | bytes 524320 | tf_op jit(solution)/shard_map/ppermute | solution.py:397
  213.0 0.1 collective-permute-start.10
  213.2 3.5 %collective-permute-start.11 = (bf16[8,2,64,128]{3,2,1,0:T(8,128)(2,1)S(1)}, bf16[8,2,64,128]{3,2,1,0:T(8,128)(2,1)S(1)}, u32[]{:S(2)}, u32[]{:S(2)}) collective-permute-start(bf16[8,2,64,128]{3,2,1,0:T(8,128)(2,1)S(1)} %slice.22), channel_id=1, source_target_pairs={{16,0},{32,16},{48,32},{0,48},{80,64},{96,80},{112,96},{64,112},{1... | collective-permute-start | bytes 786440 | tf_op jit(solution)/shard_map/ppermute | solution.py:400
  216.7 0.1 pad_add_fusion.place_ref
  216.7 2.0 collective-permute-done.15.low_ref
  218.7 6.6 %project_first.1.rest_0_ = f32[2,512,640]{2,1,0:T(8,128)S(1)} custom-call(s32[2]{0:T(128)S(1)} %pad_add_fusion.place_ref, bf16[16,2,64,128]{3,2,1,0:T(8,128)(2,1)S(1)} %hold.12.rest_1_.mine_ref, bf16[16,2,64,128]{3,2,1,0:T(8,128)(2,1)S(1)} %collective-permute-done.13.left_ref, bf16[16,2,64,128]{3,2,1,0:T(8,128)(2,1)S(1)} %collective-permute-done.14.right_ref, ...), custom_call_target="tpu_custom_call" | custom-call | flops 2684354560 | bytes 8388608 | tf_op jit(solution)/shard_map/project_first/pallas_call | solution.py:263
  225.4 6.7 %project_last.1 = bf16[8,2,64,640]{3,2,1,0:T(8,128)(2,1)S(1)} custom-call(s32[2]{0:T(128)S(1)} %pad_add_fusion.place_ref, bf16[16,2,64,128]{3,2,1,0:T(8,128)(2,1)S(1)} %all-to-all-done.4.mine_ref, bf16[16,2,64,128]{3,2,1,0:T(8,128)(2,1)S(1)} %collective-permute-done.8.left_ref, bf16[16,2,64,128]{3,2,1,0:T(8,128)(2,1)S(1)} %collective-permute-done.9.right_ref, ...), custom_call_target="tpu_custom_call" | custom-call | flops 2684354560 | bytes 8388608 | tf_op jit(solution)/shard_map/project_last/pallas_call | solution.py:263
  232.1 0.0 copy-start.8
  232.1 19.0 %all_to_all.30 = bf16[8,2,64,640]{3,2,1,0:T(8,128)(2,1)S(1)} all-to-all(bf16[8,2,64,640]{3,2,1,0:T(8,128)(2,1)S(1)} %project_last.1), channel_id=1, replica_groups={{0,16,32,48},{64,80,96,112},{1,17,33,49},{65,81,97,113},{2,18,34,50},{6..., dimensions={0} | all-to-all | bytes 2621440 | tf_op jit(solution)/shard_map/all_to_all | solution.py:422
  251.1 2.5 add_branch.1
  (48 shorter events, 0.2 us)
Async XLA Ops:
  6.5 12.9 %copy-start = (f32[50,640]{1,0:T(8,128)S(1)}, f32[50,640]{1,0:T(8,128)}, u32[]{:S(2)}) copy-start(f32[50,640]{1,0:T(8,128)} %param.13) | copy-start | bytes 384004
  11.1 8.3 %copy-start.14 = (s32[16]{0:T(128)S(1)}, s32[16]{0:T(128)}, u32[]{:S(2)}) copy-start(s32[16]{0:T(128)} %param.14) | copy-start | bytes 196
  11.1 26.7 %copy-start.6 = (bf16[16,2,2,64,128]{4,3,2,1,0:T(8,128)(2,1)S(1)}, bf16[16,2,2,64,128]{4,3,2,1,0:T(8,128)(2,1)}, u32[]{:S(2)}) copy-start(bf16[16,2,2,64,128]{4,3,2,1,0:T(8,128)(2,1)} %get-tuple-element.18.refs_0_) | copy-start | bytes 3145732
  11.1 26.7 %all-to-all-start = ((bf16[16,2,2,64,128]{4,3,2,1,0:T(8,128)(2,1)}), bf16[16,2,2,64,128]{4,3,2,1,0:T(8,128)(2,1)S(1)}, u32[]{:S(2)}, u32[]{:S(2)}) async-start(bf16[16,2,2,64,128]{4,3,2,1,0:T(8,128)(2,1)} %get-tuple-element.19), calls=%async_computation | async-start | bytes 2097152 | tf_op jit(solution)/shard_map/all_to_all | solution.py:377
  19.6 14.0 %collective-permute-start = (f32[16,640]{1,0:T(8,128)S(1)}, f32[16,640]{1,0:T(8,128)S(1)}, u32[]{:S(2)}, u32[]{:S(2)}) collective-permute-start(f32[16,640]{1,0:T(8,128)S(1)} %fusion), channel_id=1, source_target_pairs={{0,64},{16,80},{32,96},{48,112},{64,0},{80,16},{96,32},{112,48},{1... | collective-permute-start | bytes 122888 | tf_op jit(solution)/shard_map/ppermute | solution.py:366
  37.8 1.0 copy-start.7
  38.8 21.8 %copy-start.4 = (bf16[16,2,64,256]{3,2,1,0:T(8,128)(2,1)S(1)}, bf16[16,2,64,256]{3,2,1,0:T(8,128)(2,1)}, u32[]{:S(2)}) copy-start(bf16[16,2,64,256]{3,2,1,0:T(8,128)(2,1)} %get-tuple-element.17.refs_0_) | copy-start | bytes 3145732
  38.8 21.8 %all-to-all-start.1 = ((bf16[16,2,2,64,128]{4,3,2,1,0:T(8,128)(2,1)}), bf16[16,2,2,64,128]{4,3,2,1,0:T(8,128)(2,1)S(1)}, u32[]{:S(2)}, u32[]{:S(2)}) async-start(bf16[16,2,2,64,128]{4,3,2,1,0:T(8,128)(2,1)} %copy-done.7), calls=%async_computation.1 | async-start | bytes 2097152 | tf_op jit(solution)/shard_map/all_to_all | solution.py:378
  42.6 31.6 %all-gather.5.cloned.1.call-start = ((), (), s32[]{:S(2)}) async-start(), calls=%async_computation.6 | async-start | bytes 1638400 | tf_op jit(solution)/shard_map/all_gather | solution.py:385
  60.6 1.0 copy-start.5
  61.5 22.9 %all-to-all-start.2 = ((bf16[16,2,64,256]{3,2,1,0:T(8,128)(2,1)}), bf16[16,2,64,256]{3,2,1,0:T(8,128)(2,1)S(1)}, u32[]{:S(2)}, u32[]{:S(2)}) async-start(bf16[16,2,64,256]{3,2,1,0:T(8,128)(2,1)} %copy-done.5), calls=%async_computation.2 | async-start | bytes 2097152 | tf_op jit(solution)/shard_map/all_to_all | solution.py:379
  65.2 112.7 %all-gather.7.cloned.1.call-start = ((), (), s32[]{:S(2)}) async-start(), calls=%async_computation.7 | async-start | bytes 6553600 | tf_op jit(solution)/shard_map/all_gather | solution.py:387
  84.5 1.0 copy-start.1
  86.2 1.2 copy-start.2
  87.4 26.9 %collective-permute-start.3 = (bf16[16,2,2,64,128]{4,3,2,1,0:T(8,128)(2,1)S(1)}, bf16[16,2,2,64,128]{4,3,2,1,0:T(8,128)(2,1)}, u32[]{:S(2)}, u32[]{:S(2)}) collective-permute-start(bf16[16,2,2,64,128]{4,3,2,1,0:T(8,128)(2,1)S(1)} %hold.11.own_ref), channel_id=1, source_target_pairs={{0,16},{16,32},{32,48},{48,64},{64,80},{80,96},{96,112},{1,17},{17... | collective-permute-start | bytes 3145736 | tf_op jit(solution)/shard_map/ppermute | solution.py:381
  91.7 28.1 %collective-permute-start.4 = (bf16[16,2,2,64,128]{4,3,2,1,0:T(8,128)(2,1)S(1)}, bf16[16,2,2,64,128]{4,3,2,1,0:T(8,128)(2,1)}, u32[]{:S(2)}, u32[]{:S(2)}) collective-permute-start(bf16[16,2,2,64,128]{4,3,2,1,0:T(8,128)(2,1)S(1)} %hold.11.own_ref), channel_id=1, source_target_pairs={{16,0},{32,16},{48,32},{64,48},{80,64},{96,80},{112,96},{17,1},{33... | collective-permute-start | bytes 3145736 | tf_op jit(solution)/shard_map/ppermute | solution.py:381
  93.0 45.5 %collective-permute-start.1 = (bf16[16,2,2,64,128]{4,3,2,1,0:T(8,128)(2,1)S(1)}, bf16[16,2,2,64,128]{4,3,2,1,0:T(8,128)(2,1)}, u32[]{:S(2)}, u32[]{:S(2)}) collective-permute-start(bf16[16,2,2,64,128]{4,3,2,1,0:T(8,128)(2,1)S(1)} %hold.10.own_ref), channel_id=1, source_target_pairs={{0,16},{16,32},{32,48},{48,64},{64,80},{80,96},{96,112},{1,17},{17... | collective-permute-start | bytes 3145736 | tf_op jit(solution)/shard_map/ppermute | solution.py:383
  98.5 49.5 %collective-permute-start.2 = (bf16[16,2,2,64,128]{4,3,2,1,0:T(8,128)(2,1)S(1)}, bf16[16,2,2,64,128]{4,3,2,1,0:T(8,128)(2,1)}, u32[]{:S(2)}, u32[]{:S(2)}) collective-permute-start(bf16[16,2,2,64,128]{4,3,2,1,0:T(8,128)(2,1)S(1)} %hold.10.own_ref), channel_id=1, source_target_pairs={{16,0},{32,16},{48,32},{64,48},{80,64},{96,80},{112,96},{17,1},{33... | collective-permute-start | bytes 3145736 | tf_op jit(solution)/shard_map/ppermute | solution.py:383
  128.7 13.8 %collective-permute-start.5 = (bf16[16,1,64,128]{3,2,1,0:T(8,128)(2,1)S(1)}, bf16[16,1,64,128]{3,2,1,0:T(8,128)(2,1)S(1)}, u32[]{:S(2)}, u32[]{:S(2)}) collective-permute-start(bf16[16,1,64,128]{3,2,1,0:T(8,128)(2,1)S(1)} %get-tuple-element.23), channel_id=1, source_target_pairs={{48,112},{49,113},{50,114},{51,115},{52,116},{53,117},{54,118},{55... | collective-permute-start | bytes 786440 | tf_op jit(solution)/shard_map/ppermute | solution.py:406
  139.2 28.4 %collective-permute-start.6 = (bf16[1,64,5120]{2,1,0:T(8,128)(2,1)}, bf16[1,64,5120]{2,1,0:T(8,128)(2,1)}, u32[]{:S(2)}, u32[]{:S(2)}) collective-permute-start(bf16[1,64,5120]{2,1,0:T(8,128)(2,1)} %hold.13), channel_id=1, source_target_pairs={{0,16},{16,32},{32,48},{48,64},{64,80},{80,96},{96,112},{1,17},{17... | collective-permute-start | bytes 1966088 | tf_op jit(solution)/shard_map/ppermute | solution.py:409
  143.4 24.2 %all-to-all-start.3 = ((bf16[16,2,64,128]{3,2,1,0:T(8,128)(2,1)}), bf16[16,2,64,128]{3,2,1,0:T(8,128)(2,1)S(1)}, u32[]{:S(2)}, u32[]{:S(2)}) async-start(bf16[16,2,64,128]{3,2,1,0:T(8,128)(2,1)} %pad_maximum_fusion.rest_1_), calls=%async_computation.3 | async-start | bytes 1048576 | tf_op jit(solution)/shard_map/all_to_all | solution.py:412
  157.0 0.7 copy-start.9
  176.6 0.7 copy-start.11
  177.4 0.6 copy-start.13
  177.9 1.0 copy-start.10
  177.9 1.7 copy-start.12
  178.7 40.1 %collective-permute-start.12 = (bf16[4,2,2,256,640]{4,3,2,1,0:T(8,128)(2,1)}, bf16[4,2,2,256,640]{4,3,2,1,0:T(8,128)(2,1)}, u32[]{:S(2)}, u32[]{:S(2)}) collective-permute-start(bf16[4,2,2,256,640]{4,3,2,1,0:T(8,128)(2,1)} %hold.15.wo_ref), channel_id=1, source_target_pairs={{0,1},{1,0},{2,3},{3,2},{4,5},{5,4},{6,7},{7,6},{8,9},{9,8},{10,11... | collective-permute-start | bytes 15728648 | tf_op jit(solution)/shard_map/ppermute | solution.py:416
  178.9 0.7 collective-permute-start.7
  180.5 16.5 %all-to-all-start.4 = ((bf16[16,2,64,128]{3,2,1,0:T(8,128)(2,1)}), bf16[16,2,64,128]{3,2,1,0:T(8,128)(2,1)S(1)}, u32[]{:S(2)}, u32[]{:S(2)}) async-start(bf16[16,2,64,128]{3,2,1,0:T(8,128)(2,1)} %pad_maximum_fusion.1), calls=%async_computation.4 | async-start | bytes 1048576 | tf_op jit(solution)/shard_map/all_to_all | solution.py:417
  184.6 15.6 %collective-permute-start.13 = (bf16[16,2,64,128]{3,2,1,0:T(8,128)(2,1)S(1)}, bf16[16,2,64,128]{3,2,1,0:T(8,128)(2,1)S(1)}, u32[]{:S(2)}, u32[]{:S(2)}) collective-permute-start(bf16[16,2,64,128]{3,2,1,0:T(8,128)(2,1)S(1)} %hold.12.rest_1_.mine_ref), channel_id=1, source_target_pairs={{0,16},{16,32},{32,48},{48,0},{64,80},{80,96},{96,112},{112,64},{1... | collective-permute-start | bytes 1572872 | tf_op jit(solution)/shard_map/ppermute | solution.py:397
  184.7 16.3 %collective-permute-start.14 = (bf16[16,2,64,128]{3,2,1,0:T(8,128)(2,1)S(1)}, bf16[16,2,64,128]{3,2,1,0:T(8,128)(2,1)S(1)}, u32[]{:S(2)}, u32[]{:S(2)}) collective-permute-start(bf16[16,2,64,128]{3,2,1,0:T(8,128)(2,1)S(1)} %hold.12.rest_1_.mine_ref), channel_id=1, source_target_pairs={{16,0},{32,16},{48,32},{0,48},{80,64},{96,80},{112,96},{64,112},{1... | collective-permute-start | bytes 1572872 | tf_op jit(solution)/shard_map/ppermute | solution.py:398
  196.9 16.1 %collective-permute-start.8 = (bf16[16,2,64,128]{3,2,1,0:T(8,128)(2,1)S(1)}, bf16[16,2,64,128]{3,2,1,0:T(8,128)(2,1)S(1)}, u32[]{:S(2)}, u32[]{:S(2)}) collective-permute-start(bf16[16,2,64,128]{3,2,1,0:T(8,128)(2,1)S(1)} %all-to-all-done.4.mine_ref), channel_id=1, source_target_pairs={{0,16},{16,32},{32,48},{48,0},{64,80},{80,96},{96,112},{112,64},{1... | collective-permute-start | bytes 1572872 | tf_op jit(solution)/shard_map/ppermute | solution.py:397
  197.0 16.2 %collective-permute-start.9 = (bf16[16,2,64,128]{3,2,1,0:T(8,128)(2,1)S(1)}, bf16[16,2,64,128]{3,2,1,0:T(8,128)(2,1)S(1)}, u32[]{:S(2)}, u32[]{:S(2)}) collective-permute-start(bf16[16,2,64,128]{3,2,1,0:T(8,128)(2,1)S(1)} %all-to-all-done.4.mine_ref), channel_id=1, source_target_pairs={{16,0},{32,16},{48,32},{0,48},{80,64},{96,80},{112,96},{64,112},{1... | collective-permute-start | bytes 1572872 | tf_op jit(solution)/shard_map/ppermute | solution.py:398
  200.9 17.8 %collective-permute-start.15 = (bf16[8,2,64,128]{3,2,1,0:T(8,128)(2,1)}, bf16[8,2,64,128]{3,2,1,0:T(8,128)(2,1)}, u32[]{:S(2)}, u32[]{:S(2)}) collective-permute-start(bf16[8,2,64,128]{3,2,1,0:T(8,128)(2,1)} %slice.23), channel_id=1, source_target_pairs={{0,16},{16,32},{32,48},{48,0},{64,80},{80,96},{96,112},{112,64},{1... | collective-permute-start | bytes 786440 | tf_op jit(solution)/shard_map/ppermute | solution.py:399
  201.7 17.1 %collective-permute-start.16 = (bf16[8,2,64,128]{3,2,1,0:T(8,128)(2,1)}, bf16[8,2,64,128]{3,2,1,0:T(8,128)(2,1)}, u32[]{:S(2)}, u32[]{:S(2)}) collective-permute-start(bf16[8,2,64,128]{3,2,1,0:T(8,128)(2,1)} %slice.24), channel_id=1, source_target_pairs={{16,0},{32,16},{48,32},{0,48},{80,64},{96,80},{112,96},{64,112},{1... | collective-permute-start | bytes 786440 | tf_op jit(solution)/shard_map/ppermute | solution.py:400
  213.0 12.3 %collective-permute-start.10 = (bf16[8,2,64,128]{3,2,1,0:T(8,128)(2,1)S(1)}, bf16[8,2,64,128]{3,2,1,0:T(8,128)(2,1)S(1)}, u32[]{:S(2)}, u32[]{:S(2)}) collective-permute-start(bf16[8,2,64,128]{3,2,1,0:T(8,128)(2,1)S(1)} %slice.21), channel_id=1, source_target_pairs={{0,16},{16,32},{32,48},{48,0},{64,80},{80,96},{96,112},{112,64},{1... | collective-permute-start | bytes 786440 | tf_op jit(solution)/shard_map/ppermute | solution.py:399
  213.2 12.2 %collective-permute-start.11 = (bf16[8,2,64,128]{3,2,1,0:T(8,128)(2,1)S(1)}, bf16[8,2,64,128]{3,2,1,0:T(8,128)(2,1)S(1)}, u32[]{:S(2)}, u32[]{:S(2)}) collective-permute-start(bf16[8,2,64,128]{3,2,1,0:T(8,128)(2,1)S(1)} %slice.22), channel_id=1, source_target_pairs={{16,0},{32,16},{48,32},{0,48},{80,64},{96,80},{112,96},{64,112},{1... | collective-permute-start | bytes 786440 | tf_op jit(solution)/shard_map/ppermute | solution.py:400
  232.0 19.1 %copy-start.3 = (bf16[2,64,5120]{2,1,0:T(8,128)(2,1)S(1)}, bf16[2,64,5120]{2,1,0:T(8,128)(2,1)}, u32[]{:S(2)}) copy-start(bf16[2,64,5120]{2,1,0:T(8,128)(2,1)} %hidden_ref.3) | copy-start | bytes 3932164
  232.1 19.0 %copy-start.8 = (bf16[64,5120]{1,0:T(8,128)(2,1)S(1)}, bf16[64,5120]{1,0:T(8,128)(2,1)}, u32[]{:S(2)}) copy-start(bf16[64,5120]{1,0:T(8,128)(2,1)} %entering_ref.1) | copy-start | bytes 1966084
Sparse Core Ops, SparseCore 0:
  45.1 29.0 all-gather.4
  86.3 56.1 all-gather.6
